TPU v7x, 32 devices: a whole 2x2x4 slice. The times are simulated.
32 devices in a mesh: ctx: 16 (over z, x, core), head: 2 (over y).
Axes of the slice: x: 2, y: 2, z: 4, core: 2. Of those that a mesh axis runs over, the one named last changes fastest.
Arguments:
- hidden_in: bfloat16 [16384, 2048], P('ctx', 'head'), may hold values from -6 to 6
- proj_weight: bfloat16 [2048, 3584], P(None, 'head'), may hold values from -0.125 to 0.125
- conv_weight: float32 [3, 1024], P(None, 'head'), may hold values from -3 to 3
- norm_gain: float32 [1024], P('head'), may hold values from 0.1 to 1.9
- out_weight: bfloat16 [1024, 2048], P('head'), may hold values from -0.25 to 0.25
Outputs:
- layer_out: bfloat16 [16384, 2048], P('ctx', 'head')
All inputs are finite; a program needn't handle non-finite values.
Results may differ from a plain program's by a relative error of at most 0.014.
Values may be sent and summed in bfloat16 or wider, within the bound.
No kernel may reach another device: no remote copies, remote signals or barrier semaphores. Data moves between devices by JAX's collectives and lax.ppermute only.
A program may use at most 128 MiB of HBM per device.

v0:
```python
import functools

import jax
import jax.numpy as jnp
import numpy as np
from jax import lax
from jax.experimental import pallas as pl
from jax.experimental.pallas import tpu as pltpu
from jax.sharding import PartitionSpec as P

DV = 64
FQK = 16
WIN = 64
CONV = 3
LANES = 128
FEATS = 160
QFEATS = 256
EDGE = 16
HALO = EDGE + 2 * WIN
PLANE = 4
F32 = jnp.float32
BF16 = jnp.bfloat16


def call(body, out_shape, *, flops=0, moved=0, vmem=48 << 20, **kwargs):
    return pl.pallas_call(
        body,
        out_shape=out_shape,
        compiler_params=pltpu.CompilerParams(vmem_limit_bytes=vmem),
        cost_estimate=pl.CostEstimate(flops=flops, bytes_accessed=moved, transcendentals=0),
        **kwargs,
    )


def feature_tables(heads):
    first = [FQK] + [FQK] * FQK
    second = [FQK] + list(range(FQK))
    weight = [1.0] + [1.0 / FQK**0.5] * FQK
    for i in range(FQK):
        for j in range(i, FQK):
            first.append(i)
            second.append(j)
            weight.append((1.0 if i == j else 2.0) / (2.0 * FQK))
    sel_a = np.zeros((heads, QFEATS, LANES), np.float32)
    sel_b = np.zeros((heads, QFEATS, LANES), np.float32)
    sel_w = np.zeros((heads, QFEATS, LANES), np.float32)
    for h in range(heads):
        for f, (i, j, w) in enumerate(zip(first, second, weight)):
            sel_a[h, f, (h * FQK + i) % LANES] = 1.0
            sel_b[h, f, (h * FQK + j) % LANES] = 1.0
            sel_w[h, f, (h * FQK + i) % LANES] = w
    return tuple(jnp.asarray(t, BF16) for t in (sel_a, sel_b, sel_w))


def mean_table():
    block = np.kron(np.eye(LANES // DV), np.ones((DV, DV))) / DV
    return jnp.asarray(np.concatenate([block, block], 0), BF16)


def head_mean(values, table):
    high = values.astype(BF16)
    low = (values - high.astype(F32)).astype(BF16)
    return jnp.dot(jnp.concatenate([high, low], 1), table, preferred_element_type=F32)


def nt_dot(a, b):
    return lax.dot_general(a, b, (((1,), (1,)), ((), ())), preferred_element_type=F32)


def with_one(vectors, lane, h):
    return jnp.where(lane == ((h + 1) * FQK) % LANES, 1.0, vectors).astype(BF16)


def arrange_kernel(w_ref, o_ref, *, heads):
    per_head = 2 * FQK + 3 * DV
    w = w_ref[...]
    at = 0
    for begin, width in ((0, FQK), (FQK, FQK), (2 * FQK, DV), (2 * FQK + DV, DV), (2 * FQK + 2 * DV, DV)):
        parts = [w[:, h * per_head + begin : h * per_head + begin + width] for h in range(heads)]
        total = heads * width
        padded = -(-total // LANES) * LANES
        if padded > total:
            parts.append(jnp.zeros((w.shape[0], padded - total), w.dtype))
        o_ref[:, at : at + padded] = jnp.concatenate(parts, 1)
        at += padded


def block_kernel(j_ref, mean_ref, conv_ref, sel_w_ref, sel_b_ref, w_ref, *refs, n, heads, extra, others, sends):
    xs, refs = refs[:n], refs[n:]
    prev_ref = None
    if not extra:
        prev_ref, refs = refs[0], refs[1:]
    other_refs, refs = refs[:others], refs[others:]
    q_ref, k_ref, v_ref, wq_ref, wk_ref, halo_ref, s_ref = refs[:7]
    send_refs, (ext_ref,) = refs[7 : 7 + sends], refs[7 + sends :]
    rows, depth = v_ref.shape[0], xs[0].shape[1]
    me = j_ref[0]

    def project(begin, width, skip):
        total = None
        for r in range(n):
            src = lax.rem(me - r + n, n)
            from_rows = pl.ds(pl.multiple_of(src * depth, depth), depth)
            part = jnp.dot(xs[r][skip:, :], w_ref[from_rows, begin : begin + width], preferred_element_type=F32)
            total = part if total is None else total + part
        return total.astype(BF16)

    widths = [ref.shape[1] for ref in (q_ref, k_ref, v_ref, wq_ref, wk_ref)]
    starts = [sum(widths[:i]) for i in range(5)]
    k_ref[...] = project(starts[1], widths[1], extra)
    raw = project(starts[2], widths[2], 0)
    if extra:
        ext_ref[...] = raw.astype(F32)
    else:
        ext_ref[0:EDGE, :] = prev_ref[0:EDGE, :].astype(F32)
        ext_ref[EDGE:, :] = raw.astype(F32)
    halo_ref[0:EDGE, :] = raw[raw.shape[0] - EDGE :]
    total = jnp.zeros((rows, widths[2]), F32)
    for tap in range(CONV):
        total = total + conv_ref[tap : tap + 1, :] * ext_ref[EDGE - tap : EDGE - tap + rows, :]
    v_ref[...] = total.astype(BF16)
    halo_ref[EDGE : EDGE + WIN, :] = v_ref[rows - WIN : rows, :]

    lane = lax.broadcasted_iota(jnp.int32, (rows, LANES), 1)
    low_half = lax.broadcasted_iota(jnp.int32, (FEATS, LANES), 1) < DV
    k = k_ref[...].astype(F32)
    for p in range(heads * DV // LANES):
        v = v_ref[:, p * LANES : (p + 1) * LANES]
        both = []
        for h in (2 * p, 2 * p + 1):
            own = with_one(k, lane, h)
            phi = nt_dot(sel_w_ref[h, 0:FEATS, :], own) * nt_dot(sel_b_ref[h, 0:FEATS, :], own)
            both.append(jnp.dot(phi.astype(BF16), v, preferred_element_type=F32))
        s_ref[p] = jnp.where(low_half, both[0], both[1])
    for r in range(sends):
        pair = jnp.bitwise_xor(j_ref[1], r)
        total = s_ref[pair]
        for ref in other_refs:
            total = total + ref[pair]
        send_refs[r][...] = total.astype(BF16)

    q_ref[...] = project(starts[0], widths[0], extra)
    for ref, start, width, scale in (
        (wk_ref, starts[4], widths[4], 1.0),
        (wq_ref, starts[3], widths[3], 1.0 / DV**0.5),
    ):
        got = project(start, width, extra)
        for p in range(width // LANES):
            cols = slice(p * LANES, (p + 1) * LANES)
            x = got[:, cols].astype(F32)
            x = x * lax.rsqrt(head_mean(x * x, mean_ref[...]) + 1e-6)
            ref[:, cols] = x.astype(BF16) * jnp.asarray(scale, BF16)
    halo_ref[EDGE + WIN : HALO, :] = wk_ref[rows - WIN : rows, :]


def attend_kernel(
    a_ref, sel_a_ref, sel_b_ref, prev_ref, q_ref, k_ref, v_ref, wq_ref, wk_ref, phi_ref, lin_ref, win_ref,
    vext_ref, kext_ref, *, heads, first
):
    rows = q_ref.shape[0]
    tile = 128
    span = tile + WIN
    vext_ref[0:WIN, :] = prev_ref[EDGE : EDGE + WIN, :]
    vext_ref[WIN : WIN + rows, :] = v_ref[...]
    kext_ref[0:WIN, :] = prev_ref[EDGE + WIN : HALO, :]
    kext_ref[WIN : WIN + rows, :] = wk_ref[...]
    lane = lax.broadcasted_iota(jnp.int32, (rows, LANES), 1)
    low_half = lane < DV
    causal = lax.broadcasted_iota(jnp.int32, (rows, rows), 1) <= lax.broadcasted_iota(jnp.int32, (rows, rows), 0)
    col = lax.broadcasted_iota(jnp.int32, (tile, span), 1)
    ahead = col - lax.broadcasted_iota(jnp.int32, (tile, span), 0)
    band = (ahead >= 1) & (ahead <= WIN)
    first_band = band
    if first:
        first_band = band & (col >= jnp.where(a_ref[2] == 0, WIN, 0))
    q = q_ref[...]
    q_full = q.astype(F32)
    k = k_ref[...]
    for p in range(heads * DV // LANES):
        cols = slice(p * LANES, (p + 1) * LANES)
        v = v_ref[:, cols]
        both = []
        for h in (2 * p, 2 * p + 1):
            own = with_one(q_full, lane, h)
            phi = nt_dot(own, sel_a_ref[h]) * nt_dot(own, sel_b_ref[h])
            phi_ref[:, h * QFEATS : (h + 1) * QFEATS] = phi.astype(BF16)
            own = jnp.where((lane >= h * FQK) & (lane < (h + 1) * FQK), q, jnp.zeros_like(q))
            t = nt_dot(own, k) * (1.0 / FQK**0.5) + 1.0
            kernel = jnp.where(causal, 0.5 * (t * t) + 0.5, 0.0).astype(BF16)
            both.append(jnp.dot(kernel, v, preferred_element_type=F32))
        lin_ref[:, cols] = jnp.where(low_half, both[0], both[1])
        for i in range(rows // tile):
            here = slice(i * tile, (i + 1) * tile)
            wq = wq_ref[here, cols]
            keys = kext_ref[i * tile : i * tile + span, cols]
            values = vext_ref[i * tile : i * tile + span, cols]
            both = []
            for half in range(2):
                keep = low_half[0:tile] if half == 0 else ~low_half[0:tile]
                scores = nt_dot(jnp.where(keep, wq, jnp.zeros_like(wq)), keys)
                expo = jnp.where(first_band if i == 0 else band, jnp.exp(scores), 0.0)
                weights = expo * (1.0 / jnp.sum(expo, axis=1, keepdims=True))
                both.append(jnp.dot(weights.astype(BF16), values, preferred_element_type=F32))
            win_ref[here, cols] = jnp.where(low_half[0:tile], both[0], both[1])


def finish_kernel(a_ref, mean_ref, gain_ref, *refs, heads, before):
    pairs = heads * DV // LANES
    prior_refs, refs = refs[:pairs], refs[pairs:]
    states, (phi_ref, lin_ref, win_ref, mix_ref, held_ref) = refs[:before], refs[before:]
    rows = phi_ref.shape[0]
    for r in range(pairs):
        held_ref[r] = prior_refs[r][...].astype(F32)
    low_half = lax.broadcasted_iota(jnp.int32, (rows, LANES), 1) < DV
    for p in range(pairs):
        cols = slice(p * LANES, (p + 1) * LANES)
        state = held_ref[jnp.bitwise_xor(a_ref[1], p)]
        for ref in states:
            state = state + ref[p]
        state = jnp.concatenate([state.astype(BF16), jnp.zeros((QFEATS - FEATS, LANES), BF16)], 0)
        both = [
            jnp.dot(phi_ref[:, h * QFEATS : (h + 1) * QFEATS], state, preferred_element_type=F32)
            for h in (2 * p, 2 * p + 1)
        ]
        lin = lin_ref[:, cols] + jnp.where(low_half, both[0], both[1])
        scale = lax.rsqrt(head_mean(lin * lin, mean_ref[...]) + 1e-5)
        mix_ref[:, cols] = (lin * scale * gain_ref[:, cols] + win_ref[:, cols]).astype(BF16)


def output_kernel(a_ref, own_ref, w_ref, *refs, n, offset, parts):
    others, weights, (o_ref, held_ref, sem) = refs[: n - 1], refs[n - 1 : n - 1 + parts * (n - 1)], refs[-3:]
    cols = held_ref.shape[1]
    mine = pl.ds(pl.multiple_of(a_ref[0] * cols, cols), cols)
    total = jnp.dot(own_ref[...], w_ref[:, mine], preferred_element_type=F32).astype(BF16).astype(F32)
    for r, m_ref in enumerate(others):
        part = None
        for i in range(parts):
            ref = weights[r * parts + i]
            depth = ref.shape[0]
            at = depth * (jnp.bitwise_xor(a_ref[2] % 2, i) if parts > 1 else 0)
            got = jnp.dot(m_ref[:, pl.ds(pl.multiple_of(at, depth), depth)], ref[...], preferred_element_type=F32)
            part = got if part is None else part + got
        total = total + part.astype(BF16).astype(F32)
    held_ref[...] = total.astype(BF16)
    copy = pltpu.make_async_copy(held_ref, o_ref.at[pl.ds(offset, held_ref.shape[0]), :], sem)
    copy.start()
    copy.wait()


def pick_kernel(a_ref, w_ref, o_ref):
    o_ref[...] = w_ref[...]


def exchange(value, axis, flip):
    count = lax.axis_size(axis)
    return lax.ppermute(value, axis, [(i, i ^ flip) for i in range(count)])


def plane_kernel(a_ref, *refs):
    helds, plane_ref, ahead_refs = refs[:PLANE], refs[PLANE], refs[PLANE + 1 :]
    place = a_ref[1]
    held = [ref[...].astype(F32) for ref in helds]
    plane_ref[...] = (held[0] + held[1] + held[2] + held[3]).astype(BF16)
    for r in range(PLANE):
        total = jnp.zeros_like(held[0])
        for s in range(PLANE):
            before = jnp.bitwise_xor(place, s) < jnp.bitwise_xor(place, r)
            total = total + held[s] * before.astype(F32)
        ahead_refs[r][...] = total


def earlier_kernel(_, *refs, planes):
    ahead_refs, earlier_refs, back_refs = refs[:PLANE], refs[PLANE : PLANE + planes], refs[PLANE + planes :]
    earlier = jnp.zeros(ahead_refs[0].shape, F32)
    for ref in earlier_refs:
        earlier = earlier + ref[...].astype(F32)
    for r in range(PLANE):
        back_refs[r][...] = (ahead_refs[r][...] + earlier).astype(BF16)


def after(value, earlier):
    return lax.optimization_barrier((value, earlier))[0]


def prior_in_planes(own, places, beside):
    ctx = lax.axis_size("ctx")
    whole = pl.BlockSpec(memory_space=pltpu.VMEM)
    scalar = pl.BlockSpec(memory_space=pltpu.SMEM)
    narrow = jax.ShapeDtypeStruct((FEATS, LANES), BF16)
    wide = jax.ShapeDtypeStruct((FEATS, LANES), F32)
    held = [own[0]] + [exchange(own[r], "ctx", r) for r in range(1, PLANE)]
    plane, *ahead = call(
        plane_kernel,
        [narrow] + [wide] * PLANE,
        in_specs=[scalar] + [whole] * PLANE,
        out_specs=[whole] * (1 + PLANE),
        moved=24 * FEATS * LANES,
        vmem=4 << 20,
    )(after(places, beside[0]), *held)
    earlier = []
    for d in range(1, ctx // PLANE):
        pairs = [(i, i + d * PLANE) for i in range(ctx - d * PLANE)]
        earlier.append(lax.ppermute(plane, "ctx", pairs))
    back = call(
        functools.partial(earlier_kernel, planes=len(earlier)),
        [narrow] * PLANE,
        in_specs=[scalar] + [whole] * (PLANE + len(earlier)),
        out_specs=[whole] * PLANE,
        moved=24 * FEATS * LANES,
        vmem=4 << 20,
    )(after(places, beside[1]), *ahead, *earlier)
    return back[0], [back[0]] + [exchange(back[r], "ctx", r) for r in range(1, PLANE)]


def prior_by_doubling(total, position):
    ctx = lax.axis_size("ctx")
    prior = jnp.zeros_like(total)
    bit = 1
    while bit < ctx:
        got = exchange(total.astype(BF16), "ctx", bit).astype(F32)
        prior = prior + jnp.where((position & bit) != 0, got, 0.0)
        total = total + got
        bit *= 2
    return [prior[p].astype(BF16) for p in range(total.shape[0])]


def per_device(hidden_in, proj_weight, conv_weight, norm_gain, out_weight):
    n = lax.axis_size("head")
    ctx = lax.axis_size("ctx")
    me = lax.axis_index("head").astype(jnp.int32)
    position = lax.axis_index("ctx").astype(jnp.int32)
    row_count = hidden_in.shape[0]
    model = proj_weight.shape[0]
    heads = out_weight.shape[0] // DV
    width = heads * DV
    pairs = width // LANES
    in_planes = pairs == PLANE and ctx % PLANE == 0
    places = jnp.stack([me, position % PLANE if in_planes else jnp.zeros_like(position), position])
    hidden_in, places = lax.optimization_barrier((hidden_in, places))
    step = row_count // 8
    blocks = [(0, 2 * step), (2 * step, 2 * step), (4 * step, 2 * step), (6 * step, step), (7 * step, step)]
    last = len(blocks) - 1
    sel_a, sel_b, sel_w = feature_tables(heads)
    means = mean_table()
    gain = norm_gain.reshape(1, width)
    whole = pl.BlockSpec(memory_space=pltpu.VMEM)
    scalar = pl.BlockSpec(memory_space=pltpu.SMEM)

    def from_head(value, by):
        return lax.ppermute(value, "head", [(i, (i + by) % n) for i in range(n)])

    pieces = {}
    for b in [last] + list(range(last)):
        at, rows = blocks[b]
        extra = EDGE if b == last else 0
        own = hidden_in[at - extra : at + rows]
        pieces[b] = [own] + [from_head(own, r) for r in range(1, n)]

    cols = out_weight.shape[1] // n
    out_parts = 2 if width // 2 % LANES == 0 and ctx % 2 == 0 else 1
    share = width // out_parts
    fetched = []
    for r in range(1, n):
        block = call(
            pick_kernel,
            jax.ShapeDtypeStruct((share, cols), BF16),
            grid_spec=pltpu.PrefetchScalarGridSpec(
                num_scalar_prefetch=1,
                grid=(1,),
                in_specs=[
                    pl.BlockSpec((share, cols), functools.partial(lambda i, a, r: (a[2] % out_parts, (a[0] + r) % n), r=r))
                ],
                out_specs=pl.BlockSpec((share, cols), lambda i, a: (0, 0)),
            ),
            moved=4 * share * cols,
            vmem=8 << 20,
        )(places, out_weight)
        fetched.append(from_head(after(block, pieces[0][1]), r))

    qk_width = -(-heads * FQK // LANES) * LANES
    arranged_width = 2 * qk_width + 3 * width
    slab = 256
    arranged = call(
        functools.partial(arrange_kernel, heads=heads),
        jax.ShapeDtypeStruct((model, arranged_width), BF16),
        grid=(model // slab,),
        in_specs=[pl.BlockSpec((slab, proj_weight.shape[1]), lambda i: (i, 0))],
        out_specs=pl.BlockSpec((slab, arranged_width), lambda i: (i, 0)),
        moved=4 * model * arranged_width,
        vmem=32 << 20,
    )(proj_weight)

    def do_block(b, prev, behind, others=()):
        rows = blocks[b][1]
        extra = EDGE if prev is None else 0
        sends = PLANE if in_planes and others else 0
        tokens = places if behind is None else after(places, behind)
        shapes = [jax.ShapeDtypeStruct((rows, w), BF16) for w in (qk_width, qk_width, width, width, width)]
        shapes.append(jax.ShapeDtypeStruct((HALO, width), BF16))
        shapes.append(jax.ShapeDtypeStruct((pairs, FEATS, LANES), F32))
        shapes += [jax.ShapeDtypeStruct((FEATS, LANES), BF16)] * sends
        operands = [tokens, means, conv_weight, sel_w, sel_b, arranged, *pieces[b]]
        if prev is not None:
            operands.append(prev)
        operands += others
        return call(
            functools.partial(
                block_kernel, n=n, heads=heads, extra=extra, others=len(others), sends=sends
            ),
            shapes,
            in_specs=[scalar] + [whole] * (len(operands) - 1),
            out_specs=[whole] * len(shapes),
            scratch_shapes=[pltpu.VMEM((EDGE + rows, width), F32)],
            flops=2 * rows * model * arranged_width + 6 * rows * FEATS * LANES * heads,
            moved=2 * model * arranged_width,
            vmem=32 << 20,
        )(*operands)

    def attend(b, prev):
        rows = blocks[b][1]
        q, k, v, wq, wk = done[b][:5]
        return call(
            functools.partial(attend_kernel, heads=heads, first=b == 0),
            [jax.ShapeDtypeStruct((rows, heads * QFEATS), BF16)] + [jax.ShapeDtypeStruct((rows, width), F32)] * 2,
            in_specs=[scalar] + [whole] * 8,
            out_specs=[whole] * 3,
            scratch_shapes=[pltpu.VMEM((WIN + rows, width), BF16)] * 2,
            flops=heads * rows * 4096 * 256,
            moved=16 * rows * width,
            vmem=16 << 20,
        )(places, sel_a, sel_b, prev, q, k, v, wq, wk)

    done, attended = {}, {}
    done[last] = do_block(last, None, None)
    halo = lax.ppermute(done[last][5], "ctx", [(i, i + 1) for i in range(ctx - 1)])
    for b in range(last):
        prev = halo if b == 0 else done[b - 1][5]
        others = [done[c][6] for c in [last] + list(range(b))] if b == last - 1 else ()
        done[b] = do_block(b, prev, attended[b - 1][1] if b else None, others)
        if b < last - 1:
            attended[b] = attend(b, prev)

    for b in (last - 1, last):
        attended[b] = attend(b, done[b - 1][5])
    if in_planes:
        beside = [attended[b][1] for b in (last - 1, last)]
        mark, priors = prior_in_planes(done[last - 1][7:], places, beside)
    else:
        mark = sum(done[b][6] for b in range(last + 1))
        priors = prior_by_doubling(mark, position)

    out_rows = []
    for got in fetched:
        out_rows += [got] + ([exchange(after(got, mark), "ctx", 1)] if out_parts > 1 else [])

    result = mixed = None
    for b in (3, 0, 1, 2, 4):
        at, rows = blocks[b]
        mixed = call(
            functools.partial(finish_kernel, heads=heads, before=b),
            jax.ShapeDtypeStruct((rows, width), BF16),
            in_specs=[scalar] + [whole] * (2 + pairs + b + 3),
            out_specs=whole,
            scratch_shapes=[pltpu.VMEM((pairs, FEATS, LANES), F32)],
            flops=6 * rows * QFEATS * LANES * heads,
            moved=12 * rows * width,
            vmem=16 << 20,
        )(places if mixed is None else after(places, mixed), means, gain, *priors, *[done[c][6] for c in range(b)], *attended[b])
        operands = [places, mixed, out_weight] + [from_head(mixed, r) for r in range(1, n)] + out_rows
        specs = [scalar] + [whole] * (len(operands) - 1)
        aliases = {}
        if result is not None:
            aliases = {len(operands): 0}
            operands.append(result)
            specs.append(pl.BlockSpec(memory_space=pl.ANY))
        result = call(
            functools.partial(output_kernel, n=n, offset=at, parts=out_parts),
            jax.ShapeDtypeStruct((row_count, cols), BF16),
            in_specs=specs,
            out_specs=pl.BlockSpec(memory_space=pl.ANY),
            scratch_shapes=[pltpu.VMEM((rows, cols), BF16), pltpu.SemaphoreType.DMA],
            input_output_aliases=aliases,
            flops=2 * rows * n * width * cols,
            moved=2 * n * width * cols,
            vmem=16 << 20,
        )(*operands)
    return result


def solution(mesh):
    return jax.shard_map(
        per_device,
        mesh=mesh,
        in_specs=(P("ctx", "head"), P(None, "head"), P(None, "head"), P("head"), P("head", None)),
        out_specs=P("ctx", "head"),
        check_vma=False,
    )
```

profile of v0, /device:TPU:0, one launch (start us, length us, event | category | flops | bytes accessed | tf_op | source)
XLA Modules:
  0.0 126.5 jit_solution(12860282887474983311)
XLA Ops:
  1.1 3.0 %collective-permute-start = (bf16[144,1024]{1,0:T(8,128)(2,1)S(1)}, bf16[144,1024]{1,0:T(8,128)(2,1)S(1)}, u32[]{:S(2)}, u32[]{:S(2)}) collective-permute-start(bf16[144,1024]{1,0:T(8,128)(2,1)S(1)} %slice.15.refs_0_), channel_id=1, source_target_pairs={{0,1},{1,0},{2,3},{3,2},{4,5},{5,4},{6,7},{7,6},{8,9},{9,8},{10,11... | collective-permute-start | bytes 884744 | tf_op jit(solution)/shard_map/ppermute | solution.py:350
  5.7 3.1 %copy-done.3 = bf16[2048,1792]{1,0:T(8,128)(2,1)S(1)} copy-done((bf16[2048,1792]{1,0:T(8,128)(2,1)S(1)}, bf16[2048,1792]{1,0:T(8,128)(2,1)}, u32[]{:S(2)}) %copy-start.3) | copy-done | bytes 7340056
  8.8 5.1 %shard_map.91.w_ref = bf16[2048,1792]{1,0:T(8,128)(2,1)S(1)} custom-call(bf16[2048,1792]{1,0:T(8,128)(2,1)S(1)} %copy-done.3), custom_call_target="tpu_custom_call" | custom-call | bytes 14680064 | tf_op jit(solution)/shard_map/pallas_call | solution.py:383
  14.0 3.5 %shard_map.92 = (bf16[128,128]{1,0:T(8,128)(2,1)S(1)}, bf16[128,128]{1,0:T(8,128)(2,1)S(1)}, bf16[128,512]{1,0:T(8,128)(2,1)S(1)}, bf16[128,512]{1,0:T(8,128)(2,...) custom-call(s32[3]{0:T(128)S(1)} %pad_add_fusion.j_ref.a_ref._, ...), custom_call_target="tpu_custom_call" | custom-call | flops 1065353216 | bytes 7340032 | tf_op jit(solution)/shard_map/pallas_call | solution.py:406
  17.5 1.6 %collective-permute-start.1 = (bf16[144,512]{1,0:T(8,128)(2,1)S(1)}, bf16[144,512]{1,0:T(8,128)(2,1)S(1)}, u32[]{:S(2)}, u32[]{:S(2)}) collective-permute-start(bf16[144,512]{1,0:T(8,128)(2,1)S(1)} %get-tuple-element.83), channel_id=1, source_target_pairs={{0,2},{2,4},{4,6},{6,8},{8,10},{10,12},{12,14},{14,16},{16,18},{18... | collective-permute-start | bytes 442376 | tf_op jit(solution)/shard_map/ppermute | solution.py:435
  19.2 1.8 %collective-permute-start.3 = (bf16[256,1024]{1,0:T(8,128)(2,1)S(1)}, bf16[256,1024]{1,0:T(8,128)(2,1)S(1)}, u32[]{:S(2)}, u32[]{:S(2)}) collective-permute-start(bf16[256,1024]{1,0:T(8,128)(2,1)S(1)} %get-tuple-element.158.refs_0_), channel_id=1, source_target_pairs={{0,1},{1,0},{2,3},{3,2},{4,5},{5,4},{6,7},{7,6},{8,9},{9,8},{10,11... | collective-permute-start | bytes 1572872 | tf_op jit(solution)/shard_map/ppermute | solution.py:350
  22.3 1.8 %collective-permute-start.4 = (bf16[256,1024]{1,0:T(8,128)(2,1)S(1)}, bf16[256,1024]{1,0:T(8,128)(2,1)S(1)}, u32[]{:S(2)}, u32[]{:S(2)}) collective-permute-start(bf16[256,1024]{1,0:T(8,128)(2,1)S(1)} %get-tuple-element.157.refs_0_), channel_id=1, source_target_pairs={{0,1},{1,0},{2,3},{3,2},{4,5},{5,4},{6,7},{7,6},{8,9},{9,8},{10,11... | collective-permute-start | bytes 1572872 | tf_op jit(solution)/shard_map/ppermute | solution.py:350
  25.0 4.8 %shard_map.93 = (bf16[256,128]{1,0:T(8,128)(2,1)S(1)}, bf16[256,128]{1,0:T(8,128)(2,1)S(1)}, bf16[256,512]{1,0:T(8,128)(2,1)S(1)}, bf16[256,512]{1,0:T(8,128)(2,...) custom-call(s32[3]{0:T(128)S(1)} %pad_add_fusion.j_ref.a_ref._, ...), custom_call_target="tpu_custom_call" | custom-call | flops 2130706432 | bytes 7340032 | tf_op jit(solution)/shard_map/pallas_call | solution.py:406
  29.8 5.1 %shard_map.94 = (bf16[256,2048]{1,0:T(8,128)(2,1)S(1)}, f32[256,512]{1,0:T(8,128)S(1)}, f32[256,512]{1,0:T(8,128)S(1)}) custom-call(s32[3]{0:T(128)S(1)} %pad_add_fusion.j_ref.a_ref._, bf16[8,256,128]{2,1,0:T(8,128)(2,1)S(1)} %copy-done.7, bf16[8,256,128]{2,1,0:T(8,128)(2,1)S(1)} %copy-done.1, bf16[144,512]{1,0:T(8,128)(2,1)S(1)} %collective-permute-done.1.refs_2_.prev_ref, ...), custom_call_target="tpu_custom_call" | custom-call | flops 2147483648 | bytes 2097152 | tf_op jit(solution)/shard_map/pallas_call | solution.py:422
  34.9 4.8 %shard_map.95 = (bf16[256,128]{1,0:T(8,128)(2,1)S(1)}, bf16[256,128]{1,0:T(8,128)(2,1)S(1)}, bf16[256,512]{1,0:T(8,128)(2,1)S(1)}, bf16[256,512]{1,0:T(8,128)(2,...) custom-call(s32[3]{0:T(128)S(1)} %pad_add_fusion.j_ref.a_ref._, ...), custom_call_target="tpu_custom_call" | custom-call | flops 2130706432 | bytes 7340032 | tf_op jit(solution)/shard_map/pallas_call | solution.py:406
  39.7 5.3 %shard_map.96 = (bf16[256,2048]{1,0:T(8,128)(2,1)S(1)}, f32[256,512]{1,0:T(8,128)S(1)}, f32[256,512]{1,0:T(8,128)S(1)}) custom-call(s32[3]{0:T(128)S(1)} %pad_add_fusion.j_ref.a_ref._, bf16[8,256,128]{2,1,0:T(8,128)(2,1)S(1)} %copy-done.7, bf16[8,256,128]{2,1,0:T(8,128)(2,1)S(1)} %copy-done.1, bf16[144,512]{1,0:T(8,128)(2,1)S(1)} %get-tuple-element.91.refs_2_.prev_ref, ...), custom_call_target="tpu_custom_call" | custom-call | flops 2147483648 | bytes 2097152 | tf_op jit(solution)/shard_map/pallas_call | solution.py:422
  45.0 4.3 %collective-permute-done.4.refs_1_ = bf16[256,1024]{1,0:T(8,128)(2,1)S(1)} collective-permute-done((bf16[256,1024]{1,0:T(8,128)(2,1)S(1)}, bf16[256,1024]{1,0:T(8,128)(2,1)S(1)}, u32[]{:S(2)}, u32[]{:S(2)}) %collective-permute-start.4) | collective-permute-done | bytes 524320 | tf_op jit(solution)/shard_map/ppermute | solution.py:350
  49.3 4.8 %shard_map.97 = (bf16[256,128]{1,0:T(8,128)(2,1)S(1)}, bf16[256,128]{1,0:T(8,128)(2,1)S(1)}, bf16[256,512]{1,0:T(8,128)(2,1)S(1)}, bf16[256,512]{1,0:T(8,128)(2,...) custom-call(s32[3]{0:T(128)S(1)} %pad_add_fusion.j_ref.a_ref._, ...), custom_call_target="tpu_custom_call" | custom-call | flops 2130706432 | bytes 7340032 | tf_op jit(solution)/shard_map/pallas_call | solution.py:406
  54.1 5.1 %shard_map.98 = (bf16[256,2048]{1,0:T(8,128)(2,1)S(1)}, f32[256,512]{1,0:T(8,128)S(1)}, f32[256,512]{1,0:T(8,128)S(1)}) custom-call(s32[3]{0:T(128)S(1)} %pad_add_fusion.j_ref.a_ref._, bf16[8,256,128]{2,1,0:T(8,128)(2,1)S(1)} %copy-done.7, bf16[8,256,128]{2,1,0:T(8,128)(2,1)S(1)} %copy-done.1, bf16[144,512]{1,0:T(8,128)(2,1)S(1)} %get-tuple-element.92.refs_2_.prev_ref, ...), custom_call_target="tpu_custom_call" | custom-call | flops 2147483648 | bytes 2097152 | tf_op jit(solution)/shard_map/pallas_call | solution.py:422
  59.2 3.7 %shard_map.99 = (bf16[128,128]{1,0:T(8,128)(2,1)S(1)}, bf16[128,128]{1,0:T(8,128)(2,1)S(1)}, bf16[128,512]{1,0:T(8,128)(2,1)S(1)}, bf16[128,512]{1,0:T(8,128)(2,...) custom-call(s32[3]{0:T(128)S(1)} %pad_add_fusion.j_ref.a_ref._, ...), custom_call_target="tpu_custom_call" | custom-call | flops 1065353216 | bytes 7340032 | tf_op jit(solution)/shard_map/pallas_call | solution.py:406
  62.9 3.3 %collective-permute-start.6 = (bf16[160,128]{1,0:T(8,128)(2,1)S(1)}, bf16[160,128]{1,0:T(8,128)(2,1)S(1)}, u32[]{:S(2)}, u32[]{:S(2)}) collective-permute-start(bf16[160,128]{1,0:T(8,128)(2,1)S(1)} %get-tuple-element.128), channel_id=1, source_target_pairs={{0,2},{2,0},{4,6},{6,4},{8,10},{10,8},{12,14},{14,12},{16,18},{18,... | collective-permute-start | bytes 122888 | tf_op jit(solution)/shard_map/ppermute | solution.py:256
  67.7 3.0 %shard_map.101 = (bf16[128,2048]{1,0:T(8,128)(2,1)S(1)}, f32[128,512]{1,0:T(8,128)S(1)}, f32[128,512]{1,0:T(8,128)S(1)}) custom-call(s32[3]{0:T(128)S(1)} %pad_add_fusion.j_ref.a_ref._, bf16[8,256,128]{2,1,0:T(8,128)(2,1)S(1)} %copy-done.7, bf16[8,256,128]{2,1,0:T(8,128)(2,1)S(1)} %copy-done.1, bf16[144,512]{1,0:T(8,128)(2,1)S(1)} %get-tuple-element.107.refs_2_.prev_ref, ...), custom_call_target="tpu_custom_call" | custom-call | flops 1073741824 | bytes 1048576 | tf_op jit(solution)/shard_map/pallas_call | solution.py:422
  72.1 4.7 %collective-permute-start.11 = (bf16[160,128]{1,0:T(8,128)(2,1)S(1)}, bf16[160,128]{1,0:T(8,128)(2,1)S(1)}, u32[]{:S(2)}, u32[]{:S(2)}) collective-permute-start(bf16[160,128]{1,0:T(8,128)(2,1)S(1)} %get-tuple-element.135), channel_id=1, source_target_pairs={{0,24},{2,26},{4,28},{6,30},{1,25},{3,27},{5,29},{7,31}} | collective-permute-start | bytes 122888 | tf_op jit(solution)/shard_map/ppermute | solution.py:303
  78.2 2.5 %collective-permute-start.9 = (bf16[160,128]{1,0:T(8,128)(2,1)S(1)}, bf16[160,128]{1,0:T(8,128)(2,1)S(1)}, u32[]{:S(2)}, u32[]{:S(2)}) collective-permute-start(bf16[160,128]{1,0:T(8,128)(2,1)S(1)} %get-tuple-element.135), channel_id=1, source_target_pairs={{0,8},{2,10},{4,12},{6,14},{8,16},{10,18},{12,20},{14,22},{16,24},... | collective-permute-start | bytes 122888 | tf_op jit(solution)/shard_map/ppermute | solution.py:303
  80.6 2.8 %shard_map.100 = (bf16[128,2048]{1,0:T(8,128)(2,1)S(1)}, f32[128,512]{1,0:T(8,128)S(1)}, f32[128,512]{1,0:T(8,128)S(1)}) custom-call(s32[3]{0:T(128)S(1)} %pad_add_fusion.j_ref.a_ref._, bf16[8,256,128]{2,1,0:T(8,128)(2,1)S(1)} %copy-done.7, bf16[8,256,128]{2,1,0:T(8,128)(2,1)S(1)} %copy-done.1, bf16[144,512]{1,0:T(8,128)(2,1)S(1)} %get-tuple-element.112.prev_ref, ...), custom_call_target="tpu_custom_call" | custom-call | flops 1073741824 | bytes 1048576 | tf_op jit(solution)/shard_map/pallas_call | solution.py:422
  86.1 2.5 %collective-permute-done.13.refs_2_ = bf16[160,128]{1,0:T(8,128)(2,1)S(1)} collective-permute-done((bf16[160,128]{1,0:T(8,128)(2,1)S(1)}, bf16[160,128]{1,0:T(8,128)(2,1)S(1)}, u32[]{:S(2)}, u32[]{:S(2)}) %collective-permute-start.13) | collective-permute-done | bytes 40992 | tf_op jit(solution)/shard_map/ppermute | solution.py:256
  91.1 1.6 %shard_map.105.own_ref = bf16[256,512]{1,0:T(8,128)(2,1)S(1)} custom-call(s32[3]{0:T(128)S(1)} %pad_add_fusion.j_ref.a_ref._, bf16[256,128]{1,0:T(8,128)(2,1)S(1)} %copy-done.4, f32[1,512]{1,0:T(1,128)S(1)} %bitcast.5, bf16[160,128]{1,0:T(8,128)(2,1)S(1)} %get-tuple-element.136.refs_0_, bf16[160,128]{1,0:T(8,128)(2,1)S(1)} %collective-permute-done.12.refs_1_, ...), custom_call_target="tpu_custom_call" | custom-call | flops 402653184 | bytes 1572864 | tf_op jit(solution)/shard_map/pallas_call | solution.py:459
  92.6 1.6 %collective-permute-start.20 = (bf16[256,512]{1,0:T(8,128)(2,1)S(1)}, bf16[256,512]{1,0:T(8,128)(2,1)S(1)}, u32[]{:S(2)}, u32[]{:S(2)}) collective-permute-start(bf16[256,512]{1,0:T(8,128)(2,1)S(1)} %shard_map.105.own_ref), channel_id=1, source_target_pairs={{0,1},{1,0},{2,3},{3,2},{4,5},{5,4},{6,7},{7,6},{8,9},{9,8},{10,11... | collective-permute-start | bytes 786440 | tf_op jit(solution)/shard_map/ppermute | solution.py:350
  94.2 1.6 %shard_map.106.own_ref = bf16[256,512]{1,0:T(8,128)(2,1)S(1)} custom-call(s32[3]{0:T(128)S(1)} %pad_add_fusion.j_ref.a_ref._, bf16[256,128]{1,0:T(8,128)(2,1)S(1)} %copy-done.4, f32[1,512]{1,0:T(1,128)S(1)} %bitcast.6, bf16[160,128]{1,0:T(8,128)(2,1)S(1)} %get-tuple-element.136.refs_0_, bf16[160,128]{1,0:T(8,128)(2,1)S(1)} %collective-permute-done.12.refs_1_, ...), custom_call_target="tpu_custom_call" | custom-call | flops 402653184 | bytes 1572864 | tf_op jit(solution)/shard_map/pallas_call | solution.py:459
  96.3 1.6 %shard_map.107.own_ref = bf16[256,512]{1,0:T(8,128)(2,1)S(1)} custom-call(s32[3]{0:T(128)S(1)} %pad_add_fusion.j_ref.a_ref._, bf16[256,128]{1,0:T(8,128)(2,1)S(1)} %copy-done.4, f32[1,512]{1,0:T(1,128)S(1)} %bitcast.7, bf16[160,128]{1,0:T(8,128)(2,1)S(1)} %get-tuple-element.136.refs_0_, bf16[160,128]{1,0:T(8,128)(2,1)S(1)} %collective-permute-done.12.refs_1_, ...), custom_call_target="tpu_custom_call" | custom-call | flops 402653184 | bytes 1572864 | tf_op jit(solution)/shard_map/pallas_call | solution.py:459
  97.9 1.6 %collective-permute-start.18 = (bf16[256,512]{1,0:T(8,128)(2,1)S(1)}, bf16[256,512]{1,0:T(8,128)(2,1)S(1)}, u32[]{:S(2)}, u32[]{:S(2)}) collective-permute-start(bf16[256,512]{1,0:T(8,128)(2,1)S(1)} %shard_map.107.own_ref), channel_id=1, source_target_pairs={{0,1},{1,0},{2,3},{3,2},{4,5},{5,4},{6,7},{7,6},{8,9},{9,8},{10,11... | collective-permute-start | bytes 786440 | tf_op jit(solution)/shard_map/ppermute | solution.py:350
  101.4 13.7 %collective-permute-done.21.refs_0_ = bf16[128,512]{1,0:T(8,128)(2,1)S(1)} collective-permute-done((bf16[128,512]{1,0:T(8,128)(2,1)S(1)}, bf16[128,512]{1,0:T(8,128)(2,1)S(1)}, u32[]{:S(2)}, u32[]{:S(2)}) %collective-permute-start.21) | collective-permute-done | bytes 131104 | tf_op jit(solution)/shard_map/ppermute | solution.py:350
  116.6 1.7 %shard_map.110.refs_3_ = bf16[1024,1024]{1,0:T(8,128)(2,1)} custom-call(s32[3]{0:T(128)S(1)} %pad_add_fusion.j_ref.a_ref._, bf16[128,512]{1,0:T(8,128)(2,1)S(1)} %shard_map.104.own_ref, bf16[512,2048]{1,0:T(8,128)(2,1)S(1)} %copy-done, bf16[128,512]{1,0:T(8,128)(2,1)S(1)} %collective-permute-done.21.refs_0_, ...), custom_call_target="tpu_custom_call" | custom-call | flops 268435456 | bytes 2097152 | tf_op jit(solution)/shard_map/pallas_call | solution.py:476
  118.3 2.1 %shard_map.111.refs_3_ = bf16[1024,1024]{1,0:T(8,128)(2,1)} custom-call(s32[3]{0:T(128)S(1)} %pad_add_fusion.j_ref.a_ref._, bf16[256,512]{1,0:T(8,128)(2,1)S(1)} %shard_map.105.own_ref, bf16[512,2048]{1,0:T(8,128)(2,1)S(1)} %copy-done, bf16[256,512]{1,0:T(8,128)(2,1)S(1)} %collective-permute-done.20.refs_0_, ...), custom_call_target="tpu_custom_call", output_to_operand_aliasing={{}: (6, {})} | custom-call | flops 536870912 | bytes 2097152 | tf_op jit(solution)/shard_map/pallas_call | solution.py:476
  120.4 2.1 %shard_map.112.refs_3_ = bf16[1024,1024]{1,0:T(8,128)(2,1)} custom-call(s32[3]{0:T(128)S(1)} %pad_add_fusion.j_ref.a_ref._, bf16[256,512]{1,0:T(8,128)(2,1)S(1)} %shard_map.106.own_ref, bf16[512,2048]{1,0:T(8,128)(2,1)S(1)} %copy-done, bf16[256,512]{1,0:T(8,128)(2,1)S(1)} %collective-permute-done.19.refs_0_, ...), custom_call_target="tpu_custom_call", output_to_operand_aliasing={{}: (6, {})} | custom-call | flops 536870912 | bytes 2097152 | tf_op jit(solution)/shard_map/pallas_call | solution.py:476
  122.5 2.1 %shard_map.113.refs_3_ = bf16[1024,1024]{1,0:T(8,128)(2,1)} custom-call(s32[3]{0:T(128)S(1)} %pad_add_fusion.j_ref.a_ref._, bf16[256,512]{1,0:T(8,128)(2,1)S(1)} %shard_map.107.own_ref, bf16[512,2048]{1,0:T(8,128)(2,1)S(1)} %copy-done, bf16[256,512]{1,0:T(8,128)(2,1)S(1)} %collective-permute-done.18.refs_0_, ...), custom_call_target="tpu_custom_call", output_to_operand_aliasing={{}: (6, {})} | custom-call | flops 536870912 | bytes 2097152 | tf_op jit(solution)/shard_map/pallas_call | solution.py:476
  124.6 1.7 %shard_map.114 = bf16[1024,1024]{1,0:T(8,128)(2,1)} custom-call(s32[3]{0:T(128)S(1)} %pad_add_fusion.j_ref.a_ref._, bf16[128,512]{1,0:T(8,128)(2,1)S(1)} %shard_map.108.own_ref, bf16[512,2048]{1,0:T(8,128)(2,1)S(1)} %copy-done, bf16[128,512]{1,0:T(8,128)(2,1)S(1)} %collective-permute-done.15.refs_0_, ...), custom_call_target="tpu_custom_call", output_to_operand_aliasing={{}: (6, {})} | custom-call | flops 268435456 | bytes 2097152 | tf_op jit(solution)/shard_map/pallas_call | solution.py:476
  (56 shorter events, 18.1 us)
Async XLA Ops:
  1.1 12.9 %collective-permute-start = (bf16[144,1024]{1,0:T(8,128)(2,1)S(1)}, bf16[144,1024]{1,0:T(8,128)(2,1)S(1)}, u32[]{:S(2)}, u32[]{:S(2)}) collective-permute-start(bf16[144,1024]{1,0:T(8,128)(2,1)S(1)} %slice.15.refs_0_), channel_id=1, source_target_pairs={{0,1},{1,0},{2,3},{3,2},{4,5},{5,4},{6,7},{7,6},{8,9},{9,8},{10,11... | collective-permute-start | bytes 884744 | tf_op jit(solution)/shard_map/ppermute | solution.py:350
  5.6 8.4 %copy-start.1 = (bf16[8,256,128]{2,1,0:T(8,128)(2,1)S(1)}, bf16[8,256,128]{2,1,0:T(8,128)(2,1)}, u32[]{:S(2)}) copy-start(bf16[8,256,128]{2,1,0:T(8,128)(2,1)} %constant.30.clone.sel_b_ref) | copy-start | bytes 1572868
  5.6 8.4 %copy-start.2 = (bf16[8,256,128]{2,1,0:T(8,128)(2,1)S(1)}, bf16[8,256,128]{2,1,0:T(8,128)(2,1)}, u32[]{:S(2)}) copy-start(bf16[8,256,128]{2,1,0:T(8,128)(2,1)} %constant.31.clone.sel_w_ref) | copy-start | bytes 1572868
  5.6 19.1 %collective-permute-start.2 = (bf16[256,1024]{1,0:T(8,128)(2,1)S(1)}, bf16[256,1024]{1,0:T(8,128)(2,1)S(1)}, u32[]{:S(2)}, u32[]{:S(2)}) collective-permute-start(bf16[256,1024]{1,0:T(8,128)(2,1)S(1)} %get-tuple-element.159.refs_0_), channel_id=1, source_target_pairs={{0,1},{1,0},{2,3},{3,2},{4,5},{5,4},{6,7},{7,6},{8,9},{9,8},{10,11... | collective-permute-start | bytes 1572872 | tf_op jit(solution)/shard_map/ppermute | solution.py:350
  5.7 3.2 %copy-start.3 = (bf16[2048,1792]{1,0:T(8,128)(2,1)S(1)}, bf16[2048,1792]{1,0:T(8,128)(2,1)}, u32[]{:S(2)}) copy-start(bf16[2048,1792]{1,0:T(8,128)(2,1)} %w_ref.7) | copy-start | bytes 22020100
  8.8 5.1 %copy-start.4 = (bf16[256,128]{1,0:T(8,128)(2,1)S(1)}, bf16[256,128]{1,0:T(8,128)(2,1)}, u32[]{:S(2)}) copy-start(bf16[256,128]{1,0:T(8,128)(2,1)} %constant.32.clone.mean_ref) | copy-start | bytes 196612
  8.8 5.2 %copy-start.5 = (f32[3,512]{1,0:T(4,128)S(1)}, f32[3,512]{1,0:T(4,128)}, u32[]{:S(2)}) copy-start(f32[3,512]{1,0:T(4,128)} %conv_ref.9) | copy-start | bytes 18436
  13.9 10.1 %copy-start = (bf16[512,2048]{1,0:T(8,128)(2,1)S(1)}, bf16[512,2048]{1,0:T(8,128)(2,1)}, u32[]{:S(2)}) copy-start(bf16[512,2048]{1,0:T(8,128)(2,1)} %w_ref.13) | copy-start | bytes 6291460
  17.5 7.5 %collective-permute-start.1 = (bf16[144,512]{1,0:T(8,128)(2,1)S(1)}, bf16[144,512]{1,0:T(8,128)(2,1)S(1)}, u32[]{:S(2)}, u32[]{:S(2)}) collective-permute-start(bf16[144,512]{1,0:T(8,128)(2,1)S(1)} %get-tuple-element.83), channel_id=1, source_target_pairs={{0,2},{2,4},{4,6},{6,8},{8,10},{10,12},{12,14},{14,16},{16,18},{18... | collective-permute-start | bytes 442376 | tf_op jit(solution)/shard_map/ppermute | solution.py:435
  19.2 15.7 %collective-permute-start.3 = (bf16[256,1024]{1,0:T(8,128)(2,1)S(1)}, bf16[256,1024]{1,0:T(8,128)(2,1)S(1)}, u32[]{:S(2)}, u32[]{:S(2)}) collective-permute-start(bf16[256,1024]{1,0:T(8,128)(2,1)S(1)} %get-tuple-element.158.refs_0_), channel_id=1, source_target_pairs={{0,1},{1,0},{2,3},{3,2},{4,5},{5,4},{6,7},{7,6},{8,9},{9,8},{10,11... | collective-permute-start | bytes 1572872 | tf_op jit(solution)/shard_map/ppermute | solution.py:350
  22.0 37.2 %collective-permute-start.5 = (bf16[128,1024]{1,0:T(8,128)(2,1)S(1)}, bf16[128,1024]{1,0:T(8,128)(2,1)S(1)}, u32[]{:S(2)}, u32[]{:S(2)}) collective-permute-start(bf16[128,1024]{1,0:T(8,128)(2,1)S(1)} %slice.19.refs_0_), channel_id=1, source_target_pairs={{0,1},{1,0},{2,3},{3,2},{4,5},{5,4},{6,7},{7,6},{8,9},{9,8},{10,11... | collective-permute-start | bytes 786440 | tf_op jit(solution)/shard_map/ppermute | solution.py:350
  22.3 27.0 %collective-permute-start.4 = (bf16[256,1024]{1,0:T(8,128)(2,1)S(1)}, bf16[256,1024]{1,0:T(8,128)(2,1)S(1)}, u32[]{:S(2)}, u32[]{:S(2)}) collective-permute-start(bf16[256,1024]{1,0:T(8,128)(2,1)S(1)} %get-tuple-element.157.refs_0_), channel_id=1, source_target_pairs={{0,1},{1,0},{2,3},{3,2},{4,5},{5,4},{6,7},{7,6},{8,9},{9,8},{10,11... | collective-permute-start | bytes 1572872 | tf_op jit(solution)/shard_map/ppermute | solution.py:350
  24.7 5.1 %copy-start.7 = (bf16[8,256,128]{2,1,0:T(8,128)(2,1)S(1)}, bf16[8,256,128]{2,1,0:T(8,128)(2,1)}, u32[]{:S(2)}) copy-start(bf16[8,256,128]{2,1,0:T(8,128)(2,1)} %constant.29.clone.sel_a_ref) | copy-start | bytes 1572868
  24.7 59.3 %collective-permute-start.16 = (bf16[256,1024]{1,0:T(8,128)(2,1)S(1)}, bf16[256,1024]{1,0:T(8,128)(2,1)S(1)}, u32[]{:S(2)}, u32[]{:S(2)}) collective-permute-start(bf16[256,1024]{1,0:T(8,128)(2,1)S(1)} %shard_map.109), channel_id=1, source_target_pairs={{0,1},{1,0},{2,3},{3,2},{4,5},{5,4},{6,7},{7,6},{8,9},{9,8},{10,11... | collective-permute-start | bytes 1572872 | tf_op jit(solution)/shard_map/ppermute | solution.py:350
  62.9 7.8 %collective-permute-start.6 = (bf16[160,128]{1,0:T(8,128)(2,1)S(1)}, bf16[160,128]{1,0:T(8,128)(2,1)S(1)}, u32[]{:S(2)}, u32[]{:S(2)}) collective-permute-start(bf16[160,128]{1,0:T(8,128)(2,1)S(1)} %get-tuple-element.128), channel_id=1, source_target_pairs={{0,2},{2,0},{4,6},{6,4},{8,10},{10,8},{12,14},{14,12},{16,18},{18,... | collective-permute-start | bytes 122888 | tf_op jit(solution)/shard_map/ppermute | solution.py:256
  66.2 4.5 %collective-permute-start.7 = (bf16[160,128]{1,0:T(8,128)(2,1)S(1)}, bf16[160,128]{1,0:T(8,128)(2,1)S(1)}, u32[]{:S(2)}, u32[]{:S(2)}) collective-permute-start(bf16[160,128]{1,0:T(8,128)(2,1)S(1)} %get-tuple-element.129), channel_id=1, source_target_pairs={{0,4},{2,6},{4,0},{6,2},{8,12},{10,14},{12,8},{14,10},{16,20},{18,... | collective-permute-start | bytes 122888 | tf_op jit(solution)/shard_map/ppermute | solution.py:256
  67.7 3.8 %collective-permute-start.8 = (bf16[160,128]{1,0:T(8,128)(2,1)S(1)}, bf16[160,128]{1,0:T(8,128)(2,1)S(1)}, u32[]{:S(2)}, u32[]{:S(2)}) collective-permute-start(bf16[160,128]{1,0:T(8,128)(2,1)S(1)} %get-tuple-element.130), channel_id=1, source_target_pairs={{0,6},{2,4},{4,2},{6,0},{8,14},{10,12},{12,10},{14,8},{16,22},{18,... | collective-permute-start | bytes 122888 | tf_op jit(solution)/shard_map/ppermute | solution.py:256
  72.1 11.3 %collective-permute-start.11 = (bf16[160,128]{1,0:T(8,128)(2,1)S(1)}, bf16[160,128]{1,0:T(8,128)(2,1)S(1)}, u32[]{:S(2)}, u32[]{:S(2)}) collective-permute-start(bf16[160,128]{1,0:T(8,128)(2,1)S(1)} %get-tuple-element.135), channel_id=1, source_target_pairs={{0,24},{2,26},{4,28},{6,30},{1,25},{3,27},{5,29},{7,31}} | collective-permute-start | bytes 122888 | tf_op jit(solution)/shard_map/ppermute | solution.py:303
  76.9 6.6 %collective-permute-start.10 = (bf16[160,128]{1,0:T(8,128)(2,1)S(1)}, bf16[160,128]{1,0:T(8,128)(2,1)S(1)}, u32[]{:S(2)}, u32[]{:S(2)}) collective-permute-start(bf16[160,128]{1,0:T(8,128)(2,1)S(1)} %get-tuple-element.135), channel_id=1, source_target_pairs={{0,16},{2,18},{4,20},{6,22},{8,24},{10,26},{12,28},{14,30},{1,17},... | collective-permute-start | bytes 122888 | tf_op jit(solution)/shard_map/ppermute | solution.py:303
  78.2 5.3 %collective-permute-start.9 = (bf16[160,128]{1,0:T(8,128)(2,1)S(1)}, bf16[160,128]{1,0:T(8,128)(2,1)S(1)}, u32[]{:S(2)}, u32[]{:S(2)}) collective-permute-start(bf16[160,128]{1,0:T(8,128)(2,1)S(1)} %get-tuple-element.135), channel_id=1, source_target_pairs={{0,8},{2,10},{4,12},{6,14},{8,16},{10,18},{12,20},{14,22},{16,24},... | collective-permute-start | bytes 122888 | tf_op jit(solution)/shard_map/ppermute | solution.py:303
  80.6 9.1 %copy-start.6 = (f32[512]{0:T(512)S(1)}, f32[512]{0:T(512)}, u32[]{:S(2)}) copy-start(f32[512]{0:T(512)} %param.12) | copy-start | bytes 6148
  84.0 32.5 %collective-permute-start.17 = (bf16[256,1024]{1,0:T(8,128)(2,1)S(1)}, bf16[256,1024]{1,0:T(8,128)(2,1)S(1)}, u32[]{:S(2)}, u32[]{:S(2)}) collective-permute-start(bf16[256,1024]{1,0:T(8,128)(2,1)S(1)} %collective-permute-done.16.refs_1_), channel_id=1, source_target_pairs={{0,2},{2,0},{4,6},{6,4},{8,10},{10,8},{12,14},{14,12},{16,18},{18,... | collective-permute-start | bytes 1572872 | tf_op jit(solution)/shard_map/ppermute | solution.py:256
  84.1 2.0 %collective-permute-start.12 = (bf16[160,128]{1,0:T(8,128)(2,1)S(1)}, bf16[160,128]{1,0:T(8,128)(2,1)S(1)}, u32[]{:S(2)}, u32[]{:S(2)}) collective-permute-start(bf16[160,128]{1,0:T(8,128)(2,1)S(1)} %get-tuple-element.137), channel_id=1, source_target_pairs={{0,2},{2,0},{4,6},{6,4},{8,10},{10,8},{12,14},{14,12},{16,18},{18,... | collective-permute-start | bytes 122888 | tf_op jit(solution)/shard_map/ppermute | solution.py:256
  84.6 4.0 %collective-permute-start.13 = (bf16[160,128]{1,0:T(8,128)(2,1)S(1)}, bf16[160,128]{1,0:T(8,128)(2,1)S(1)}, u32[]{:S(2)}, u32[]{:S(2)}) collective-permute-start(bf16[160,128]{1,0:T(8,128)(2,1)S(1)} %get-tuple-element.138), channel_id=1, source_target_pairs={{0,4},{2,6},{4,0},{6,2},{8,12},{10,14},{12,8},{14,10},{16,20},{18,... | collective-permute-start | bytes 122888 | tf_op jit(solution)/shard_map/ppermute | solution.py:256
  85.9 3.8 %collective-permute-start.14 = (bf16[160,128]{1,0:T(8,128)(2,1)S(1)}, bf16[160,128]{1,0:T(8,128)(2,1)S(1)}, u32[]{:S(2)}, u32[]{:S(2)}) collective-permute-start(bf16[160,128]{1,0:T(8,128)(2,1)S(1)} %get-tuple-element.139), channel_id=1, source_target_pairs={{0,6},{2,4},{4,2},{6,0},{8,14},{10,12},{12,10},{14,8},{16,22},{18,... | collective-permute-start | bytes 122888 | tf_op jit(solution)/shard_map/ppermute | solution.py:256
  92.6 25.6 %collective-permute-start.20 = (bf16[256,512]{1,0:T(8,128)(2,1)S(1)}, bf16[256,512]{1,0:T(8,128)(2,1)S(1)}, u32[]{:S(2)}, u32[]{:S(2)}) collective-permute-start(bf16[256,512]{1,0:T(8,128)(2,1)S(1)} %shard_map.105.own_ref), channel_id=1, source_target_pairs={{0,1},{1,0},{2,3},{3,2},{4,5},{5,4},{6,7},{7,6},{8,9},{9,8},{10,11... | collective-permute-start | bytes 786440 | tf_op jit(solution)/shard_map/ppermute | solution.py:350
  95.8 24.6 %collective-permute-start.19 = (bf16[256,512]{1,0:T(8,128)(2,1)S(1)}, bf16[256,512]{1,0:T(8,128)(2,1)S(1)}, u32[]{:S(2)}, u32[]{:S(2)}) collective-permute-start(bf16[256,512]{1,0:T(8,128)(2,1)S(1)} %shard_map.106.own_ref), channel_id=1, source_target_pairs={{0,1},{1,0},{2,3},{3,2},{4,5},{5,4},{6,7},{7,6},{8,9},{9,8},{10,11... | collective-permute-start | bytes 786440 | tf_op jit(solution)/shard_map/ppermute | solution.py:350
  97.9 24.6 %collective-permute-start.18 = (bf16[256,512]{1,0:T(8,128)(2,1)S(1)}, bf16[256,512]{1,0:T(8,128)(2,1)S(1)}, u32[]{:S(2)}, u32[]{:S(2)}) collective-permute-start(bf16[256,512]{1,0:T(8,128)(2,1)S(1)} %shard_map.107.own_ref), channel_id=1, source_target_pairs={{0,1},{1,0},{2,3},{3,2},{4,5},{5,4},{6,7},{7,6},{8,9},{9,8},{10,11... | collective-permute-start | bytes 786440 | tf_op jit(solution)/shard_map/ppermute | solution.py:350
  99.5 15.5 %collective-permute-start.21 = (bf16[128,512]{1,0:T(8,128)(2,1)S(1)}, bf16[128,512]{1,0:T(8,128)(2,1)S(1)}, u32[]{:S(2)}, u32[]{:S(2)}) collective-permute-start(bf16[128,512]{1,0:T(8,128)(2,1)S(1)} %shard_map.104.own_ref), channel_id=1, source_target_pairs={{0,1},{1,0},{2,3},{3,2},{4,5},{5,4},{6,7},{7,6},{8,9},{9,8},{10,11... | collective-permute-start | bytes 393224 | tf_op jit(solution)/shard_map/ppermute | solution.py:350
  115.0 9.5 %collective-permute-start.15 = (bf16[128,512]{1,0:T(8,128)(2,1)S(1)}, bf16[128,512]{1,0:T(8,128)(2,1)S(1)}, u32[]{:S(2)}, u32[]{:S(2)}) collective-permute-start(bf16[128,512]{1,0:T(8,128)(2,1)S(1)} %shard_map.108.own_ref), channel_id=1, source_target_pairs={{0,1},{1,0},{2,3},{3,2},{4,5},{5,4},{6,7},{7,6},{8,9},{9,8},{10,11... | collective-permute-start | bytes 393224 | tf_op jit(solution)/shard_map/ppermute | solution.py:350
where the time goes:
time: 127 us; the launch traced here: 126 us
  Pallas kernels  66.7 us (53%)
  starting transfers between devices  30 us (24%)
  waiting for transfers between devices  22.5 us (18%)
  local copies, waits for them, and re-layouts  6.61 us (5%)
    pallas_call x5, Pallas kernels, do_block(): call(functools.partial(block_kernel, n=n, heads=heads, extra=extra, other...  21.5 us
    pallas_call x5, Pallas kernels, attend(): call(functools.partial(attend_kernel, heads=heads, first=b == 0), [jax.Sh...  21.3 us
    ppermute x11, waiting for transfers between devices, from_head(): return lax.ppermute(value, 'head', [(i, (i + by) % n) for i in range(n)])  18 us
    ppermute x11, starting transfers between devices, from_head(): return lax.ppermute(value, 'head', [(i, (i + by) % n) for i in range(n)])  13.1 us
    pallas_call x5, Pallas kernels, per_device(): call(functools.partial(output_kernel, n=n, offset=at, parts=out_parts), j...  9.64 us
    ppermute x3, starting transfers between devices, prior_in_planes(): earlier.append(lax.ppermute(plane, 'ctx', pairs))  8.48 us
    pallas_call x5, Pallas kernels, per_device(): call(functools.partial(finish_kernel, heads=heads, before=b), jax.ShapeDt...  7.39 us
    ppermute x7, starting transfers between devices, exchange(): return lax.ppermute(value, axis, [(i, i ^ flip) for i in range(count)])  6.78 us
  transfers between devices with their start and end apart: 22, of which 5 were waited for; matrix products, arithmetic and copies ran while one was open for 2% of the time, Pallas kernels for 51%

commit v1 on v0

--- a/solution.py
+++ b/solution.py
@@ -27,7 +27,7 @@
         body,
         out_shape=out_shape,
         compiler_params=pltpu.CompilerParams(vmem_limit_bytes=vmem),
-        cost_estimate=pl.CostEstimate(flops=flops, bytes_accessed=moved, transcendentals=0),
+        cost_estimate=pl.CostEstimate(flops=1, bytes_accessed=1, transcendentals=0),
         **kwargs,
     )
 
@@ -350,11 +350,19 @@
         return lax.ppermute(value, "head", [(i, (i + by) % n) for i in range(n)])
 
     pieces = {}
-    for b in [last] + list(range(last)):
+
+    def send_block(b, behind=None):
         at, rows = blocks[b]
         extra = EDGE if b == last else 0
         own = hidden_in[at - extra : at + rows]
+        if behind is not None:
+            own = after(own, behind)
         pieces[b] = [own] + [from_head(own, r) for r in range(1, n)]
+
+    send_block(last)
+    send_block(0, pieces[last][0])
+    for b in range(1, last):
+        send_block(b, pieces[last][0])
 
     cols = out_weight.shape[1] // n
     out_parts = 2 if width // 2 % LANES == 0 and ctx % 2 == 0 else 1
@@ -375,7 +383,7 @@
             moved=4 * share * cols,
             vmem=8 << 20,
         )(places, out_weight)
-        fetched.append(from_head(after(block, pieces[0][1]), r))
+        fetched.append(from_head(after(block, pieces[1][-1]), r))
 
     qk_width = -(-heads * FQK // LANES) * LANES
     arranged_width = 2 * qk_width + 3 * width
@@ -436,14 +444,14 @@
     for b in range(last):
         prev = halo if b == 0 else done[b - 1][5]
         others = [done[c][6] for c in [last] + list(range(b))] if b == last - 1 else ()
-        done[b] = do_block(b, prev, attended[b - 1][1] if b else None, others)
-        if b < last - 1:
+        done[b] = do_block(b, prev, attended[b - 1][1] if b - 1 in attended else None, others)
+        if b < last - 2:
             attended[b] = attend(b, prev)
 
-    for b in (last - 1, last):
+    for b in range(last - 2, last + 1):
         attended[b] = attend(b, done[b - 1][5])
     if in_planes:
-        beside = [attended[b][1] for b in (last - 1, last)]
+        beside = [attended[b][1] for b in (last - 2, last - 1)]
         mark, priors = prior_in_planes(done[last - 1][7:], places, beside)
     else:
         mark = sum(done[b][6] for b in range(last + 1))
@@ -453,9 +461,11 @@
     for got in fetched:
         out_rows += [got] + ([exchange(after(got, mark), "ctx", 1)] if out_parts > 1 else [])
 
-    result = mixed = None
-    for b in (3, 0, 1, 2, 4):
+    result = None
+    arrived = []
+    for i, b in enumerate((3, 0, 1, 2, 4)):
         at, rows = blocks[b]
+        behind = after(places, arrived[i - 2] if i >= 2 else attended[last][1])
         mixed = call(
             functools.partial(finish_kernel, heads=heads, before=b),
             jax.ShapeDtypeStruct((rows, width), BF16),
@@ -465,8 +475,10 @@
             flops=6 * rows * QFEATS * LANES * heads,
             moved=12 * rows * width,
             vmem=16 << 20,
-        )(places if mixed is None else after(places, mixed), means, gain, *priors, *[done[c][6] for c in range(b)], *attended[b])
-        operands = [places, mixed, out_weight] + [from_head(mixed, r) for r in range(1, n)] + out_rows
+        )(behind, means, gain, *priors, *[done[c][6] for c in range(b)], *attended[b])
+        others = [from_head(mixed, r) for r in range(1, n)]
+        arrived.append(others[-1])
+        operands = [places, mixed, out_weight] + others + out_rows
         specs = [scalar] + [whole] * (len(operands) - 1)
         aliases = {}
         if result is not None:

time: 127 us -> 145 us (1.14)
  waiting for transfers between devices: 22.5 us -> 36.1 us
  starting transfers between devices: 30 us -> 34.6 us
    ppermute x11, waiting for transfers between devices: 18 us -> 35.3 us  [from_head(): return lax.ppermute(value, 'head', [(i, (i + by) % n) for i in range(n)])]
    ppermute x7, waiting for transfers between devices: 4.47 us -> 0.02 us  [exchange(): return lax.ppermute(value, axis, [(i, i ^ flip) for i in range(count)])]
    ppermute x3, starting transfers between devices: 8.48 us -> 10.7 us  [prior_in_planes(): earlier.append(lax.ppermute(plane, 'ctx', pairs))]
    ppermute x7, starting transfers between devices: 6.78 us -> 8.36 us  [exchange(): return lax.ppermute(value, axis, [(i, i ^ flip) for i in range(count)])]
  transfers between devices with their start and end apart: 22 -> 22, of which waited for: 5 -> 6; matrix products, arithmetic and copies ran while one was open for 2% -> 1% of each run, Pallas kernels for 51% -> 45%
where the time goes in v1:
time: 145 us
  Pallas kernels  66.4 us (46%)
  waiting for transfers between devices  36.1 us (25%)
  starting transfers between devices  34.6 us (24%)
  local copies, waits for them, and re-layouts  6.75 us (5%)
    ppermute x11, waiting for transfers between devices, from_head(): return lax.ppermute(value, 'head', [(i, (i + by) % n) for i in range(n)])  35.3 us
    pallas_call x5, Pallas kernels, do_block(): call(functools.partial(block_kernel, n=n, heads=heads, extra=extra, other...  21.4 us
    pallas_call x5, Pallas kernels, attend(): call(functools.partial(attend_kernel, heads=heads, first=b == 0), [jax.Sh...  21.1 us
    ppermute x11, starting transfers between devices, from_head(): return lax.ppermute(value, 'head', [(i, (i + by) % n) for i in range(n)])  14 us
    ppermute x3, starting transfers between devices, prior_in_planes(): earlier.append(lax.ppermute(plane, 'ctx', pairs))  10.7 us
    pallas_call x5, Pallas kernels, per_device(): call(functools.partial(output_kernel, n=n, offset=at, parts=out_parts), j...  9.66 us
    ppermute x7, starting transfers between devices, exchange(): return lax.ppermute(value, axis, [(i, i ^ flip) for i in range(count)])  8.36 us
    pallas_call x5, Pallas kernels, per_device(): call(functools.partial(finish_kernel, heads=heads, before=b), jax.ShapeDt...  7.39 us
  transfers between devices with their start and end apart: 22, of which 6 were waited for; matrix products, arithmetic and copies ran while one was open for 1% of the time, Pallas kernels for 45%

profile of v1, /device:TPU:0, one launch (start us, length us, event | category | flops | bytes accessed | tf_op | source)
XLA Modules:
  0.0 144.5 jit_solution(5058173782878411854)
XLA Ops:
  2.7 3.0 %collective-permute-start.4 = (bf16[256,1024]{1,0:T(8,128)(2,1)S(1)}, bf16[256,1024]{1,0:T(8,128)(2,1)S(1)}, u32[]{:S(2)}, u32[]{:S(2)}) collective-permute-start(bf16[256,1024]{1,0:T(8,128)(2,1)S(1)} %get-tuple-element.97.refs_0_), channel_id=1, source_target_pairs={{0,1},{1,0},{2,3},{3,2},{4,5},{5,4},{6,7},{7,6},{8,9},{9,8},{10,11... | collective-permute-start | bytes 1572872 | tf_op jit(solution)/shard_map/ppermute | solution.py:350
  5.8 1.9 %collective-permute-start.5 = (bf16[256,1024]{1,0:T(8,128)(2,1)S(1)}, bf16[256,1024]{1,0:T(8,128)(2,1)S(1)}, u32[]{:S(2)}, u32[]{:S(2)}) collective-permute-start(bf16[256,1024]{1,0:T(8,128)(2,1)S(1)} %get-tuple-element.105.refs_0_), channel_id=1, source_target_pairs={{0,1},{1,0},{2,3},{3,2},{4,5},{5,4},{6,7},{7,6},{8,9},{9,8},{10,11... | collective-permute-start | bytes 1572872 | tf_op jit(solution)/shard_map/ppermute | solution.py:350
  8.4 10.1 %collective-permute-done.4.refs_1_ = bf16[256,1024]{1,0:T(8,128)(2,1)S(1)} collective-permute-done((bf16[256,1024]{1,0:T(8,128)(2,1)S(1)}, bf16[256,1024]{1,0:T(8,128)(2,1)S(1)}, u32[]{:S(2)}, u32[]{:S(2)}) %collective-permute-start.4) | collective-permute-done | bytes 524320 | tf_op jit(solution)/shard_map/ppermute | solution.py:350
  18.5 2.1 %collective-permute-start.18 = (bf16[256,1024]{1,0:T(8,128)(2,1)S(1)}, bf16[256,1024]{1,0:T(8,128)(2,1)S(1)}, u32[]{:S(2)}, u32[]{:S(2)}) collective-permute-start(bf16[256,1024]{1,0:T(8,128)(2,1)S(1)} %shard_map.107), channel_id=1, source_target_pairs={{0,1},{1,0},{2,3},{3,2},{4,5},{5,4},{6,7},{7,6},{8,9},{9,8},{10,11... | collective-permute-start | bytes 1572872 | tf_op jit(solution)/shard_map/ppermute | solution.py:350
  21.6 3.1 %copy-done.4 = bf16[2048,1792]{1,0:T(8,128)(2,1)S(1)} copy-done((bf16[2048,1792]{1,0:T(8,128)(2,1)S(1)}, bf16[2048,1792]{1,0:T(8,128)(2,1)}, u32[]{:S(2)}) %copy-start.4) | copy-done | bytes 7340056
  24.8 5.1 %shard_map.91.w_ref = bf16[2048,1792]{1,0:T(8,128)(2,1)S(1)} custom-call(bf16[2048,1792]{1,0:T(8,128)(2,1)S(1)} %copy-done.4), custom_call_target="tpu_custom_call" | custom-call | flops 1 | bytes 1 | tf_op jit(solution)/shard_map/pallas_call | solution.py:391
  29.9 17.4 %collective-permute-done.2.refs_1_ = bf16[144,1024]{1,0:T(8,128)(2,1)S(1)} collective-permute-done((bf16[144,1024]{1,0:T(8,128)(2,1)S(1)}, bf16[144,1024]{1,0:T(8,128)(2,1)S(1)}, u32[]{:S(2)}, u32[]{:S(2)}) %collective-permute-start.2) | collective-permute-done | bytes 294944 | tf_op jit(solution)/shard_map/ppermute | solution.py:350
  47.3 3.5 %shard_map.92 = (bf16[128,128]{1,0:T(8,128)(2,1)S(1)}, bf16[128,128]{1,0:T(8,128)(2,1)S(1)}, bf16[128,512]{1,0:T(8,128)(2,1)S(1)}, bf16[128,512]{1,0:T(8,128)(2,...) custom-call(s32[3]{0:T(128)S(1)} %pad_add_fusion.j_ref.a_ref._, ...), custom_call_target="tpu_custom_call" | custom-call | flops 1 | bytes 1 | tf_op jit(solution)/shard_map/pallas_call | solution.py:414
  50.8 1.6 %collective-permute-start.3 = (bf16[144,512]{1,0:T(8,128)(2,1)S(1)}, bf16[144,512]{1,0:T(8,128)(2,1)S(1)}, u32[]{:S(2)}, u32[]{:S(2)}) collective-permute-start(bf16[144,512]{1,0:T(8,128)(2,1)S(1)} %get-tuple-element.88), channel_id=1, source_target_pairs={{0,2},{2,4},{4,6},{6,8},{8,10},{10,12},{12,14},{14,16},{16,18},{18... | collective-permute-start | bytes 442376 | tf_op jit(solution)/shard_map/ppermute | solution.py:443
  53.2 4.8 %shard_map.93 = (bf16[256,128]{1,0:T(8,128)(2,1)S(1)}, bf16[256,128]{1,0:T(8,128)(2,1)S(1)}, bf16[256,512]{1,0:T(8,128)(2,1)S(1)}, bf16[256,512]{1,0:T(8,128)(2,...) custom-call(s32[3]{0:T(128)S(1)} %pad_add_fusion.j_ref.a_ref._, ...), custom_call_target="tpu_custom_call" | custom-call | flops 1 | bytes 1 | tf_op jit(solution)/shard_map/pallas_call | solution.py:414
  58.0 5.1 %shard_map.94 = (bf16[256,2048]{1,0:T(8,128)(2,1)S(1)}, f32[256,512]{1,0:T(8,128)S(1)}, f32[256,512]{1,0:T(8,128)S(1)}) custom-call(s32[3]{0:T(128)S(1)} %pad_add_fusion.j_ref.a_ref._, bf16[8,256,128]{2,1,0:T(8,128)(2,1)S(1)} %copy-done.2, bf16[8,256,128]{2,1,0:T(8,128)(2,1)S(1)} %copy-done.1, bf16[144,512]{1,0:T(8,128)(2,1)S(1)} %collective-permute-done.3.refs_2_.prev_ref, ...), custom_call_target="tpu_custom_call" | custom-call | flops 1 | bytes 1 | tf_op jit(solution)/shard_map/pallas_call | solution.py:430
  63.1 4.8 %shard_map.95 = (bf16[256,128]{1,0:T(8,128)(2,1)S(1)}, bf16[256,128]{1,0:T(8,128)(2,1)S(1)}, bf16[256,512]{1,0:T(8,128)(2,1)S(1)}, bf16[256,512]{1,0:T(8,128)(2,...) custom-call(s32[3]{0:T(128)S(1)} %pad_add_fusion.j_ref.a_ref._, ...), custom_call_target="tpu_custom_call" | custom-call | flops 1 | bytes 1 | tf_op jit(solution)/shard_map/pallas_call | solution.py:414
  67.9 5.3 %shard_map.96 = (bf16[256,2048]{1,0:T(8,128)(2,1)S(1)}, f32[256,512]{1,0:T(8,128)S(1)}, f32[256,512]{1,0:T(8,128)S(1)}) custom-call(s32[3]{0:T(128)S(1)} %pad_add_fusion.j_ref.a_ref._, bf16[8,256,128]{2,1,0:T(8,128)(2,1)S(1)} %copy-done.2, bf16[8,256,128]{2,1,0:T(8,128)(2,1)S(1)} %copy-done.1, bf16[144,512]{1,0:T(8,128)(2,1)S(1)} %get-tuple-element.89.refs_2_.prev_ref, ...), custom_call_target="tpu_custom_call" | custom-call | flops 1 | bytes 1 | tf_op jit(solution)/shard_map/pallas_call | solution.py:430
  73.2 4.8 %shard_map.97 = (bf16[256,128]{1,0:T(8,128)(2,1)S(1)}, bf16[256,128]{1,0:T(8,128)(2,1)S(1)}, bf16[256,512]{1,0:T(8,128)(2,1)S(1)}, bf16[256,512]{1,0:T(8,128)(2,...) custom-call(s32[3]{0:T(128)S(1)} %pad_add_fusion.j_ref.a_ref._, ...), custom_call_target="tpu_custom_call" | custom-call | flops 1 | bytes 1 | tf_op jit(solution)/shard_map/pallas_call | solution.py:414
  78.0 3.6 %shard_map.98 = (bf16[128,128]{1,0:T(8,128)(2,1)S(1)}, bf16[128,128]{1,0:T(8,128)(2,1)S(1)}, bf16[128,512]{1,0:T(8,128)(2,1)S(1)}, bf16[128,512]{1,0:T(8,128)(2,...) custom-call(s32[3]{0:T(128)S(1)} %pad_add_fusion.j_ref.a_ref._, ...), custom_call_target="tpu_custom_call" | custom-call | flops 1 | bytes 1 | tf_op jit(solution)/shard_map/pallas_call | solution.py:414
  81.6 3.9 %collective-permute-start.6 = (bf16[160,128]{1,0:T(8,128)(2,1)S(1)}, bf16[160,128]{1,0:T(8,128)(2,1)S(1)}, u32[]{:S(2)}, u32[]{:S(2)}) collective-permute-start(bf16[160,128]{1,0:T(8,128)(2,1)S(1)} %get-tuple-element.135), channel_id=1, source_target_pairs={{0,2},{2,0},{4,6},{6,4},{8,10},{10,8},{12,14},{14,12},{16,18},{18,... | collective-permute-start | bytes 122888 | tf_op jit(solution)/shard_map/ppermute | solution.py:256
  85.5 2.4 %collective-permute-start.7 = (bf16[160,128]{1,0:T(8,128)(2,1)S(1)}, bf16[160,128]{1,0:T(8,128)(2,1)S(1)}, u32[]{:S(2)}, u32[]{:S(2)}) collective-permute-start(bf16[160,128]{1,0:T(8,128)(2,1)S(1)} %get-tuple-element.136), channel_id=1, source_target_pairs={{0,4},{2,6},{4,0},{6,2},{8,12},{10,14},{12,8},{14,10},{16,20},{18,... | collective-permute-start | bytes 122888 | tf_op jit(solution)/shard_map/ppermute | solution.py:256
  88.0 5.1 %shard_map.101 = (bf16[256,2048]{1,0:T(8,128)(2,1)S(1)}, f32[256,512]{1,0:T(8,128)S(1)}, f32[256,512]{1,0:T(8,128)S(1)}) custom-call(s32[3]{0:T(128)S(1)} %pad_add_fusion.j_ref.a_ref._, bf16[8,256,128]{2,1,0:T(8,128)(2,1)S(1)} %copy-done.2, bf16[8,256,128]{2,1,0:T(8,128)(2,1)S(1)} %copy-done.1, bf16[144,512]{1,0:T(8,128)(2,1)S(1)} %get-tuple-element.106.refs_2_.prev_ref, ...), custom_call_target="tpu_custom_call" | custom-call | flops 1 | bytes 1 | tf_op jit(solution)/shard_map/pallas_call | solution.py:430
  93.8 6.6 %collective-permute-start.11 = (bf16[160,128]{1,0:T(8,128)(2,1)S(1)}, bf16[160,128]{1,0:T(8,128)(2,1)S(1)}, u32[]{:S(2)}, u32[]{:S(2)}) collective-permute-start(bf16[160,128]{1,0:T(8,128)(2,1)S(1)} %get-tuple-element.142), channel_id=1, source_target_pairs={{0,24},{2,26},{4,28},{6,30},{1,25},{3,27},{5,29},{7,31}} | collective-permute-start | bytes 122888 | tf_op jit(solution)/shard_map/ppermute | solution.py:303
  101.8 2.7 %collective-permute-start.9 = (bf16[160,128]{1,0:T(8,128)(2,1)S(1)}, bf16[160,128]{1,0:T(8,128)(2,1)S(1)}, u32[]{:S(2)}, u32[]{:S(2)}) collective-permute-start(bf16[160,128]{1,0:T(8,128)(2,1)S(1)} %get-tuple-element.142), channel_id=1, source_target_pairs={{0,8},{2,10},{4,12},{6,14},{8,16},{10,18},{12,20},{14,22},{16,24},... | collective-permute-start | bytes 122888 | tf_op jit(solution)/shard_map/ppermute | solution.py:303
  104.5 2.8 %shard_map.100 = (bf16[128,2048]{1,0:T(8,128)(2,1)S(1)}, f32[128,512]{1,0:T(8,128)S(1)}, f32[128,512]{1,0:T(8,128)S(1)}) custom-call(s32[3]{0:T(128)S(1)} %pad_add_fusion.j_ref.a_ref._, bf16[8,256,128]{2,1,0:T(8,128)(2,1)S(1)} %copy-done.2, bf16[8,256,128]{2,1,0:T(8,128)(2,1)S(1)} %copy-done.1, bf16[144,512]{1,0:T(8,128)(2,1)S(1)} %get-tuple-element.107.refs_2_.prev_ref, ...), custom_call_target="tpu_custom_call" | custom-call | flops 1 | bytes 1 | tf_op jit(solution)/shard_map/pallas_call | solution.py:430
  109.8 2.8 %shard_map.99 = (bf16[128,2048]{1,0:T(8,128)(2,1)S(1)}, f32[128,512]{1,0:T(8,128)S(1)}, f32[128,512]{1,0:T(8,128)S(1)}) custom-call(s32[3]{0:T(128)S(1)} %pad_add_fusion.j_ref.a_ref._, bf16[8,256,128]{2,1,0:T(8,128)(2,1)S(1)} %copy-done.2, bf16[8,256,128]{2,1,0:T(8,128)(2,1)S(1)} %copy-done.1, bf16[144,512]{1,0:T(8,128)(2,1)S(1)} %get-tuple-element.112.prev_ref, ...), custom_call_target="tpu_custom_call" | custom-call | flops 1 | bytes 1 | tf_op jit(solution)/shard_map/pallas_call | solution.py:430
  114.0 1.6 %collective-permute-start.15 = (bf16[128,512]{1,0:T(8,128)(2,1)S(1)}, bf16[128,512]{1,0:T(8,128)(2,1)S(1)}, u32[]{:S(2)}, u32[]{:S(2)}) collective-permute-start(bf16[128,512]{1,0:T(8,128)(2,1)S(1)} %shard_map.104.own_ref), channel_id=1, source_target_pairs={{0,1},{1,0},{2,3},{3,2},{4,5},{5,4},{6,7},{7,6},{8,9},{9,8},{10,11... | collective-permute-start | bytes 393224 | tf_op jit(solution)/shard_map/ppermute | solution.py:350
  117.7 2.1 %collective-permute-done.15.refs_0_ = bf16[128,512]{1,0:T(8,128)(2,1)S(1)} collective-permute-done((bf16[128,512]{1,0:T(8,128)(2,1)S(1)}, bf16[128,512]{1,0:T(8,128)(2,1)S(1)}, u32[]{:S(2)}, u32[]{:S(2)}) %collective-permute-start.15) | collective-permute-done | bytes 131104 | tf_op jit(solution)/shard_map/ppermute | solution.py:350
  121.4 2.2 %collective-permute-start.16 = (bf16[256,512]{1,0:T(8,128)(2,1)S(1)}, bf16[256,512]{1,0:T(8,128)(2,1)S(1)}, u32[]{:S(2)}, u32[]{:S(2)}) collective-permute-start(bf16[256,512]{1,0:T(8,128)(2,1)S(1)} %shard_map.105.own_ref), channel_id=1, source_target_pairs={{0,1},{1,0},{2,3},{3,2},{4,5},{5,4},{6,7},{7,6},{8,9},{9,8},{10,11... | collective-permute-start | bytes 786440 | tf_op jit(solution)/shard_map/ppermute | solution.py:350
  123.5 2.9 %collective-permute-done.20.refs_0_ = bf16[256,512]{1,0:T(8,128)(2,1)S(1)} collective-permute-done((bf16[256,512]{1,0:T(8,128)(2,1)S(1)}, bf16[256,512]{1,0:T(8,128)(2,1)S(1)}, u32[]{:S(2)}, u32[]{:S(2)}) %collective-permute-start.20) | collective-permute-done | bytes 262176 | tf_op jit(solution)/shard_map/ppermute | solution.py:350
  129.2 2.8 %collective-permute-done.16.refs_0_ = bf16[256,512]{1,0:T(8,128)(2,1)S(1)} collective-permute-done((bf16[256,512]{1,0:T(8,128)(2,1)S(1)}, bf16[256,512]{1,0:T(8,128)(2,1)S(1)}, u32[]{:S(2)}, u32[]{:S(2)}) %collective-permute-start.16) | collective-permute-done | bytes 262176 | tf_op jit(solution)/shard_map/ppermute | solution.py:350
  134.6 1.7 %shard_map.110.refs_3_ = bf16[1024,1024]{1,0:T(8,128)(2,1)} custom-call(s32[3]{0:T(128)S(1)} %pad_add_fusion.j_ref.a_ref._, bf16[128,512]{1,0:T(8,128)(2,1)S(1)} %shard_map.104.own_ref, bf16[512,2048]{1,0:T(8,128)(2,1)S(1)} %copy-done, bf16[128,512]{1,0:T(8,128)(2,1)S(1)} %collective-permute-done.15.refs_0_, ...), custom_call_target="tpu_custom_call" | custom-call | flops 1 | bytes 1 | tf_op jit(solution)/shard_map/pallas_call | solution.py:488
  136.3 2.1 %shard_map.111.refs_3_ = bf16[1024,1024]{1,0:T(8,128)(2,1)} custom-call(s32[3]{0:T(128)S(1)} %pad_add_fusion.j_ref.a_ref._, bf16[256,512]{1,0:T(8,128)(2,1)S(1)} %shard_map.108.own_ref, bf16[512,2048]{1,0:T(8,128)(2,1)S(1)} %copy-done, bf16[256,512]{1,0:T(8,128)(2,1)S(1)} %collective-permute-done.20.refs_0_, ...), custom_call_target="tpu_custom_call", output_to_operand_aliasing={{}: (6, {})} | custom-call | flops 1 | bytes 1 | tf_op jit(solution)/shard_map/pallas_call | solution.py:488
  138.4 2.1 %shard_map.112.refs_3_ = bf16[1024,1024]{1,0:T(8,128)(2,1)} custom-call(s32[3]{0:T(128)S(1)} %pad_add_fusion.j_ref.a_ref._, bf16[256,512]{1,0:T(8,128)(2,1)S(1)} %shard_map.105.own_ref, bf16[512,2048]{1,0:T(8,128)(2,1)S(1)} %copy-done, bf16[256,512]{1,0:T(8,128)(2,1)S(1)} %collective-permute-done.16.refs_0_, ...), custom_call_target="tpu_custom_call", output_to_operand_aliasing={{}: (6, {})} | custom-call | flops 1 | bytes 1 | tf_op jit(solution)/shard_map/pallas_call | solution.py:488
  140.5 2.1 %shard_map.113.refs_3_ = bf16[1024,1024]{1,0:T(8,128)(2,1)} custom-call(s32[3]{0:T(128)S(1)} %pad_add_fusion.j_ref.a_ref._, bf16[256,512]{1,0:T(8,128)(2,1)S(1)} %shard_map.109.own_ref, bf16[512,2048]{1,0:T(8,128)(2,1)S(1)} %copy-done, bf16[256,512]{1,0:T(8,128)(2,1)S(1)} %collective-permute-done.21.refs_0_, ...), custom_call_target="tpu_custom_call", output_to_operand_aliasing={{}: (6, {})} | custom-call | flops 1 | bytes 1 | tf_op jit(solution)/shard_map/pallas_call | solution.py:488
  142.6 1.7 %shard_map.114 = bf16[1024,1024]{1,0:T(8,128)(2,1)} custom-call(s32[3]{0:T(128)S(1)} %pad_add_fusion.j_ref.a_ref._, bf16[128,512]{1,0:T(8,128)(2,1)S(1)} %shard_map.106.own_ref, bf16[512,2048]{1,0:T(8,128)(2,1)S(1)} %copy-done, bf16[128,512]{1,0:T(8,128)(2,1)S(1)} %collective-permute-done.17.refs_0_, ...), custom_call_target="tpu_custom_call", output_to_operand_aliasing={{}: (6, {})} | custom-call | flops 1 | bytes 1 | tf_op jit(solution)/shard_map/pallas_call | solution.py:488
  (56 shorter events, 20.2 us)
Async XLA Ops:
  0.0 7.8 %copy-start = (bf16[512,2048]{1,0:T(8,128)(2,1)S(1)}, bf16[512,2048]{1,0:T(8,128)(2,1)}, u32[]{:S(2)}) copy-start(bf16[512,2048]{1,0:T(8,128)(2,1)} %w_ref.13) | copy-start | bytes 6291460
  2.7 15.8 %collective-permute-start.4 = (bf16[256,1024]{1,0:T(8,128)(2,1)S(1)}, bf16[256,1024]{1,0:T(8,128)(2,1)S(1)}, u32[]{:S(2)}, u32[]{:S(2)}) collective-permute-start(bf16[256,1024]{1,0:T(8,128)(2,1)S(1)} %get-tuple-element.97.refs_0_), channel_id=1, source_target_pairs={{0,1},{1,0},{2,3},{3,2},{4,5},{5,4},{6,7},{7,6},{8,9},{9,8},{10,11... | collective-permute-start | bytes 1572872 | tf_op jit(solution)/shard_map/ppermute | solution.py:350
  5.7 47.5 %collective-permute-start.1 = (bf16[256,1024]{1,0:T(8,128)(2,1)S(1)}, bf16[256,1024]{1,0:T(8,128)(2,1)S(1)}, u32[]{:S(2)}, u32[]{:S(2)}) collective-permute-start(bf16[256,1024]{1,0:T(8,128)(2,1)S(1)} %get-tuple-element.87.refs_0_), channel_id=1, source_target_pairs={{0,1},{1,0},{2,3},{3,2},{4,5},{5,4},{6,7},{7,6},{8,9},{9,8},{10,11... | collective-permute-start | bytes 1572872 | tf_op jit(solution)/shard_map/ppermute | solution.py:350
  5.8 67.4 %collective-permute-start.5 = (bf16[256,1024]{1,0:T(8,128)(2,1)S(1)}, bf16[256,1024]{1,0:T(8,128)(2,1)S(1)}, u32[]{:S(2)}, u32[]{:S(2)}) collective-permute-start(bf16[256,1024]{1,0:T(8,128)(2,1)S(1)} %get-tuple-element.105.refs_0_), channel_id=1, source_target_pairs={{0,1},{1,0},{2,3},{3,2},{4,5},{5,4},{6,7},{7,6},{8,9},{9,8},{10,11... | collective-permute-start | bytes 1572872 | tf_op jit(solution)/shard_map/ppermute | solution.py:350
  7.7 39.5 %collective-permute-start.2 = (bf16[144,1024]{1,0:T(8,128)(2,1)S(1)}, bf16[144,1024]{1,0:T(8,128)(2,1)S(1)}, u32[]{:S(2)}, u32[]{:S(2)}) collective-permute-start(bf16[144,1024]{1,0:T(8,128)(2,1)S(1)} %slice.16.refs_0_), channel_id=1, source_target_pairs={{0,1},{1,0},{2,3},{3,2},{4,5},{5,4},{6,7},{7,6},{8,9},{9,8},{10,11... | collective-permute-start | bytes 884744 | tf_op jit(solution)/shard_map/ppermute | solution.py:350
  18.5 99.3 %collective-permute-start.18 = (bf16[256,1024]{1,0:T(8,128)(2,1)S(1)}, bf16[256,1024]{1,0:T(8,128)(2,1)S(1)}, u32[]{:S(2)}, u32[]{:S(2)}) collective-permute-start(bf16[256,1024]{1,0:T(8,128)(2,1)S(1)} %shard_map.107), channel_id=1, source_target_pairs={{0,1},{1,0},{2,3},{3,2},{4,5},{5,4},{6,7},{7,6},{8,9},{9,8},{10,11... | collective-permute-start | bytes 1572872 | tf_op jit(solution)/shard_map/ppermute | solution.py:350
  21.5 25.8 %copy-start.1 = (bf16[8,256,128]{2,1,0:T(8,128)(2,1)S(1)}, bf16[8,256,128]{2,1,0:T(8,128)(2,1)}, u32[]{:S(2)}) copy-start(bf16[8,256,128]{2,1,0:T(8,128)(2,1)} %constant.30.clone.sel_b_ref) | copy-start | bytes 1572868
  21.5 25.8 %copy-start.3 = (bf16[8,256,128]{2,1,0:T(8,128)(2,1)S(1)}, bf16[8,256,128]{2,1,0:T(8,128)(2,1)}, u32[]{:S(2)}) copy-start(bf16[8,256,128]{2,1,0:T(8,128)(2,1)} %constant.31.clone.sel_w_ref) | copy-start | bytes 1572868
  21.5 56.5 %collective-permute-start = (bf16[128,1024]{1,0:T(8,128)(2,1)S(1)}, bf16[128,1024]{1,0:T(8,128)(2,1)S(1)}, u32[]{:S(2)}, u32[]{:S(2)}) collective-permute-start(bf16[128,1024]{1,0:T(8,128)(2,1)S(1)} %slice.15.refs_0_), channel_id=1, source_target_pairs={{0,1},{1,0},{2,3},{3,2},{4,5},{5,4},{6,7},{7,6},{8,9},{9,8},{10,11... | collective-permute-start | bytes 786440 | tf_op jit(solution)/shard_map/ppermute | solution.py:350
  21.6 3.2 %copy-start.4 = (bf16[2048,1792]{1,0:T(8,128)(2,1)S(1)}, bf16[2048,1792]{1,0:T(8,128)(2,1)}, u32[]{:S(2)}) copy-start(bf16[2048,1792]{1,0:T(8,128)(2,1)} %w_ref.7) | copy-start | bytes 22020100
  24.8 22.5 %copy-start.5 = (bf16[256,128]{1,0:T(8,128)(2,1)S(1)}, bf16[256,128]{1,0:T(8,128)(2,1)}, u32[]{:S(2)}) copy-start(bf16[256,128]{1,0:T(8,128)(2,1)} %constant.32.clone.mean_ref) | copy-start | bytes 196612
  24.8 22.5 %copy-start.6 = (f32[3,512]{1,0:T(4,128)S(1)}, f32[3,512]{1,0:T(4,128)}, u32[]{:S(2)}) copy-start(f32[3,512]{1,0:T(4,128)} %conv_ref.9) | copy-start | bytes 18436
  50.8 7.2 %copy-start.2 = (bf16[8,256,128]{2,1,0:T(8,128)(2,1)S(1)}, bf16[8,256,128]{2,1,0:T(8,128)(2,1)}, u32[]{:S(2)}) copy-start(bf16[8,256,128]{2,1,0:T(8,128)(2,1)} %constant.29.clone.sel_a_ref) | copy-start | bytes 1572868
  50.8 2.4 %collective-permute-start.3 = (bf16[144,512]{1,0:T(8,128)(2,1)S(1)}, bf16[144,512]{1,0:T(8,128)(2,1)S(1)}, u32[]{:S(2)}, u32[]{:S(2)}) collective-permute-start(bf16[144,512]{1,0:T(8,128)(2,1)S(1)} %get-tuple-element.88), channel_id=1, source_target_pairs={{0,2},{2,4},{4,6},{6,8},{8,10},{10,12},{12,14},{14,16},{16,18},{18... | collective-permute-start | bytes 442376 | tf_op jit(solution)/shard_map/ppermute | solution.py:443
  81.6 11.5 %collective-permute-start.6 = (bf16[160,128]{1,0:T(8,128)(2,1)S(1)}, bf16[160,128]{1,0:T(8,128)(2,1)S(1)}, u32[]{:S(2)}, u32[]{:S(2)}) collective-permute-start(bf16[160,128]{1,0:T(8,128)(2,1)S(1)} %get-tuple-element.135), channel_id=1, source_target_pairs={{0,2},{2,0},{4,6},{6,4},{8,10},{10,8},{12,14},{14,12},{16,18},{18,... | collective-permute-start | bytes 122888 | tf_op jit(solution)/shard_map/ppermute | solution.py:256
  85.5 7.6 %collective-permute-start.7 = (bf16[160,128]{1,0:T(8,128)(2,1)S(1)}, bf16[160,128]{1,0:T(8,128)(2,1)S(1)}, u32[]{:S(2)}, u32[]{:S(2)}) collective-permute-start(bf16[160,128]{1,0:T(8,128)(2,1)S(1)} %get-tuple-element.136), channel_id=1, source_target_pairs={{0,4},{2,6},{4,0},{6,2},{8,12},{10,14},{12,8},{14,10},{16,20},{18,... | collective-permute-start | bytes 122888 | tf_op jit(solution)/shard_map/ppermute | solution.py:256
  88.0 5.2 %collective-permute-start.8 = (bf16[160,128]{1,0:T(8,128)(2,1)S(1)}, bf16[160,128]{1,0:T(8,128)(2,1)S(1)}, u32[]{:S(2)}, u32[]{:S(2)}) collective-permute-start(bf16[160,128]{1,0:T(8,128)(2,1)S(1)} %get-tuple-element.137), channel_id=1, source_target_pairs={{0,6},{2,4},{4,2},{6,0},{8,14},{10,12},{12,10},{14,8},{16,22},{18,... | collective-permute-start | bytes 122888 | tf_op jit(solution)/shard_map/ppermute | solution.py:256
  93.1 19.5 %copy-start.7 = (f32[512]{0:T(512)S(1)}, f32[512]{0:T(512)}, u32[]{:S(2)}) copy-start(f32[512]{0:T(512)} %param.12) | copy-start | bytes 6148
  93.8 13.5 %collective-permute-start.11 = (bf16[160,128]{1,0:T(8,128)(2,1)S(1)}, bf16[160,128]{1,0:T(8,128)(2,1)S(1)}, u32[]{:S(2)}, u32[]{:S(2)}) collective-permute-start(bf16[160,128]{1,0:T(8,128)(2,1)S(1)} %get-tuple-element.142), channel_id=1, source_target_pairs={{0,24},{2,26},{4,28},{6,30},{1,25},{3,27},{5,29},{7,31}} | collective-permute-start | bytes 122888 | tf_op jit(solution)/shard_map/ppermute | solution.py:303
  100.5 6.8 %collective-permute-start.10 = (bf16[160,128]{1,0:T(8,128)(2,1)S(1)}, bf16[160,128]{1,0:T(8,128)(2,1)S(1)}, u32[]{:S(2)}, u32[]{:S(2)}) collective-permute-start(bf16[160,128]{1,0:T(8,128)(2,1)S(1)} %get-tuple-element.142), channel_id=1, source_target_pairs={{0,16},{2,18},{4,20},{6,22},{8,24},{10,26},{12,28},{14,30},{1,17},... | collective-permute-start | bytes 122888 | tf_op jit(solution)/shard_map/ppermute | solution.py:303
  101.8 5.5 %collective-permute-start.9 = (bf16[160,128]{1,0:T(8,128)(2,1)S(1)}, bf16[160,128]{1,0:T(8,128)(2,1)S(1)}, u32[]{:S(2)}, u32[]{:S(2)}) collective-permute-start(bf16[160,128]{1,0:T(8,128)(2,1)S(1)} %get-tuple-element.142), channel_id=1, source_target_pairs={{0,8},{2,10},{4,12},{6,14},{8,16},{10,18},{12,20},{14,22},{16,24},... | collective-permute-start | bytes 122888 | tf_op jit(solution)/shard_map/ppermute | solution.py:303
  107.9 4.7 %collective-permute-start.12 = (bf16[160,128]{1,0:T(8,128)(2,1)S(1)}, bf16[160,128]{1,0:T(8,128)(2,1)S(1)}, u32[]{:S(2)}, u32[]{:S(2)}) collective-permute-start(bf16[160,128]{1,0:T(8,128)(2,1)S(1)} %get-tuple-element.144), channel_id=1, source_target_pairs={{0,2},{2,0},{4,6},{6,4},{8,10},{10,8},{12,14},{14,12},{16,18},{18,... | collective-permute-start | bytes 122888 | tf_op jit(solution)/shard_map/ppermute | solution.py:256
  108.0 4.6 %collective-permute-start.13 = (bf16[160,128]{1,0:T(8,128)(2,1)S(1)}, bf16[160,128]{1,0:T(8,128)(2,1)S(1)}, u32[]{:S(2)}, u32[]{:S(2)}) collective-permute-start(bf16[160,128]{1,0:T(8,128)(2,1)S(1)} %get-tuple-element.145), channel_id=1, source_target_pairs={{0,4},{2,6},{4,0},{6,2},{8,12},{10,14},{12,8},{14,10},{16,20},{18,... | collective-permute-start | bytes 122888 | tf_op jit(solution)/shard_map/ppermute | solution.py:256
  108.6 4.0 %collective-permute-start.14 = (bf16[160,128]{1,0:T(8,128)(2,1)S(1)}, bf16[160,128]{1,0:T(8,128)(2,1)S(1)}, u32[]{:S(2)}, u32[]{:S(2)}) collective-permute-start(bf16[160,128]{1,0:T(8,128)(2,1)S(1)} %get-tuple-element.146), channel_id=1, source_target_pairs={{0,6},{2,4},{4,2},{6,0},{8,14},{10,12},{12,10},{14,8},{16,22},{18,... | collective-permute-start | bytes 122888 | tf_op jit(solution)/shard_map/ppermute | solution.py:256
  114.0 5.8 %collective-permute-start.15 = (bf16[128,512]{1,0:T(8,128)(2,1)S(1)}, bf16[128,512]{1,0:T(8,128)(2,1)S(1)}, u32[]{:S(2)}, u32[]{:S(2)}) collective-permute-start(bf16[128,512]{1,0:T(8,128)(2,1)S(1)} %shard_map.104.own_ref), channel_id=1, source_target_pairs={{0,1},{1,0},{2,3},{3,2},{4,5},{5,4},{6,7},{7,6},{8,9},{9,8},{10,11... | collective-permute-start | bytes 393224 | tf_op jit(solution)/shard_map/ppermute | solution.py:350
  117.2 9.2 %collective-permute-start.20 = (bf16[256,512]{1,0:T(8,128)(2,1)S(1)}, bf16[256,512]{1,0:T(8,128)(2,1)S(1)}, u32[]{:S(2)}, u32[]{:S(2)}) collective-permute-start(bf16[256,512]{1,0:T(8,128)(2,1)S(1)} %shard_map.108.own_ref), channel_id=1, source_target_pairs={{0,1},{1,0},{2,3},{3,2},{4,5},{5,4},{6,7},{7,6},{8,9},{9,8},{10,11... | collective-permute-start | bytes 786440 | tf_op jit(solution)/shard_map/ppermute | solution.py:350
  117.7 16.9 %collective-permute-start.19 = (bf16[256,1024]{1,0:T(8,128)(2,1)S(1)}, bf16[256,1024]{1,0:T(8,128)(2,1)S(1)}, u32[]{:S(2)}, u32[]{:S(2)}) collective-permute-start(bf16[256,1024]{1,0:T(8,128)(2,1)S(1)} %collective-permute-done.18.refs_1_), channel_id=1, source_target_pairs={{0,2},{2,0},{4,6},{6,4},{8,10},{10,8},{12,14},{14,12},{16,18},{18,... | collective-permute-start | bytes 1572872 | tf_op jit(solution)/shard_map/ppermute | solution.py:256
  121.4 10.6 %collective-permute-start.16 = (bf16[256,512]{1,0:T(8,128)(2,1)S(1)}, bf16[256,512]{1,0:T(8,128)(2,1)S(1)}, u32[]{:S(2)}, u32[]{:S(2)}) collective-permute-start(bf16[256,512]{1,0:T(8,128)(2,1)S(1)} %shard_map.105.own_ref), channel_id=1, source_target_pairs={{0,1},{1,0},{2,3},{3,2},{4,5},{5,4},{6,7},{7,6},{8,9},{9,8},{10,11... | collective-permute-start | bytes 786440 | tf_op jit(solution)/shard_map/ppermute | solution.py:350
  127.9 12.5 %collective-permute-start.21 = (bf16[256,512]{1,0:T(8,128)(2,1)S(1)}, bf16[256,512]{1,0:T(8,128)(2,1)S(1)}, u32[]{:S(2)}, u32[]{:S(2)}) collective-permute-start(bf16[256,512]{1,0:T(8,128)(2,1)S(1)} %shard_map.109.own_ref), channel_id=1, source_target_pairs={{0,1},{1,0},{2,3},{3,2},{4,5},{5,4},{6,7},{7,6},{8,9},{9,8},{10,11... | collective-permute-start | bytes 786440 | tf_op jit(solution)/shard_map/ppermute | solution.py:350
  133.4 9.2 %collective-permute-start.17 = (bf16[128,512]{1,0:T(8,128)(2,1)S(1)}, bf16[128,512]{1,0:T(8,128)(2,1)S(1)}, u32[]{:S(2)}, u32[]{:S(2)}) collective-permute-start(bf16[128,512]{1,0:T(8,128)(2,1)S(1)} %shard_map.106.own_ref), channel_id=1, source_target_pairs={{0,1},{1,0},{2,3},{3,2},{4,5},{5,4},{6,7},{7,6},{8,9},{9,8},{10,11... | collective-permute-start | bytes 393224 | tf_op jit(solution)/shard_map/ppermute | solution.py:350

commit v2 on v1

--- a/solution.py
+++ b/solution.py
@@ -338,7 +338,7 @@
     places = jnp.stack([me, position % PLANE if in_planes else jnp.zeros_like(position), position])
     hidden_in, places = lax.optimization_barrier((hidden_in, places))
     step = row_count // 8
-    blocks = [(0, 2 * step), (2 * step, 2 * step), (4 * step, 2 * step), (6 * step, step), (7 * step, step)]
+    blocks = [(0, 2 * step), (2 * step, 2 * step), (4 * step, step), (5 * step, step), (6 * step, 2 * step)]
     last = len(blocks) - 1
     sel_a, sel_b, sel_w = feature_tables(heads)
     means = mean_table()
@@ -367,7 +367,7 @@
     cols = out_weight.shape[1] // n
     out_parts = 2 if width // 2 % LANES == 0 and ctx % 2 == 0 else 1
     share = width // out_parts
-    fetched = []
+    picked = []
     for r in range(1, n):
         block = call(
             pick_kernel,
@@ -383,7 +383,7 @@
             moved=4 * share * cols,
             vmem=8 << 20,
         )(places, out_weight)
-        fetched.append(from_head(after(block, pieces[1][-1]), r))
+        picked.append(block)
 
     qk_width = -(-heads * FQK // LANES) * LANES
     arranged_width = 2 * qk_width + 3 * width
@@ -448,6 +448,8 @@
         if b < last - 2:
             attended[b] = attend(b, prev)
 
+    fetched = [from_head(after(block, done[last - 1][5]), r) for r, block in enumerate(picked, 1)]
+
     for b in range(last - 2, last + 1):
         attended[b] = attend(b, done[b - 1][5])
     if in_planes:
@@ -463,7 +465,7 @@
 
     result = None
     arrived = []
-    for i, b in enumerate((3, 0, 1, 2, 4)):
+    for i, b in enumerate((3, 0, 1, 4, 2)):
         at, rows = blocks[b]
         behind = after(places, arrived[i - 2] if i >= 2 else attended[last][1])
         mixed = call(

time: 145 us -> 117 us (0.81)
  waiting for transfers between devices: 36.1 us -> 14.5 us
  starting transfers between devices: 34.6 us -> 28.3 us
    ppermute x11, waiting for transfers between devices: 35.3 us -> 14.1 us  [from_head(): return lax.ppermute(value, 'head', [(i, (i + by) % n) for i in range(n)])]
    ppermute x7, starting transfers between devices: 8.36 us -> 3.8 us  [exchange(): return lax.ppermute(value, axis, [(i, i ^ flip) for i in range(count)])]
  transfers between devices with their start and end apart: 22 -> 22, of which waited for: 6 -> 6; matrix products, arithmetic and copies ran while one was open for 1% -> 2% of each run, Pallas kernels for 45% -> 52%
where the time goes in v2:
time: 117 us; the launch traced here: 116 us
  Pallas kernels  66.4 us (57%)
  starting transfers between devices  28.3 us (24%)
  waiting for transfers between devices  14.5 us (12%)
  local copies, waits for them, and re-layouts  6.54 us (6%)
    pallas_call x5, Pallas kernels, do_block(): call(functools.partial(block_kernel, n=n, heads=heads, extra=extra, other...  21.3 us
    pallas_call x5, Pallas kernels, attend(): call(functools.partial(attend_kernel, heads=heads, first=b == 0), [jax.Sh...  21.1 us
    ppermute x11, waiting for transfers between devices, from_head(): return lax.ppermute(value, 'head', [(i, (i + by) % n) for i in range(n)])  14.1 us
    ppermute x11, starting transfers between devices, from_head(): return lax.ppermute(value, 'head', [(i, (i + by) % n) for i in range(n)])  13.4 us
    pallas_call x5, Pallas kernels, per_device(): call(functools.partial(output_kernel, n=n, offset=at, parts=out_parts), j...  9.66 us
    ppermute x3, starting transfers between devices, prior_in_planes(): earlier.append(lax.ppermute(plane, 'ctx', pairs))  9.53 us
    pallas_call x5, Pallas kernels, per_device(): call(functools.partial(finish_kernel, heads=heads, before=b), jax.ShapeDt...  7.4 us
    pallas_call x1, Pallas kernels, per_device(): call(functools.partial(arrange_kernel, heads=heads), jax.ShapeDtypeStruct...  5.09 us
  transfers between devices with their start and end apart: 22, of which 6 were waited for; matrix products, arithmetic and copies ran while one was open for 2% of the time, Pallas kernels for 52%

profile of v2, /device:TPU:0, one launch (start us, length us, event | category | flops | bytes accessed | tf_op | source)
XLA Modules:
  0.0 116.4 jit_solution(13776316687255468122)
XLA Ops:
  1.2 3.0 %collective-permute-start.2 = (bf16[272,1024]{1,0:T(8,128)(2,1)S(1)}, bf16[272,1024]{1,0:T(8,128)(2,1)S(1)}, u32[]{:S(2)}, u32[]{:S(2)}) collective-permute-start(bf16[272,1024]{1,0:T(8,128)(2,1)S(1)} %slice.16.refs_0_), channel_id=1, source_target_pairs={{0,1},{1,0},{2,3},{3,2},{4,5},{5,4},{6,7},{7,6},{8,9},{9,8},{10,11... | collective-permute-start | bytes 1671176 | tf_op jit(solution)/shard_map/ppermute | solution.py:350
  5.6 2.0 %collective-permute-start.4 = (bf16[256,1024]{1,0:T(8,128)(2,1)S(1)}, bf16[256,1024]{1,0:T(8,128)(2,1)S(1)}, u32[]{:S(2)}, u32[]{:S(2)}) collective-permute-start(bf16[256,1024]{1,0:T(8,128)(2,1)S(1)} %get-tuple-element.97.refs_0_), channel_id=1, source_target_pairs={{0,1},{1,0},{2,3},{3,2},{4,5},{5,4},{6,7},{7,6},{8,9},{9,8},{10,11... | collective-permute-start | bytes 1572872 | tf_op jit(solution)/shard_map/ppermute | solution.py:350
  8.8 1.9 %collective-permute-start = (bf16[128,1024]{1,0:T(8,128)(2,1)S(1)}, bf16[128,1024]{1,0:T(8,128)(2,1)S(1)}, u32[]{:S(2)}, u32[]{:S(2)}) collective-permute-start(bf16[128,1024]{1,0:T(8,128)(2,1)S(1)} %get-tuple-element.86.refs_0_), channel_id=1, source_target_pairs={{0,1},{1,0},{2,3},{3,2},{4,5},{5,4},{6,7},{7,6},{8,9},{9,8},{10,11... | collective-permute-start | bytes 786440 | tf_op jit(solution)/shard_map/ppermute | solution.py:350
  10.7 3.1 %copy-done.4 = bf16[2048,1792]{1,0:T(8,128)(2,1)S(1)} copy-done((bf16[2048,1792]{1,0:T(8,128)(2,1)S(1)}, bf16[2048,1792]{1,0:T(8,128)(2,1)}, u32[]{:S(2)}) %copy-start.4) | copy-done | bytes 7340056
  13.8 5.1 %shard_map.91.w_ref = bf16[2048,1792]{1,0:T(8,128)(2,1)S(1)} custom-call(bf16[2048,1792]{1,0:T(8,128)(2,1)S(1)} %copy-done.4), custom_call_target="tpu_custom_call" | custom-call | flops 1 | bytes 1 | tf_op jit(solution)/shard_map/pallas_call | solution.py:391
  19.0 4.8 %shard_map.92 = (bf16[256,128]{1,0:T(8,128)(2,1)S(1)}, bf16[256,128]{1,0:T(8,128)(2,1)S(1)}, bf16[256,512]{1,0:T(8,128)(2,1)S(1)}, bf16[256,512]{1,0:T(8,128)(2,...) custom-call(s32[3]{0:T(128)S(1)} %pad_add_fusion.j_ref.a_ref._, ...), custom_call_target="tpu_custom_call" | custom-call | flops 1 | bytes 1 | tf_op jit(solution)/shard_map/pallas_call | solution.py:414
  25.9 3.0 %collective-permute-done.1.refs_1_ = bf16[256,1024]{1,0:T(8,128)(2,1)S(1)} collective-permute-done((bf16[256,1024]{1,0:T(8,128)(2,1)S(1)}, bf16[256,1024]{1,0:T(8,128)(2,1)S(1)}, u32[]{:S(2)}, u32[]{:S(2)}) %collective-permute-start.1) | collective-permute-done | bytes 524320 | tf_op jit(solution)/shard_map/ppermute | solution.py:350
  28.9 4.8 %shard_map.93 = (bf16[256,128]{1,0:T(8,128)(2,1)S(1)}, bf16[256,128]{1,0:T(8,128)(2,1)S(1)}, bf16[256,512]{1,0:T(8,128)(2,1)S(1)}, bf16[256,512]{1,0:T(8,128)(2,...) custom-call(s32[3]{0:T(128)S(1)} %pad_add_fusion.j_ref.a_ref._, ...), custom_call_target="tpu_custom_call" | custom-call | flops 1 | bytes 1 | tf_op jit(solution)/shard_map/pallas_call | solution.py:414
  33.7 5.1 %shard_map.94 = (bf16[256,2048]{1,0:T(8,128)(2,1)S(1)}, f32[256,512]{1,0:T(8,128)S(1)}, f32[256,512]{1,0:T(8,128)S(1)}) custom-call(s32[3]{0:T(128)S(1)} %pad_add_fusion.j_ref.a_ref._, bf16[8,256,128]{2,1,0:T(8,128)(2,1)S(1)} %copy-done.2, bf16[8,256,128]{2,1,0:T(8,128)(2,1)S(1)} %copy-done.1, bf16[144,512]{1,0:T(8,128)(2,1)S(1)} %collective-permute-done.3.refs_2_.prev_ref, ...), custom_call_target="tpu_custom_call" | custom-call | flops 1 | bytes 1 | tf_op jit(solution)/shard_map/pallas_call | solution.py:430
  40.1 4.8 %shard_map.95 = (bf16[256,128]{1,0:T(8,128)(2,1)S(1)}, bf16[256,128]{1,0:T(8,128)(2,1)S(1)}, bf16[256,512]{1,0:T(8,128)(2,1)S(1)}, bf16[256,512]{1,0:T(8,128)(2,...) custom-call(s32[3]{0:T(128)S(1)} %pad_add_fusion.j_ref.a_ref._, ...), custom_call_target="tpu_custom_call" | custom-call | flops 1 | bytes 1 | tf_op jit(solution)/shard_map/pallas_call | solution.py:414
  44.9 5.3 %shard_map.96 = (bf16[256,2048]{1,0:T(8,128)(2,1)S(1)}, f32[256,512]{1,0:T(8,128)S(1)}, f32[256,512]{1,0:T(8,128)S(1)}) custom-call(s32[3]{0:T(128)S(1)} %pad_add_fusion.j_ref.a_ref._, bf16[8,256,128]{2,1,0:T(8,128)(2,1)S(1)} %copy-done.2, bf16[8,256,128]{2,1,0:T(8,128)(2,1)S(1)} %copy-done.1, bf16[144,512]{1,0:T(8,128)(2,1)S(1)} %get-tuple-element.89.refs_2_.prev_ref, ...), custom_call_target="tpu_custom_call" | custom-call | flops 1 | bytes 1 | tf_op jit(solution)/shard_map/pallas_call | solution.py:430
  50.2 3.5 %shard_map.97 = (bf16[128,128]{1,0:T(8,128)(2,1)S(1)}, bf16[128,128]{1,0:T(8,128)(2,1)S(1)}, bf16[128,512]{1,0:T(8,128)(2,1)S(1)}, bf16[128,512]{1,0:T(8,128)(2,...) custom-call(s32[3]{0:T(128)S(1)} %pad_add_fusion.j_ref.a_ref._, ...), custom_call_target="tpu_custom_call" | custom-call | flops 1 | bytes 1 | tf_op jit(solution)/shard_map/pallas_call | solution.py:414
  53.7 3.6 %shard_map.98 = (bf16[128,128]{1,0:T(8,128)(2,1)S(1)}, bf16[128,128]{1,0:T(8,128)(2,1)S(1)}, bf16[128,512]{1,0:T(8,128)(2,1)S(1)}, bf16[128,512]{1,0:T(8,128)(2,...) custom-call(s32[3]{0:T(128)S(1)} %pad_add_fusion.j_ref.a_ref._, ...), custom_call_target="tpu_custom_call" | custom-call | flops 1 | bytes 1 | tf_op jit(solution)/shard_map/pallas_call | solution.py:414
  57.3 2.1 %collective-permute-start.18 = (bf16[256,1024]{1,0:T(8,128)(2,1)S(1)}, bf16[256,1024]{1,0:T(8,128)(2,1)S(1)}, u32[]{:S(2)}, u32[]{:S(2)}) collective-permute-start(bf16[256,1024]{1,0:T(8,128)(2,1)S(1)} %shard_map.107), channel_id=1, source_target_pairs={{0,1},{1,0},{2,3},{3,2},{4,5},{5,4},{6,7},{7,6},{8,9},{9,8},{10,11... | collective-permute-start | bytes 1572872 | tf_op jit(solution)/shard_map/ppermute | solution.py:350
  61.3 2.8 %shard_map.101 = (bf16[128,2048]{1,0:T(8,128)(2,1)S(1)}, f32[128,512]{1,0:T(8,128)S(1)}, f32[128,512]{1,0:T(8,128)S(1)}) custom-call(s32[3]{0:T(128)S(1)} %pad_add_fusion.j_ref.a_ref._, bf16[8,256,128]{2,1,0:T(8,128)(2,1)S(1)} %copy-done.2, bf16[8,256,128]{2,1,0:T(8,128)(2,1)S(1)} %copy-done.1, bf16[144,512]{1,0:T(8,128)(2,1)S(1)} %get-tuple-element.106.refs_2_.prev_ref, ...), custom_call_target="tpu_custom_call" | custom-call | flops 1 | bytes 1 | tf_op jit(solution)/shard_map/pallas_call | solution.py:430
  65.1 3.5 %collective-permute-start.9 = (bf16[160,128]{1,0:T(8,128)(2,1)S(1)}, bf16[160,128]{1,0:T(8,128)(2,1)S(1)}, u32[]{:S(2)}, u32[]{:S(2)}) collective-permute-start(bf16[160,128]{1,0:T(8,128)(2,1)S(1)} %get-tuple-element.142), channel_id=1, source_target_pairs={{0,8},{2,10},{4,12},{6,14},{8,16},{10,18},{12,20},{14,22},{16,24},... | collective-permute-start | bytes 122888 | tf_op jit(solution)/shard_map/ppermute | solution.py:303
  68.6 4.5 %collective-permute-start.10 = (bf16[160,128]{1,0:T(8,128)(2,1)S(1)}, bf16[160,128]{1,0:T(8,128)(2,1)S(1)}, u32[]{:S(2)}, u32[]{:S(2)}) collective-permute-start(bf16[160,128]{1,0:T(8,128)(2,1)S(1)} %get-tuple-element.142), channel_id=1, source_target_pairs={{0,16},{2,18},{4,20},{6,22},{8,24},{10,26},{12,28},{14,30},{1,17},... | collective-permute-start | bytes 122888 | tf_op jit(solution)/shard_map/ppermute | solution.py:303
  73.1 1.6 %collective-permute-start.11 = (bf16[160,128]{1,0:T(8,128)(2,1)S(1)}, bf16[160,128]{1,0:T(8,128)(2,1)S(1)}, u32[]{:S(2)}, u32[]{:S(2)}) collective-permute-start(bf16[160,128]{1,0:T(8,128)(2,1)S(1)} %get-tuple-element.142), channel_id=1, source_target_pairs={{0,24},{2,26},{4,28},{6,30},{1,25},{3,27},{5,29},{7,31}} | collective-permute-start | bytes 122888 | tf_op jit(solution)/shard_map/ppermute | solution.py:303
  74.7 2.8 %shard_map.100 = (bf16[128,2048]{1,0:T(8,128)(2,1)S(1)}, f32[128,512]{1,0:T(8,128)S(1)}, f32[128,512]{1,0:T(8,128)S(1)}) custom-call(s32[3]{0:T(128)S(1)} %pad_add_fusion.j_ref.a_ref._, bf16[8,256,128]{2,1,0:T(8,128)(2,1)S(1)} %copy-done.2, bf16[8,256,128]{2,1,0:T(8,128)(2,1)S(1)} %copy-done.1, bf16[144,512]{1,0:T(8,128)(2,1)S(1)} %get-tuple-element.107.refs_2_.prev_ref, ...), custom_call_target="tpu_custom_call" | custom-call | flops 1 | bytes 1 | tf_op jit(solution)/shard_map/pallas_call | solution.py:430
  80.0 5.1 %shard_map.99 = (bf16[256,2048]{1,0:T(8,128)(2,1)S(1)}, f32[256,512]{1,0:T(8,128)S(1)}, f32[256,512]{1,0:T(8,128)S(1)}) custom-call(s32[3]{0:T(128)S(1)} %pad_add_fusion.j_ref.a_ref._, bf16[8,256,128]{2,1,0:T(8,128)(2,1)S(1)} %copy-done.2, bf16[8,256,128]{2,1,0:T(8,128)(2,1)S(1)} %copy-done.1, bf16[144,512]{1,0:T(8,128)(2,1)S(1)} %get-tuple-element.112.prev_ref, ...), custom_call_target="tpu_custom_call" | custom-call | flops 1 | bytes 1 | tf_op jit(solution)/shard_map/pallas_call | solution.py:430
  87.1 1.6 %shard_map.108.own_ref = bf16[256,512]{1,0:T(8,128)(2,1)S(1)} custom-call(s32[3]{0:T(128)S(1)} %pad_add_fusion.j_ref.a_ref._, bf16[256,128]{1,0:T(8,128)(2,1)S(1)} %copy-done.5, f32[1,512]{1,0:T(1,128)S(1)} %bitcast.5, bf16[160,128]{1,0:T(8,128)(2,1)S(1)} %get-tuple-element.143.refs_0_, bf16[160,128]{1,0:T(8,128)(2,1)S(1)} %collective-permute-done.12.refs_1_, ...), custom_call_target="tpu_custom_call" | custom-call | flops 1 | bytes 1 | tf_op jit(solution)/shard_map/pallas_call | solution.py:471
  88.7 1.6 %collective-permute-start.20 = (bf16[256,512]{1,0:T(8,128)(2,1)S(1)}, bf16[256,512]{1,0:T(8,128)(2,1)S(1)}, u32[]{:S(2)}, u32[]{:S(2)}) collective-permute-start(bf16[256,512]{1,0:T(8,128)(2,1)S(1)} %shard_map.108.own_ref), channel_id=1, source_target_pairs={{0,1},{1,0},{2,3},{3,2},{4,5},{5,4},{6,7},{7,6},{8,9},{9,8},{10,11... | collective-permute-start | bytes 786440 | tf_op jit(solution)/shard_map/ppermute | solution.py:350
  90.3 2.7 %collective-permute-done.15.refs_0_ = bf16[128,512]{1,0:T(8,128)(2,1)S(1)} collective-permute-done((bf16[128,512]{1,0:T(8,128)(2,1)S(1)}, bf16[128,512]{1,0:T(8,128)(2,1)S(1)}, u32[]{:S(2)}, u32[]{:S(2)}) %collective-permute-start.15) | collective-permute-done | bytes 131104 | tf_op jit(solution)/shard_map/ppermute | solution.py:350
  92.9 1.6 %shard_map.105.own_ref = bf16[256,512]{1,0:T(8,128)(2,1)S(1)} custom-call(s32[3]{0:T(128)S(1)} %pad_add_fusion.j_ref.a_ref._, bf16[256,128]{1,0:T(8,128)(2,1)S(1)} %copy-done.5, f32[1,512]{1,0:T(1,128)S(1)} %bitcast.6, bf16[160,128]{1,0:T(8,128)(2,1)S(1)} %get-tuple-element.143.refs_0_, bf16[160,128]{1,0:T(8,128)(2,1)S(1)} %collective-permute-done.12.refs_1_, ...), custom_call_target="tpu_custom_call" | custom-call | flops 1 | bytes 1 | tf_op jit(solution)/shard_map/pallas_call | solution.py:471
  94.5 4.0 %collective-permute-done.20.refs_0_ = bf16[256,512]{1,0:T(8,128)(2,1)S(1)} collective-permute-done((bf16[256,512]{1,0:T(8,128)(2,1)S(1)}, bf16[256,512]{1,0:T(8,128)(2,1)S(1)}, u32[]{:S(2)}, u32[]{:S(2)}) %collective-permute-start.20) | collective-permute-done | bytes 262176 | tf_op jit(solution)/shard_map/ppermute | solution.py:350
  98.5 1.6 %shard_map.109.own_ref = bf16[256,512]{1,0:T(8,128)(2,1)S(1)} custom-call(s32[3]{0:T(128)S(1)} %pad_add_fusion.j_ref.a_ref._, bf16[256,128]{1,0:T(8,128)(2,1)S(1)} %copy-done.5, f32[1,512]{1,0:T(1,128)S(1)} %bitcast.7, bf16[160,128]{1,0:T(8,128)(2,1)S(1)} %get-tuple-element.143.refs_0_, bf16[160,128]{1,0:T(8,128)(2,1)S(1)} %collective-permute-done.12.refs_1_, ...), custom_call_target="tpu_custom_call" | custom-call | flops 1 | bytes 1 | tf_op jit(solution)/shard_map/pallas_call | solution.py:471
  101.0 3.1 %collective-permute-done.16.refs_0_ = bf16[256,512]{1,0:T(8,128)(2,1)S(1)} collective-permute-done((bf16[256,512]{1,0:T(8,128)(2,1)S(1)}, bf16[256,512]{1,0:T(8,128)(2,1)S(1)}, u32[]{:S(2)}, u32[]{:S(2)}) %collective-permute-start.16) | collective-permute-done | bytes 262176 | tf_op jit(solution)/shard_map/ppermute | solution.py:350
  106.5 1.7 %shard_map.110.refs_3_ = bf16[1024,1024]{1,0:T(8,128)(2,1)} custom-call(s32[3]{0:T(128)S(1)} %pad_add_fusion.j_ref.a_ref._, bf16[128,512]{1,0:T(8,128)(2,1)S(1)} %shard_map.104.own_ref, bf16[512,2048]{1,0:T(8,128)(2,1)S(1)} %copy-done, bf16[128,512]{1,0:T(8,128)(2,1)S(1)} %collective-permute-done.15.refs_0_, ...), custom_call_target="tpu_custom_call" | custom-call | flops 1 | bytes 1 | tf_op jit(solution)/shard_map/pallas_call | solution.py:490
  108.2 2.1 %shard_map.111.refs_3_ = bf16[1024,1024]{1,0:T(8,128)(2,1)} custom-call(s32[3]{0:T(128)S(1)} %pad_add_fusion.j_ref.a_ref._, bf16[256,512]{1,0:T(8,128)(2,1)S(1)} %shard_map.108.own_ref, bf16[512,2048]{1,0:T(8,128)(2,1)S(1)} %copy-done, bf16[256,512]{1,0:T(8,128)(2,1)S(1)} %collective-permute-done.20.refs_0_, ...), custom_call_target="tpu_custom_call", output_to_operand_aliasing={{}: (6, {})} | custom-call | flops 1 | bytes 1 | tf_op jit(solution)/shard_map/pallas_call | solution.py:490
  110.3 2.1 %shard_map.112.refs_3_ = bf16[1024,1024]{1,0:T(8,128)(2,1)} custom-call(s32[3]{0:T(128)S(1)} %pad_add_fusion.j_ref.a_ref._, bf16[256,512]{1,0:T(8,128)(2,1)S(1)} %shard_map.105.own_ref, bf16[512,2048]{1,0:T(8,128)(2,1)S(1)} %copy-done, bf16[256,512]{1,0:T(8,128)(2,1)S(1)} %collective-permute-done.16.refs_0_, ...), custom_call_target="tpu_custom_call", output_to_operand_aliasing={{}: (6, {})} | custom-call | flops 1 | bytes 1 | tf_op jit(solution)/shard_map/pallas_call | solution.py:490
  112.4 2.1 %shard_map.113.refs_3_ = bf16[1024,1024]{1,0:T(8,128)(2,1)} custom-call(s32[3]{0:T(128)S(1)} %pad_add_fusion.j_ref.a_ref._, bf16[256,512]{1,0:T(8,128)(2,1)S(1)} %shard_map.109.own_ref, bf16[512,2048]{1,0:T(8,128)(2,1)S(1)} %copy-done, bf16[256,512]{1,0:T(8,128)(2,1)S(1)} %collective-permute-done.21.refs_0_, ...), custom_call_target="tpu_custom_call", output_to_operand_aliasing={{}: (6, {})} | custom-call | flops 1 | bytes 1 | tf_op jit(solution)/shard_map/pallas_call | solution.py:490
  114.5 1.7 %shard_map.114 = bf16[1024,1024]{1,0:T(8,128)(2,1)} custom-call(s32[3]{0:T(128)S(1)} %pad_add_fusion.j_ref.a_ref._, bf16[128,512]{1,0:T(8,128)(2,1)S(1)} %shard_map.106.own_ref, bf16[512,2048]{1,0:T(8,128)(2,1)S(1)} %copy-done, bf16[128,512]{1,0:T(8,128)(2,1)S(1)} %collective-permute-done.17.refs_0_, ...), custom_call_target="tpu_custom_call", output_to_operand_aliasing={{}: (6, {})} | custom-call | flops 1 | bytes 1 | tf_op jit(solution)/shard_map/pallas_call | solution.py:490
  (56 shorter events, 17.9 us)
Async XLA Ops:
  1.2 17.8 %collective-permute-start.2 = (bf16[272,1024]{1,0:T(8,128)(2,1)S(1)}, bf16[272,1024]{1,0:T(8,128)(2,1)S(1)}, u32[]{:S(2)}, u32[]{:S(2)}) collective-permute-start(bf16[272,1024]{1,0:T(8,128)(2,1)S(1)} %slice.16.refs_0_), channel_id=1, source_target_pairs={{0,1},{1,0},{2,3},{3,2},{4,5},{5,4},{6,7},{7,6},{8,9},{9,8},{10,11... | collective-permute-start | bytes 1671176 | tf_op jit(solution)/shard_map/ppermute | solution.py:350
  5.5 23.4 %collective-permute-start.1 = (bf16[256,1024]{1,0:T(8,128)(2,1)S(1)}, bf16[256,1024]{1,0:T(8,128)(2,1)S(1)}, u32[]{:S(2)}, u32[]{:S(2)}) collective-permute-start(bf16[256,1024]{1,0:T(8,128)(2,1)S(1)} %get-tuple-element.87.refs_0_), channel_id=1, source_target_pairs={{0,1},{1,0},{2,3},{3,2},{4,5},{5,4},{6,7},{7,6},{8,9},{9,8},{10,11... | collective-permute-start | bytes 1572872 | tf_op jit(solution)/shard_map/ppermute | solution.py:350
  5.6 34.6 %collective-permute-start.4 = (bf16[256,1024]{1,0:T(8,128)(2,1)S(1)}, bf16[256,1024]{1,0:T(8,128)(2,1)S(1)}, u32[]{:S(2)}, u32[]{:S(2)}) collective-permute-start(bf16[256,1024]{1,0:T(8,128)(2,1)S(1)} %get-tuple-element.97.refs_0_), channel_id=1, source_target_pairs={{0,1},{1,0},{2,3},{3,2},{4,5},{5,4},{6,7},{7,6},{8,9},{9,8},{10,11... | collective-permute-start | bytes 1572872 | tf_op jit(solution)/shard_map/ppermute | solution.py:350
  8.6 41.6 %collective-permute-start.5 = (bf16[128,1024]{1,0:T(8,128)(2,1)S(1)}, bf16[128,1024]{1,0:T(8,128)(2,1)S(1)}, u32[]{:S(2)}, u32[]{:S(2)}) collective-permute-start(bf16[128,1024]{1,0:T(8,128)(2,1)S(1)} %get-tuple-element.105.refs_0_), channel_id=1, source_target_pairs={{0,1},{1,0},{2,3},{3,2},{4,5},{5,4},{6,7},{7,6},{8,9},{9,8},{10,11... | collective-permute-start | bytes 786440 | tf_op jit(solution)/shard_map/ppermute | solution.py:350
  8.8 10.2 %copy-start.1 = (bf16[8,256,128]{2,1,0:T(8,128)(2,1)S(1)}, bf16[8,256,128]{2,1,0:T(8,128)(2,1)}, u32[]{:S(2)}) copy-start(bf16[8,256,128]{2,1,0:T(8,128)(2,1)} %constant.30.clone.sel_b_ref) | copy-start | bytes 1572868
  8.8 10.2 %copy-start.3 = (bf16[8,256,128]{2,1,0:T(8,128)(2,1)S(1)}, bf16[8,256,128]{2,1,0:T(8,128)(2,1)}, u32[]{:S(2)}) copy-start(bf16[8,256,128]{2,1,0:T(8,128)(2,1)} %constant.31.clone.sel_w_ref) | copy-start | bytes 1572868
  8.8 44.9 %collective-permute-start = (bf16[128,1024]{1,0:T(8,128)(2,1)S(1)}, bf16[128,1024]{1,0:T(8,128)(2,1)S(1)}, u32[]{:S(2)}, u32[]{:S(2)}) collective-permute-start(bf16[128,1024]{1,0:T(8,128)(2,1)S(1)} %get-tuple-element.86.refs_0_), channel_id=1, source_target_pairs={{0,1},{1,0},{2,3},{3,2},{4,5},{5,4},{6,7},{7,6},{8,9},{9,8},{10,11... | collective-permute-start | bytes 786440 | tf_op jit(solution)/shard_map/ppermute | solution.py:350
  10.7 3.1 %copy-start.4 = (bf16[2048,1792]{1,0:T(8,128)(2,1)S(1)}, bf16[2048,1792]{1,0:T(8,128)(2,1)}, u32[]{:S(2)}) copy-start(bf16[2048,1792]{1,0:T(8,128)(2,1)} %w_ref.7) | copy-start | bytes 22020100
  13.8 5.1 %copy-start.5 = (bf16[256,128]{1,0:T(8,128)(2,1)S(1)}, bf16[256,128]{1,0:T(8,128)(2,1)}, u32[]{:S(2)}) copy-start(bf16[256,128]{1,0:T(8,128)(2,1)} %constant.32.clone.mean_ref) | copy-start | bytes 196612
  13.8 5.2 %copy-start.6 = (f32[3,512]{1,0:T(4,128)S(1)}, f32[3,512]{1,0:T(4,128)}, u32[]{:S(2)}) copy-start(f32[3,512]{1,0:T(4,128)} %conv_ref.9) | copy-start | bytes 18436
  18.9 6.4 %copy-start = (bf16[512,2048]{1,0:T(8,128)(2,1)S(1)}, bf16[512,2048]{1,0:T(8,128)(2,1)}, u32[]{:S(2)}) copy-start(bf16[512,2048]{1,0:T(8,128)(2,1)} %w_ref.13) | copy-start | bytes 6291460
  23.8 5.1 %collective-permute-start.3 = (bf16[144,512]{1,0:T(8,128)(2,1)S(1)}, bf16[144,512]{1,0:T(8,128)(2,1)S(1)}, u32[]{:S(2)}, u32[]{:S(2)}) collective-permute-start(bf16[144,512]{1,0:T(8,128)(2,1)S(1)} %get-tuple-element.88), channel_id=1, source_target_pairs={{0,2},{2,4},{4,6},{6,8},{8,10},{10,12},{12,14},{14,16},{16,18},{18... | collective-permute-start | bytes 442376 | tf_op jit(solution)/shard_map/ppermute | solution.py:443
  25.9 7.8 %copy-start.2 = (bf16[8,256,128]{2,1,0:T(8,128)(2,1)S(1)}, bf16[8,256,128]{2,1,0:T(8,128)(2,1)}, u32[]{:S(2)}) copy-start(bf16[8,256,128]{2,1,0:T(8,128)(2,1)} %constant.29.clone.sel_a_ref) | copy-start | bytes 1572868
  57.3 32.9 %collective-permute-start.18 = (bf16[256,1024]{1,0:T(8,128)(2,1)S(1)}, bf16[256,1024]{1,0:T(8,128)(2,1)S(1)}, u32[]{:S(2)}, u32[]{:S(2)}) collective-permute-start(bf16[256,1024]{1,0:T(8,128)(2,1)S(1)} %shard_map.107), channel_id=1, source_target_pairs={{0,1},{1,0},{2,3},{3,2},{4,5},{5,4},{6,7},{7,6},{8,9},{9,8},{10,11... | collective-permute-start | bytes 1572872 | tf_op jit(solution)/shard_map/ppermute | solution.py:350
  59.4 4.6 %collective-permute-start.6 = (bf16[160,128]{1,0:T(8,128)(2,1)S(1)}, bf16[160,128]{1,0:T(8,128)(2,1)S(1)}, u32[]{:S(2)}, u32[]{:S(2)}) collective-permute-start(bf16[160,128]{1,0:T(8,128)(2,1)S(1)} %get-tuple-element.135), channel_id=1, source_target_pairs={{0,2},{2,0},{4,6},{6,4},{8,10},{10,8},{12,14},{14,12},{16,18},{18,... | collective-permute-start | bytes 122888 | tf_op jit(solution)/shard_map/ppermute | solution.py:256
  59.4 4.6 %collective-permute-start.7 = (bf16[160,128]{1,0:T(8,128)(2,1)S(1)}, bf16[160,128]{1,0:T(8,128)(2,1)S(1)}, u32[]{:S(2)}, u32[]{:S(2)}) collective-permute-start(bf16[160,128]{1,0:T(8,128)(2,1)S(1)} %get-tuple-element.136), channel_id=1, source_target_pairs={{0,4},{2,6},{4,0},{6,2},{8,12},{10,14},{12,8},{14,10},{16,20},{18,... | collective-permute-start | bytes 122888 | tf_op jit(solution)/shard_map/ppermute | solution.py:256
  60.9 3.5 %collective-permute-start.8 = (bf16[160,128]{1,0:T(8,128)(2,1)S(1)}, bf16[160,128]{1,0:T(8,128)(2,1)S(1)}, u32[]{:S(2)}, u32[]{:S(2)}) collective-permute-start(bf16[160,128]{1,0:T(8,128)(2,1)S(1)} %get-tuple-element.137), channel_id=1, source_target_pairs={{0,6},{2,4},{4,2},{6,0},{8,14},{10,12},{12,10},{14,8},{16,22},{18,... | collective-permute-start | bytes 122888 | tf_op jit(solution)/shard_map/ppermute | solution.py:256
  65.1 12.3 %collective-permute-start.9 = (bf16[160,128]{1,0:T(8,128)(2,1)S(1)}, bf16[160,128]{1,0:T(8,128)(2,1)S(1)}, u32[]{:S(2)}, u32[]{:S(2)}) collective-permute-start(bf16[160,128]{1,0:T(8,128)(2,1)S(1)} %get-tuple-element.142), channel_id=1, source_target_pairs={{0,8},{2,10},{4,12},{6,14},{8,16},{10,18},{12,20},{14,22},{16,24},... | collective-permute-start | bytes 122888 | tf_op jit(solution)/shard_map/ppermute | solution.py:303
  68.6 8.9 %collective-permute-start.10 = (bf16[160,128]{1,0:T(8,128)(2,1)S(1)}, bf16[160,128]{1,0:T(8,128)(2,1)S(1)}, u32[]{:S(2)}, u32[]{:S(2)}) collective-permute-start(bf16[160,128]{1,0:T(8,128)(2,1)S(1)} %get-tuple-element.142), channel_id=1, source_target_pairs={{0,16},{2,18},{4,20},{6,22},{8,24},{10,26},{12,28},{14,30},{1,17},... | collective-permute-start | bytes 122888 | tf_op jit(solution)/shard_map/ppermute | solution.py:303
  73.1 4.4 %collective-permute-start.11 = (bf16[160,128]{1,0:T(8,128)(2,1)S(1)}, bf16[160,128]{1,0:T(8,128)(2,1)S(1)}, u32[]{:S(2)}, u32[]{:S(2)}) collective-permute-start(bf16[160,128]{1,0:T(8,128)(2,1)S(1)} %get-tuple-element.142), channel_id=1, source_target_pairs={{0,24},{2,26},{4,28},{6,30},{1,25},{3,27},{5,29},{7,31}} | collective-permute-start | bytes 122888 | tf_op jit(solution)/shard_map/ppermute | solution.py:303
  74.7 10.5 %copy-start.7 = (f32[512]{0:T(512)S(1)}, f32[512]{0:T(512)}, u32[]{:S(2)}) copy-start(f32[512]{0:T(512)} %param.12) | copy-start | bytes 6148
  78.1 7.0 %collective-permute-start.12 = (bf16[160,128]{1,0:T(8,128)(2,1)S(1)}, bf16[160,128]{1,0:T(8,128)(2,1)S(1)}, u32[]{:S(2)}, u32[]{:S(2)}) collective-permute-start(bf16[160,128]{1,0:T(8,128)(2,1)S(1)} %get-tuple-element.144), channel_id=1, source_target_pairs={{0,2},{2,0},{4,6},{6,4},{8,10},{10,8},{12,14},{14,12},{16,18},{18,... | collective-permute-start | bytes 122888 | tf_op jit(solution)/shard_map/ppermute | solution.py:256
  78.1 7.0 %collective-permute-start.13 = (bf16[160,128]{1,0:T(8,128)(2,1)S(1)}, bf16[160,128]{1,0:T(8,128)(2,1)S(1)}, u32[]{:S(2)}, u32[]{:S(2)}) collective-permute-start(bf16[160,128]{1,0:T(8,128)(2,1)S(1)} %get-tuple-element.145), channel_id=1, source_target_pairs={{0,4},{2,6},{4,0},{6,2},{8,12},{10,14},{12,8},{14,10},{16,20},{18,... | collective-permute-start | bytes 122888 | tf_op jit(solution)/shard_map/ppermute | solution.py:256
  79.3 5.8 %collective-permute-start.14 = (bf16[160,128]{1,0:T(8,128)(2,1)S(1)}, bf16[160,128]{1,0:T(8,128)(2,1)S(1)}, u32[]{:S(2)}, u32[]{:S(2)}) collective-permute-start(bf16[160,128]{1,0:T(8,128)(2,1)S(1)} %get-tuple-element.146), channel_id=1, source_target_pairs={{0,6},{2,4},{4,2},{6,0},{8,14},{10,12},{12,10},{14,8},{16,22},{18,... | collective-permute-start | bytes 122888 | tf_op jit(solution)/shard_map/ppermute | solution.py:256
  86.5 6.4 %collective-permute-start.15 = (bf16[128,512]{1,0:T(8,128)(2,1)S(1)}, bf16[128,512]{1,0:T(8,128)(2,1)S(1)}, u32[]{:S(2)}, u32[]{:S(2)}) collective-permute-start(bf16[128,512]{1,0:T(8,128)(2,1)S(1)} %shard_map.104.own_ref), channel_id=1, source_target_pairs={{0,1},{1,0},{2,3},{3,2},{4,5},{5,4},{6,7},{7,6},{8,9},{9,8},{10,11... | collective-permute-start | bytes 393224 | tf_op jit(solution)/shard_map/ppermute | solution.py:350
  88.7 9.9 %collective-permute-start.20 = (bf16[256,512]{1,0:T(8,128)(2,1)S(1)}, bf16[256,512]{1,0:T(8,128)(2,1)S(1)}, u32[]{:S(2)}, u32[]{:S(2)}) collective-permute-start(bf16[256,512]{1,0:T(8,128)(2,1)S(1)} %shard_map.108.own_ref), channel_id=1, source_target_pairs={{0,1},{1,0},{2,3},{3,2},{4,5},{5,4},{6,7},{7,6},{8,9},{9,8},{10,11... | collective-permute-start | bytes 786440 | tf_op jit(solution)/shard_map/ppermute | solution.py:350
  90.2 16.2 %collective-permute-start.19 = (bf16[256,1024]{1,0:T(8,128)(2,1)S(1)}, bf16[256,1024]{1,0:T(8,128)(2,1)S(1)}, u32[]{:S(2)}, u32[]{:S(2)}) collective-permute-start(bf16[256,1024]{1,0:T(8,128)(2,1)S(1)} %collective-permute-done.18.refs_1_), channel_id=1, source_target_pairs={{0,2},{2,0},{4,6},{6,4},{8,10},{10,8},{12,14},{14,12},{16,18},{18,... | collective-permute-start | bytes 1572872 | tf_op jit(solution)/shard_map/ppermute | solution.py:256
  94.5 9.7 %collective-permute-start.16 = (bf16[256,512]{1,0:T(8,128)(2,1)S(1)}, bf16[256,512]{1,0:T(8,128)(2,1)S(1)}, u32[]{:S(2)}, u32[]{:S(2)}) collective-permute-start(bf16[256,512]{1,0:T(8,128)(2,1)S(1)} %shard_map.105.own_ref), channel_id=1, source_target_pairs={{0,1},{1,0},{2,3},{3,2},{4,5},{5,4},{6,7},{7,6},{8,9},{9,8},{10,11... | collective-permute-start | bytes 786440 | tf_op jit(solution)/shard_map/ppermute | solution.py:350
  100.1 12.2 %collective-permute-start.21 = (bf16[256,512]{1,0:T(8,128)(2,1)S(1)}, bf16[256,512]{1,0:T(8,128)(2,1)S(1)}, u32[]{:S(2)}, u32[]{:S(2)}) collective-permute-start(bf16[256,512]{1,0:T(8,128)(2,1)S(1)} %shard_map.109.own_ref), channel_id=1, source_target_pairs={{0,1},{1,0},{2,3},{3,2},{4,5},{5,4},{6,7},{7,6},{8,9},{9,8},{10,11... | collective-permute-start | bytes 786440 | tf_op jit(solution)/shard_map/ppermute | solution.py:350
  105.5 8.9 %collective-permute-start.17 = (bf16[128,512]{1,0:T(8,128)(2,1)S(1)}, bf16[128,512]{1,0:T(8,128)(2,1)S(1)}, u32[]{:S(2)}, u32[]{:S(2)}) collective-permute-start(bf16[128,512]{1,0:T(8,128)(2,1)S(1)} %shard_map.106.own_ref), channel_id=1, source_target_pairs={{0,1},{1,0},{2,3},{3,2},{4,5},{5,4},{6,7},{7,6},{8,9},{9,8},{10,11... | collective-permute-start | bytes 393224 | tf_op jit(solution)/shard_map/ppermute | solution.py:350

commit v3 on v2

--- a/solution.py
+++ b/solution.py
@@ -269,11 +269,13 @@
         ahead_refs[r][...] = total
 
 
-def earlier_kernel(_, *refs, planes):
-    ahead_refs, earlier_refs, back_refs = refs[:PLANE], refs[PLANE : PLANE + planes], refs[PLANE + planes :]
+def earlier_kernel(a_ref, *refs, planes):
+    ahead_refs, plane_refs, back_refs = refs[:PLANE], refs[PLANE : PLANE + planes], refs[PLANE + planes :]
+    mine = a_ref[2] // PLANE
     earlier = jnp.zeros(ahead_refs[0].shape, F32)
-    for ref in earlier_refs:
-        earlier = earlier + ref[...].astype(F32)
+    for d, ref in enumerate(plane_refs, 1):
+        before = jnp.bitwise_xor(mine, d) < mine
+        earlier = earlier + ref[...].astype(F32) * before.astype(F32)
     for r in range(PLANE):
         back_refs[r][...] = (ahead_refs[r][...] + earlier).astype(BF16)
 
@@ -299,8 +301,7 @@
     )(after(places, beside[0]), *held)
     earlier = []
     for d in range(1, ctx // PLANE):
-        pairs = [(i, i + d * PLANE) for i in range(ctx - d * PLANE)]
-        earlier.append(lax.ppermute(plane, "ctx", pairs))
+        earlier.append(exchange(plane, "ctx", d * PLANE))
     back = call(
         functools.partial(earlier_kernel, planes=len(earlier)),
         [narrow] * PLANE,
@@ -334,7 +335,7 @@
     heads = out_weight.shape[0] // DV
     width = heads * DV
     pairs = width // LANES
-    in_planes = pairs == PLANE and ctx % PLANE == 0
+    in_planes = pairs == PLANE and ctx % PLANE == 0 and ctx & (ctx - 1) == 0
     places = jnp.stack([me, position % PLANE if in_planes else jnp.zeros_like(position), position])
     hidden_in, places = lax.optimization_barrier((hidden_in, places))
     step = row_count // 8
@@ -464,10 +465,9 @@
         out_rows += [got] + ([exchange(after(got, mark), "ctx", 1)] if out_parts > 1 else [])
 
     result = None
-    arrived = []
-    for i, b in enumerate((3, 0, 1, 4, 2)):
+    mixed = attended[last][1]
+    for b in (0, 1, 4, 2, 3):
         at, rows = blocks[b]
-        behind = after(places, arrived[i - 2] if i >= 2 else attended[last][1])
         mixed = call(
             functools.partial(finish_kernel, heads=heads, before=b),
             jax.ShapeDtypeStruct((rows, width), BF16),
@@ -477,9 +477,8 @@
             flops=6 * rows * QFEATS * LANES * heads,
             moved=12 * rows * width,
             vmem=16 << 20,
-        )(behind, means, gain, *priors, *[done[c][6] for c in range(b)], *attended[b])
+        )(after(places, mixed), means, gain, *priors, *[done[c][6] for c in range(b)], *attended[b])
         others = [from_head(mixed, r) for r in range(1, n)]
-        arrived.append(others[-1])
         operands = [places, mixed, out_weight] + others + out_rows
         specs = [scalar] + [whole] * (len(operands) - 1)
         aliases = {}

time: 117 us -> 113 us (0.966)
  starting transfers between devices: 28.3 us -> 24 us
    ppermute x3 -> x0, starting transfers between devices: 9.53 us -> none  [prior_in_planes(): earlier.append(lax.ppermute(plane, 'ctx', pairs))]
    ppermute x7 -> x10, starting transfers between devices: 3.8 us -> 8.31 us  [exchange(): return lax.ppermute(value, axis, [(i, i ^ flip) for i in range(count)])]
    ppermute x7 -> x10, waiting for transfers between devices: 0.41 us -> 3.21 us  [exchange(): return lax.ppermute(value, axis, [(i, i ^ flip) for i in range(count)])]
    ppermute x11, waiting for transfers between devices: 14.1 us -> 11.5 us  [from_head(): return lax.ppermute(value, 'head', [(i, (i + by) % n) for i in range(n)])]
  transfers between devices with their start and end apart: 22 -> 22, of which waited for: 6 -> 9; matrix products, arithmetic and copies ran while one was open for 2% -> 2% of each run, Pallas kernels for 52% -> 55%
where the time goes in v3:
time: 113 us; the launch traced here: 112 us
  Pallas kernels  66.6 us (59%)
  starting transfers between devices  24 us (21%)
  waiting for transfers between devices  14.7 us (13%)
  local copies, waits for them, and re-layouts  6.54 us (6%)
    pallas_call x5, Pallas kernels, do_block(): call(functools.partial(block_kernel, n=n, heads=heads, extra=extra, other...  21.3 us
    pallas_call x5, Pallas kernels, attend(): call(functools.partial(attend_kernel, heads=heads, first=b == 0), [jax.Sh...  21.3 us
    ppermute x11, starting transfers between devices, from_head(): return lax.ppermute(value, 'head', [(i, (i + by) % n) for i in range(n)])  14.2 us
    ppermute x11, waiting for transfers between devices, from_head(): return lax.ppermute(value, 'head', [(i, (i + by) % n) for i in range(n)])  11.5 us
    pallas_call x5, Pallas kernels, per_device(): call(functools.partial(output_kernel, n=n, offset=at, parts=out_parts), j...  9.64 us
    ppermute x10, starting transfers between devices, exchange(): return lax.ppermute(value, axis, [(i, i ^ flip) for i in range(count)])  8.31 us
    pallas_call x5, Pallas kernels, per_device(): call(functools.partial(finish_kernel, heads=heads, before=b), jax.ShapeDt...  7.39 us
    pallas_call x1, Pallas kernels, per_device(): call(functools.partial(arrange_kernel, heads=heads), jax.ShapeDtypeStruct...  5.09 us
  transfers between devices with their start and end apart: 22, of which 9 were waited for; matrix products, arithmetic and copies ran while one was open for 2% of the time, Pallas kernels for 55%

profile of v3, /device:TPU:0, one launch (start us, length us, event | category | flops | bytes accessed | tf_op | source)
XLA Modules:
  0.0 112.5 jit_solution(15626116734616136093)
XLA Ops:
  1.2 3.0 %collective-permute-start.2 = (bf16[272,1024]{1,0:T(8,128)(2,1)S(1)}, bf16[272,1024]{1,0:T(8,128)(2,1)S(1)}, u32[]{:S(2)}, u32[]{:S(2)}) collective-permute-start(bf16[272,1024]{1,0:T(8,128)(2,1)S(1)} %slice.16.refs_0_), channel_id=1, source_target_pairs={{0,1},{1,0},{2,3},{3,2},{4,5},{5,4},{6,7},{7,6},{8,9},{9,8},{10,11... | collective-permute-start | bytes 1671176 | tf_op jit(solution)/shard_map/ppermute | solution.py:351
  5.6 2.0 %collective-permute-start.4 = (bf16[256,1024]{1,0:T(8,128)(2,1)S(1)}, bf16[256,1024]{1,0:T(8,128)(2,1)S(1)}, u32[]{:S(2)}, u32[]{:S(2)}) collective-permute-start(bf16[256,1024]{1,0:T(8,128)(2,1)S(1)} %get-tuple-element.98.refs_0_), channel_id=1, source_target_pairs={{0,1},{1,0},{2,3},{3,2},{4,5},{5,4},{6,7},{7,6},{8,9},{9,8},{10,11... | collective-permute-start | bytes 1572872 | tf_op jit(solution)/shard_map/ppermute | solution.py:351
  8.8 1.9 %collective-permute-start = (bf16[128,1024]{1,0:T(8,128)(2,1)S(1)}, bf16[128,1024]{1,0:T(8,128)(2,1)S(1)}, u32[]{:S(2)}, u32[]{:S(2)}) collective-permute-start(bf16[128,1024]{1,0:T(8,128)(2,1)S(1)} %get-tuple-element.87.refs_0_), channel_id=1, source_target_pairs={{0,1},{1,0},{2,3},{3,2},{4,5},{5,4},{6,7},{7,6},{8,9},{9,8},{10,11... | collective-permute-start | bytes 786440 | tf_op jit(solution)/shard_map/ppermute | solution.py:351
  10.7 3.1 %copy-done.4 = bf16[2048,1792]{1,0:T(8,128)(2,1)S(1)} copy-done((bf16[2048,1792]{1,0:T(8,128)(2,1)S(1)}, bf16[2048,1792]{1,0:T(8,128)(2,1)}, u32[]{:S(2)}) %copy-start.4) | copy-done | bytes 7340056
  13.8 5.1 %shard_map.91.w_ref = bf16[2048,1792]{1,0:T(8,128)(2,1)S(1)} custom-call(bf16[2048,1792]{1,0:T(8,128)(2,1)S(1)} %copy-done.4), custom_call_target="tpu_custom_call" | custom-call | flops 1 | bytes 1 | tf_op jit(solution)/shard_map/pallas_call | solution.py:392
  19.0 4.8 %shard_map.92 = (bf16[256,128]{1,0:T(8,128)(2,1)S(1)}, bf16[256,128]{1,0:T(8,128)(2,1)S(1)}, bf16[256,512]{1,0:T(8,128)(2,1)S(1)}, bf16[256,512]{1,0:T(8,128)(2,...) custom-call(s32[3]{0:T(128)S(1)} %pad_add_fusion.j_ref.a_ref, ...), custom_call_target="tpu_custom_call" | custom-call | flops 1 | bytes 1 | tf_op jit(solution)/shard_map/pallas_call | solution.py:415
  25.9 3.0 %collective-permute-done.1.refs_1_ = bf16[256,1024]{1,0:T(8,128)(2,1)S(1)} collective-permute-done((bf16[256,1024]{1,0:T(8,128)(2,1)S(1)}, bf16[256,1024]{1,0:T(8,128)(2,1)S(1)}, u32[]{:S(2)}, u32[]{:S(2)}) %collective-permute-start.1) | collective-permute-done | bytes 524320 | tf_op jit(solution)/shard_map/ppermute | solution.py:351
  28.9 4.8 %shard_map.93 = (bf16[256,128]{1,0:T(8,128)(2,1)S(1)}, bf16[256,128]{1,0:T(8,128)(2,1)S(1)}, bf16[256,512]{1,0:T(8,128)(2,1)S(1)}, bf16[256,512]{1,0:T(8,128)(2,...) custom-call(s32[3]{0:T(128)S(1)} %pad_add_fusion.j_ref.a_ref, ...), custom_call_target="tpu_custom_call" | custom-call | flops 1 | bytes 1 | tf_op jit(solution)/shard_map/pallas_call | solution.py:415
  33.7 5.1 %shard_map.94 = (bf16[256,2048]{1,0:T(8,128)(2,1)S(1)}, f32[256,512]{1,0:T(8,128)S(1)}, f32[256,512]{1,0:T(8,128)S(1)}) custom-call(s32[3]{0:T(128)S(1)} %pad_add_fusion.j_ref.a_ref, bf16[8,256,128]{2,1,0:T(8,128)(2,1)S(1)} %copy-done.2, bf16[8,256,128]{2,1,0:T(8,128)(2,1)S(1)} %copy-done.1, bf16[144,512]{1,0:T(8,128)(2,1)S(1)} %collective-permute-done.3.refs_2_.prev_ref, ...), custom_call_target="tpu_custom_call" | custom-call | flops 1 | bytes 1 | tf_op jit(solution)/shard_map/pallas_call | solution.py:431
  40.1 4.7 %shard_map.95 = (bf16[256,128]{1,0:T(8,128)(2,1)S(1)}, bf16[256,128]{1,0:T(8,128)(2,1)S(1)}, bf16[256,512]{1,0:T(8,128)(2,1)S(1)}, bf16[256,512]{1,0:T(8,128)(2,...) custom-call(s32[3]{0:T(128)S(1)} %pad_add_fusion.j_ref.a_ref, ...), custom_call_target="tpu_custom_call" | custom-call | flops 1 | bytes 1 | tf_op jit(solution)/shard_map/pallas_call | solution.py:415
  44.9 5.3 %shard_map.96 = (bf16[256,2048]{1,0:T(8,128)(2,1)S(1)}, f32[256,512]{1,0:T(8,128)S(1)}, f32[256,512]{1,0:T(8,128)S(1)}) custom-call(s32[3]{0:T(128)S(1)} %pad_add_fusion.j_ref.a_ref, bf16[8,256,128]{2,1,0:T(8,128)(2,1)S(1)} %copy-done.2, bf16[8,256,128]{2,1,0:T(8,128)(2,1)S(1)} %copy-done.1, bf16[144,512]{1,0:T(8,128)(2,1)S(1)} %get-tuple-element.90.refs_2_.prev_ref, ...), custom_call_target="tpu_custom_call" | custom-call | flops 1 | bytes 1 | tf_op jit(solution)/shard_map/pallas_call | solution.py:431
  50.2 3.5 %shard_map.97 = (bf16[128,128]{1,0:T(8,128)(2,1)S(1)}, bf16[128,128]{1,0:T(8,128)(2,1)S(1)}, bf16[128,512]{1,0:T(8,128)(2,1)S(1)}, bf16[128,512]{1,0:T(8,128)(2,...) custom-call(s32[3]{0:T(128)S(1)} %pad_add_fusion.j_ref.a_ref, ...), custom_call_target="tpu_custom_call" | custom-call | flops 1 | bytes 1 | tf_op jit(solution)/shard_map/pallas_call | solution.py:415
  53.7 3.6 %shard_map.98 = (bf16[128,128]{1,0:T(8,128)(2,1)S(1)}, bf16[128,128]{1,0:T(8,128)(2,1)S(1)}, bf16[128,512]{1,0:T(8,128)(2,1)S(1)}, bf16[128,512]{1,0:T(8,128)(2,...) custom-call(s32[3]{0:T(128)S(1)} %pad_add_fusion.j_ref.a_ref, ...), custom_call_target="tpu_custom_call" | custom-call | flops 1 | bytes 1 | tf_op jit(solution)/shard_map/pallas_call | solution.py:415
  57.3 2.1 %collective-permute-start.16 = (bf16[256,1024]{1,0:T(8,128)(2,1)S(1)}, bf16[256,1024]{1,0:T(8,128)(2,1)S(1)}, u32[]{:S(2)}, u32[]{:S(2)}) collective-permute-start(bf16[256,1024]{1,0:T(8,128)(2,1)S(1)} %shard_map.109), channel_id=1, source_target_pairs={{0,1},{1,0},{2,3},{3,2},{4,5},{5,4},{6,7},{7,6},{8,9},{9,8},{10,11... | collective-permute-start | bytes 1572872 | tf_op jit(solution)/shard_map/ppermute | solution.py:351
  61.3 2.8 %shard_map.101 = (bf16[128,2048]{1,0:T(8,128)(2,1)S(1)}, f32[128,512]{1,0:T(8,128)S(1)}, f32[128,512]{1,0:T(8,128)S(1)}) custom-call(s32[3]{0:T(128)S(1)} %pad_add_fusion.j_ref.a_ref, bf16[8,256,128]{2,1,0:T(8,128)(2,1)S(1)} %copy-done.2, bf16[8,256,128]{2,1,0:T(8,128)(2,1)S(1)} %copy-done.1, bf16[144,512]{1,0:T(8,128)(2,1)S(1)} %get-tuple-element.107.refs_2_.prev_ref, ...), custom_call_target="tpu_custom_call" | custom-call | flops 1 | bytes 1 | tf_op jit(solution)/shard_map/pallas_call | solution.py:431
  65.1 1.6 %collective-permute-start.9 = (bf16[160,128]{1,0:T(8,128)(2,1)S(1)}, bf16[160,128]{1,0:T(8,128)(2,1)S(1)}, u32[]{:S(2)}, u32[]{:S(2)}) collective-permute-start(bf16[160,128]{1,0:T(8,128)(2,1)S(1)} %get-tuple-element.143), channel_id=1, source_target_pairs={{0,8},{2,10},{4,12},{6,14},{8,0},{10,2},{12,4},{14,6},{16,24},{18,... | collective-permute-start | bytes 122888 | tf_op jit(solution)/shard_map/ppermute | solution.py:256
  66.8 2.6 %collective-permute-start.10 = (bf16[160,128]{1,0:T(8,128)(2,1)S(1)}, bf16[160,128]{1,0:T(8,128)(2,1)S(1)}, u32[]{:S(2)}, u32[]{:S(2)}) collective-permute-start(bf16[160,128]{1,0:T(8,128)(2,1)S(1)} %get-tuple-element.143), channel_id=1, source_target_pairs={{0,16},{2,18},{4,20},{6,22},{8,24},{10,26},{12,28},{14,30},{16,0},... | collective-permute-start | bytes 122888 | tf_op jit(solution)/shard_map/ppermute | solution.py:256
  69.6 2.8 %shard_map.100 = (bf16[128,2048]{1,0:T(8,128)(2,1)S(1)}, f32[128,512]{1,0:T(8,128)S(1)}, f32[128,512]{1,0:T(8,128)S(1)}) custom-call(s32[3]{0:T(128)S(1)} %pad_add_fusion.j_ref.a_ref, bf16[8,256,128]{2,1,0:T(8,128)(2,1)S(1)} %copy-done.2, bf16[8,256,128]{2,1,0:T(8,128)(2,1)S(1)} %copy-done.1, bf16[144,512]{1,0:T(8,128)(2,1)S(1)} %get-tuple-element.108.refs_2_.prev_ref, ...), custom_call_target="tpu_custom_call" | custom-call | flops 1 | bytes 1 | tf_op jit(solution)/shard_map/pallas_call | solution.py:431
  72.5 2.6 %collective-permute-done.11.refs_6_ = bf16[160,128]{1,0:T(8,128)(2,1)S(1)} collective-permute-done((bf16[160,128]{1,0:T(8,128)(2,1)S(1)}, bf16[160,128]{1,0:T(8,128)(2,1)S(1)}, u32[]{:S(2)}, u32[]{:S(2)}) %collective-permute-start.11) | collective-permute-done | bytes 40992 | tf_op jit(solution)/shard_map/ppermute | solution.py:256
  77.8 5.4 %shard_map.99 = (bf16[256,2048]{1,0:T(8,128)(2,1)S(1)}, f32[256,512]{1,0:T(8,128)S(1)}, f32[256,512]{1,0:T(8,128)S(1)}) custom-call(s32[3]{0:T(128)S(1)} %pad_add_fusion.j_ref.a_ref, bf16[8,256,128]{2,1,0:T(8,128)(2,1)S(1)} %copy-done.2, bf16[8,256,128]{2,1,0:T(8,128)(2,1)S(1)} %copy-done.1, bf16[144,512]{1,0:T(8,128)(2,1)S(1)} %get-tuple-element.113.prev_ref, ...), custom_call_target="tpu_custom_call" | custom-call | flops 1 | bytes 1 | tf_op jit(solution)/shard_map/pallas_call | solution.py:431
  83.2 1.6 %shard_map.104.own_ref = bf16[256,512]{1,0:T(8,128)(2,1)S(1)} custom-call(s32[3]{0:T(128)S(1)} %pad_add_fusion.j_ref.a_ref, bf16[256,128]{1,0:T(8,128)(2,1)S(1)} %copy-done.5, f32[1,512]{1,0:T(1,128)S(1)} %bitcast.4, bf16[160,128]{1,0:T(8,128)(2,1)S(1)} %get-tuple-element.144.refs_0_, bf16[160,128]{1,0:T(8,128)(2,1)S(1)} %collective-permute-done.12.refs_1_, ...), custom_call_target="tpu_custom_call" | custom-call | flops 1 | bytes 1 | tf_op jit(solution)/shard_map/pallas_call | solution.py:471
  85.3 1.5 %shard_map.105.own_ref = bf16[256,512]{1,0:T(8,128)(2,1)S(1)} custom-call(s32[3]{0:T(128)S(1)} %pad_add_fusion.j_ref.a_ref, bf16[256,128]{1,0:T(8,128)(2,1)S(1)} %copy-done.5, f32[1,512]{1,0:T(1,128)S(1)} %bitcast.5, bf16[160,128]{1,0:T(8,128)(2,1)S(1)} %get-tuple-element.144.refs_0_, bf16[160,128]{1,0:T(8,128)(2,1)S(1)} %collective-permute-done.12.refs_1_, ...), custom_call_target="tpu_custom_call" | custom-call | flops 1 | bytes 1 | tf_op jit(solution)/shard_map/pallas_call | solution.py:471
  86.9 1.6 %collective-permute-start.20 = (bf16[256,512]{1,0:T(8,128)(2,1)S(1)}, bf16[256,512]{1,0:T(8,128)(2,1)S(1)}, u32[]{:S(2)}, u32[]{:S(2)}) collective-permute-start(bf16[256,512]{1,0:T(8,128)(2,1)S(1)} %shard_map.105.own_ref), channel_id=1, source_target_pairs={{0,1},{1,0},{2,3},{3,2},{4,5},{5,4},{6,7},{7,6},{8,9},{9,8},{10,11... | collective-permute-start | bytes 786440 | tf_op jit(solution)/shard_map/ppermute | solution.py:351
  88.4 1.6 %shard_map.106.own_ref = bf16[256,512]{1,0:T(8,128)(2,1)S(1)} custom-call(s32[3]{0:T(128)S(1)} %pad_add_fusion.j_ref.a_ref, bf16[256,128]{1,0:T(8,128)(2,1)S(1)} %copy-done.5, f32[1,512]{1,0:T(1,128)S(1)} %bitcast.6, bf16[160,128]{1,0:T(8,128)(2,1)S(1)} %get-tuple-element.144.refs_0_, bf16[160,128]{1,0:T(8,128)(2,1)S(1)} %collective-permute-done.12.refs_1_, ...), custom_call_target="tpu_custom_call" | custom-call | flops 1 | bytes 1 | tf_op jit(solution)/shard_map/pallas_call | solution.py:471
  91.9 1.6 %collective-permute-start.18 = (bf16[128,512]{1,0:T(8,128)(2,1)S(1)}, bf16[128,512]{1,0:T(8,128)(2,1)S(1)}, u32[]{:S(2)}, u32[]{:S(2)}) collective-permute-start(bf16[128,512]{1,0:T(8,128)(2,1)S(1)} %shard_map.107.own_ref), channel_id=1, source_target_pairs={{0,1},{1,0},{2,3},{3,2},{4,5},{5,4},{6,7},{7,6},{8,9},{9,8},{10,11... | collective-permute-start | bytes 393224 | tf_op jit(solution)/shard_map/ppermute | solution.py:351
  95.5 2.1 %shard_map.110.refs_3_ = bf16[1024,1024]{1,0:T(8,128)(2,1)} custom-call(s32[3]{0:T(128)S(1)} %pad_add_fusion.j_ref.a_ref, bf16[256,512]{1,0:T(8,128)(2,1)S(1)} %shard_map.104.own_ref, bf16[512,2048]{1,0:T(8,128)(2,1)S(1)} %copy-done, bf16[256,512]{1,0:T(8,128)(2,1)S(1)} %collective-permute-done.21.refs_0_, ...), custom_call_target="tpu_custom_call" | custom-call | flops 1 | bytes 1 | tf_op jit(solution)/shard_map/pallas_call | solution.py:489
  97.6 2.0 %collective-permute-done.20.refs_0_ = bf16[256,512]{1,0:T(8,128)(2,1)S(1)} collective-permute-done((bf16[256,512]{1,0:T(8,128)(2,1)S(1)}, bf16[256,512]{1,0:T(8,128)(2,1)S(1)}, u32[]{:S(2)}, u32[]{:S(2)}) %collective-permute-start.20) | collective-permute-done | bytes 262176 | tf_op jit(solution)/shard_map/ppermute | solution.py:351
  99.6 2.1 %shard_map.111.refs_3_ = bf16[1024,1024]{1,0:T(8,128)(2,1)} custom-call(s32[3]{0:T(128)S(1)} %pad_add_fusion.j_ref.a_ref, bf16[256,512]{1,0:T(8,128)(2,1)S(1)} %shard_map.105.own_ref, bf16[512,2048]{1,0:T(8,128)(2,1)S(1)} %copy-done, bf16[256,512]{1,0:T(8,128)(2,1)S(1)} %collective-permute-done.20.refs_0_, ...), custom_call_target="tpu_custom_call", output_to_operand_aliasing={{}: (6, {})} | custom-call | flops 1 | bytes 1 | tf_op jit(solution)/shard_map/pallas_call | solution.py:489
  101.7 3.5 %collective-permute-done.19.refs_0_ = bf16[256,512]{1,0:T(8,128)(2,1)S(1)} collective-permute-done((bf16[256,512]{1,0:T(8,128)(2,1)S(1)}, bf16[256,512]{1,0:T(8,128)(2,1)S(1)}, u32[]{:S(2)}, u32[]{:S(2)}) %collective-permute-start.19) | collective-permute-done | bytes 262176 | tf_op jit(solution)/shard_map/ppermute | solution.py:351
  105.2 2.1 %shard_map.112.refs_3_ = bf16[1024,1024]{1,0:T(8,128)(2,1)} custom-call(s32[3]{0:T(128)S(1)} %pad_add_fusion.j_ref.a_ref, bf16[256,512]{1,0:T(8,128)(2,1)S(1)} %shard_map.106.own_ref, bf16[512,2048]{1,0:T(8,128)(2,1)S(1)} %copy-done, bf16[256,512]{1,0:T(8,128)(2,1)S(1)} %collective-permute-done.19.refs_0_, ...), custom_call_target="tpu_custom_call", output_to_operand_aliasing={{}: (6, {})} | custom-call | flops 1 | bytes 1 | tf_op jit(solution)/shard_map/pallas_call | solution.py:489
  108.0 1.7 %shard_map.113.refs_3_ = bf16[1024,1024]{1,0:T(8,128)(2,1)} custom-call(s32[3]{0:T(128)S(1)} %pad_add_fusion.j_ref.a_ref, bf16[128,512]{1,0:T(8,128)(2,1)S(1)} %shard_map.107.own_ref, bf16[512,2048]{1,0:T(8,128)(2,1)S(1)} %copy-done, bf16[128,512]{1,0:T(8,128)(2,1)S(1)} %collective-permute-done.18.refs_0_, ...), custom_call_target="tpu_custom_call", output_to_operand_aliasing={{}: (6, {})} | custom-call | flops 1 | bytes 1 | tf_op jit(solution)/shard_map/pallas_call | solution.py:489
  110.6 1.7 %shard_map.114 = bf16[1024,1024]{1,0:T(8,128)(2,1)} custom-call(s32[3]{0:T(128)S(1)} %pad_add_fusion.j_ref.a_ref, bf16[128,512]{1,0:T(8,128)(2,1)S(1)} %shard_map.108.own_ref, bf16[512,2048]{1,0:T(8,128)(2,1)S(1)} %copy-done, bf16[128,512]{1,0:T(8,128)(2,1)S(1)} %collective-permute-done.15.refs_0_, ...), custom_call_target="tpu_custom_call", output_to_operand_aliasing={{}: (6, {})} | custom-call | flops 1 | bytes 1 | tf_op jit(solution)/shard_map/pallas_call | solution.py:489
  (56 shorter events, 19.1 us)
Async XLA Ops:
  1.2 17.8 %collective-permute-start.2 = (bf16[272,1024]{1,0:T(8,128)(2,1)S(1)}, bf16[272,1024]{1,0:T(8,128)(2,1)S(1)}, u32[]{:S(2)}, u32[]{:S(2)}) collective-permute-start(bf16[272,1024]{1,0:T(8,128)(2,1)S(1)} %slice.16.refs_0_), channel_id=1, source_target_pairs={{0,1},{1,0},{2,3},{3,2},{4,5},{5,4},{6,7},{7,6},{8,9},{9,8},{10,11... | collective-permute-start | bytes 1671176 | tf_op jit(solution)/shard_map/ppermute | solution.py:351
  5.5 23.4 %collective-permute-start.1 = (bf16[256,1024]{1,0:T(8,128)(2,1)S(1)}, bf16[256,1024]{1,0:T(8,128)(2,1)S(1)}, u32[]{:S(2)}, u32[]{:S(2)}) collective-permute-start(bf16[256,1024]{1,0:T(8,128)(2,1)S(1)} %get-tuple-element.88.refs_0_), channel_id=1, source_target_pairs={{0,1},{1,0},{2,3},{3,2},{4,5},{5,4},{6,7},{7,6},{8,9},{9,8},{10,11... | collective-permute-start | bytes 1572872 | tf_op jit(solution)/shard_map/ppermute | solution.py:351
  5.6 34.6 %collective-permute-start.4 = (bf16[256,1024]{1,0:T(8,128)(2,1)S(1)}, bf16[256,1024]{1,0:T(8,128)(2,1)S(1)}, u32[]{:S(2)}, u32[]{:S(2)}) collective-permute-start(bf16[256,1024]{1,0:T(8,128)(2,1)S(1)} %get-tuple-element.98.refs_0_), channel_id=1, source_target_pairs={{0,1},{1,0},{2,3},{3,2},{4,5},{5,4},{6,7},{7,6},{8,9},{9,8},{10,11... | collective-permute-start | bytes 1572872 | tf_op jit(solution)/shard_map/ppermute | solution.py:351
  8.6 41.6 %collective-permute-start.5 = (bf16[128,1024]{1,0:T(8,128)(2,1)S(1)}, bf16[128,1024]{1,0:T(8,128)(2,1)S(1)}, u32[]{:S(2)}, u32[]{:S(2)}) collective-permute-start(bf16[128,1024]{1,0:T(8,128)(2,1)S(1)} %get-tuple-element.106.refs_0_), channel_id=1, source_target_pairs={{0,1},{1,0},{2,3},{3,2},{4,5},{5,4},{6,7},{7,6},{8,9},{9,8},{10,11... | collective-permute-start | bytes 786440 | tf_op jit(solution)/shard_map/ppermute | solution.py:351
  8.8 10.2 %copy-start.1 = (bf16[8,256,128]{2,1,0:T(8,128)(2,1)S(1)}, bf16[8,256,128]{2,1,0:T(8,128)(2,1)}, u32[]{:S(2)}) copy-start(bf16[8,256,128]{2,1,0:T(8,128)(2,1)} %constant.30.clone.sel_b_ref) | copy-start | bytes 1572868
  8.8 10.2 %copy-start.3 = (bf16[8,256,128]{2,1,0:T(8,128)(2,1)S(1)}, bf16[8,256,128]{2,1,0:T(8,128)(2,1)}, u32[]{:S(2)}) copy-start(bf16[8,256,128]{2,1,0:T(8,128)(2,1)} %constant.31.clone.sel_w_ref) | copy-start | bytes 1572868
  8.8 44.9 %collective-permute-start = (bf16[128,1024]{1,0:T(8,128)(2,1)S(1)}, bf16[128,1024]{1,0:T(8,128)(2,1)S(1)}, u32[]{:S(2)}, u32[]{:S(2)}) collective-permute-start(bf16[128,1024]{1,0:T(8,128)(2,1)S(1)} %get-tuple-element.87.refs_0_), channel_id=1, source_target_pairs={{0,1},{1,0},{2,3},{3,2},{4,5},{5,4},{6,7},{7,6},{8,9},{9,8},{10,11... | collective-permute-start | bytes 786440 | tf_op jit(solution)/shard_map/ppermute | solution.py:351
  10.7 3.1 %copy-start.4 = (bf16[2048,1792]{1,0:T(8,128)(2,1)S(1)}, bf16[2048,1792]{1,0:T(8,128)(2,1)}, u32[]{:S(2)}) copy-start(bf16[2048,1792]{1,0:T(8,128)(2,1)} %w_ref.7) | copy-start | bytes 22020100
  13.8 5.1 %copy-start.5 = (bf16[256,128]{1,0:T(8,128)(2,1)S(1)}, bf16[256,128]{1,0:T(8,128)(2,1)}, u32[]{:S(2)}) copy-start(bf16[256,128]{1,0:T(8,128)(2,1)} %constant.32.clone.mean_ref) | copy-start | bytes 196612
  13.8 5.2 %copy-start.6 = (f32[3,512]{1,0:T(4,128)S(1)}, f32[3,512]{1,0:T(4,128)}, u32[]{:S(2)}) copy-start(f32[3,512]{1,0:T(4,128)} %conv_ref.9) | copy-start | bytes 18436
  18.9 6.4 %copy-start = (bf16[512,2048]{1,0:T(8,128)(2,1)S(1)}, bf16[512,2048]{1,0:T(8,128)(2,1)}, u32[]{:S(2)}) copy-start(bf16[512,2048]{1,0:T(8,128)(2,1)} %w_ref.13) | copy-start | bytes 6291460
  23.8 5.1 %collective-permute-start.3 = (bf16[144,512]{1,0:T(8,128)(2,1)S(1)}, bf16[144,512]{1,0:T(8,128)(2,1)S(1)}, u32[]{:S(2)}, u32[]{:S(2)}) collective-permute-start(bf16[144,512]{1,0:T(8,128)(2,1)S(1)} %get-tuple-element.89), channel_id=1, source_target_pairs={{0,2},{2,4},{4,6},{6,8},{8,10},{10,12},{12,14},{14,16},{16,18},{18... | collective-permute-start | bytes 442376 | tf_op jit(solution)/shard_map/ppermute | solution.py:444
  25.9 7.8 %copy-start.2 = (bf16[8,256,128]{2,1,0:T(8,128)(2,1)S(1)}, bf16[8,256,128]{2,1,0:T(8,128)(2,1)}, u32[]{:S(2)}) copy-start(bf16[8,256,128]{2,1,0:T(8,128)(2,1)} %constant.29.clone.sel_a_ref) | copy-start | bytes 1572868
  57.3 18.4 %collective-permute-start.16 = (bf16[256,1024]{1,0:T(8,128)(2,1)S(1)}, bf16[256,1024]{1,0:T(8,128)(2,1)S(1)}, u32[]{:S(2)}, u32[]{:S(2)}) collective-permute-start(bf16[256,1024]{1,0:T(8,128)(2,1)S(1)} %shard_map.109), channel_id=1, source_target_pairs={{0,1},{1,0},{2,3},{3,2},{4,5},{5,4},{6,7},{7,6},{8,9},{9,8},{10,11... | collective-permute-start | bytes 1572872 | tf_op jit(solution)/shard_map/ppermute | solution.py:351
  59.4 4.6 %collective-permute-start.6 = (bf16[160,128]{1,0:T(8,128)(2,1)S(1)}, bf16[160,128]{1,0:T(8,128)(2,1)S(1)}, u32[]{:S(2)}, u32[]{:S(2)}) collective-permute-start(bf16[160,128]{1,0:T(8,128)(2,1)S(1)} %get-tuple-element.136), channel_id=1, source_target_pairs={{0,2},{2,0},{4,6},{6,4},{8,10},{10,8},{12,14},{14,12},{16,18},{18,... | collective-permute-start | bytes 122888 | tf_op jit(solution)/shard_map/ppermute | solution.py:256
  59.4 4.6 %collective-permute-start.7 = (bf16[160,128]{1,0:T(8,128)(2,1)S(1)}, bf16[160,128]{1,0:T(8,128)(2,1)S(1)}, u32[]{:S(2)}, u32[]{:S(2)}) collective-permute-start(bf16[160,128]{1,0:T(8,128)(2,1)S(1)} %get-tuple-element.137), channel_id=1, source_target_pairs={{0,4},{2,6},{4,0},{6,2},{8,12},{10,14},{12,8},{14,10},{16,20},{18,... | collective-permute-start | bytes 122888 | tf_op jit(solution)/shard_map/ppermute | solution.py:256
  60.9 3.5 %collective-permute-start.8 = (bf16[160,128]{1,0:T(8,128)(2,1)S(1)}, bf16[160,128]{1,0:T(8,128)(2,1)S(1)}, u32[]{:S(2)}, u32[]{:S(2)}) collective-permute-start(bf16[160,128]{1,0:T(8,128)(2,1)S(1)} %get-tuple-element.138), channel_id=1, source_target_pairs={{0,6},{2,4},{4,2},{6,0},{8,14},{10,12},{12,10},{14,8},{16,22},{18,... | collective-permute-start | bytes 122888 | tf_op jit(solution)/shard_map/ppermute | solution.py:256
  65.1 7.2 %collective-permute-start.9 = (bf16[160,128]{1,0:T(8,128)(2,1)S(1)}, bf16[160,128]{1,0:T(8,128)(2,1)S(1)}, u32[]{:S(2)}, u32[]{:S(2)}) collective-permute-start(bf16[160,128]{1,0:T(8,128)(2,1)S(1)} %get-tuple-element.143), channel_id=1, source_target_pairs={{0,8},{2,10},{4,12},{6,14},{8,0},{10,2},{12,4},{14,6},{16,24},{18,... | collective-permute-start | bytes 122888 | tf_op jit(solution)/shard_map/ppermute | solution.py:256
  66.8 5.8 %collective-permute-start.10 = (bf16[160,128]{1,0:T(8,128)(2,1)S(1)}, bf16[160,128]{1,0:T(8,128)(2,1)S(1)}, u32[]{:S(2)}, u32[]{:S(2)}) collective-permute-start(bf16[160,128]{1,0:T(8,128)(2,1)S(1)} %get-tuple-element.143), channel_id=1, source_target_pairs={{0,16},{2,18},{4,20},{6,22},{8,24},{10,26},{12,28},{14,30},{16,0},... | collective-permute-start | bytes 122888 | tf_op jit(solution)/shard_map/ppermute | solution.py:256
  69.4 5.8 %collective-permute-start.11 = (bf16[160,128]{1,0:T(8,128)(2,1)S(1)}, bf16[160,128]{1,0:T(8,128)(2,1)S(1)}, u32[]{:S(2)}, u32[]{:S(2)}) collective-permute-start(bf16[160,128]{1,0:T(8,128)(2,1)S(1)} %get-tuple-element.143), channel_id=1, source_target_pairs={{0,24},{2,26},{4,28},{6,30},{8,16},{10,18},{12,20},{14,22},{16,8},... | collective-permute-start | bytes 122888 | tf_op jit(solution)/shard_map/ppermute | solution.py:256
  69.6 13.6 %copy-start.7 = (f32[512]{0:T(512)S(1)}, f32[512]{0:T(512)}, u32[]{:S(2)}) copy-start(f32[512]{0:T(512)} %param.12) | copy-start | bytes 6148
  75.8 19.7 %collective-permute-start.17 = (bf16[256,1024]{1,0:T(8,128)(2,1)S(1)}, bf16[256,1024]{1,0:T(8,128)(2,1)S(1)}, u32[]{:S(2)}, u32[]{:S(2)}) collective-permute-start(bf16[256,1024]{1,0:T(8,128)(2,1)S(1)} %collective-permute-done.16.refs_1_), channel_id=1, source_target_pairs={{0,2},{2,0},{4,6},{6,4},{8,10},{10,8},{12,14},{14,12},{16,18},{18,... | collective-permute-start | bytes 1572872 | tf_op jit(solution)/shard_map/ppermute | solution.py:256
  75.8 7.3 %collective-permute-start.12 = (bf16[160,128]{1,0:T(8,128)(2,1)S(1)}, bf16[160,128]{1,0:T(8,128)(2,1)S(1)}, u32[]{:S(2)}, u32[]{:S(2)}) collective-permute-start(bf16[160,128]{1,0:T(8,128)(2,1)S(1)} %get-tuple-element.145), channel_id=1, source_target_pairs={{0,2},{2,0},{4,6},{6,4},{8,10},{10,8},{12,14},{14,12},{16,18},{18,... | collective-permute-start | bytes 122888 | tf_op jit(solution)/shard_map/ppermute | solution.py:256
  76.3 6.8 %collective-permute-start.13 = (bf16[160,128]{1,0:T(8,128)(2,1)S(1)}, bf16[160,128]{1,0:T(8,128)(2,1)S(1)}, u32[]{:S(2)}, u32[]{:S(2)}) collective-permute-start(bf16[160,128]{1,0:T(8,128)(2,1)S(1)} %get-tuple-element.146), channel_id=1, source_target_pairs={{0,4},{2,6},{4,0},{6,2},{8,12},{10,14},{12,8},{14,10},{16,20},{18,... | collective-permute-start | bytes 122888 | tf_op jit(solution)/shard_map/ppermute | solution.py:256
  77.4 5.7 %collective-permute-start.14 = (bf16[160,128]{1,0:T(8,128)(2,1)S(1)}, bf16[160,128]{1,0:T(8,128)(2,1)S(1)}, u32[]{:S(2)}, u32[]{:S(2)}) collective-permute-start(bf16[160,128]{1,0:T(8,128)(2,1)S(1)} %get-tuple-element.147), channel_id=1, source_target_pairs={{0,6},{2,4},{4,2},{6,0},{8,14},{10,12},{12,10},{14,8},{16,22},{18,... | collective-permute-start | bytes 122888 | tf_op jit(solution)/shard_map/ppermute | solution.py:256
  84.7 10.2 %collective-permute-start.21 = (bf16[256,512]{1,0:T(8,128)(2,1)S(1)}, bf16[256,512]{1,0:T(8,128)(2,1)S(1)}, u32[]{:S(2)}, u32[]{:S(2)}) collective-permute-start(bf16[256,512]{1,0:T(8,128)(2,1)S(1)} %shard_map.104.own_ref), channel_id=1, source_target_pairs={{0,1},{1,0},{2,3},{3,2},{4,5},{5,4},{6,7},{7,6},{8,9},{9,8},{10,11... | collective-permute-start | bytes 786440 | tf_op jit(solution)/shard_map/ppermute | solution.py:351
  86.9 12.7 %collective-permute-start.20 = (bf16[256,512]{1,0:T(8,128)(2,1)S(1)}, bf16[256,512]{1,0:T(8,128)(2,1)S(1)}, u32[]{:S(2)}, u32[]{:S(2)}) collective-permute-start(bf16[256,512]{1,0:T(8,128)(2,1)S(1)} %shard_map.105.own_ref), channel_id=1, source_target_pairs={{0,1},{1,0},{2,3},{3,2},{4,5},{5,4},{6,7},{7,6},{8,9},{9,8},{10,11... | collective-permute-start | bytes 786440 | tf_op jit(solution)/shard_map/ppermute | solution.py:351
  90.0 15.2 %collective-permute-start.19 = (bf16[256,512]{1,0:T(8,128)(2,1)S(1)}, bf16[256,512]{1,0:T(8,128)(2,1)S(1)}, u32[]{:S(2)}, u32[]{:S(2)}) collective-permute-start(bf16[256,512]{1,0:T(8,128)(2,1)S(1)} %shard_map.106.own_ref), channel_id=1, source_target_pairs={{0,1},{1,0},{2,3},{3,2},{4,5},{5,4},{6,7},{7,6},{8,9},{9,8},{10,11... | collective-permute-start | bytes 786440 | tf_op jit(solution)/shard_map/ppermute | solution.py:351
  91.9 16.1 %collective-permute-start.18 = (bf16[128,512]{1,0:T(8,128)(2,1)S(1)}, bf16[128,512]{1,0:T(8,128)(2,1)S(1)}, u32[]{:S(2)}, u32[]{:S(2)}) collective-permute-start(bf16[128,512]{1,0:T(8,128)(2,1)S(1)} %shard_map.107.own_ref), channel_id=1, source_target_pairs={{0,1},{1,0},{2,3},{3,2},{4,5},{5,4},{6,7},{7,6},{8,9},{9,8},{10,11... | collective-permute-start | bytes 393224 | tf_op jit(solution)/shard_map/ppermute | solution.py:351
  94.9 15.7 %collective-permute-start.15 = (bf16[128,512]{1,0:T(8,128)(2,1)S(1)}, bf16[128,512]{1,0:T(8,128)(2,1)S(1)}, u32[]{:S(2)}, u32[]{:S(2)}) collective-permute-start(bf16[128,512]{1,0:T(8,128)(2,1)S(1)} %shard_map.108.own_ref), channel_id=1, source_target_pairs={{0,1},{1,0},{2,3},{3,2},{4,5},{5,4},{6,7},{7,6},{8,9},{9,8},{10,11... | collective-permute-start | bytes 393224 | tf_op jit(solution)/shard_map/ppermute | solution.py:351

commit v4 on v3

--- a/solution.py
+++ b/solution.py
@@ -13,8 +13,8 @@
 WIN = 64
 CONV = 3
 LANES = 128
-FEATS = 160
-QFEATS = 256
+SHIFTS = FQK // 2 + 1
+FEATS = (SHIFTS + 1) * FQK
 EDGE = 16
 HALO = EDGE + 2 * WIN
 PLANE = 4
@@ -22,7 +22,7 @@
 BF16 = jnp.bfloat16
 
 
-def call(body, out_shape, *, flops=0, moved=0, vmem=48 << 20, **kwargs):
+def call(body, out_shape, *, vmem, **kwargs):
     return pl.pallas_call(
         body,
         out_shape=out_shape,
@@ -32,24 +32,30 @@
     )
 
 
+def feature_layout(heads):
+    in_group = min(heads, 4)
+    lanes = in_group * FQK
+    per_tile = LANES // lanes
+    return in_group, lanes, -(-(SHIFTS + 1) // per_tile) * per_tile
+
+
 def feature_tables(heads):
-    first = [FQK] + [FQK] * FQK
-    second = [FQK] + list(range(FQK))
-    weight = [1.0] + [1.0 / FQK**0.5] * FQK
-    for i in range(FQK):
-        for j in range(i, FQK):
-            first.append(i)
-            second.append(j)
-            weight.append((1.0 if i == j else 2.0) / (2.0 * FQK))
-    sel_a = np.zeros((heads, QFEATS, LANES), np.float32)
-    sel_b = np.zeros((heads, QFEATS, LANES), np.float32)
-    sel_w = np.zeros((heads, QFEATS, LANES), np.float32)
-    for h in range(heads):
-        for f, (i, j, w) in enumerate(zip(first, second, weight)):
-            sel_a[h, f, (h * FQK + i) % LANES] = 1.0
-            sel_b[h, f, (h * FQK + j) % LANES] = 1.0
-            sel_w[h, f, (h * FQK + i) % LANES] = w
-    return tuple(jnp.asarray(t, BF16) for t in (sel_a, sel_b, sel_w))
+    in_group, lanes, slots = feature_layout(heads)
+    groups = heads // in_group
+    turn = np.zeros((LANES, groups, slots, in_group, FQK), np.float32)
+    for g in range(groups):
+        for s in range(SHIFTS):
+            for h in range(in_group):
+                for i in range(FQK if s < SHIFTS - 1 else FQK // 2):
+                    turn[g * lanes + h * FQK + (i + s) % FQK, g, s, h, i] = 1.0
+    weight = np.zeros((SHIFTS + 1, FQK, LANES), np.float32)
+    weight[0] = 1.0 / (2.0 * FQK)
+    weight[1:SHIFTS] = 2.0 / (2.0 * FQK)
+    weight[SHIFTS - 1, FQK // 2] = 1.0
+    weight[SHIFTS] = 1.0 / FQK**0.5
+    turn = turn.reshape(LANES, -1)
+    by_rows = np.concatenate([turn.T, np.eye(LANES, dtype=np.float32)], 0)
+    return jnp.asarray(turn, BF16), jnp.asarray(by_rows, BF16), jnp.asarray(weight.reshape(FEATS, LANES))
 
 
 def mean_table():
@@ -65,10 +71,6 @@
 
 def nt_dot(a, b):
     return lax.dot_general(a, b, (((1,), (1,)), ((), ())), preferred_element_type=F32)
-
-
-def with_one(vectors, lane, h):
-    return jnp.where(lane == ((h + 1) * FQK) % LANES, 1.0, vectors).astype(BF16)
 
 
 def arrange_kernel(w_ref, o_ref, *, heads):
@@ -85,7 +87,7 @@
         at += padded
 
 
-def block_kernel(j_ref, mean_ref, conv_ref, sel_w_ref, sel_b_ref, w_ref, *refs, n, heads, extra, others, sends):
+def block_kernel(j_ref, mean_ref, conv_ref, turn_ref, weight_ref, w_ref, *refs, n, heads, extra, others, sends):
     xs, refs = refs[:n], refs[n:]
     prev_ref = None
     if not extra:
@@ -107,7 +109,9 @@
 
     widths = [ref.shape[1] for ref in (q_ref, k_ref, v_ref, wq_ref, wk_ref)]
     starts = [sum(widths[:i]) for i in range(5)]
-    k_ref[...] = project(starts[1], widths[1], extra)
+    qk = project(starts[0], widths[0] + widths[1], extra)
+    q_ref[...] = qk[:, : widths[0]]
+    k_ref[...] = qk[:, widths[0] :]
     raw = project(starts[2], widths[2], 0)
     if extra:
         ext_ref[...] = raw.astype(F32)
@@ -121,17 +125,28 @@
     v_ref[...] = total.astype(BF16)
     halo_ref[EDGE : EDGE + WIN, :] = v_ref[rows - WIN : rows, :]
 
-    lane = lax.broadcasted_iota(jnp.int32, (rows, LANES), 1)
-    low_half = lax.broadcasted_iota(jnp.int32, (FEATS, LANES), 1) < DV
-    k = k_ref[...].astype(F32)
-    for p in range(heads * DV // LANES):
-        v = v_ref[:, p * LANES : (p + 1) * LANES]
-        both = []
-        for h in (2 * p, 2 * p + 1):
-            own = with_one(k, lane, h)
-            phi = nt_dot(sel_w_ref[h, 0:FEATS, :], own) * nt_dot(sel_b_ref[h, 0:FEATS, :], own)
-            both.append(jnp.dot(phi.astype(BF16), v, preferred_element_type=F32))
-        s_ref[p] = jnp.where(low_half, both[0], both[1])
+    in_group, lanes, slots = feature_layout(heads)
+    groups = heads // in_group
+    turned = nt_dot(turn_ref[...], k_ref[...])
+    keys = turned[groups * slots * lanes :]
+    constant = lax.broadcasted_iota(jnp.int32, (lanes, rows), 0) % FQK == FQK // 2
+    low_half = lax.broadcasted_iota(jnp.int32, (SHIFTS + 1, FQK, LANES), 2) < DV
+    for g in range(groups):
+        own = keys[g * lanes : (g + 1) * lanes]
+        phi = []
+        for s in range(SHIFTS):
+            at = (g * slots + s) * lanes
+            phi.append(own * turned[at : at + lanes])
+        phi[-1] = jnp.where(constant, 1.0, phi[-1])
+        phi = jnp.concatenate([part.astype(BF16) for part in phi + [own]], 0)
+        v = v_ref[:, g * in_group * DV : (g + 1) * in_group * DV]
+        got = jnp.dot(phi, v, preferred_element_type=F32).reshape(SHIFTS + 1, lanes, in_group * DV)
+        for p in range(in_group * DV // LANES):
+            cols = slice(p * LANES, (p + 1) * LANES)
+            first = got[:, 2 * p * FQK : (2 * p + 1) * FQK, cols]
+            second = got[:, (2 * p + 1) * FQK : (2 * p + 2) * FQK, cols]
+            state = jnp.where(low_half, first, second).reshape(FEATS, LANES)
+            s_ref[g * in_group * DV // LANES + p] = state * weight_ref[...]
     for r in range(sends):
         pair = jnp.bitwise_xor(j_ref[1], r)
         total = s_ref[pair]
@@ -139,7 +154,6 @@
             total = total + ref[pair]
         send_refs[r][...] = total.astype(BF16)
 
-    q_ref[...] = project(starts[0], widths[0], extra)
     for ref, start, width, scale in (
         (wk_ref, starts[4], widths[4], 1.0),
         (wq_ref, starts[3], widths[3], 1.0 / DV**0.5),
@@ -154,7 +168,7 @@
 
 
 def attend_kernel(
-    a_ref, sel_a_ref, sel_b_ref, prev_ref, q_ref, k_ref, v_ref, wq_ref, wk_ref, phi_ref, lin_ref, win_ref,
+    a_ref, turn_ref, prev_ref, q_ref, k_ref, v_ref, wq_ref, wk_ref, phi_ref, lin_ref, win_ref,
     vext_ref, kext_ref, *, heads, first
 ):
     rows = q_ref.shape[0]
@@ -164,44 +178,60 @@
     vext_ref[WIN : WIN + rows, :] = v_ref[...]
     kext_ref[0:WIN, :] = prev_ref[EDGE + WIN : HALO, :]
     kext_ref[WIN : WIN + rows, :] = wk_ref[...]
+    q = q_ref[...]
+    k = k_ref[...]
     lane = lax.broadcasted_iota(jnp.int32, (rows, LANES), 1)
     low_half = lane < DV
-    causal = lax.broadcasted_iota(jnp.int32, (rows, rows), 1) <= lax.broadcasted_iota(jnp.int32, (rows, rows), 0)
-    col = lax.broadcasted_iota(jnp.int32, (tile, span), 1)
-    ahead = col - lax.broadcasted_iota(jnp.int32, (tile, span), 0)
-    band = (ahead >= 1) & (ahead <= WIN)
+
+    in_group, lanes, slots = feature_layout(heads)
+    per_tile = LANES // lanes
+    turned = jnp.dot(q, turn_ref[...], preferred_element_type=F32)
+    slot = lane // lanes
+    for g in range(heads // in_group):
+        own = q[:, g * lanes : (g + 1) * lanes].astype(F32)
+        own = jnp.concatenate([own] * per_tile, 1)
+        for t in range(slots // per_tile):
+            at = (g * slots // per_tile + t) * LANES
+            part = own * turned[:, at : at + LANES]
+            if t == (SHIFTS - 1) // per_tile:
+                here = (slot == (SHIFTS - 1) % per_tile) & (lane % FQK == FQK // 2)
+                part = jnp.where(here, 1.0, part)
+            if t == SHIFTS // per_tile:
+                part = jnp.where(slot == SHIFTS % per_tile, own, part)
+            phi_ref[:, at : at + LANES] = part.astype(BF16)
+
+    down = lax.broadcasted_iota(jnp.int32, (2 * rows, rows), 0) % rows
+    causal = lax.broadcasted_iota(jnp.int32, (2 * rows, rows), 1) <= down
+    col = lax.broadcasted_iota(jnp.int32, (2 * tile, span), 1)
+    ahead = col - lax.broadcasted_iota(jnp.int32, (2 * tile, span), 0) % tile
+    inside = (ahead >= 1) & (ahead <= WIN)
+    band = inside.astype(F32).astype(BF16)
     first_band = band
     if first:
-        first_band = band & (col >= jnp.where(a_ref[2] == 0, WIN, 0))
-    q = q_ref[...]
-    q_full = q.astype(F32)
-    k = k_ref[...]
+        first_band = (inside & (col >= jnp.where(a_ref[2] == 0, WIN, 0))).astype(F32).astype(BF16)
+    ones = jnp.ones((span, LANES), BF16)
+    q = q * jnp.asarray(1.0 / FQK**0.5, BF16)
     for p in range(heads * DV // LANES):
         cols = slice(p * LANES, (p + 1) * LANES)
-        v = v_ref[:, cols]
-        both = []
-        for h in (2 * p, 2 * p + 1):
-            own = with_one(q_full, lane, h)
-            phi = nt_dot(own, sel_a_ref[h]) * nt_dot(own, sel_b_ref[h])
-            phi_ref[:, h * QFEATS : (h + 1) * QFEATS] = phi.astype(BF16)
-            own = jnp.where((lane >= h * FQK) & (lane < (h + 1) * FQK), q, jnp.zeros_like(q))
-            t = nt_dot(own, k) * (1.0 / FQK**0.5) + 1.0
-            kernel = jnp.where(causal, 0.5 * (t * t) + 0.5, 0.0).astype(BF16)
-            both.append(jnp.dot(kernel, v, preferred_element_type=F32))
-        lin_ref[:, cols] = jnp.where(low_half, both[0], both[1])
+        both = [
+            jnp.where((lane >= h * FQK) & (lane < (h + 1) * FQK), q, jnp.zeros_like(q)) for h in (2 * p, 2 * p + 1)
+        ]
+        t = nt_dot(jnp.concatenate(both, 0), k) + 1.0
+        kernel = jnp.where(causal, t * t + 1.0, 0.0).astype(BF16)
+        got = jnp.dot(kernel, v_ref[:, cols], preferred_element_type=F32)
+        lin_ref[:, cols] = 0.5 * jnp.where(low_half, got[:rows], got[rows:])
         for i in range(rows // tile):
             here = slice(i * tile, (i + 1) * tile)
             wq = wq_ref[here, cols]
+            none = jnp.zeros_like(wq)
+            low = low_half[:tile]
             keys = kext_ref[i * tile : i * tile + span, cols]
             values = vext_ref[i * tile : i * tile + span, cols]
-            both = []
-            for half in range(2):
-                keep = low_half[0:tile] if half == 0 else ~low_half[0:tile]
-                scores = nt_dot(jnp.where(keep, wq, jnp.zeros_like(wq)), keys)
-                expo = jnp.where(first_band if i == 0 else band, jnp.exp(scores), 0.0)
-                weights = expo * (1.0 / jnp.sum(expo, axis=1, keepdims=True))
-                both.append(jnp.dot(weights.astype(BF16), values, preferred_element_type=F32))
-            win_ref[here, cols] = jnp.where(low_half[0:tile], both[0], both[1])
+            scores = nt_dot(jnp.concatenate([jnp.where(low, wq, none), jnp.where(low, none, wq)], 0), keys)
+            expo = jnp.exp(scores).astype(BF16) * (first_band if i == 0 else band)
+            got = jnp.dot(expo, jnp.concatenate([values, ones], 1), preferred_element_type=F32)
+            got = jnp.where(jnp.concatenate([low, low], 1), got[:tile], got[tile:])
+            win_ref[here, cols] = got[:, :LANES] / got[:, LANES:]
 
 
 def finish_kernel(a_ref, mean_ref, gain_ref, *refs, heads, before):
@@ -211,20 +241,34 @@
     rows = phi_ref.shape[0]
     for r in range(pairs):
         held_ref[r] = prior_refs[r][...].astype(F32)
-    low_half = lax.broadcasted_iota(jnp.int32, (rows, LANES), 1) < DV
-    for p in range(pairs):
-        cols = slice(p * LANES, (p + 1) * LANES)
-        state = held_ref[jnp.bitwise_xor(a_ref[1], p)]
-        for ref in states:
-            state = state + ref[p]
-        state = jnp.concatenate([state.astype(BF16), jnp.zeros((QFEATS - FEATS, LANES), BF16)], 0)
-        both = [
-            jnp.dot(phi_ref[:, h * QFEATS : (h + 1) * QFEATS], state, preferred_element_type=F32)
-            for h in (2 * p, 2 * p + 1)
-        ]
-        lin = lin_ref[:, cols] + jnp.where(low_half, both[0], both[1])
-        scale = lax.rsqrt(head_mean(lin * lin, mean_ref[...]) + 1e-5)
-        mix_ref[:, cols] = (lin * scale * gain_ref[:, cols] + win_ref[:, cols]).astype(BF16)
+    in_group, lanes, slots = feature_layout(heads)
+    in_pairs = in_group * DV // LANES
+    low_half = lax.broadcasted_iota(jnp.int32, (SHIFTS + 1, FQK, LANES), 2) < DV
+    for g in range(heads // in_group):
+        columns = []
+        for p in range(in_pairs):
+            pair = g * in_pairs + p
+            state = held_ref[jnp.bitwise_xor(a_ref[1], pair)]
+            for ref in states:
+                state = state + ref[pair]
+            state = state.reshape(SHIFTS + 1, FQK, LANES)
+            parts = [jnp.where(low_half, state, 0.0), jnp.where(low_half, 0.0, state)]
+            none = jnp.zeros_like(state)
+            parts = [none] * (2 * p) + parts + [none] * (in_group - 2 * p - 2)
+            parts = jnp.concatenate(parts, 1).reshape((SHIFTS + 1) * lanes, LANES)
+            if slots > SHIFTS + 1:
+                parts = jnp.concatenate([parts, jnp.zeros(((slots - SHIFTS - 1) * lanes, LANES), F32)], 0)
+            columns.append(parts.astype(BF16))
+        table = jnp.concatenate(columns, 1)
+        carried = jnp.dot(
+            phi_ref[:, g * slots * lanes : (g + 1) * slots * lanes], table, preferred_element_type=F32
+        )
+        for p in range(in_pairs):
+            at = (g * in_pairs + p) * LANES
+            cols = slice(at, at + LANES)
+            lin = lin_ref[:, cols] + carried[:, p * LANES : (p + 1) * LANES]
+            scale = lax.rsqrt(head_mean(lin * lin, mean_ref[...]) + 1e-5)
+            mix_ref[:, cols] = (lin * scale * gain_ref[:, cols] + win_ref[:, cols]).astype(BF16)
 
 
 def output_kernel(a_ref, own_ref, w_ref, *refs, n, offset, parts):
@@ -296,7 +340,6 @@
         [narrow] + [wide] * PLANE,
         in_specs=[scalar] + [whole] * PLANE,
         out_specs=[whole] * (1 + PLANE),
-        moved=24 * FEATS * LANES,
         vmem=4 << 20,
     )(after(places, beside[0]), *held)
     earlier = []
@@ -307,7 +350,6 @@
         [narrow] * PLANE,
         in_specs=[scalar] + [whole] * (PLANE + len(earlier)),
         out_specs=[whole] * PLANE,
-        moved=24 * FEATS * LANES,
         vmem=4 << 20,
     )(after(places, beside[1]), *ahead, *earlier)
     return back[0], [back[0]] + [exchange(back[r], "ctx", r) for r in range(1, PLANE)]
@@ -341,7 +383,7 @@
     step = row_count // 8
     blocks = [(0, 2 * step), (2 * step, 2 * step), (4 * step, step), (5 * step, step), (6 * step, 2 * step)]
     last = len(blocks) - 1
-    sel_a, sel_b, sel_w = feature_tables(heads)
+    turn, turn_rows, weight = feature_tables(heads)
     means = mean_table()
     gain = norm_gain.reshape(1, width)
     whole = pl.BlockSpec(memory_space=pltpu.VMEM)
@@ -381,7 +423,6 @@
                 ],
                 out_specs=pl.BlockSpec((share, cols), lambda i, a: (0, 0)),
             ),
-            moved=4 * share * cols,
             vmem=8 << 20,
         )(places, out_weight)
         picked.append(block)
@@ -395,7 +436,6 @@
         grid=(model // slab,),
         in_specs=[pl.BlockSpec((slab, proj_weight.shape[1]), lambda i: (i, 0))],
         out_specs=pl.BlockSpec((slab, arranged_width), lambda i: (i, 0)),
-        moved=4 * model * arranged_width,
         vmem=32 << 20,
     )(proj_weight)
 
@@ -408,7 +448,7 @@
         shapes.append(jax.ShapeDtypeStruct((HALO, width), BF16))
         shapes.append(jax.ShapeDtypeStruct((pairs, FEATS, LANES), F32))
         shapes += [jax.ShapeDtypeStruct((FEATS, LANES), BF16)] * sends
-        operands = [tokens, means, conv_weight, sel_w, sel_b, arranged, *pieces[b]]
+        operands = [tokens, means, conv_weight, turn_rows, weight, arranged, *pieces[b]]
         if prev is not None:
             operands.append(prev)
         operands += others
@@ -420,8 +460,6 @@
             in_specs=[scalar] + [whole] * (len(operands) - 1),
             out_specs=[whole] * len(shapes),
             scratch_shapes=[pltpu.VMEM((EDGE + rows, width), F32)],
-            flops=2 * rows * model * arranged_width + 6 * rows * FEATS * LANES * heads,
-            moved=2 * model * arranged_width,
             vmem=32 << 20,
         )(*operands)
 
@@ -430,14 +468,12 @@
         q, k, v, wq, wk = done[b][:5]
         return call(
             functools.partial(attend_kernel, heads=heads, first=b == 0),
-            [jax.ShapeDtypeStruct((rows, heads * QFEATS), BF16)] + [jax.ShapeDtypeStruct((rows, width), F32)] * 2,
-            in_specs=[scalar] + [whole] * 8,
+            [jax.ShapeDtypeStruct((rows, turn.shape[1]), BF16)] + [jax.ShapeDtypeStruct((rows, width), F32)] * 2,
+            in_specs=[scalar] + [whole] * 7,
             out_specs=[whole] * 3,
             scratch_shapes=[pltpu.VMEM((WIN + rows, width), BF16)] * 2,
-            flops=heads * rows * 4096 * 256,
-            moved=16 * rows * width,
             vmem=16 << 20,
-        )(places, sel_a, sel_b, prev, q, k, v, wq, wk)
+        )(places, turn, prev, q, k, v, wq, wk)
 
     done, attended = {}, {}
     done[last] = do_block(last, None, None)
@@ -449,10 +485,9 @@
         if b < last - 2:
             attended[b] = attend(b, prev)
 
-    fetched = [from_head(after(block, done[last - 1][5]), r) for r, block in enumerate(picked, 1)]
-
     for b in range(last - 2, last + 1):
         attended[b] = attend(b, done[b - 1][5])
+    fetched = [from_head(after(block, attended[last - 2][1]), r) for r, block in enumerate(picked, 1)]
     if in_planes:
         beside = [attended[b][1] for b in (last - 2, last - 1)]
         mark, priors = prior_in_planes(done[last - 1][7:], places, beside)
@@ -474,8 +509,6 @@
             in_specs=[scalar] + [whole] * (2 + pairs + b + 3),
             out_specs=whole,
             scratch_shapes=[pltpu.VMEM((pairs, FEATS, LANES), F32)],
-            flops=6 * rows * QFEATS * LANES * heads,
-            moved=12 * rows * width,
             vmem=16 << 20,
         )(after(places, mixed), means, gain, *priors, *[done[c][6] for c in range(b)], *attended[b])
         others = [from_head(mixed, r) for r in range(1, n)]
@@ -493,8 +526,6 @@
             out_specs=pl.BlockSpec(memory_space=pl.ANY),
             scratch_shapes=[pltpu.VMEM((rows, cols), BF16), pltpu.SemaphoreType.DMA],
             input_output_aliases=aliases,
-            flops=2 * rows * n * width * cols,
-            moved=2 * n * width * cols,
             vmem=16 << 20,
         )(*operands)
     return result

time: 113 us -> 122 us (1.080)
  waiting for transfers between devices: 14.7 us -> 41 us
  Pallas kernels: 66.6 us -> 50.4 us
    ppermute x11, waiting for transfers between devices: 11.5 us -> 32.8 us  [from_head(): return lax.ppermute(value, 'head', [(i, (i + by) % n) for i in range(n)])]
    pallas_call x5, Pallas kernels: 21.3 us -> 9.75 us  [attend(): call(functools.partial(attend_kernel, heads=heads, first=b == 0), [jax.Sh...]
    ppermute x10, waiting for transfers between devices: 3.21 us -> 8.19 us  [exchange(): return lax.ppermute(value, axis, [(i, i ^ flip) for i in range(count)])]
    pallas_call x5, Pallas kernels: 21.3 us -> 17.1 us  [do_block(): call(functools.partial(block_kernel, n=n, heads=heads, extra=extra, other...]
  transfers between devices with their start and end apart: 22 -> 22, of which waited for: 9 -> 14; matrix products, arithmetic and copies ran while one was open for 2% -> 2% of each run, Pallas kernels for 55% -> 36%
where the time goes in v4:
time: 122 us
  Pallas kernels  50.4 us (41%)
  waiting for transfers between devices  41 us (34%)
  starting transfers between devices  23.2 us (19%)
  local copies, waits for them, and re-layouts  6.54 us (5%)
    ppermute x11, waiting for transfers between devices, from_head(): return lax.ppermute(value, 'head', [(i, (i + by) % n) for i in range(n)])  32.8 us
    pallas_call x5, Pallas kernels, do_block(): call(functools.partial(block_kernel, n=n, heads=heads, extra=extra, other...  17.1 us
    ppermute x11, starting transfers between devices, from_head(): return lax.ppermute(value, 'head', [(i, (i + by) % n) for i in range(n)])  13.4 us
    pallas_call x5, Pallas kernels, attend(): call(functools.partial(attend_kernel, heads=heads, first=b == 0), [jax.Sh...  9.75 us
    pallas_call x5, Pallas kernels, per_device(): call(functools.partial(output_kernel, n=n, offset=at, parts=out_parts), j...  9.63 us
    ppermute x10, starting transfers between devices, exchange(): return lax.ppermute(value, axis, [(i, i ^ flip) for i in range(count)])  8.38 us
    ppermute x10, waiting for transfers between devices, exchange(): return lax.ppermute(value, axis, [(i, i ^ flip) for i in range(count)])  8.19 us
    pallas_call x5, Pallas kernels, per_device(): call(functools.partial(finish_kernel, heads=heads, before=b), jax.ShapeDt...  7.03 us
  transfers between devices with their start and end apart: 22, of which 14 were waited for; matrix products, arithmetic and copies ran while one was open for 2% of the time, Pallas kernels for 36%

profile of v4, /device:TPU:0, one launch (start us, length us, event | category | flops | bytes accessed | tf_op | source)
XLA Modules:
  0.0 121.7 jit_solution(17566542867654947880)
XLA Ops:
  1.2 3.0 %collective-permute-start.2 = (bf16[272,1024]{1,0:T(8,128)(2,1)S(1)}, bf16[272,1024]{1,0:T(8,128)(2,1)S(1)}, u32[]{:S(2)}, u32[]{:S(2)}) collective-permute-start(bf16[272,1024]{1,0:T(8,128)(2,1)S(1)} %slice.16.refs_0_), channel_id=1, source_target_pairs={{0,1},{1,0},{2,3},{3,2},{4,5},{5,4},{6,7},{7,6},{8,9},{9,8},{10,11... | collective-permute-start | bytes 1671176 | tf_op jit(solution)/shard_map/ppermute | solution.py:393
  5.6 2.0 %collective-permute-start.4 = (bf16[256,1024]{1,0:T(8,128)(2,1)S(1)}, bf16[256,1024]{1,0:T(8,128)(2,1)S(1)}, u32[]{:S(2)}, u32[]{:S(2)}) collective-permute-start(bf16[256,1024]{1,0:T(8,128)(2,1)S(1)} %get-tuple-element.98.refs_0_), channel_id=1, source_target_pairs={{0,1},{1,0},{2,3},{3,2},{4,5},{5,4},{6,7},{7,6},{8,9},{9,8},{10,11... | collective-permute-start | bytes 1572872 | tf_op jit(solution)/shard_map/ppermute | solution.py:393
  8.8 3.1 %copy-done.3 = bf16[2048,1792]{1,0:T(8,128)(2,1)S(1)} copy-done((bf16[2048,1792]{1,0:T(8,128)(2,1)S(1)}, bf16[2048,1792]{1,0:T(8,128)(2,1)}, u32[]{:S(2)}) %copy-start.3) | copy-done | bytes 7340056
  11.9 5.1 %shard_map.91.w_ref = bf16[2048,1792]{1,0:T(8,128)(2,1)S(1)} custom-call(bf16[2048,1792]{1,0:T(8,128)(2,1)S(1)} %copy-done.3), custom_call_target="tpu_custom_call" | custom-call | flops 1 | bytes 1 | tf_op jit(solution)/shard_map/pallas_call | solution.py:433
  17.7 3.8 %shard_map.92 = (bf16[256,128]{1,0:T(8,128)(2,1)S(1)}, bf16[256,128]{1,0:T(8,128)(2,1)S(1)}, bf16[256,512]{1,0:T(8,128)(2,1)S(1)}, bf16[256,512]{1,0:T(8,128)(2,...) custom-call(s32[3]{0:T(128)S(1)} %pad_add_fusion.j_ref.a_ref, ...), custom_call_target="tpu_custom_call" | custom-call | flops 1 | bytes 1 | tf_op jit(solution)/shard_map/pallas_call | solution.py:455
  23.6 5.3 %collective-permute-done.1.refs_1_ = bf16[256,1024]{1,0:T(8,128)(2,1)S(1)} collective-permute-done((bf16[256,1024]{1,0:T(8,128)(2,1)S(1)}, bf16[256,1024]{1,0:T(8,128)(2,1)S(1)}, u32[]{:S(2)}, u32[]{:S(2)}) %collective-permute-start.1) | collective-permute-done | bytes 524320 | tf_op jit(solution)/shard_map/ppermute | solution.py:393
  28.9 3.8 %shard_map.93 = (bf16[256,128]{1,0:T(8,128)(2,1)S(1)}, bf16[256,128]{1,0:T(8,128)(2,1)S(1)}, bf16[256,512]{1,0:T(8,128)(2,1)S(1)}, bf16[256,512]{1,0:T(8,128)(2,...) custom-call(s32[3]{0:T(128)S(1)} %pad_add_fusion.j_ref.a_ref, ...), custom_call_target="tpu_custom_call" | custom-call | flops 1 | bytes 1 | tf_op jit(solution)/shard_map/pallas_call | solution.py:455
  32.7 2.1 %shard_map.94 = (bf16[256,1280]{1,0:T(8,128)(2,1)S(1)}, f32[256,512]{1,0:T(8,128)S(1)}, f32[256,512]{1,0:T(8,128)S(1)}) custom-call(s32[3]{0:T(128)S(1)} %pad_add_fusion.j_ref.a_ref, bf16[128,1280]{1,0:T(8,128)(2,1)S(1)} %copy-done.2, bf16[144,512]{1,0:T(8,128)(2,1)S(1)} %collective-permute-done.3.refs_2_.prev_ref, ...), custom_call_target="tpu_custom_call" | custom-call | flops 1 | bytes 1 | tf_op jit(solution)/shard_map/pallas_call | solution.py:469
  34.9 5.2 %collective-permute-done.4.refs_1_ = bf16[256,1024]{1,0:T(8,128)(2,1)S(1)} collective-permute-done((bf16[256,1024]{1,0:T(8,128)(2,1)S(1)}, bf16[256,1024]{1,0:T(8,128)(2,1)S(1)}, u32[]{:S(2)}, u32[]{:S(2)}) %collective-permute-start.4) | collective-permute-done | bytes 524320 | tf_op jit(solution)/shard_map/ppermute | solution.py:393
  40.1 3.8 %shard_map.95 = (bf16[256,128]{1,0:T(8,128)(2,1)S(1)}, bf16[256,128]{1,0:T(8,128)(2,1)S(1)}, bf16[256,512]{1,0:T(8,128)(2,1)S(1)}, bf16[256,512]{1,0:T(8,128)(2,...) custom-call(s32[3]{0:T(128)S(1)} %pad_add_fusion.j_ref.a_ref, ...), custom_call_target="tpu_custom_call" | custom-call | flops 1 | bytes 1 | tf_op jit(solution)/shard_map/pallas_call | solution.py:455
  44.0 2.1 %shard_map.96 = (bf16[256,1280]{1,0:T(8,128)(2,1)S(1)}, f32[256,512]{1,0:T(8,128)S(1)}, f32[256,512]{1,0:T(8,128)S(1)}) custom-call(s32[3]{0:T(128)S(1)} %pad_add_fusion.j_ref.a_ref, bf16[128,1280]{1,0:T(8,128)(2,1)S(1)} %copy-done.2, bf16[144,512]{1,0:T(8,128)(2,1)S(1)} %get-tuple-element.90.refs_2_.prev_ref, bf16[256,128]{1,0:T(8,128)(2,1)S(1)} %get-tuple-element.99.q_ref, ...), custom_call_target="tpu_custom_call" | custom-call | flops 1 | bytes 1 | tf_op jit(solution)/shard_map/pallas_call | solution.py:469
  46.1 2.6 %shard_map.97 = (bf16[128,128]{1,0:T(8,128)(2,1)S(1)}, bf16[128,128]{1,0:T(8,128)(2,1)S(1)}, bf16[128,512]{1,0:T(8,128)(2,1)S(1)}, bf16[128,512]{1,0:T(8,128)(2,...) custom-call(s32[3]{0:T(128)S(1)} %pad_add_fusion.j_ref.a_ref, ...), custom_call_target="tpu_custom_call" | custom-call | flops 1 | bytes 1 | tf_op jit(solution)/shard_map/pallas_call | solution.py:455
  48.7 1.7 %shard_map.101 = (bf16[128,1280]{1,0:T(8,128)(2,1)S(1)}, f32[128,512]{1,0:T(8,128)S(1)}, f32[128,512]{1,0:T(8,128)S(1)}) custom-call(s32[3]{0:T(128)S(1)} %pad_add_fusion.j_ref.a_ref, bf16[128,1280]{1,0:T(8,128)(2,1)S(1)} %copy-done.2, bf16[144,512]{1,0:T(8,128)(2,1)S(1)} %get-tuple-element.107.refs_2_.prev_ref, ...), custom_call_target="tpu_custom_call" | custom-call | flops 1 | bytes 1 | tf_op jit(solution)/shard_map/pallas_call | solution.py:469
  50.4 2.1 %collective-permute-start.16 = (bf16[256,1024]{1,0:T(8,128)(2,1)S(1)}, bf16[256,1024]{1,0:T(8,128)(2,1)S(1)}, u32[]{:S(2)}, u32[]{:S(2)}) collective-permute-start(bf16[256,1024]{1,0:T(8,128)(2,1)S(1)} %shard_map.109), channel_id=1, source_target_pairs={{0,1},{1,0},{2,3},{3,2},{4,5},{5,4},{6,7},{7,6},{8,9},{9,8},{10,11... | collective-permute-start | bytes 1572872 | tf_op jit(solution)/shard_map/ppermute | solution.py:393
  52.6 15.8 %collective-permute-done.refs_1_ = bf16[128,1024]{1,0:T(8,128)(2,1)S(1)} collective-permute-done((bf16[128,1024]{1,0:T(8,128)(2,1)S(1)}, bf16[128,1024]{1,0:T(8,128)(2,1)S(1)}, u32[]{:S(2)}, u32[]{:S(2)}) %collective-permute-start) | collective-permute-done | bytes 262176 | tf_op jit(solution)/shard_map/ppermute | solution.py:393
  68.4 3.0 %shard_map.98 = (bf16[128,128]{1,0:T(8,128)(2,1)S(1)}, bf16[128,128]{1,0:T(8,128)(2,1)S(1)}, bf16[128,512]{1,0:T(8,128)(2,1)S(1)}, bf16[128,512]{1,0:T(8,128)(2,...) custom-call(s32[3]{0:T(128)S(1)} %pad_add_fusion.j_ref.a_ref, ...), custom_call_target="tpu_custom_call" | custom-call | flops 1 | bytes 1 | tf_op jit(solution)/shard_map/pallas_call | solution.py:455
  73.3 2.2 %collective-permute-done.7.refs_2_ = bf16[160,128]{1,0:T(8,128)(2,1)S(1)} collective-permute-done((bf16[160,128]{1,0:T(8,128)(2,1)S(1)}, bf16[160,128]{1,0:T(8,128)(2,1)S(1)}, u32[]{:S(2)}, u32[]{:S(2)}) %collective-permute-start.7) | collective-permute-done | bytes 40992 | tf_op jit(solution)/shard_map/ppermute | solution.py:300
  77.1 1.6 %collective-permute-start.9 = (bf16[160,128]{1,0:T(8,128)(2,1)S(1)}, bf16[160,128]{1,0:T(8,128)(2,1)S(1)}, u32[]{:S(2)}, u32[]{:S(2)}) collective-permute-start(bf16[160,128]{1,0:T(8,128)(2,1)S(1)} %get-tuple-element.143), channel_id=1, source_target_pairs={{0,8},{2,10},{4,12},{6,14},{8,0},{10,2},{12,4},{14,6},{16,24},{18,... | collective-permute-start | bytes 122888 | tf_op jit(solution)/shard_map/ppermute | solution.py:300
  78.7 2.6 %collective-permute-start.10 = (bf16[160,128]{1,0:T(8,128)(2,1)S(1)}, bf16[160,128]{1,0:T(8,128)(2,1)S(1)}, u32[]{:S(2)}, u32[]{:S(2)}) collective-permute-start(bf16[160,128]{1,0:T(8,128)(2,1)S(1)} %get-tuple-element.143), channel_id=1, source_target_pairs={{0,16},{2,18},{4,20},{6,22},{8,24},{10,26},{12,28},{14,30},{16,0},... | collective-permute-start | bytes 122888 | tf_op jit(solution)/shard_map/ppermute | solution.py:300
  81.5 1.7 %shard_map.100 = (bf16[128,1280]{1,0:T(8,128)(2,1)S(1)}, f32[128,512]{1,0:T(8,128)S(1)}, f32[128,512]{1,0:T(8,128)S(1)}) custom-call(s32[3]{0:T(128)S(1)} %pad_add_fusion.j_ref.a_ref, bf16[128,1280]{1,0:T(8,128)(2,1)S(1)} %copy-done.2, bf16[144,512]{1,0:T(8,128)(2,1)S(1)} %get-tuple-element.108.refs_2_.prev_ref, ...), custom_call_target="tpu_custom_call" | custom-call | flops 1 | bytes 1 | tf_op jit(solution)/shard_map/pallas_call | solution.py:469
  84.4 2.7 %collective-permute-done.11.refs_6_ = bf16[160,128]{1,0:T(8,128)(2,1)S(1)} collective-permute-done((bf16[160,128]{1,0:T(8,128)(2,1)S(1)}, bf16[160,128]{1,0:T(8,128)(2,1)S(1)}, u32[]{:S(2)}, u32[]{:S(2)}) %collective-permute-start.11) | collective-permute-done | bytes 40992 | tf_op jit(solution)/shard_map/ppermute | solution.py:300
  89.7 2.1 %shard_map.99 = (bf16[256,1280]{1,0:T(8,128)(2,1)S(1)}, f32[256,512]{1,0:T(8,128)S(1)}, f32[256,512]{1,0:T(8,128)S(1)}) custom-call(s32[3]{0:T(128)S(1)} %pad_add_fusion.j_ref.a_ref, bf16[128,1280]{1,0:T(8,128)(2,1)S(1)} %copy-done.2, bf16[144,512]{1,0:T(8,128)(2,1)S(1)} %get-tuple-element.113.prev_ref, bf16[256,128]{1,0:T(8,128)(2,1)S(1)} %get-tuple-element.114.q_ref, ...), custom_call_target="tpu_custom_call" | custom-call | flops 1 | bytes 1 | tf_op jit(solution)/shard_map/pallas_call | solution.py:469
  94.6 1.6 %collective-permute-start.21 = (bf16[256,512]{1,0:T(8,128)(2,1)S(1)}, bf16[256,512]{1,0:T(8,128)(2,1)S(1)}, u32[]{:S(2)}, u32[]{:S(2)}) collective-permute-start(bf16[256,512]{1,0:T(8,128)(2,1)S(1)} %shard_map.104.own_ref), channel_id=1, source_target_pairs={{0,1},{1,0},{2,3},{3,2},{4,5},{5,4},{6,7},{7,6},{8,9},{9,8},{10,11... | collective-permute-start | bytes 786440 | tf_op jit(solution)/shard_map/ppermute | solution.py:393
  98.2 1.5 %shard_map.106.own_ref = bf16[256,512]{1,0:T(8,128)(2,1)S(1)} custom-call(s32[3]{0:T(128)S(1)} %pad_add_fusion.j_ref.a_ref, bf16[256,128]{1,0:T(8,128)(2,1)S(1)} %copy-done.4, f32[1,512]{1,0:T(1,128)S(1)} %bitcast.6, bf16[160,128]{1,0:T(8,128)(2,1)S(1)} %get-tuple-element.144.refs_0_, bf16[160,128]{1,0:T(8,128)(2,1)S(1)} %collective-permute-done.12.refs_1_, ...), custom_call_target="tpu_custom_call" | custom-call | flops 1 | bytes 1 | tf_op jit(solution)/shard_map/pallas_call | solution.py:506
  99.8 1.6 %collective-permute-start.19 = (bf16[256,512]{1,0:T(8,128)(2,1)S(1)}, bf16[256,512]{1,0:T(8,128)(2,1)S(1)}, u32[]{:S(2)}, u32[]{:S(2)}) collective-permute-start(bf16[256,512]{1,0:T(8,128)(2,1)S(1)} %shard_map.106.own_ref), channel_id=1, source_target_pairs={{0,1},{1,0},{2,3},{3,2},{4,5},{5,4},{6,7},{7,6},{8,9},{9,8},{10,11... | collective-permute-start | bytes 786440 | tf_op jit(solution)/shard_map/ppermute | solution.py:393
  104.4 1.6 %collective-permute-start.15 = (bf16[128,512]{1,0:T(8,128)(2,1)S(1)}, bf16[128,512]{1,0:T(8,128)(2,1)S(1)}, u32[]{:S(2)}, u32[]{:S(2)}) collective-permute-start(bf16[128,512]{1,0:T(8,128)(2,1)S(1)} %shard_map.108.own_ref), channel_id=1, source_target_pairs={{0,1},{1,0},{2,3},{3,2},{4,5},{5,4},{6,7},{7,6},{8,9},{9,8},{10,11... | collective-permute-start | bytes 393224 | tf_op jit(solution)/shard_map/ppermute | solution.py:393
  106.0 2.1 %shard_map.110.refs_3_ = bf16[1024,1024]{1,0:T(8,128)(2,1)} custom-call(s32[3]{0:T(128)S(1)} %pad_add_fusion.j_ref.a_ref, bf16[256,512]{1,0:T(8,128)(2,1)S(1)} %shard_map.104.own_ref, bf16[512,2048]{1,0:T(8,128)(2,1)S(1)} %copy-done, bf16[256,512]{1,0:T(8,128)(2,1)S(1)} %collective-permute-done.21.refs_0_, ...), custom_call_target="tpu_custom_call" | custom-call | flops 1 | bytes 1 | tf_op jit(solution)/shard_map/pallas_call | solution.py:522
  109.4 2.1 %shard_map.111.refs_3_ = bf16[1024,1024]{1,0:T(8,128)(2,1)} custom-call(s32[3]{0:T(128)S(1)} %pad_add_fusion.j_ref.a_ref, bf16[256,512]{1,0:T(8,128)(2,1)S(1)} %shard_map.105.own_ref, bf16[512,2048]{1,0:T(8,128)(2,1)S(1)} %copy-done, bf16[256,512]{1,0:T(8,128)(2,1)S(1)} %collective-permute-done.20.refs_0_, ...), custom_call_target="tpu_custom_call", output_to_operand_aliasing={{}: (6, {})} | custom-call | flops 1 | bytes 1 | tf_op jit(solution)/shard_map/pallas_call | solution.py:522
  111.5 3.5 %collective-permute-done.19.refs_0_ = bf16[256,512]{1,0:T(8,128)(2,1)S(1)} collective-permute-done((bf16[256,512]{1,0:T(8,128)(2,1)S(1)}, bf16[256,512]{1,0:T(8,128)(2,1)S(1)}, u32[]{:S(2)}, u32[]{:S(2)}) %collective-permute-start.19) | collective-permute-done | bytes 262176 | tf_op jit(solution)/shard_map/ppermute | solution.py:393
  115.0 2.1 %shard_map.112.refs_3_ = bf16[1024,1024]{1,0:T(8,128)(2,1)} custom-call(s32[3]{0:T(128)S(1)} %pad_add_fusion.j_ref.a_ref, bf16[256,512]{1,0:T(8,128)(2,1)S(1)} %shard_map.106.own_ref, bf16[512,2048]{1,0:T(8,128)(2,1)S(1)} %copy-done, bf16[256,512]{1,0:T(8,128)(2,1)S(1)} %collective-permute-done.19.refs_0_, ...), custom_call_target="tpu_custom_call", output_to_operand_aliasing={{}: (6, {})} | custom-call | flops 1 | bytes 1 | tf_op jit(solution)/shard_map/pallas_call | solution.py:522
  117.8 1.7 %shard_map.113.refs_3_ = bf16[1024,1024]{1,0:T(8,128)(2,1)} custom-call(s32[3]{0:T(128)S(1)} %pad_add_fusion.j_ref.a_ref, bf16[128,512]{1,0:T(8,128)(2,1)S(1)} %shard_map.107.own_ref, bf16[512,2048]{1,0:T(8,128)(2,1)S(1)} %copy-done, bf16[128,512]{1,0:T(8,128)(2,1)S(1)} %collective-permute-done.18.refs_0_, ...), custom_call_target="tpu_custom_call", output_to_operand_aliasing={{}: (6, {})} | custom-call | flops 1 | bytes 1 | tf_op jit(solution)/shard_map/pallas_call | solution.py:522
  119.8 1.7 %shard_map.114 = bf16[1024,1024]{1,0:T(8,128)(2,1)} custom-call(s32[3]{0:T(128)S(1)} %pad_add_fusion.j_ref.a_ref, bf16[128,512]{1,0:T(8,128)(2,1)S(1)} %shard_map.108.own_ref, bf16[512,2048]{1,0:T(8,128)(2,1)S(1)} %copy-done, bf16[128,512]{1,0:T(8,128)(2,1)S(1)} %collective-permute-done.15.refs_0_, ...), custom_call_target="tpu_custom_call", output_to_operand_aliasing={{}: (6, {})} | custom-call | flops 1 | bytes 1 | tf_op jit(solution)/shard_map/pallas_call | solution.py:522
  (56 shorter events, 24.2 us)
Async XLA Ops:
  1.2 16.5 %collective-permute-start.2 = (bf16[272,1024]{1,0:T(8,128)(2,1)S(1)}, bf16[272,1024]{1,0:T(8,128)(2,1)S(1)}, u32[]{:S(2)}, u32[]{:S(2)}) collective-permute-start(bf16[272,1024]{1,0:T(8,128)(2,1)S(1)} %slice.16.refs_0_), channel_id=1, source_target_pairs={{0,1},{1,0},{2,3},{3,2},{4,5},{5,4},{6,7},{7,6},{8,9},{9,8},{10,11... | collective-permute-start | bytes 1671176 | tf_op jit(solution)/shard_map/ppermute | solution.py:393
  5.5 23.4 %collective-permute-start.1 = (bf16[256,1024]{1,0:T(8,128)(2,1)S(1)}, bf16[256,1024]{1,0:T(8,128)(2,1)S(1)}, u32[]{:S(2)}, u32[]{:S(2)}) collective-permute-start(bf16[256,1024]{1,0:T(8,128)(2,1)S(1)} %get-tuple-element.88.refs_0_), channel_id=1, source_target_pairs={{0,1},{1,0},{2,3},{3,2},{4,5},{5,4},{6,7},{7,6},{8,9},{9,8},{10,11... | collective-permute-start | bytes 1572872 | tf_op jit(solution)/shard_map/ppermute | solution.py:393
  5.6 34.6 %collective-permute-start.4 = (bf16[256,1024]{1,0:T(8,128)(2,1)S(1)}, bf16[256,1024]{1,0:T(8,128)(2,1)S(1)}, u32[]{:S(2)}, u32[]{:S(2)}) collective-permute-start(bf16[256,1024]{1,0:T(8,128)(2,1)S(1)} %get-tuple-element.98.refs_0_), channel_id=1, source_target_pairs={{0,1},{1,0},{2,3},{3,2},{4,5},{5,4},{6,7},{7,6},{8,9},{9,8},{10,11... | collective-permute-start | bytes 1572872 | tf_op jit(solution)/shard_map/ppermute | solution.py:393
  8.6 9.0 %copy-start.1 = (bf16[1408,128]{1,0:T(8,128)(2,1)S(1)}, bf16[1408,128]{1,0:T(8,128)(2,1)}, u32[]{:S(2)}) copy-start(bf16[1408,128]{1,0:T(8,128)(2,1)} %constant.30.clone.turn_ref) | copy-start | bytes 1081348
  8.6 37.5 %collective-permute-start.5 = (bf16[128,1024]{1,0:T(8,128)(2,1)S(1)}, bf16[128,1024]{1,0:T(8,128)(2,1)S(1)}, u32[]{:S(2)}, u32[]{:S(2)}) collective-permute-start(bf16[128,1024]{1,0:T(8,128)(2,1)S(1)} %get-tuple-element.106.refs_0_), channel_id=1, source_target_pairs={{0,1},{1,0},{2,3},{3,2},{4,5},{5,4},{6,7},{7,6},{8,9},{9,8},{10,11... | collective-permute-start | bytes 786440 | tf_op jit(solution)/shard_map/ppermute | solution.py:393
  8.8 3.1 %copy-start.3 = (bf16[2048,1792]{1,0:T(8,128)(2,1)S(1)}, bf16[2048,1792]{1,0:T(8,128)(2,1)}, u32[]{:S(2)}) copy-start(bf16[2048,1792]{1,0:T(8,128)(2,1)} %w_ref.7) | copy-start | bytes 22020100
  11.9 5.8 %copy-start.4 = (bf16[256,128]{1,0:T(8,128)(2,1)S(1)}, bf16[256,128]{1,0:T(8,128)(2,1)}, u32[]{:S(2)}) copy-start(bf16[256,128]{1,0:T(8,128)(2,1)} %constant.32.clone.mean_ref) | copy-start | bytes 196612
  11.9 5.8 %copy-start.5 = (f32[160,128]{1,0:T(8,128)S(1)}, f32[160,128]{1,0:T(8,128)}, u32[]{:S(2)}) copy-start(f32[160,128]{1,0:T(8,128)} %constant.31.clone.weight_ref) | copy-start | bytes 245764
  11.9 5.8 %copy-start.6 = (f32[3,512]{1,0:T(4,128)S(1)}, f32[3,512]{1,0:T(4,128)}, u32[]{:S(2)}) copy-start(f32[3,512]{1,0:T(4,128)} %conv_ref.9) | copy-start | bytes 18436
  17.0 6.0 %copy-start = (bf16[512,2048]{1,0:T(8,128)(2,1)S(1)}, bf16[512,2048]{1,0:T(8,128)(2,1)}, u32[]{:S(2)}) copy-start(bf16[512,2048]{1,0:T(8,128)(2,1)} %w_ref.13) | copy-start | bytes 6291460
  21.5 7.4 %collective-permute-start.3 = (bf16[144,512]{1,0:T(8,128)(2,1)S(1)}, bf16[144,512]{1,0:T(8,128)(2,1)S(1)}, u32[]{:S(2)}, u32[]{:S(2)}) collective-permute-start(bf16[144,512]{1,0:T(8,128)(2,1)S(1)} %get-tuple-element.89), channel_id=1, source_target_pairs={{0,2},{2,4},{4,6},{6,8},{8,10},{10,12},{12,14},{14,16},{16,18},{18... | collective-permute-start | bytes 442376 | tf_op jit(solution)/shard_map/ppermute | solution.py:480
  23.6 9.1 %copy-start.2 = (bf16[128,1280]{1,0:T(8,128)(2,1)S(1)}, bf16[128,1280]{1,0:T(8,128)(2,1)}, u32[]{:S(2)}) copy-start(bf16[128,1280]{1,0:T(8,128)(2,1)} %constant.29.clone.turn_ref) | copy-start | bytes 983044
  50.4 37.3 %collective-permute-start.16 = (bf16[256,1024]{1,0:T(8,128)(2,1)S(1)}, bf16[256,1024]{1,0:T(8,128)(2,1)S(1)}, u32[]{:S(2)}, u32[]{:S(2)}) collective-permute-start(bf16[256,1024]{1,0:T(8,128)(2,1)S(1)} %shard_map.109), channel_id=1, source_target_pairs={{0,1},{1,0},{2,3},{3,2},{4,5},{5,4},{6,7},{7,6},{8,9},{9,8},{10,11... | collective-permute-start | bytes 1572872 | tf_op jit(solution)/shard_map/ppermute | solution.py:393
  52.5 15.8 %collective-permute-start = (bf16[128,1024]{1,0:T(8,128)(2,1)S(1)}, bf16[128,1024]{1,0:T(8,128)(2,1)S(1)}, u32[]{:S(2)}, u32[]{:S(2)}) collective-permute-start(bf16[128,1024]{1,0:T(8,128)(2,1)S(1)} %get-tuple-element.87.refs_0_), channel_id=1, source_target_pairs={{0,1},{1,0},{2,3},{3,2},{4,5},{5,4},{6,7},{7,6},{8,9},{9,8},{10,11... | collective-permute-start | bytes 786440 | tf_op jit(solution)/shard_map/ppermute | solution.py:393
  71.4 21.7 %copy-start.7 = (f32[512]{0:T(512)S(1)}, f32[512]{0:T(512)}, u32[]{:S(2)}) copy-start(f32[512]{0:T(512)} %param.12) | copy-start | bytes 6148
  71.4 1.9 %collective-permute-start.6 = (bf16[160,128]{1,0:T(8,128)(2,1)S(1)}, bf16[160,128]{1,0:T(8,128)(2,1)S(1)}, u32[]{:S(2)}, u32[]{:S(2)}) collective-permute-start(bf16[160,128]{1,0:T(8,128)(2,1)S(1)} %get-tuple-element.136), channel_id=1, source_target_pairs={{0,2},{2,0},{4,6},{6,4},{8,10},{10,8},{12,14},{14,12},{16,18},{18,... | collective-permute-start | bytes 122888 | tf_op jit(solution)/shard_map/ppermute | solution.py:300
  71.4 4.1 %collective-permute-start.7 = (bf16[160,128]{1,0:T(8,128)(2,1)S(1)}, bf16[160,128]{1,0:T(8,128)(2,1)S(1)}, u32[]{:S(2)}, u32[]{:S(2)}) collective-permute-start(bf16[160,128]{1,0:T(8,128)(2,1)S(1)} %get-tuple-element.137), channel_id=1, source_target_pairs={{0,4},{2,6},{4,0},{6,2},{8,12},{10,14},{12,8},{14,10},{16,20},{18,... | collective-permute-start | bytes 122888 | tf_op jit(solution)/shard_map/ppermute | solution.py:300
  72.9 3.5 %collective-permute-start.8 = (bf16[160,128]{1,0:T(8,128)(2,1)S(1)}, bf16[160,128]{1,0:T(8,128)(2,1)S(1)}, u32[]{:S(2)}, u32[]{:S(2)}) collective-permute-start(bf16[160,128]{1,0:T(8,128)(2,1)S(1)} %get-tuple-element.138), channel_id=1, source_target_pairs={{0,6},{2,4},{4,2},{6,0},{8,14},{10,12},{12,10},{14,8},{16,22},{18,... | collective-permute-start | bytes 122888 | tf_op jit(solution)/shard_map/ppermute | solution.py:300
  77.1 6.1 %collective-permute-start.9 = (bf16[160,128]{1,0:T(8,128)(2,1)S(1)}, bf16[160,128]{1,0:T(8,128)(2,1)S(1)}, u32[]{:S(2)}, u32[]{:S(2)}) collective-permute-start(bf16[160,128]{1,0:T(8,128)(2,1)S(1)} %get-tuple-element.143), channel_id=1, source_target_pairs={{0,8},{2,10},{4,12},{6,14},{8,0},{10,2},{12,4},{14,6},{16,24},{18,... | collective-permute-start | bytes 122888 | tf_op jit(solution)/shard_map/ppermute | solution.py:300
  78.7 5.7 %collective-permute-start.10 = (bf16[160,128]{1,0:T(8,128)(2,1)S(1)}, bf16[160,128]{1,0:T(8,128)(2,1)S(1)}, u32[]{:S(2)}, u32[]{:S(2)}) collective-permute-start(bf16[160,128]{1,0:T(8,128)(2,1)S(1)} %get-tuple-element.143), channel_id=1, source_target_pairs={{0,16},{2,18},{4,20},{6,22},{8,24},{10,26},{12,28},{14,30},{16,0},... | collective-permute-start | bytes 122888 | tf_op jit(solution)/shard_map/ppermute | solution.py:300
  81.3 5.8 %collective-permute-start.11 = (bf16[160,128]{1,0:T(8,128)(2,1)S(1)}, bf16[160,128]{1,0:T(8,128)(2,1)S(1)}, u32[]{:S(2)}, u32[]{:S(2)}) collective-permute-start(bf16[160,128]{1,0:T(8,128)(2,1)S(1)} %get-tuple-element.143), channel_id=1, source_target_pairs={{0,24},{2,26},{4,28},{6,30},{8,16},{10,18},{12,20},{14,22},{16,8},... | collective-permute-start | bytes 122888 | tf_op jit(solution)/shard_map/ppermute | solution.py:300
  87.7 18.3 %collective-permute-start.17 = (bf16[256,1024]{1,0:T(8,128)(2,1)S(1)}, bf16[256,1024]{1,0:T(8,128)(2,1)S(1)}, u32[]{:S(2)}, u32[]{:S(2)}) collective-permute-start(bf16[256,1024]{1,0:T(8,128)(2,1)S(1)} %collective-permute-done.16.refs_1_), channel_id=1, source_target_pairs={{0,2},{2,0},{4,6},{6,4},{8,10},{10,8},{12,14},{14,12},{16,18},{18,... | collective-permute-start | bytes 1572872 | tf_op jit(solution)/shard_map/ppermute | solution.py:300
  87.8 4.1 %collective-permute-start.12 = (bf16[160,128]{1,0:T(8,128)(2,1)S(1)}, bf16[160,128]{1,0:T(8,128)(2,1)S(1)}, u32[]{:S(2)}, u32[]{:S(2)}) collective-permute-start(bf16[160,128]{1,0:T(8,128)(2,1)S(1)} %get-tuple-element.145), channel_id=1, source_target_pairs={{0,2},{2,0},{4,6},{6,4},{8,10},{10,8},{12,14},{14,12},{16,18},{18,... | collective-permute-start | bytes 122888 | tf_op jit(solution)/shard_map/ppermute | solution.py:300
  88.3 4.2 %collective-permute-start.13 = (bf16[160,128]{1,0:T(8,128)(2,1)S(1)}, bf16[160,128]{1,0:T(8,128)(2,1)S(1)}, u32[]{:S(2)}, u32[]{:S(2)}) collective-permute-start(bf16[160,128]{1,0:T(8,128)(2,1)S(1)} %get-tuple-element.146), channel_id=1, source_target_pairs={{0,4},{2,6},{4,0},{6,2},{8,12},{10,14},{12,8},{14,10},{16,20},{18,... | collective-permute-start | bytes 122888 | tf_op jit(solution)/shard_map/ppermute | solution.py:300
  89.2 3.9 %collective-permute-start.14 = (bf16[160,128]{1,0:T(8,128)(2,1)S(1)}, bf16[160,128]{1,0:T(8,128)(2,1)S(1)}, u32[]{:S(2)}, u32[]{:S(2)}) collective-permute-start(bf16[160,128]{1,0:T(8,128)(2,1)S(1)} %get-tuple-element.147), channel_id=1, source_target_pairs={{0,6},{2,4},{4,2},{6,0},{8,14},{10,12},{12,10},{14,8},{16,22},{18,... | collective-permute-start | bytes 122888 | tf_op jit(solution)/shard_map/ppermute | solution.py:300
  94.6 9.9 %collective-permute-start.21 = (bf16[256,512]{1,0:T(8,128)(2,1)S(1)}, bf16[256,512]{1,0:T(8,128)(2,1)S(1)}, u32[]{:S(2)}, u32[]{:S(2)}) collective-permute-start(bf16[256,512]{1,0:T(8,128)(2,1)S(1)} %shard_map.104.own_ref), channel_id=1, source_target_pairs={{0,1},{1,0},{2,3},{3,2},{4,5},{5,4},{6,7},{7,6},{8,9},{9,8},{10,11... | collective-permute-start | bytes 786440 | tf_op jit(solution)/shard_map/ppermute | solution.py:393
  97.7 11.7 %collective-permute-start.20 = (bf16[256,512]{1,0:T(8,128)(2,1)S(1)}, bf16[256,512]{1,0:T(8,128)(2,1)S(1)}, u32[]{:S(2)}, u32[]{:S(2)}) collective-permute-start(bf16[256,512]{1,0:T(8,128)(2,1)S(1)} %shard_map.105.own_ref), channel_id=1, source_target_pairs={{0,1},{1,0},{2,3},{3,2},{4,5},{5,4},{6,7},{7,6},{8,9},{9,8},{10,11... | collective-permute-start | bytes 786440 | tf_op jit(solution)/shard_map/ppermute | solution.py:393
  99.8 15.2 %collective-permute-start.19 = (bf16[256,512]{1,0:T(8,128)(2,1)S(1)}, bf16[256,512]{1,0:T(8,128)(2,1)S(1)}, u32[]{:S(2)}, u32[]{:S(2)}) collective-permute-start(bf16[256,512]{1,0:T(8,128)(2,1)S(1)} %shard_map.106.own_ref), channel_id=1, source_target_pairs={{0,1},{1,0},{2,3},{3,2},{4,5},{5,4},{6,7},{7,6},{8,9},{9,8},{10,11... | collective-permute-start | bytes 786440 | tf_op jit(solution)/shard_map/ppermute | solution.py:393
  102.6 15.2 %collective-permute-start.18 = (bf16[128,512]{1,0:T(8,128)(2,1)S(1)}, bf16[128,512]{1,0:T(8,128)(2,1)S(1)}, u32[]{:S(2)}, u32[]{:S(2)}) collective-permute-start(bf16[128,512]{1,0:T(8,128)(2,1)S(1)} %shard_map.107.own_ref), channel_id=1, source_target_pairs={{0,1},{1,0},{2,3},{3,2},{4,5},{5,4},{6,7},{7,6},{8,9},{9,8},{10,11... | collective-permute-start | bytes 393224 | tf_op jit(solution)/shard_map/ppermute | solution.py:393
  104.4 15.4 %collective-permute-start.15 = (bf16[128,512]{1,0:T(8,128)(2,1)S(1)}, bf16[128,512]{1,0:T(8,128)(2,1)S(1)}, u32[]{:S(2)}, u32[]{:S(2)}) collective-permute-start(bf16[128,512]{1,0:T(8,128)(2,1)S(1)} %shard_map.108.own_ref), channel_id=1, source_target_pairs={{0,1},{1,0},{2,3},{3,2},{4,5},{5,4},{6,7},{7,6},{8,9},{9,8},{10,11... | collective-permute-start | bytes 393224 | tf_op jit(solution)/shard_map/ppermute | solution.py:393

commit v5 on v4

--- a/solution.py
+++ b/solution.py
@@ -22,12 +22,12 @@
 BF16 = jnp.bfloat16
 
 
-def call(body, out_shape, *, vmem, **kwargs):
+def call(body, out_shape, *, vmem, flops=1, **kwargs):
     return pl.pallas_call(
         body,
         out_shape=out_shape,
         compiler_params=pltpu.CompilerParams(vmem_limit_bytes=vmem),
-        cost_estimate=pl.CostEstimate(flops=1, bytes_accessed=1, transcendentals=0),
+        cost_estimate=pl.CostEstimate(flops=flops, bytes_accessed=1, transcendentals=0),
         **kwargs,
     )
 
@@ -87,43 +87,54 @@
         at += padded
 
 
+def project(me, xs, w_ref, begin, width, skip):
+    depth = xs[0].shape[1]
+    total = None
+    for r, x_ref in enumerate(xs):
+        src = lax.rem(me - r + len(xs), len(xs))
+        from_rows = pl.ds(pl.multiple_of(src * depth, depth), depth)
+        part = jnp.dot(x_ref[skip:, :], w_ref[from_rows, begin : begin + width], preferred_element_type=F32)
+        total = part if total is None else total + part
+    return total.astype(BF16)
+
+
+def normalize(got, ref, mean_ref, scale):
+    for p in range(ref.shape[1] // LANES):
+        cols = slice(p * LANES, (p + 1) * LANES)
+        x = got[:, cols].astype(F32)
+        x = x * lax.rsqrt(head_mean(x * x, mean_ref[...]) + 1e-6)
+        ref[:, cols] = x.astype(BF16) * jnp.asarray(scale, BF16)
+
+
 def block_kernel(j_ref, mean_ref, conv_ref, turn_ref, weight_ref, w_ref, *refs, n, heads, extra, others, sends):
     xs, refs = refs[:n], refs[n:]
     prev_ref = None
     if not extra:
         prev_ref, refs = refs[0], refs[1:]
     other_refs, refs = refs[:others], refs[others:]
-    q_ref, k_ref, v_ref, wq_ref, wk_ref, halo_ref, s_ref = refs[:7]
-    send_refs, (ext_ref,) = refs[7 : 7 + sends], refs[7 + sends :]
-    rows, depth = v_ref.shape[0], xs[0].shape[1]
+    k_ref, v_ref, s_ref, refs = *refs[:3], refs[3:]
+    send_refs, ext_ref = refs[:sends], refs[-1]
+    q_ref, wq_ref, wk_ref, halo_ref = (None,) * 4 if others else refs[:4]
+    rows = v_ref.shape[0]
+    qk_width, width = k_ref.shape[1], v_ref.shape[1]
     me = j_ref[0]
 
-    def project(begin, width, skip):
-        total = None
-        for r in range(n):
-            src = lax.rem(me - r + n, n)
-            from_rows = pl.ds(pl.multiple_of(src * depth, depth), depth)
-            part = jnp.dot(xs[r][skip:, :], w_ref[from_rows, begin : begin + width], preferred_element_type=F32)
-            total = part if total is None else total + part
-        return total.astype(BF16)
-
-    widths = [ref.shape[1] for ref in (q_ref, k_ref, v_ref, wq_ref, wk_ref)]
-    starts = [sum(widths[:i]) for i in range(5)]
-    qk = project(starts[0], widths[0] + widths[1], extra)
-    q_ref[...] = qk[:, : widths[0]]
-    k_ref[...] = qk[:, widths[0] :]
-    raw = project(starts[2], widths[2], 0)
+    if others:
+        k_ref[...] = project(me, xs, w_ref, qk_width, qk_width, extra)
+    else:
+        qk = project(me, xs, w_ref, 0, 2 * qk_width, extra)
+        q_ref[...] = qk[:, :qk_width]
+        k_ref[...] = qk[:, qk_width:]
+    raw = project(me, xs, w_ref, 2 * qk_width, width, 0)
     if extra:
         ext_ref[...] = raw.astype(F32)
     else:
         ext_ref[0:EDGE, :] = prev_ref[0:EDGE, :].astype(F32)
         ext_ref[EDGE:, :] = raw.astype(F32)
-    halo_ref[0:EDGE, :] = raw[raw.shape[0] - EDGE :]
-    total = jnp.zeros((rows, widths[2]), F32)
+    total = jnp.zeros((rows, width), F32)
     for tap in range(CONV):
         total = total + conv_ref[tap : tap + 1, :] * ext_ref[EDGE - tap : EDGE - tap + rows, :]
     v_ref[...] = total.astype(BF16)
-    halo_ref[EDGE : EDGE + WIN, :] = v_ref[rows - WIN : rows, :]
 
     in_group, lanes, slots = feature_layout(heads)
     groups = heads // in_group
@@ -154,17 +165,25 @@
             total = total + ref[pair]
         send_refs[r][...] = total.astype(BF16)
 
-    for ref, start, width, scale in (
-        (wk_ref, starts[4], widths[4], 1.0),
-        (wq_ref, starts[3], widths[3], 1.0 / DV**0.5),
-    ):
-        got = project(start, width, extra)
-        for p in range(width // LANES):
-            cols = slice(p * LANES, (p + 1) * LANES)
-            x = got[:, cols].astype(F32)
-            x = x * lax.rsqrt(head_mean(x * x, mean_ref[...]) + 1e-6)
-            ref[:, cols] = x.astype(BF16) * jnp.asarray(scale, BF16)
+    if not others:
+        halo_ref[0:EDGE, :] = raw[raw.shape[0] - EDGE :]
+        query_part(me, xs, w_ref, mean_ref, v_ref, wq_ref, wk_ref, halo_ref, 2 * qk_width + width, extra)
+
+
+def query_part(me, xs, w_ref, mean_ref, v_ref, wq_ref, wk_ref, halo_ref, begin, skip):
+    rows, width = v_ref.shape
+    normalize(project(me, xs, w_ref, begin, width, skip), wq_ref, mean_ref, 1.0 / DV**0.5)
+    normalize(project(me, xs, w_ref, begin + width, width, skip), wk_ref, mean_ref, 1.0)
+    halo_ref[EDGE : EDGE + WIN, :] = v_ref[rows - WIN : rows, :]
     halo_ref[EDGE + WIN : HALO, :] = wk_ref[rows - WIN : rows, :]
+
+
+def query_kernel(j_ref, mean_ref, w_ref, v_ref, *refs, n):
+    xs, (q_ref, wq_ref, wk_ref, halo_ref) = refs[:n], refs[n:]
+    qk_width, width = q_ref.shape[1], v_ref.shape[1]
+    q_ref[...] = project(j_ref[0], xs, w_ref, 0, qk_width, 0)
+    halo_ref[0:EDGE, :] = jnp.zeros((EDGE, width), BF16)
+    query_part(j_ref[0], xs, w_ref, mean_ref, v_ref, wq_ref, wk_ref, halo_ref, 2 * qk_width + width, 0)
 
 
 def attend_kernel(
@@ -328,13 +347,12 @@
     return lax.optimization_barrier((value, earlier))[0]
 
 
-def prior_in_planes(own, places, beside):
+def prior_in_planes(held, places, beside):
     ctx = lax.axis_size("ctx")
     whole = pl.BlockSpec(memory_space=pltpu.VMEM)
     scalar = pl.BlockSpec(memory_space=pltpu.SMEM)
     narrow = jax.ShapeDtypeStruct((FEATS, LANES), BF16)
     wide = jax.ShapeDtypeStruct((FEATS, LANES), F32)
-    held = [own[0]] + [exchange(own[r], "ctx", r) for r in range(1, PLANE)]
     plane, *ahead = call(
         plane_kernel,
         [narrow] + [wide] * PLANE,
@@ -352,7 +370,7 @@
         out_specs=[whole] * PLANE,
         vmem=4 << 20,
     )(after(places, beside[1]), *ahead, *earlier)
-    return back[0], [back[0]] + [exchange(back[r], "ctx", r) for r in range(1, PLANE)]
+    return [back[0]] + [exchange(back[r], "ctx", r) for r in range(1, PLANE)]
 
 
 def prior_by_doubling(total, position):
@@ -439,15 +457,19 @@
         vmem=32 << 20,
     )(proj_weight)
 
+    def bf16(rows, *widths):
+        return [jax.ShapeDtypeStruct((rows, w), BF16) for w in widths]
+
     def do_block(b, prev, behind, others=()):
         rows = blocks[b][1]
         extra = EDGE if prev is None else 0
         sends = PLANE if in_planes and others else 0
         tokens = places if behind is None else after(places, behind)
-        shapes = [jax.ShapeDtypeStruct((rows, w), BF16) for w in (qk_width, qk_width, width, width, width)]
-        shapes.append(jax.ShapeDtypeStruct((HALO, width), BF16))
-        shapes.append(jax.ShapeDtypeStruct((pairs, FEATS, LANES), F32))
-        shapes += [jax.ShapeDtypeStruct((FEATS, LANES), BF16)] * sends
+        shapes = bf16(rows, qk_width, width) + [jax.ShapeDtypeStruct((pairs, FEATS, LANES), F32)]
+        if others:
+            shapes += bf16(FEATS, LANES) * sends
+        else:
+            shapes += bf16(rows, qk_width, width, width) + bf16(HALO, width)
         operands = [tokens, means, conv_weight, turn_rows, weight, arranged, *pieces[b]]
         if prev is not None:
             operands.append(prev)
@@ -463,43 +485,53 @@
             vmem=32 << 20,
         )(*operands)
 
+    def do_queries(b, v):
+        rows = blocks[b][1]
+        return call(
+            functools.partial(query_kernel, n=n),
+            bf16(rows, qk_width, width, width) + bf16(HALO, width),
+            in_specs=[scalar] + [whole] * (3 + n),
+            out_specs=[whole] * 4,
+            vmem=32 << 20,
+        )(places, means, arranged, v, *pieces[b])
+
     def attend(b, prev):
         rows = blocks[b][1]
-        q, k, v, wq, wk = done[b][:5]
+        k, v, _, q, wq, wk, _ = done[b]
         return call(
             functools.partial(attend_kernel, heads=heads, first=b == 0),
             [jax.ShapeDtypeStruct((rows, turn.shape[1]), BF16)] + [jax.ShapeDtypeStruct((rows, width), F32)] * 2,
             in_specs=[scalar] + [whole] * 7,
             out_specs=[whole] * 3,
             scratch_shapes=[pltpu.VMEM((WIN + rows, width), BF16)] * 2,
+            flops=20 * 10**9 if b == last else 1,
             vmem=16 << 20,
         )(places, turn, prev, q, k, v, wq, wk)
 
     done, attended = {}, {}
     done[last] = do_block(last, None, None)
-    halo = lax.ppermute(done[last][5], "ctx", [(i, i + 1) for i in range(ctx - 1)])
-    for b in range(last):
-        prev = halo if b == 0 else done[b - 1][5]
-        others = [done[c][6] for c in [last] + list(range(b))] if b == last - 1 else ()
-        done[b] = do_block(b, prev, attended[b - 1][1] if b - 1 in attended else None, others)
-        if b < last - 2:
-            attended[b] = attend(b, prev)
-
-    for b in range(last - 2, last + 1):
-        attended[b] = attend(b, done[b - 1][5])
-    fetched = [from_head(after(block, attended[last - 2][1]), r) for r, block in enumerate(picked, 1)]
+    halo = lax.ppermute(done[last][6], "ctx", [(i, i + 1) for i in range(ctx - 1)])
+    prevs = {0: halo}
+    for b in range(last - 1):
+        done[b] = do_block(b, prevs[b], attended[b - 1][1] if b else None)
+        prevs[b + 1] = done[b][6]
+        attended[b] = attend(b, prevs[b])
+    b = last - 1
+    k, v, state, *sends = do_block(b, prevs[b], attended[b - 1][1], [done[c][2] for c in (last, *range(b))])
+    done[b] = (k, v, state, *do_queries(b, v))
+    prevs[last] = done[b][6]
+    for b in (last - 1, last):
+        attended[b] = attend(b, prevs[b])
+    held = sends[:1] + [exchange(sends[r], "ctx", r) for r in range(1, len(sends))]
+    mark = attended[last - 1][1]
+    fetched = [from_head(after(block, mark), r) for r, block in enumerate(picked, 1)]
     if in_planes:
-        beside = [attended[b][1] for b in (last - 2, last - 1)]
-        mark, priors = prior_in_planes(done[last - 1][7:], places, beside)
+        priors = prior_in_planes(held, places, [done[last - 1][6], attended[last - 1][1]])
     else:
-        mark = sum(done[b][6] for b in range(last + 1))
-        priors = prior_by_doubling(mark, position)
-
+        priors = prior_by_doubling(sum(done[b][2] for b in range(last + 1)), position)
+
+    result = None
     out_rows = []
-    for got in fetched:
-        out_rows += [got] + ([exchange(after(got, mark), "ctx", 1)] if out_parts > 1 else [])
-
-    result = None
     mixed = attended[last][1]
     for b in (0, 1, 4, 2, 3):
         at, rows = blocks[b]
@@ -510,8 +542,11 @@
             out_specs=whole,
             scratch_shapes=[pltpu.VMEM((pairs, FEATS, LANES), F32)],
             vmem=16 << 20,
-        )(after(places, mixed), means, gain, *priors, *[done[c][6] for c in range(b)], *attended[b])
+        )(after(places, mixed), means, gain, *priors, *[done[c][2] for c in range(b)], *attended[b])
         others = [from_head(mixed, r) for r in range(1, n)]
+        if not out_rows:
+            for got in fetched:
+                out_rows += [got] + ([exchange(after(got, mixed), "ctx", 1)] if out_parts > 1 else [])
         operands = [places, mixed, out_weight] + others + out_rows
         specs = [scalar] + [whole] * (len(operands) - 1)
         aliases = {}

time: 122 us -> 106 us (0.87)
  waiting for transfers between devices: 41 us -> 23.4 us
  starting transfers between devices: 23.2 us -> 24.8 us
    ppermute x11, waiting for transfers between devices: 32.8 us -> 20.7 us  [from_head(): return lax.ppermute(value, 'head', [(i, (i + by) % n) for i in range(n)])]
    ppermute x10, waiting for transfers between devices: 8.19 us -> 2.77 us  [exchange(): return lax.ppermute(value, axis, [(i, i ^ flip) for i in range(count)])]
    pallas_call x0 -> x1, Pallas kernels: none -> 1.76 us  [do_queries(): call(functools.partial(query_kernel, n=n), bf16(rows, qk_width, width, wi...]
    ppermute x11, starting transfers between devices: 13.4 us -> 14.6 us  [from_head(): return lax.ppermute(value, 'head', [(i, (i + by) % n) for i in range(n)])]
  transfers between devices with their start and end apart: 22 -> 22, of which waited for: 14 -> 13; matrix products, arithmetic and copies ran while one was open for 2% -> 2% of each run, Pallas kernels for 36% -> 44%
where the time goes in v5:
time: 106 us
  Pallas kernels  51 us (48%)
  starting transfers between devices  24.8 us (23%)
  waiting for transfers between devices  23.4 us (22%)
  local copies, waits for them, and re-layouts  6.53 us (6%)
    ppermute x11, waiting for transfers between devices, from_head(): return lax.ppermute(value, 'head', [(i, (i + by) % n) for i in range(n)])  20.7 us
    pallas_call x5, Pallas kernels, do_block(): call(functools.partial(block_kernel, n=n, heads=heads, extra=extra, other...  15.9 us
    ppermute x11, starting transfers between devices, from_head(): return lax.ppermute(value, 'head', [(i, (i + by) % n) for i in range(n)])  14.6 us
    pallas_call x5, Pallas kernels, attend(): call(functools.partial(attend_kernel, heads=heads, first=b == 0), [jax.Sh...  9.73 us
    pallas_call x5, Pallas kernels, per_device(): call(functools.partial(output_kernel, n=n, offset=at, parts=out_parts), j...  9.62 us
    ppermute x10, starting transfers between devices, exchange(): return lax.ppermute(value, axis, [(i, i ^ flip) for i in range(count)])  8.5 us
    pallas_call x5, Pallas kernels, per_device(): call(functools.partial(finish_kernel, heads=heads, before=b), jax.ShapeDt...  7.04 us
    pallas_call x1, Pallas kernels, per_device(): call(functools.partial(arrange_kernel, heads=heads), jax.ShapeDtypeStruct...  5.09 us
  transfers between devices with their start and end apart: 22, of which 13 were waited for; matrix products, arithmetic and copies ran while one was open for 2% of the time, Pallas kernels for 44%

profile of v5, /device:TPU:0, one launch (start us, length us, event | category | flops | bytes accessed | tf_op | source)
XLA Modules:
  0.0 106.2 jit_solution(516827194474295157)
XLA Ops:
  1.2 3.0 %collective-permute-start = (bf16[272,1024]{1,0:T(8,128)(2,1)S(1)}, bf16[272,1024]{1,0:T(8,128)(2,1)S(1)}, u32[]{:S(2)}, u32[]{:S(2)}) collective-permute-start(bf16[272,1024]{1,0:T(8,128)(2,1)S(1)} %slice.15.refs_0_), channel_id=1, source_target_pairs={{0,1},{1,0},{2,3},{3,2},{4,5},{5,4},{6,7},{7,6},{8,9},{9,8},{10,11... | collective-permute-start | bytes 1671176 | tf_op jit(solution)/shard_map/ppermute | solution.py:411
  5.6 2.0 %collective-permute-start.3 = (bf16[256,1024]{1,0:T(8,128)(2,1)S(1)}, bf16[256,1024]{1,0:T(8,128)(2,1)S(1)}, u32[]{:S(2)}, u32[]{:S(2)}) collective-permute-start(bf16[256,1024]{1,0:T(8,128)(2,1)S(1)} %get-tuple-element.97.refs_0_), channel_id=1, source_target_pairs={{0,1},{1,0},{2,3},{3,2},{4,5},{5,4},{6,7},{7,6},{8,9},{9,8},{10,11... | collective-permute-start | bytes 1572872 | tf_op jit(solution)/shard_map/ppermute | solution.py:411
  8.8 1.9 %collective-permute-start.5 = (bf16[128,1024]{1,0:T(8,128)(2,1)S(1)}, bf16[128,1024]{1,0:T(8,128)(2,1)S(1)}, u32[]{:S(2)}, u32[]{:S(2)}) collective-permute-start(bf16[128,1024]{1,0:T(8,128)(2,1)S(1)} %get-tuple-element.115.refs_0_), channel_id=1, source_target_pairs={{0,1},{1,0},{2,3},{3,2},{4,5},{5,4},{6,7},{7,6},{8,9},{9,8},{10,11... | collective-permute-start | bytes 786440 | tf_op jit(solution)/shard_map/ppermute | solution.py:411
  10.7 3.1 %copy-done.3 = bf16[2048,1792]{1,0:T(8,128)(2,1)S(1)} copy-done((bf16[2048,1792]{1,0:T(8,128)(2,1)S(1)}, bf16[2048,1792]{1,0:T(8,128)(2,1)}, u32[]{:S(2)}) %copy-start.3) | copy-done | bytes 7340056
  13.8 5.1 %shard_map.91.w_ref = bf16[2048,1792]{1,0:T(8,128)(2,1)S(1)} custom-call(bf16[2048,1792]{1,0:T(8,128)(2,1)S(1)} %copy-done.3), custom_call_target="tpu_custom_call" | custom-call | flops 1 | bytes 1 | tf_op jit(solution)/shard_map/pallas_call | solution.py:451
  19.0 3.9 %shard_map.92 = (bf16[256,128]{1,0:T(8,128)(2,1)S(1)}, bf16[256,512]{1,0:T(8,128)(2,1)S(1)}, f32[4,160,128]{2,1,0:T(8,128)S(1)}, bf16[256,128]{1,0:T(8,128)(2,1)...) custom-call(s32[3]{0:T(128)S(1)} %pad_add_fusion.j_ref.a_ref, ...), custom_call_target="tpu_custom_call" | custom-call | flops 1 | bytes 1 | tf_op jit(solution)/shard_map/pallas_call | solution.py:477
  22.8 1.6 %collective-permute-start.1 = (bf16[144,512]{1,0:T(8,128)(2,1)S(1)}, bf16[144,512]{1,0:T(8,128)(2,1)S(1)}, u32[]{:S(2)}, u32[]{:S(2)}) collective-permute-start(bf16[144,512]{1,0:T(8,128)(2,1)S(1)} %get-tuple-element.88), channel_id=1, source_target_pairs={{0,2},{2,4},{4,6},{6,8},{8,10},{10,12},{12,14},{14,16},{16,18},{18... | collective-permute-start | bytes 442376 | tf_op jit(solution)/shard_map/ppermute | solution.py:513
  24.4 4.4 %collective-permute-done.2.refs_1_ = bf16[256,1024]{1,0:T(8,128)(2,1)S(1)} collective-permute-done((bf16[256,1024]{1,0:T(8,128)(2,1)S(1)}, bf16[256,1024]{1,0:T(8,128)(2,1)S(1)}, u32[]{:S(2)}, u32[]{:S(2)}) %collective-permute-start.2) | collective-permute-done | bytes 524320 | tf_op jit(solution)/shard_map/ppermute | solution.py:411
  28.9 3.8 %shard_map.93 = (bf16[256,128]{1,0:T(8,128)(2,1)S(1)}, bf16[256,512]{1,0:T(8,128)(2,1)S(1)}, f32[4,160,128]{2,1,0:T(8,128)S(1)}, bf16[256,128]{1,0:T(8,128)(2,1)...) custom-call(s32[3]{0:T(128)S(1)} %pad_add_fusion.j_ref.a_ref, ...), custom_call_target="tpu_custom_call" | custom-call | flops 1 | bytes 1 | tf_op jit(solution)/shard_map/pallas_call | solution.py:477
  32.7 2.1 %shard_map.94 = (bf16[256,1280]{1,0:T(8,128)(2,1)S(1)}, f32[256,512]{1,0:T(8,128)S(1)}, f32[256,512]{1,0:T(8,128)S(1)}) custom-call(s32[3]{0:T(128)S(1)} %pad_add_fusion.j_ref.a_ref, bf16[128,1280]{1,0:T(8,128)(2,1)S(1)} %copy-done.4, bf16[144,512]{1,0:T(8,128)(2,1)S(1)} %collective-permute-done.1.refs_2_.prev_ref, ...), custom_call_target="tpu_custom_call" | custom-call | flops 1 | bytes 1 | tf_op jit(solution)/shard_map/pallas_call | solution.py:501
  34.9 5.2 %collective-permute-done.3.refs_1_ = bf16[256,1024]{1,0:T(8,128)(2,1)S(1)} collective-permute-done((bf16[256,1024]{1,0:T(8,128)(2,1)S(1)}, bf16[256,1024]{1,0:T(8,128)(2,1)S(1)}, u32[]{:S(2)}, u32[]{:S(2)}) %collective-permute-start.3) | collective-permute-done | bytes 524320 | tf_op jit(solution)/shard_map/ppermute | solution.py:411
  40.1 3.8 %shard_map.95 = (bf16[256,128]{1,0:T(8,128)(2,1)S(1)}, bf16[256,512]{1,0:T(8,128)(2,1)S(1)}, f32[4,160,128]{2,1,0:T(8,128)S(1)}, bf16[256,128]{1,0:T(8,128)(2,1)...) custom-call(s32[3]{0:T(128)S(1)} %pad_add_fusion.j_ref.a_ref, ...), custom_call_target="tpu_custom_call" | custom-call | flops 1 | bytes 1 | tf_op jit(solution)/shard_map/pallas_call | solution.py:477
  44.0 2.1 %shard_map.96 = (bf16[256,1280]{1,0:T(8,128)(2,1)S(1)}, f32[256,512]{1,0:T(8,128)S(1)}, f32[256,512]{1,0:T(8,128)S(1)}) custom-call(s32[3]{0:T(128)S(1)} %pad_add_fusion.j_ref.a_ref, bf16[128,1280]{1,0:T(8,128)(2,1)S(1)} %copy-done.4, bf16[144,512]{1,0:T(8,128)(2,1)S(1)} %get-tuple-element.98.refs_2_.prev_ref, ...), custom_call_target="tpu_custom_call" | custom-call | flops 1 | bytes 1 | tf_op jit(solution)/shard_map/pallas_call | solution.py:501
  46.1 2.6 %shard_map.97 = (bf16[128,128]{1,0:T(8,128)(2,1)S(1)}, bf16[128,512]{1,0:T(8,128)(2,1)S(1)}, f32[4,160,128]{2,1,0:T(8,128)S(1)}, bf16[128,128]{1,0:T(8,128)(2,1)...) custom-call(s32[3]{0:T(128)S(1)} %pad_add_fusion.j_ref.a_ref, ...), custom_call_target="tpu_custom_call" | custom-call | flops 1 | bytes 1 | tf_op jit(solution)/shard_map/pallas_call | solution.py:477
  48.7 1.7 %shard_map.98 = (bf16[128,1280]{1,0:T(8,128)(2,1)S(1)}, f32[128,512]{1,0:T(8,128)S(1)}, f32[128,512]{1,0:T(8,128)S(1)}) custom-call(s32[3]{0:T(128)S(1)} %pad_add_fusion.j_ref.a_ref, bf16[128,1280]{1,0:T(8,128)(2,1)S(1)} %copy-done.4, bf16[144,512]{1,0:T(8,128)(2,1)S(1)} %get-tuple-element.99.refs_2_.prev_ref, ...), custom_call_target="tpu_custom_call" | custom-call | flops 1 | bytes 1 | tf_op jit(solution)/shard_map/pallas_call | solution.py:501
  50.5 1.8 %shard_map.99 = (bf16[128,128]{1,0:T(8,128)(2,1)S(1)}, bf16[128,512]{1,0:T(8,128)(2,1)S(1)}, f32[4,160,128]{2,1,0:T(8,128)S(1)}, bf16[160,128]{1,0:T(8,128)(2,1)...) custom-call(s32[3]{0:T(128)S(1)} %pad_add_fusion.j_ref.a_ref, ...), custom_call_target="tpu_custom_call" | custom-call | flops 1 | bytes 1 | tf_op jit(solution)/shard_map/pallas_call | solution.py:477
  52.6 2.0 %collective-permute-start.7 = (bf16[160,128]{1,0:T(8,128)(2,1)S(1)}, bf16[160,128]{1,0:T(8,128)(2,1)S(1)}, u32[]{:S(2)}, u32[]{:S(2)}) collective-permute-start(bf16[160,128]{1,0:T(8,128)(2,1)S(1)} %get-tuple-element.139), channel_id=1, source_target_pairs={{0,4},{2,6},{4,0},{6,2},{8,12},{10,14},{12,8},{14,10},{16,20},{18,... | collective-permute-start | bytes 122888 | tf_op jit(solution)/shard_map/ppermute | solution.py:319
  54.7 1.8 %shard_map.100 = (bf16[128,128]{1,0:T(8,128)(2,1)S(1)}, bf16[128,512]{1,0:T(8,128)(2,1)S(1)}, bf16[128,512]{1,0:T(8,128)(2,1)S(1)}, bf16[144,512]{1,0:T(8,128)(2,1)S(1)}) custom-call(s32[3]{0:T(128)S(1)} %pad_add_fusion.j_ref.a_ref, bf16[256,128]{1,0:T(8,128)(2,1)S(1)} %copy-done.2, bf16[2048,1792]{1,0:T(8,128)(2,1)S(1)} %shard_map.91.w_ref, ...), custom_call_target="tpu_custom_call" | custom-call | flops 1 | bytes 1 | tf_op jit(solution)/shard_map/pallas_call | solution.py:490
  58.8 2.7 %collective-permute-start.10 = (bf16[160,128]{1,0:T(8,128)(2,1)S(1)}, bf16[160,128]{1,0:T(8,128)(2,1)S(1)}, u32[]{:S(2)}, u32[]{:S(2)}) collective-permute-start(bf16[160,128]{1,0:T(8,128)(2,1)S(1)} %get-tuple-element.145), channel_id=1, source_target_pairs={{0,16},{2,18},{4,20},{6,22},{8,24},{10,26},{12,28},{14,30},{16,0},... | collective-permute-start | bytes 122888 | tf_op jit(solution)/shard_map/ppermute | solution.py:319
  63.6 1.7 %shard_map.102 = (bf16[128,1280]{1,0:T(8,128)(2,1)S(1)}, f32[128,512]{1,0:T(8,128)S(1)}, f32[128,512]{1,0:T(8,128)S(1)}) custom-call(s32[3]{0:T(128)S(1)} %pad_add_fusion.j_ref.a_ref, bf16[128,1280]{1,0:T(8,128)(2,1)S(1)} %copy-done.4, bf16[144,512]{1,0:T(8,128)(2,1)S(1)} %get-tuple-element.116.refs_2_.prev_ref, ...), custom_call_target="tpu_custom_call" | custom-call | flops 1 | bytes 1 | tf_op jit(solution)/shard_map/pallas_call | solution.py:501
  65.3 1.6 %collective-permute-start.16 = (bf16[256,1024]{1,0:T(8,128)(2,1)S(1)}, bf16[256,1024]{1,0:T(8,128)(2,1)S(1)}, u32[]{:S(2)}, u32[]{:S(2)}) collective-permute-start(bf16[256,1024]{1,0:T(8,128)(2,1)S(1)} %shard_map.110), channel_id=1, source_target_pairs={{0,1},{1,0},{2,3},{3,2},{4,5},{5,4},{6,7},{7,6},{8,9},{9,8},{10,11... | collective-permute-start | bytes 1572872 | tf_op jit(solution)/shard_map/ppermute | solution.py:411
  69.8 2.1 %shard_map.101 = (bf16[256,1280]{1,0:T(8,128)(2,1)S(1)}, f32[256,512]{1,0:T(8,128)S(1)}, f32[256,512]{1,0:T(8,128)S(1)}) custom-call(s32[3]{0:T(128)S(1)} %pad_add_fusion.j_ref.a_ref, bf16[128,1280]{1,0:T(8,128)(2,1)S(1)} %copy-done.4, bf16[144,512]{1,0:T(8,128)(2,1)S(1)} %get-tuple-element.122.prev_ref, bf16[256,128]{1,0:T(8,128)(2,1)S(1)} %get-tuple-element.123.q_ref, ...), custom_call_target="tpu_custom_call" | custom-call | flops 20000000000 | bytes 1 | tf_op jit(solution)/shard_map/pallas_call | solution.py:501
  74.1 4.6 %collective-permute-done.16.refs_1_ = bf16[256,1024]{1,0:T(8,128)(2,1)S(1)} collective-permute-done((bf16[256,1024]{1,0:T(8,128)(2,1)S(1)}, bf16[256,1024]{1,0:T(8,128)(2,1)S(1)}, u32[]{:S(2)}, u32[]{:S(2)}) %collective-permute-start.16) | collective-permute-done | bytes 524320 | tf_op jit(solution)/shard_map/ppermute | solution.py:411
  82.4 1.5 %shard_map.107.own_ref = bf16[256,512]{1,0:T(8,128)(2,1)S(1)} custom-call(s32[3]{0:T(128)S(1)} %pad_add_fusion.j_ref.a_ref, bf16[256,128]{1,0:T(8,128)(2,1)S(1)} %copy-done.2, f32[1,512]{1,0:T(1,128)S(1)} %bitcast.6, bf16[160,128]{1,0:T(8,128)(2,1)S(1)} %get-tuple-element.146.refs_0_, bf16[160,128]{1,0:T(8,128)(2,1)S(1)} %collective-permute-done.12.refs_1_, ...), custom_call_target="tpu_custom_call" | custom-call | flops 1 | bytes 1 | tf_op jit(solution)/shard_map/pallas_call | solution.py:538
  83.9 1.6 %collective-permute-start.19 = (bf16[256,512]{1,0:T(8,128)(2,1)S(1)}, bf16[256,512]{1,0:T(8,128)(2,1)S(1)}, u32[]{:S(2)}, u32[]{:S(2)}) collective-permute-start(bf16[256,512]{1,0:T(8,128)(2,1)S(1)} %shard_map.107.own_ref), channel_id=1, source_target_pairs={{0,1},{1,0},{2,3},{3,2},{4,5},{5,4},{6,7},{7,6},{8,9},{9,8},{10,11... | collective-permute-start | bytes 786440 | tf_op jit(solution)/shard_map/ppermute | solution.py:411
  88.6 1.6 %collective-permute-start.15 = (bf16[128,512]{1,0:T(8,128)(2,1)S(1)}, bf16[128,512]{1,0:T(8,128)(2,1)S(1)}, u32[]{:S(2)}, u32[]{:S(2)}) collective-permute-start(bf16[128,512]{1,0:T(8,128)(2,1)S(1)} %shard_map.109.own_ref), channel_id=1, source_target_pairs={{0,1},{1,0},{2,3},{3,2},{4,5},{5,4},{6,7},{7,6},{8,9},{9,8},{10,11... | collective-permute-start | bytes 393224 | tf_op jit(solution)/shard_map/ppermute | solution.py:411
  90.2 2.1 %shard_map.111.refs_3_ = bf16[1024,1024]{1,0:T(8,128)(2,1)} custom-call(s32[3]{0:T(128)S(1)} %pad_add_fusion.j_ref.a_ref, bf16[256,512]{1,0:T(8,128)(2,1)S(1)} %shard_map.105.own_ref, bf16[512,2048]{1,0:T(8,128)(2,1)S(1)} %copy-done, bf16[256,512]{1,0:T(8,128)(2,1)S(1)} %collective-permute-done.21.refs_0_, ...), custom_call_target="tpu_custom_call" | custom-call | flops 1 | bytes 1 | tf_op jit(solution)/shard_map/pallas_call | solution.py:557
  93.5 2.1 %shard_map.112.refs_3_ = bf16[1024,1024]{1,0:T(8,128)(2,1)} custom-call(s32[3]{0:T(128)S(1)} %pad_add_fusion.j_ref.a_ref, bf16[256,512]{1,0:T(8,128)(2,1)S(1)} %shard_map.106.own_ref, bf16[512,2048]{1,0:T(8,128)(2,1)S(1)} %copy-done, bf16[256,512]{1,0:T(8,128)(2,1)S(1)} %collective-permute-done.20.refs_0_, ...), custom_call_target="tpu_custom_call", output_to_operand_aliasing={{}: (6, {})} | custom-call | flops 1 | bytes 1 | tf_op jit(solution)/shard_map/pallas_call | solution.py:557
  95.6 3.5 %collective-permute-done.19.refs_0_ = bf16[256,512]{1,0:T(8,128)(2,1)S(1)} collective-permute-done((bf16[256,512]{1,0:T(8,128)(2,1)S(1)}, bf16[256,512]{1,0:T(8,128)(2,1)S(1)}, u32[]{:S(2)}, u32[]{:S(2)}) %collective-permute-start.19) | collective-permute-done | bytes 262176 | tf_op jit(solution)/shard_map/ppermute | solution.py:411
  99.1 2.1 %shard_map.113.refs_3_ = bf16[1024,1024]{1,0:T(8,128)(2,1)} custom-call(s32[3]{0:T(128)S(1)} %pad_add_fusion.j_ref.a_ref, bf16[256,512]{1,0:T(8,128)(2,1)S(1)} %shard_map.107.own_ref, bf16[512,2048]{1,0:T(8,128)(2,1)S(1)} %copy-done, bf16[256,512]{1,0:T(8,128)(2,1)S(1)} %collective-permute-done.19.refs_0_, ...), custom_call_target="tpu_custom_call", output_to_operand_aliasing={{}: (6, {})} | custom-call | flops 1 | bytes 1 | tf_op jit(solution)/shard_map/pallas_call | solution.py:557
  101.9 1.7 %shard_map.114.refs_3_ = bf16[1024,1024]{1,0:T(8,128)(2,1)} custom-call(s32[3]{0:T(128)S(1)} %pad_add_fusion.j_ref.a_ref, bf16[128,512]{1,0:T(8,128)(2,1)S(1)} %shard_map.108.own_ref, bf16[512,2048]{1,0:T(8,128)(2,1)S(1)} %copy-done, bf16[128,512]{1,0:T(8,128)(2,1)S(1)} %collective-permute-done.18.refs_0_, ...), custom_call_target="tpu_custom_call", output_to_operand_aliasing={{}: (6, {})} | custom-call | flops 1 | bytes 1 | tf_op jit(solution)/shard_map/pallas_call | solution.py:557
  104.3 1.7 %shard_map.115 = bf16[1024,1024]{1,0:T(8,128)(2,1)} custom-call(s32[3]{0:T(128)S(1)} %pad_add_fusion.j_ref.a_ref, bf16[128,512]{1,0:T(8,128)(2,1)S(1)} %shard_map.109.own_ref, bf16[512,2048]{1,0:T(8,128)(2,1)S(1)} %copy-done, bf16[128,512]{1,0:T(8,128)(2,1)S(1)} %collective-permute-done.15.refs_0_, ...), custom_call_target="tpu_custom_call", output_to_operand_aliasing={{}: (6, {})} | custom-call | flops 1 | bytes 1 | tf_op jit(solution)/shard_map/pallas_call | solution.py:557
  (57 shorter events, 23.2 us)
Async XLA Ops:
  1.2 17.7 %collective-permute-start = (bf16[272,1024]{1,0:T(8,128)(2,1)S(1)}, bf16[272,1024]{1,0:T(8,128)(2,1)S(1)}, u32[]{:S(2)}, u32[]{:S(2)}) collective-permute-start(bf16[272,1024]{1,0:T(8,128)(2,1)S(1)} %slice.15.refs_0_), channel_id=1, source_target_pairs={{0,1},{1,0},{2,3},{3,2},{4,5},{5,4},{6,7},{7,6},{8,9},{9,8},{10,11... | collective-permute-start | bytes 1671176 | tf_op jit(solution)/shard_map/ppermute | solution.py:411
  5.5 23.4 %collective-permute-start.2 = (bf16[256,1024]{1,0:T(8,128)(2,1)S(1)}, bf16[256,1024]{1,0:T(8,128)(2,1)S(1)}, u32[]{:S(2)}, u32[]{:S(2)}) collective-permute-start(bf16[256,1024]{1,0:T(8,128)(2,1)S(1)} %get-tuple-element.89.refs_0_), channel_id=1, source_target_pairs={{0,1},{1,0},{2,3},{3,2},{4,5},{5,4},{6,7},{7,6},{8,9},{9,8},{10,11... | collective-permute-start | bytes 1572872 | tf_op jit(solution)/shard_map/ppermute | solution.py:411
  5.6 34.6 %collective-permute-start.3 = (bf16[256,1024]{1,0:T(8,128)(2,1)S(1)}, bf16[256,1024]{1,0:T(8,128)(2,1)S(1)}, u32[]{:S(2)}, u32[]{:S(2)}) collective-permute-start(bf16[256,1024]{1,0:T(8,128)(2,1)S(1)} %get-tuple-element.97.refs_0_), channel_id=1, source_target_pairs={{0,1},{1,0},{2,3},{3,2},{4,5},{5,4},{6,7},{7,6},{8,9},{9,8},{10,11... | collective-permute-start | bytes 1572872 | tf_op jit(solution)/shard_map/ppermute | solution.py:411
  8.6 37.5 %collective-permute-start.4 = (bf16[128,1024]{1,0:T(8,128)(2,1)S(1)}, bf16[128,1024]{1,0:T(8,128)(2,1)S(1)}, u32[]{:S(2)}, u32[]{:S(2)}) collective-permute-start(bf16[128,1024]{1,0:T(8,128)(2,1)S(1)} %get-tuple-element.107.refs_0_), channel_id=1, source_target_pairs={{0,1},{1,0},{2,3},{3,2},{4,5},{5,4},{6,7},{7,6},{8,9},{9,8},{10,11... | collective-permute-start | bytes 786440 | tf_op jit(solution)/shard_map/ppermute | solution.py:411
  8.8 10.1 %copy-start.1 = (bf16[1408,128]{1,0:T(8,128)(2,1)S(1)}, bf16[1408,128]{1,0:T(8,128)(2,1)}, u32[]{:S(2)}) copy-start(bf16[1408,128]{1,0:T(8,128)(2,1)} %constant.30.clone.turn_ref) | copy-start | bytes 1081348
  8.8 10.2 %copy-start.2 = (bf16[256,128]{1,0:T(8,128)(2,1)S(1)}, bf16[256,128]{1,0:T(8,128)(2,1)}, u32[]{:S(2)}) copy-start(bf16[256,128]{1,0:T(8,128)(2,1)} %constant.32.clone.mean_ref) | copy-start | bytes 196612
  8.8 41.8 %collective-permute-start.5 = (bf16[128,1024]{1,0:T(8,128)(2,1)S(1)}, bf16[128,1024]{1,0:T(8,128)(2,1)S(1)}, u32[]{:S(2)}, u32[]{:S(2)}) collective-permute-start(bf16[128,1024]{1,0:T(8,128)(2,1)S(1)} %get-tuple-element.115.refs_0_), channel_id=1, source_target_pairs={{0,1},{1,0},{2,3},{3,2},{4,5},{5,4},{6,7},{7,6},{8,9},{9,8},{10,11... | collective-permute-start | bytes 786440 | tf_op jit(solution)/shard_map/ppermute | solution.py:411
  10.7 3.1 %copy-start.3 = (bf16[2048,1792]{1,0:T(8,128)(2,1)S(1)}, bf16[2048,1792]{1,0:T(8,128)(2,1)}, u32[]{:S(2)}) copy-start(bf16[2048,1792]{1,0:T(8,128)(2,1)} %w_ref.7) | copy-start | bytes 22020100
  13.8 5.1 %copy-start.5 = (f32[160,128]{1,0:T(8,128)S(1)}, f32[160,128]{1,0:T(8,128)}, u32[]{:S(2)}) copy-start(f32[160,128]{1,0:T(8,128)} %constant.31.clone.weight_ref) | copy-start | bytes 245764
  13.8 5.1 %copy-start.6 = (f32[3,512]{1,0:T(4,128)S(1)}, f32[3,512]{1,0:T(4,128)}, u32[]{:S(2)}) copy-start(f32[3,512]{1,0:T(4,128)} %conv_ref.9) | copy-start | bytes 18436
  22.8 9.9 %copy-start.4 = (bf16[128,1280]{1,0:T(8,128)(2,1)S(1)}, bf16[128,1280]{1,0:T(8,128)(2,1)}, u32[]{:S(2)}) copy-start(bf16[128,1280]{1,0:T(8,128)(2,1)} %constant.29.clone.turn_ref) | copy-start | bytes 983044
  22.8 6.1 %collective-permute-start.1 = (bf16[144,512]{1,0:T(8,128)(2,1)S(1)}, bf16[144,512]{1,0:T(8,128)(2,1)S(1)}, u32[]{:S(2)}, u32[]{:S(2)}) collective-permute-start(bf16[144,512]{1,0:T(8,128)(2,1)S(1)} %get-tuple-element.88), channel_id=1, source_target_pairs={{0,2},{2,4},{4,6},{6,8},{8,10},{10,12},{12,14},{14,16},{16,18},{18... | collective-permute-start | bytes 442376 | tf_op jit(solution)/shard_map/ppermute | solution.py:513
  52.3 4.1 %collective-permute-start.6 = (bf16[160,128]{1,0:T(8,128)(2,1)S(1)}, bf16[160,128]{1,0:T(8,128)(2,1)S(1)}, u32[]{:S(2)}, u32[]{:S(2)}) collective-permute-start(bf16[160,128]{1,0:T(8,128)(2,1)S(1)} %get-tuple-element.138), channel_id=1, source_target_pairs={{0,2},{2,0},{4,6},{6,4},{8,10},{10,8},{12,14},{14,12},{16,18},{18,... | collective-permute-start | bytes 122888 | tf_op jit(solution)/shard_map/ppermute | solution.py:319
  52.6 4.1 %collective-permute-start.7 = (bf16[160,128]{1,0:T(8,128)(2,1)S(1)}, bf16[160,128]{1,0:T(8,128)(2,1)S(1)}, u32[]{:S(2)}, u32[]{:S(2)}) collective-permute-start(bf16[160,128]{1,0:T(8,128)(2,1)S(1)} %get-tuple-element.139), channel_id=1, source_target_pairs={{0,4},{2,6},{4,0},{6,2},{8,12},{10,14},{12,8},{14,10},{16,20},{18,... | collective-permute-start | bytes 122888 | tf_op jit(solution)/shard_map/ppermute | solution.py:319
  54.6 3.5 %collective-permute-start.8 = (bf16[160,128]{1,0:T(8,128)(2,1)S(1)}, bf16[160,128]{1,0:T(8,128)(2,1)S(1)}, u32[]{:S(2)}, u32[]{:S(2)}) collective-permute-start(bf16[160,128]{1,0:T(8,128)(2,1)S(1)} %get-tuple-element.140), channel_id=1, source_target_pairs={{0,6},{2,4},{4,2},{6,0},{8,14},{10,12},{12,10},{14,8},{16,22},{18,... | collective-permute-start | bytes 122888 | tf_op jit(solution)/shard_map/ppermute | solution.py:319
  54.7 8.3 %copy-start = (bf16[512,2048]{1,0:T(8,128)(2,1)S(1)}, bf16[512,2048]{1,0:T(8,128)(2,1)}, u32[]{:S(2)}) copy-start(bf16[512,2048]{1,0:T(8,128)(2,1)} %w_ref.13) | copy-start | bytes 6291460
  58.8 8.1 %collective-permute-start.10 = (bf16[160,128]{1,0:T(8,128)(2,1)S(1)}, bf16[160,128]{1,0:T(8,128)(2,1)S(1)}, u32[]{:S(2)}, u32[]{:S(2)}) collective-permute-start(bf16[160,128]{1,0:T(8,128)(2,1)S(1)} %get-tuple-element.145), channel_id=1, source_target_pairs={{0,16},{2,18},{4,20},{6,22},{8,24},{10,26},{12,28},{14,30},{16,0},... | collective-permute-start | bytes 122888 | tf_op jit(solution)/shard_map/ppermute | solution.py:319
  61.4 5.8 %collective-permute-start.11 = (bf16[160,128]{1,0:T(8,128)(2,1)S(1)}, bf16[160,128]{1,0:T(8,128)(2,1)S(1)}, u32[]{:S(2)}, u32[]{:S(2)}) collective-permute-start(bf16[160,128]{1,0:T(8,128)(2,1)S(1)} %get-tuple-element.145), channel_id=1, source_target_pairs={{0,24},{2,26},{4,28},{6,30},{8,16},{10,18},{12,20},{14,22},{16,8},... | collective-permute-start | bytes 122888 | tf_op jit(solution)/shard_map/ppermute | solution.py:319
  62.8 4.5 %collective-permute-start.9 = (bf16[160,128]{1,0:T(8,128)(2,1)S(1)}, bf16[160,128]{1,0:T(8,128)(2,1)S(1)}, u32[]{:S(2)}, u32[]{:S(2)}) collective-permute-start(bf16[160,128]{1,0:T(8,128)(2,1)S(1)} %get-tuple-element.145), channel_id=1, source_target_pairs={{0,8},{2,10},{4,12},{6,14},{8,0},{10,2},{12,4},{14,6},{16,24},{18,... | collective-permute-start | bytes 122888 | tf_op jit(solution)/shard_map/ppermute | solution.py:319
  65.3 13.5 %collective-permute-start.16 = (bf16[256,1024]{1,0:T(8,128)(2,1)S(1)}, bf16[256,1024]{1,0:T(8,128)(2,1)S(1)}, u32[]{:S(2)}, u32[]{:S(2)}) collective-permute-start(bf16[256,1024]{1,0:T(8,128)(2,1)S(1)} %shard_map.110), channel_id=1, source_target_pairs={{0,1},{1,0},{2,3},{3,2},{4,5},{5,4},{6,7},{7,6},{8,9},{9,8},{10,11... | collective-permute-start | bytes 1572872 | tf_op jit(solution)/shard_map/ppermute | solution.py:411
  67.8 4.1 %collective-permute-start.12 = (bf16[160,128]{1,0:T(8,128)(2,1)S(1)}, bf16[160,128]{1,0:T(8,128)(2,1)S(1)}, u32[]{:S(2)}, u32[]{:S(2)}) collective-permute-start(bf16[160,128]{1,0:T(8,128)(2,1)S(1)} %get-tuple-element.147), channel_id=1, source_target_pairs={{0,2},{2,0},{4,6},{6,4},{8,10},{10,8},{12,14},{14,12},{16,18},{18,... | collective-permute-start | bytes 122888 | tf_op jit(solution)/shard_map/ppermute | solution.py:319
  67.9 4.2 %collective-permute-start.13 = (bf16[160,128]{1,0:T(8,128)(2,1)S(1)}, bf16[160,128]{1,0:T(8,128)(2,1)S(1)}, u32[]{:S(2)}, u32[]{:S(2)}) collective-permute-start(bf16[160,128]{1,0:T(8,128)(2,1)S(1)} %get-tuple-element.148), channel_id=1, source_target_pairs={{0,4},{2,6},{4,0},{6,2},{8,12},{10,14},{12,8},{14,10},{16,20},{18,... | collective-permute-start | bytes 122888 | tf_op jit(solution)/shard_map/ppermute | solution.py:319
  68.9 3.8 %collective-permute-start.14 = (bf16[160,128]{1,0:T(8,128)(2,1)S(1)}, bf16[160,128]{1,0:T(8,128)(2,1)S(1)}, u32[]{:S(2)}, u32[]{:S(2)}) collective-permute-start(bf16[160,128]{1,0:T(8,128)(2,1)S(1)} %get-tuple-element.149), channel_id=1, source_target_pairs={{0,6},{2,4},{4,2},{6,0},{8,14},{10,12},{12,10},{14,8},{16,22},{18,... | collective-permute-start | bytes 122888 | tf_op jit(solution)/shard_map/ppermute | solution.py:319
  69.8 2.9 %copy-start.7 = (f32[512]{0:T(512)S(1)}, f32[512]{0:T(512)}, u32[]{:S(2)}) copy-start(f32[512]{0:T(512)} %param.12) | copy-start | bytes 6148
  78.8 11.4 %collective-permute-start.17 = (bf16[256,1024]{1,0:T(8,128)(2,1)S(1)}, bf16[256,1024]{1,0:T(8,128)(2,1)S(1)}, u32[]{:S(2)}, u32[]{:S(2)}) collective-permute-start(bf16[256,1024]{1,0:T(8,128)(2,1)S(1)} %collective-permute-done.16.refs_1_), channel_id=1, source_target_pairs={{0,2},{2,0},{4,6},{6,4},{8,10},{10,8},{12,14},{14,12},{16,18},{18,... | collective-permute-start | bytes 1572872 | tf_op jit(solution)/shard_map/ppermute | solution.py:319
  78.8 9.8 %collective-permute-start.21 = (bf16[256,512]{1,0:T(8,128)(2,1)S(1)}, bf16[256,512]{1,0:T(8,128)(2,1)S(1)}, u32[]{:S(2)}, u32[]{:S(2)}) collective-permute-start(bf16[256,512]{1,0:T(8,128)(2,1)S(1)} %shard_map.105.own_ref), channel_id=1, source_target_pairs={{0,1},{1,0},{2,3},{3,2},{4,5},{5,4},{6,7},{7,6},{8,9},{9,8},{10,11... | collective-permute-start | bytes 786440 | tf_op jit(solution)/shard_map/ppermute | solution.py:411
  81.8 11.7 %collective-permute-start.20 = (bf16[256,512]{1,0:T(8,128)(2,1)S(1)}, bf16[256,512]{1,0:T(8,128)(2,1)S(1)}, u32[]{:S(2)}, u32[]{:S(2)}) collective-permute-start(bf16[256,512]{1,0:T(8,128)(2,1)S(1)} %shard_map.106.own_ref), channel_id=1, source_target_pairs={{0,1},{1,0},{2,3},{3,2},{4,5},{5,4},{6,7},{7,6},{8,9},{9,8},{10,11... | collective-permute-start | bytes 786440 | tf_op jit(solution)/shard_map/ppermute | solution.py:411
  83.9 15.2 %collective-permute-start.19 = (bf16[256,512]{1,0:T(8,128)(2,1)S(1)}, bf16[256,512]{1,0:T(8,128)(2,1)S(1)}, u32[]{:S(2)}, u32[]{:S(2)}) collective-permute-start(bf16[256,512]{1,0:T(8,128)(2,1)S(1)} %shard_map.107.own_ref), channel_id=1, source_target_pairs={{0,1},{1,0},{2,3},{3,2},{4,5},{5,4},{6,7},{7,6},{8,9},{9,8},{10,11... | collective-permute-start | bytes 786440 | tf_op jit(solution)/shard_map/ppermute | solution.py:411
  86.8 15.2 %collective-permute-start.18 = (bf16[128,512]{1,0:T(8,128)(2,1)S(1)}, bf16[128,512]{1,0:T(8,128)(2,1)S(1)}, u32[]{:S(2)}, u32[]{:S(2)}) collective-permute-start(bf16[128,512]{1,0:T(8,128)(2,1)S(1)} %shard_map.108.own_ref), channel_id=1, source_target_pairs={{0,1},{1,0},{2,3},{3,2},{4,5},{5,4},{6,7},{7,6},{8,9},{9,8},{10,11... | collective-permute-start | bytes 393224 | tf_op jit(solution)/shard_map/ppermute | solution.py:411
  88.6 15.8 %collective-permute-start.15 = (bf16[128,512]{1,0:T(8,128)(2,1)S(1)}, bf16[128,512]{1,0:T(8,128)(2,1)S(1)}, u32[]{:S(2)}, u32[]{:S(2)}) collective-permute-start(bf16[128,512]{1,0:T(8,128)(2,1)S(1)} %shard_map.109.own_ref), channel_id=1, source_target_pairs={{0,1},{1,0},{2,3},{3,2},{4,5},{5,4},{6,7},{7,6},{8,9},{9,8},{10,11... | collective-permute-start | bytes 393224 | tf_op jit(solution)/shard_map/ppermute | solution.py:411

commit v6 on v5

--- a/solution.py
+++ b/solution.py
@@ -504,7 +504,7 @@
             in_specs=[scalar] + [whole] * 7,
             out_specs=[whole] * 3,
             scratch_shapes=[pltpu.VMEM((WIN + rows, width), BF16)] * 2,
-            flops=20 * 10**9 if b == last else 1,
+            flops=4850 * 10**6 if b == last else 1,
             vmem=16 << 20,
         )(places, turn, prev, q, k, v, wq, wk)
 
@@ -523,7 +523,7 @@
     for b in (last - 1, last):
         attended[b] = attend(b, prevs[b])
     held = sends[:1] + [exchange(sends[r], "ctx", r) for r in range(1, len(sends))]
-    mark = attended[last - 1][1]
+    mark = done[last - 1][6]
     fetched = [from_head(after(block, mark), r) for r, block in enumerate(picked, 1)]
     if in_planes:
         priors = prior_in_planes(held, places, [done[last - 1][6], attended[last - 1][1]])

time: 106 us -> 103 us (0.972)
  waiting for transfers between devices: 23.4 us -> 20.5 us
    ppermute x11, waiting for transfers between devices: 20.7 us -> 16.9 us  [from_head(): return lax.ppermute(value, 'head', [(i, (i + by) % n) for i in range(n)])]
  transfers between devices with their start and end apart: 22 -> 22, of which waited for: 13 -> 10; matrix products, arithmetic and copies ran while one was open for 2% -> 2% of each run, Pallas kernels for 44% -> 46%
where the time goes in v6:
time: 103 us
  Pallas kernels  51 us (50%)
  starting transfers between devices  24.2 us (23%)
  waiting for transfers between devices  20.5 us (20%)
  local copies, waits for them, and re-layouts  6.53 us (6%)
    ppermute x11, waiting for transfers between devices, from_head(): return lax.ppermute(value, 'head', [(i, (i + by) % n) for i in range(n)])  16.9 us
    pallas_call x5, Pallas kernels, do_block(): call(functools.partial(block_kernel, n=n, heads=heads, extra=extra, other...  15.9 us
    ppermute x11, starting transfers between devices, from_head(): return lax.ppermute(value, 'head', [(i, (i + by) % n) for i in range(n)])  13.9 us
    pallas_call x5, Pallas kernels, attend(): call(functools.partial(attend_kernel, heads=heads, first=b == 0), [jax.Sh...  9.74 us
    pallas_call x5, Pallas kernels, per_device(): call(functools.partial(output_kernel, n=n, offset=at, parts=out_parts), j...  9.63 us
    ppermute x10, starting transfers between devices, exchange(): return lax.ppermute(value, axis, [(i, i ^ flip) for i in range(count)])  8.75 us
    pallas_call x5, Pallas kernels, per_device(): call(functools.partial(finish_kernel, heads=heads, before=b), jax.ShapeDt...  7.04 us
    pallas_call x1, Pallas kernels, per_device(): call(functools.partial(arrange_kernel, heads=heads), jax.ShapeDtypeStruct...  5.09 us
  transfers between devices with their start and end apart: 22, of which 10 were waited for; matrix products, arithmetic and copies ran while one was open for 2% of the time, Pallas kernels for 46%

profile of v6, /device:TPU:0, one launch (start us, length us, event | category | flops | bytes accessed | tf_op | source)
XLA Modules:
  0.0 102.8 jit_solution(15727794324033132827)
XLA Ops:
  1.2 3.0 %collective-permute-start = (bf16[272,1024]{1,0:T(8,128)(2,1)S(1)}, bf16[272,1024]{1,0:T(8,128)(2,1)S(1)}, u32[]{:S(2)}, u32[]{:S(2)}) collective-permute-start(bf16[272,1024]{1,0:T(8,128)(2,1)S(1)} %slice.15.refs_0_), channel_id=1, source_target_pairs={{0,1},{1,0},{2,3},{3,2},{4,5},{5,4},{6,7},{7,6},{8,9},{9,8},{10,11... | collective-permute-start | bytes 1671176 | tf_op jit(solution)/shard_map/ppermute | solution.py:411
  5.6 2.0 %collective-permute-start.3 = (bf16[256,1024]{1,0:T(8,128)(2,1)S(1)}, bf16[256,1024]{1,0:T(8,128)(2,1)S(1)}, u32[]{:S(2)}, u32[]{:S(2)}) collective-permute-start(bf16[256,1024]{1,0:T(8,128)(2,1)S(1)} %get-tuple-element.97.refs_0_), channel_id=1, source_target_pairs={{0,1},{1,0},{2,3},{3,2},{4,5},{5,4},{6,7},{7,6},{8,9},{9,8},{10,11... | collective-permute-start | bytes 1572872 | tf_op jit(solution)/shard_map/ppermute | solution.py:411
  8.8 1.9 %collective-permute-start.5 = (bf16[128,1024]{1,0:T(8,128)(2,1)S(1)}, bf16[128,1024]{1,0:T(8,128)(2,1)S(1)}, u32[]{:S(2)}, u32[]{:S(2)}) collective-permute-start(bf16[128,1024]{1,0:T(8,128)(2,1)S(1)} %get-tuple-element.115.refs_0_), channel_id=1, source_target_pairs={{0,1},{1,0},{2,3},{3,2},{4,5},{5,4},{6,7},{7,6},{8,9},{9,8},{10,11... | collective-permute-start | bytes 786440 | tf_op jit(solution)/shard_map/ppermute | solution.py:411
  10.7 3.1 %copy-done.3 = bf16[2048,1792]{1,0:T(8,128)(2,1)S(1)} copy-done((bf16[2048,1792]{1,0:T(8,128)(2,1)S(1)}, bf16[2048,1792]{1,0:T(8,128)(2,1)}, u32[]{:S(2)}) %copy-start.3) | copy-done | bytes 7340056
  13.8 5.1 %shard_map.91.w_ref = bf16[2048,1792]{1,0:T(8,128)(2,1)S(1)} custom-call(bf16[2048,1792]{1,0:T(8,128)(2,1)S(1)} %copy-done.3), custom_call_target="tpu_custom_call" | custom-call | flops 1 | bytes 1 | tf_op jit(solution)/shard_map/pallas_call | solution.py:451
  19.0 3.8 %shard_map.92 = (bf16[256,128]{1,0:T(8,128)(2,1)S(1)}, bf16[256,512]{1,0:T(8,128)(2,1)S(1)}, f32[4,160,128]{2,1,0:T(8,128)S(1)}, bf16[256,128]{1,0:T(8,128)(2,1)...) custom-call(s32[3]{0:T(128)S(1)} %pad_add_fusion.j_ref.a_ref, ...), custom_call_target="tpu_custom_call" | custom-call | flops 1 | bytes 1 | tf_op jit(solution)/shard_map/pallas_call | solution.py:477
  22.8 1.6 %collective-permute-start.1 = (bf16[144,512]{1,0:T(8,128)(2,1)S(1)}, bf16[144,512]{1,0:T(8,128)(2,1)S(1)}, u32[]{:S(2)}, u32[]{:S(2)}) collective-permute-start(bf16[144,512]{1,0:T(8,128)(2,1)S(1)} %get-tuple-element.88), channel_id=1, source_target_pairs={{0,2},{2,4},{4,6},{6,8},{8,10},{10,12},{12,14},{14,16},{16,18},{18... | collective-permute-start | bytes 442376 | tf_op jit(solution)/shard_map/ppermute | solution.py:513
  24.4 4.4 %collective-permute-done.2.refs_1_ = bf16[256,1024]{1,0:T(8,128)(2,1)S(1)} collective-permute-done((bf16[256,1024]{1,0:T(8,128)(2,1)S(1)}, bf16[256,1024]{1,0:T(8,128)(2,1)S(1)}, u32[]{:S(2)}, u32[]{:S(2)}) %collective-permute-start.2) | collective-permute-done | bytes 524320 | tf_op jit(solution)/shard_map/ppermute | solution.py:411
  28.9 3.8 %shard_map.93 = (bf16[256,128]{1,0:T(8,128)(2,1)S(1)}, bf16[256,512]{1,0:T(8,128)(2,1)S(1)}, f32[4,160,128]{2,1,0:T(8,128)S(1)}, bf16[256,128]{1,0:T(8,128)(2,1)...) custom-call(s32[3]{0:T(128)S(1)} %pad_add_fusion.j_ref.a_ref, ...), custom_call_target="tpu_custom_call" | custom-call | flops 1 | bytes 1 | tf_op jit(solution)/shard_map/pallas_call | solution.py:477
  32.7 2.1 %shard_map.94 = (bf16[256,1280]{1,0:T(8,128)(2,1)S(1)}, f32[256,512]{1,0:T(8,128)S(1)}, f32[256,512]{1,0:T(8,128)S(1)}) custom-call(s32[3]{0:T(128)S(1)} %pad_add_fusion.j_ref.a_ref, bf16[128,1280]{1,0:T(8,128)(2,1)S(1)} %copy-done.4, bf16[144,512]{1,0:T(8,128)(2,1)S(1)} %collective-permute-done.1.refs_2_.prev_ref, ...), custom_call_target="tpu_custom_call" | custom-call | flops 1 | bytes 1 | tf_op jit(solution)/shard_map/pallas_call | solution.py:501
  34.9 5.2 %collective-permute-done.3.refs_1_ = bf16[256,1024]{1,0:T(8,128)(2,1)S(1)} collective-permute-done((bf16[256,1024]{1,0:T(8,128)(2,1)S(1)}, bf16[256,1024]{1,0:T(8,128)(2,1)S(1)}, u32[]{:S(2)}, u32[]{:S(2)}) %collective-permute-start.3) | collective-permute-done | bytes 524320 | tf_op jit(solution)/shard_map/ppermute | solution.py:411
  40.1 3.8 %shard_map.95 = (bf16[256,128]{1,0:T(8,128)(2,1)S(1)}, bf16[256,512]{1,0:T(8,128)(2,1)S(1)}, f32[4,160,128]{2,1,0:T(8,128)S(1)}, bf16[256,128]{1,0:T(8,128)(2,1)...) custom-call(s32[3]{0:T(128)S(1)} %pad_add_fusion.j_ref.a_ref, ...), custom_call_target="tpu_custom_call" | custom-call | flops 1 | bytes 1 | tf_op jit(solution)/shard_map/pallas_call | solution.py:477
  44.0 2.1 %shard_map.96 = (bf16[256,1280]{1,0:T(8,128)(2,1)S(1)}, f32[256,512]{1,0:T(8,128)S(1)}, f32[256,512]{1,0:T(8,128)S(1)}) custom-call(s32[3]{0:T(128)S(1)} %pad_add_fusion.j_ref.a_ref, bf16[128,1280]{1,0:T(8,128)(2,1)S(1)} %copy-done.4, bf16[144,512]{1,0:T(8,128)(2,1)S(1)} %get-tuple-element.98.refs_2_.prev_ref, ...), custom_call_target="tpu_custom_call" | custom-call | flops 1 | bytes 1 | tf_op jit(solution)/shard_map/pallas_call | solution.py:501
  46.1 2.6 %shard_map.97 = (bf16[128,128]{1,0:T(8,128)(2,1)S(1)}, bf16[128,512]{1,0:T(8,128)(2,1)S(1)}, f32[4,160,128]{2,1,0:T(8,128)S(1)}, bf16[128,128]{1,0:T(8,128)(2,1)...) custom-call(s32[3]{0:T(128)S(1)} %pad_add_fusion.j_ref.a_ref, ...), custom_call_target="tpu_custom_call" | custom-call | flops 1 | bytes 1 | tf_op jit(solution)/shard_map/pallas_call | solution.py:477
  48.7 1.7 %shard_map.98 = (bf16[128,1280]{1,0:T(8,128)(2,1)S(1)}, f32[128,512]{1,0:T(8,128)S(1)}, f32[128,512]{1,0:T(8,128)S(1)}) custom-call(s32[3]{0:T(128)S(1)} %pad_add_fusion.j_ref.a_ref, bf16[128,1280]{1,0:T(8,128)(2,1)S(1)} %copy-done.4, bf16[144,512]{1,0:T(8,128)(2,1)S(1)} %get-tuple-element.99.refs_2_.prev_ref, ...), custom_call_target="tpu_custom_call" | custom-call | flops 1 | bytes 1 | tf_op jit(solution)/shard_map/pallas_call | solution.py:501
  50.5 1.8 %shard_map.99 = (bf16[128,128]{1,0:T(8,128)(2,1)S(1)}, bf16[128,512]{1,0:T(8,128)(2,1)S(1)}, f32[4,160,128]{2,1,0:T(8,128)S(1)}, bf16[160,128]{1,0:T(8,128)(2,1)...) custom-call(s32[3]{0:T(128)S(1)} %pad_add_fusion.j_ref.a_ref, ...), custom_call_target="tpu_custom_call" | custom-call | flops 1 | bytes 1 | tf_op jit(solution)/shard_map/pallas_call | solution.py:477
  52.6 2.0 %collective-permute-start.7 = (bf16[160,128]{1,0:T(8,128)(2,1)S(1)}, bf16[160,128]{1,0:T(8,128)(2,1)S(1)}, u32[]{:S(2)}, u32[]{:S(2)}) collective-permute-start(bf16[160,128]{1,0:T(8,128)(2,1)S(1)} %get-tuple-element.139), channel_id=1, source_target_pairs={{0,4},{2,6},{4,0},{6,2},{8,12},{10,14},{12,8},{14,10},{16,20},{18,... | collective-permute-start | bytes 122888 | tf_op jit(solution)/shard_map/ppermute | solution.py:319
  55.3 1.8 %shard_map.100 = (bf16[128,128]{1,0:T(8,128)(2,1)S(1)}, bf16[128,512]{1,0:T(8,128)(2,1)S(1)}, bf16[128,512]{1,0:T(8,128)(2,1)S(1)}, bf16[144,512]{1,0:T(8,128)(2,1)S(1)}) custom-call(s32[3]{0:T(128)S(1)} %pad_add_fusion.j_ref.a_ref, bf16[256,128]{1,0:T(8,128)(2,1)S(1)} %copy-done.2, bf16[2048,1792]{1,0:T(8,128)(2,1)S(1)} %shard_map.91.w_ref, ...), custom_call_target="tpu_custom_call" | custom-call | flops 1 | bytes 1 | tf_op jit(solution)/shard_map/pallas_call | solution.py:490
  57.1 1.8 %collective-permute-start.16 = (bf16[256,1024]{1,0:T(8,128)(2,1)S(1)}, bf16[256,1024]{1,0:T(8,128)(2,1)S(1)}, u32[]{:S(2)}, u32[]{:S(2)}) collective-permute-start(bf16[256,1024]{1,0:T(8,128)(2,1)S(1)} %shard_map.110), channel_id=1, source_target_pairs={{0,1},{1,0},{2,3},{3,2},{4,5},{5,4},{6,7},{7,6},{8,9},{9,8},{10,11... | collective-permute-start | bytes 1572872 | tf_op jit(solution)/shard_map/ppermute | solution.py:411
  59.6 2.6 %collective-permute-start.10 = (bf16[160,128]{1,0:T(8,128)(2,1)S(1)}, bf16[160,128]{1,0:T(8,128)(2,1)S(1)}, u32[]{:S(2)}, u32[]{:S(2)}) collective-permute-start(bf16[160,128]{1,0:T(8,128)(2,1)S(1)} %get-tuple-element.145), channel_id=1, source_target_pairs={{0,16},{2,18},{4,20},{6,22},{8,24},{10,26},{12,28},{14,30},{16,0},... | collective-permute-start | bytes 122888 | tf_op jit(solution)/shard_map/ppermute | solution.py:319
  63.8 1.7 %shard_map.102 = (bf16[128,1280]{1,0:T(8,128)(2,1)S(1)}, f32[128,512]{1,0:T(8,128)S(1)}, f32[128,512]{1,0:T(8,128)S(1)}) custom-call(s32[3]{0:T(128)S(1)} %pad_add_fusion.j_ref.a_ref, bf16[128,1280]{1,0:T(8,128)(2,1)S(1)} %copy-done.4, bf16[144,512]{1,0:T(8,128)(2,1)S(1)} %get-tuple-element.116.refs_2_.prev_ref, ...), custom_call_target="tpu_custom_call" | custom-call | flops 1 | bytes 1 | tf_op jit(solution)/shard_map/pallas_call | solution.py:501
  65.5 2.5 %collective-permute-done.11.refs_6_ = bf16[160,128]{1,0:T(8,128)(2,1)S(1)} collective-permute-done((bf16[160,128]{1,0:T(8,128)(2,1)S(1)}, bf16[160,128]{1,0:T(8,128)(2,1)S(1)}, u32[]{:S(2)}, u32[]{:S(2)}) %collective-permute-start.11) | collective-permute-done | bytes 40992 | tf_op jit(solution)/shard_map/ppermute | solution.py:319
  70.5 2.1 %shard_map.101 = (bf16[256,1280]{1,0:T(8,128)(2,1)S(1)}, f32[256,512]{1,0:T(8,128)S(1)}, f32[256,512]{1,0:T(8,128)S(1)}) custom-call(s32[3]{0:T(128)S(1)} %pad_add_fusion.j_ref.a_ref, bf16[128,1280]{1,0:T(8,128)(2,1)S(1)} %copy-done.4, bf16[144,512]{1,0:T(8,128)(2,1)S(1)} %get-tuple-element.122.prev_ref, bf16[256,128]{1,0:T(8,128)(2,1)S(1)} %get-tuple-element.123.q_ref, ...), custom_call_target="tpu_custom_call" | custom-call | flops 4849999872 | bytes 1 | tf_op jit(solution)/shard_map/pallas_call | solution.py:501
  77.5 1.6 %collective-permute-start.20 = (bf16[256,512]{1,0:T(8,128)(2,1)S(1)}, bf16[256,512]{1,0:T(8,128)(2,1)S(1)}, u32[]{:S(2)}, u32[]{:S(2)}) collective-permute-start(bf16[256,512]{1,0:T(8,128)(2,1)S(1)} %shard_map.106.own_ref), channel_id=1, source_target_pairs={{0,1},{1,0},{2,3},{3,2},{4,5},{5,4},{6,7},{7,6},{8,9},{9,8},{10,11... | collective-permute-start | bytes 786440 | tf_op jit(solution)/shard_map/ppermute | solution.py:411
  82.5 1.6 %collective-permute-start.18 = (bf16[128,512]{1,0:T(8,128)(2,1)S(1)}, bf16[128,512]{1,0:T(8,128)(2,1)S(1)}, u32[]{:S(2)}, u32[]{:S(2)}) collective-permute-start(bf16[128,512]{1,0:T(8,128)(2,1)S(1)} %shard_map.108.own_ref), channel_id=1, source_target_pairs={{0,1},{1,0},{2,3},{3,2},{4,5},{5,4},{6,7},{7,6},{8,9},{9,8},{10,11... | collective-permute-start | bytes 393224 | tf_op jit(solution)/shard_map/ppermute | solution.py:411
  85.9 2.1 %shard_map.111.refs_3_ = bf16[1024,1024]{1,0:T(8,128)(2,1)} custom-call(s32[3]{0:T(128)S(1)} %pad_add_fusion.j_ref.a_ref, bf16[256,512]{1,0:T(8,128)(2,1)S(1)} %shard_map.105.own_ref, bf16[512,2048]{1,0:T(8,128)(2,1)S(1)} %copy-done, bf16[256,512]{1,0:T(8,128)(2,1)S(1)} %collective-permute-done.21.refs_0_, ...), custom_call_target="tpu_custom_call" | custom-call | flops 1 | bytes 1 | tf_op jit(solution)/shard_map/pallas_call | solution.py:557
  88.0 2.3 %collective-permute-done.20.refs_0_ = bf16[256,512]{1,0:T(8,128)(2,1)S(1)} collective-permute-done((bf16[256,512]{1,0:T(8,128)(2,1)S(1)}, bf16[256,512]{1,0:T(8,128)(2,1)S(1)}, u32[]{:S(2)}, u32[]{:S(2)}) %collective-permute-start.20) | collective-permute-done | bytes 262176 | tf_op jit(solution)/shard_map/ppermute | solution.py:411
  90.3 2.1 %shard_map.112.refs_3_ = bf16[1024,1024]{1,0:T(8,128)(2,1)} custom-call(s32[3]{0:T(128)S(1)} %pad_add_fusion.j_ref.a_ref, bf16[256,512]{1,0:T(8,128)(2,1)S(1)} %shard_map.106.own_ref, bf16[512,2048]{1,0:T(8,128)(2,1)S(1)} %copy-done, bf16[256,512]{1,0:T(8,128)(2,1)S(1)} %collective-permute-done.20.refs_0_, ...), custom_call_target="tpu_custom_call", output_to_operand_aliasing={{}: (6, {})} | custom-call | flops 1 | bytes 1 | tf_op jit(solution)/shard_map/pallas_call | solution.py:557
  92.3 3.5 %collective-permute-done.19.refs_0_ = bf16[256,512]{1,0:T(8,128)(2,1)S(1)} collective-permute-done((bf16[256,512]{1,0:T(8,128)(2,1)S(1)}, bf16[256,512]{1,0:T(8,128)(2,1)S(1)}, u32[]{:S(2)}, u32[]{:S(2)}) %collective-permute-start.19) | collective-permute-done | bytes 262176 | tf_op jit(solution)/shard_map/ppermute | solution.py:411
  95.9 2.1 %shard_map.113.refs_3_ = bf16[1024,1024]{1,0:T(8,128)(2,1)} custom-call(s32[3]{0:T(128)S(1)} %pad_add_fusion.j_ref.a_ref, bf16[256,512]{1,0:T(8,128)(2,1)S(1)} %shard_map.107.own_ref, bf16[512,2048]{1,0:T(8,128)(2,1)S(1)} %copy-done, bf16[256,512]{1,0:T(8,128)(2,1)S(1)} %collective-permute-done.19.refs_0_, ...), custom_call_target="tpu_custom_call", output_to_operand_aliasing={{}: (6, {})} | custom-call | flops 1 | bytes 1 | tf_op jit(solution)/shard_map/pallas_call | solution.py:557
  98.7 1.7 %shard_map.114.refs_3_ = bf16[1024,1024]{1,0:T(8,128)(2,1)} custom-call(s32[3]{0:T(128)S(1)} %pad_add_fusion.j_ref.a_ref, bf16[128,512]{1,0:T(8,128)(2,1)S(1)} %shard_map.108.own_ref, bf16[512,2048]{1,0:T(8,128)(2,1)S(1)} %copy-done, bf16[128,512]{1,0:T(8,128)(2,1)S(1)} %collective-permute-done.18.refs_0_, ...), custom_call_target="tpu_custom_call", output_to_operand_aliasing={{}: (6, {})} | custom-call | flops 1 | bytes 1 | tf_op jit(solution)/shard_map/pallas_call | solution.py:557
  100.9 1.7 %shard_map.115 = bf16[1024,1024]{1,0:T(8,128)(2,1)} custom-call(s32[3]{0:T(128)S(1)} %pad_add_fusion.j_ref.a_ref, bf16[128,512]{1,0:T(8,128)(2,1)S(1)} %shard_map.109.own_ref, bf16[512,2048]{1,0:T(8,128)(2,1)S(1)} %copy-done, bf16[128,512]{1,0:T(8,128)(2,1)S(1)} %collective-permute-done.15.refs_0_, ...), custom_call_target="tpu_custom_call", output_to_operand_aliasing={{}: (6, {})} | custom-call | flops 1 | bytes 1 | tf_op jit(solution)/shard_map/pallas_call | solution.py:557
  (57 shorter events, 20.9 us)
Async XLA Ops:
  1.2 17.7 %collective-permute-start = (bf16[272,1024]{1,0:T(8,128)(2,1)S(1)}, bf16[272,1024]{1,0:T(8,128)(2,1)S(1)}, u32[]{:S(2)}, u32[]{:S(2)}) collective-permute-start(bf16[272,1024]{1,0:T(8,128)(2,1)S(1)} %slice.15.refs_0_), channel_id=1, source_target_pairs={{0,1},{1,0},{2,3},{3,2},{4,5},{5,4},{6,7},{7,6},{8,9},{9,8},{10,11... | collective-permute-start | bytes 1671176 | tf_op jit(solution)/shard_map/ppermute | solution.py:411
  5.5 23.4 %collective-permute-start.2 = (bf16[256,1024]{1,0:T(8,128)(2,1)S(1)}, bf16[256,1024]{1,0:T(8,128)(2,1)S(1)}, u32[]{:S(2)}, u32[]{:S(2)}) collective-permute-start(bf16[256,1024]{1,0:T(8,128)(2,1)S(1)} %get-tuple-element.89.refs_0_), channel_id=1, source_target_pairs={{0,1},{1,0},{2,3},{3,2},{4,5},{5,4},{6,7},{7,6},{8,9},{9,8},{10,11... | collective-permute-start | bytes 1572872 | tf_op jit(solution)/shard_map/ppermute | solution.py:411
  5.6 34.6 %collective-permute-start.3 = (bf16[256,1024]{1,0:T(8,128)(2,1)S(1)}, bf16[256,1024]{1,0:T(8,128)(2,1)S(1)}, u32[]{:S(2)}, u32[]{:S(2)}) collective-permute-start(bf16[256,1024]{1,0:T(8,128)(2,1)S(1)} %get-tuple-element.97.refs_0_), channel_id=1, source_target_pairs={{0,1},{1,0},{2,3},{3,2},{4,5},{5,4},{6,7},{7,6},{8,9},{9,8},{10,11... | collective-permute-start | bytes 1572872 | tf_op jit(solution)/shard_map/ppermute | solution.py:411
  8.6 37.5 %collective-permute-start.4 = (bf16[128,1024]{1,0:T(8,128)(2,1)S(1)}, bf16[128,1024]{1,0:T(8,128)(2,1)S(1)}, u32[]{:S(2)}, u32[]{:S(2)}) collective-permute-start(bf16[128,1024]{1,0:T(8,128)(2,1)S(1)} %get-tuple-element.107.refs_0_), channel_id=1, source_target_pairs={{0,1},{1,0},{2,3},{3,2},{4,5},{5,4},{6,7},{7,6},{8,9},{9,8},{10,11... | collective-permute-start | bytes 786440 | tf_op jit(solution)/shard_map/ppermute | solution.py:411
  8.8 10.1 %copy-start.1 = (bf16[1408,128]{1,0:T(8,128)(2,1)S(1)}, bf16[1408,128]{1,0:T(8,128)(2,1)}, u32[]{:S(2)}) copy-start(bf16[1408,128]{1,0:T(8,128)(2,1)} %constant.30.clone.turn_ref) | copy-start | bytes 1081348
  8.8 10.2 %copy-start.2 = (bf16[256,128]{1,0:T(8,128)(2,1)S(1)}, bf16[256,128]{1,0:T(8,128)(2,1)}, u32[]{:S(2)}) copy-start(bf16[256,128]{1,0:T(8,128)(2,1)} %constant.32.clone.mean_ref) | copy-start | bytes 196612
  8.8 41.8 %collective-permute-start.5 = (bf16[128,1024]{1,0:T(8,128)(2,1)S(1)}, bf16[128,1024]{1,0:T(8,128)(2,1)S(1)}, u32[]{:S(2)}, u32[]{:S(2)}) collective-permute-start(bf16[128,1024]{1,0:T(8,128)(2,1)S(1)} %get-tuple-element.115.refs_0_), channel_id=1, source_target_pairs={{0,1},{1,0},{2,3},{3,2},{4,5},{5,4},{6,7},{7,6},{8,9},{9,8},{10,11... | collective-permute-start | bytes 786440 | tf_op jit(solution)/shard_map/ppermute | solution.py:411
  10.7 3.1 %copy-start.3 = (bf16[2048,1792]{1,0:T(8,128)(2,1)S(1)}, bf16[2048,1792]{1,0:T(8,128)(2,1)}, u32[]{:S(2)}) copy-start(bf16[2048,1792]{1,0:T(8,128)(2,1)} %w_ref.7) | copy-start | bytes 22020100
  13.8 5.1 %copy-start.5 = (f32[160,128]{1,0:T(8,128)S(1)}, f32[160,128]{1,0:T(8,128)}, u32[]{:S(2)}) copy-start(f32[160,128]{1,0:T(8,128)} %constant.31.clone.weight_ref) | copy-start | bytes 245764
  13.8 5.1 %copy-start.6 = (f32[3,512]{1,0:T(4,128)S(1)}, f32[3,512]{1,0:T(4,128)}, u32[]{:S(2)}) copy-start(f32[3,512]{1,0:T(4,128)} %conv_ref.9) | copy-start | bytes 18436
  22.8 9.9 %copy-start.4 = (bf16[128,1280]{1,0:T(8,128)(2,1)S(1)}, bf16[128,1280]{1,0:T(8,128)(2,1)}, u32[]{:S(2)}) copy-start(bf16[128,1280]{1,0:T(8,128)(2,1)} %constant.29.clone.turn_ref) | copy-start | bytes 983044
  22.8 6.1 %collective-permute-start.1 = (bf16[144,512]{1,0:T(8,128)(2,1)S(1)}, bf16[144,512]{1,0:T(8,128)(2,1)S(1)}, u32[]{:S(2)}, u32[]{:S(2)}) collective-permute-start(bf16[144,512]{1,0:T(8,128)(2,1)S(1)} %get-tuple-element.88), channel_id=1, source_target_pairs={{0,2},{2,4},{4,6},{6,8},{8,10},{10,12},{12,14},{14,16},{16,18},{18... | collective-permute-start | bytes 442376 | tf_op jit(solution)/shard_map/ppermute | solution.py:513
  50.5 4.2 %copy-start = (bf16[512,2048]{1,0:T(8,128)(2,1)S(1)}, bf16[512,2048]{1,0:T(8,128)(2,1)}, u32[]{:S(2)}) copy-start(bf16[512,2048]{1,0:T(8,128)(2,1)} %w_ref.13) | copy-start | bytes 6291460
  52.3 6.6 %collective-permute-start.6 = (bf16[160,128]{1,0:T(8,128)(2,1)S(1)}, bf16[160,128]{1,0:T(8,128)(2,1)S(1)}, u32[]{:S(2)}, u32[]{:S(2)}) collective-permute-start(bf16[160,128]{1,0:T(8,128)(2,1)S(1)} %get-tuple-element.138), channel_id=1, source_target_pairs={{0,2},{2,0},{4,6},{6,4},{8,10},{10,8},{12,14},{14,12},{16,18},{18,... | collective-permute-start | bytes 122888 | tf_op jit(solution)/shard_map/ppermute | solution.py:319
  52.6 6.3 %collective-permute-start.7 = (bf16[160,128]{1,0:T(8,128)(2,1)S(1)}, bf16[160,128]{1,0:T(8,128)(2,1)S(1)}, u32[]{:S(2)}, u32[]{:S(2)}) collective-permute-start(bf16[160,128]{1,0:T(8,128)(2,1)S(1)} %get-tuple-element.139), channel_id=1, source_target_pairs={{0,4},{2,6},{4,0},{6,2},{8,12},{10,14},{12,8},{14,10},{16,20},{18,... | collective-permute-start | bytes 122888 | tf_op jit(solution)/shard_map/ppermute | solution.py:319
  54.6 4.3 %collective-permute-start.8 = (bf16[160,128]{1,0:T(8,128)(2,1)S(1)}, bf16[160,128]{1,0:T(8,128)(2,1)S(1)}, u32[]{:S(2)}, u32[]{:S(2)}) collective-permute-start(bf16[160,128]{1,0:T(8,128)(2,1)S(1)} %get-tuple-element.140), channel_id=1, source_target_pairs={{0,6},{2,4},{4,2},{6,0},{8,14},{10,12},{12,10},{14,8},{16,22},{18,... | collective-permute-start | bytes 122888 | tf_op jit(solution)/shard_map/ppermute | solution.py:319
  57.1 18.2 %collective-permute-start.16 = (bf16[256,1024]{1,0:T(8,128)(2,1)S(1)}, bf16[256,1024]{1,0:T(8,128)(2,1)S(1)}, u32[]{:S(2)}, u32[]{:S(2)}) collective-permute-start(bf16[256,1024]{1,0:T(8,128)(2,1)S(1)} %shard_map.110), channel_id=1, source_target_pairs={{0,1},{1,0},{2,3},{3,2},{4,5},{5,4},{6,7},{7,6},{8,9},{9,8},{10,11... | collective-permute-start | bytes 1572872 | tf_op jit(solution)/shard_map/ppermute | solution.py:411
  59.6 5.9 %collective-permute-start.10 = (bf16[160,128]{1,0:T(8,128)(2,1)S(1)}, bf16[160,128]{1,0:T(8,128)(2,1)S(1)}, u32[]{:S(2)}, u32[]{:S(2)}) collective-permute-start(bf16[160,128]{1,0:T(8,128)(2,1)S(1)} %get-tuple-element.145), channel_id=1, source_target_pairs={{0,16},{2,18},{4,20},{6,22},{8,24},{10,26},{12,28},{14,30},{16,0},... | collective-permute-start | bytes 122888 | tf_op jit(solution)/shard_map/ppermute | solution.py:319
  62.2 5.8 %collective-permute-start.11 = (bf16[160,128]{1,0:T(8,128)(2,1)S(1)}, bf16[160,128]{1,0:T(8,128)(2,1)S(1)}, u32[]{:S(2)}, u32[]{:S(2)}) collective-permute-start(bf16[160,128]{1,0:T(8,128)(2,1)S(1)} %get-tuple-element.145), channel_id=1, source_target_pairs={{0,24},{2,26},{4,28},{6,30},{8,16},{10,18},{12,20},{14,22},{16,8},... | collective-permute-start | bytes 122888 | tf_op jit(solution)/shard_map/ppermute | solution.py:319
  63.6 4.4 %collective-permute-start.9 = (bf16[160,128]{1,0:T(8,128)(2,1)S(1)}, bf16[160,128]{1,0:T(8,128)(2,1)S(1)}, u32[]{:S(2)}, u32[]{:S(2)}) collective-permute-start(bf16[160,128]{1,0:T(8,128)(2,1)S(1)} %get-tuple-element.145), channel_id=1, source_target_pairs={{0,8},{2,10},{4,12},{6,14},{8,0},{10,2},{12,4},{14,6},{16,24},{18,... | collective-permute-start | bytes 122888 | tf_op jit(solution)/shard_map/ppermute | solution.py:319
  68.6 4.1 %collective-permute-start.12 = (bf16[160,128]{1,0:T(8,128)(2,1)S(1)}, bf16[160,128]{1,0:T(8,128)(2,1)S(1)}, u32[]{:S(2)}, u32[]{:S(2)}) collective-permute-start(bf16[160,128]{1,0:T(8,128)(2,1)S(1)} %get-tuple-element.147), channel_id=1, source_target_pairs={{0,2},{2,0},{4,6},{6,4},{8,10},{10,8},{12,14},{14,12},{16,18},{18,... | collective-permute-start | bytes 122888 | tf_op jit(solution)/shard_map/ppermute | solution.py:319
  68.7 4.1 %collective-permute-start.13 = (bf16[160,128]{1,0:T(8,128)(2,1)S(1)}, bf16[160,128]{1,0:T(8,128)(2,1)S(1)}, u32[]{:S(2)}, u32[]{:S(2)}) collective-permute-start(bf16[160,128]{1,0:T(8,128)(2,1)S(1)} %get-tuple-element.148), channel_id=1, source_target_pairs={{0,4},{2,6},{4,0},{6,2},{8,12},{10,14},{12,8},{14,10},{16,20},{18,... | collective-permute-start | bytes 122888 | tf_op jit(solution)/shard_map/ppermute | solution.py:319
  70.2 3.5 %collective-permute-start.14 = (bf16[160,128]{1,0:T(8,128)(2,1)S(1)}, bf16[160,128]{1,0:T(8,128)(2,1)S(1)}, u32[]{:S(2)}, u32[]{:S(2)}) collective-permute-start(bf16[160,128]{1,0:T(8,128)(2,1)S(1)} %get-tuple-element.149), channel_id=1, source_target_pairs={{0,6},{2,4},{4,2},{6,0},{8,14},{10,12},{12,10},{14,8},{16,22},{18,... | collective-permute-start | bytes 122888 | tf_op jit(solution)/shard_map/ppermute | solution.py:319
  70.5 3.2 %copy-start.7 = (f32[512]{0:T(512)S(1)}, f32[512]{0:T(512)}, u32[]{:S(2)}) copy-start(f32[512]{0:T(512)} %param.12) | copy-start | bytes 6148
  75.3 10.6 %collective-permute-start.17 = (bf16[256,1024]{1,0:T(8,128)(2,1)S(1)}, bf16[256,1024]{1,0:T(8,128)(2,1)S(1)}, u32[]{:S(2)}, u32[]{:S(2)}) collective-permute-start(bf16[256,1024]{1,0:T(8,128)(2,1)S(1)} %collective-permute-done.16.refs_1_), channel_id=1, source_target_pairs={{0,2},{2,0},{4,6},{6,4},{8,10},{10,8},{12,14},{14,12},{16,18},{18,... | collective-permute-start | bytes 1572872 | tf_op jit(solution)/shard_map/ppermute | solution.py:319
  75.5 9.8 %collective-permute-start.21 = (bf16[256,512]{1,0:T(8,128)(2,1)S(1)}, bf16[256,512]{1,0:T(8,128)(2,1)S(1)}, u32[]{:S(2)}, u32[]{:S(2)}) collective-permute-start(bf16[256,512]{1,0:T(8,128)(2,1)S(1)} %shard_map.105.own_ref), channel_id=1, source_target_pairs={{0,1},{1,0},{2,3},{3,2},{4,5},{5,4},{6,7},{7,6},{8,9},{9,8},{10,11... | collective-permute-start | bytes 786440 | tf_op jit(solution)/shard_map/ppermute | solution.py:411
  77.5 12.7 %collective-permute-start.20 = (bf16[256,512]{1,0:T(8,128)(2,1)S(1)}, bf16[256,512]{1,0:T(8,128)(2,1)S(1)}, u32[]{:S(2)}, u32[]{:S(2)}) collective-permute-start(bf16[256,512]{1,0:T(8,128)(2,1)S(1)} %shard_map.106.own_ref), channel_id=1, source_target_pairs={{0,1},{1,0},{2,3},{3,2},{4,5},{5,4},{6,7},{7,6},{8,9},{9,8},{10,11... | collective-permute-start | bytes 786440 | tf_op jit(solution)/shard_map/ppermute | solution.py:411
  80.7 15.2 %collective-permute-start.19 = (bf16[256,512]{1,0:T(8,128)(2,1)S(1)}, bf16[256,512]{1,0:T(8,128)(2,1)S(1)}, u32[]{:S(2)}, u32[]{:S(2)}) collective-permute-start(bf16[256,512]{1,0:T(8,128)(2,1)S(1)} %shard_map.107.own_ref), channel_id=1, source_target_pairs={{0,1},{1,0},{2,3},{3,2},{4,5},{5,4},{6,7},{7,6},{8,9},{9,8},{10,11... | collective-permute-start | bytes 786440 | tf_op jit(solution)/shard_map/ppermute | solution.py:411
  82.5 16.2 %collective-permute-start.18 = (bf16[128,512]{1,0:T(8,128)(2,1)S(1)}, bf16[128,512]{1,0:T(8,128)(2,1)S(1)}, u32[]{:S(2)}, u32[]{:S(2)}) collective-permute-start(bf16[128,512]{1,0:T(8,128)(2,1)S(1)} %shard_map.108.own_ref), channel_id=1, source_target_pairs={{0,1},{1,0},{2,3},{3,2},{4,5},{5,4},{6,7},{7,6},{8,9},{9,8},{10,11... | collective-permute-start | bytes 393224 | tf_op jit(solution)/shard_map/ppermute | solution.py:411
  85.3 15.6 %collective-permute-start.15 = (bf16[128,512]{1,0:T(8,128)(2,1)S(1)}, bf16[128,512]{1,0:T(8,128)(2,1)S(1)}, u32[]{:S(2)}, u32[]{:S(2)}) collective-permute-start(bf16[128,512]{1,0:T(8,128)(2,1)S(1)} %shard_map.109.own_ref), channel_id=1, source_target_pairs={{0,1},{1,0},{2,3},{3,2},{4,5},{5,4},{6,7},{7,6},{8,9},{9,8},{10,11... | collective-permute-start | bytes 393224 | tf_op jit(solution)/shard_map/ppermute | solution.py:411

commit v7 on v6

--- a/solution.py
+++ b/solution.py
@@ -106,15 +106,15 @@
         ref[:, cols] = x.astype(BF16) * jnp.asarray(scale, BF16)
 
 
-def block_kernel(j_ref, mean_ref, conv_ref, turn_ref, weight_ref, w_ref, *refs, n, heads, extra, others, sends):
+def block_kernel(j_ref, mean_ref, conv_ref, turn_ref, weight_ref, w_ref, *refs, n, heads, extra, others):
     xs, refs = refs[:n], refs[n:]
     prev_ref = None
     if not extra:
         prev_ref, refs = refs[0], refs[1:]
     other_refs, refs = refs[:others], refs[others:]
     k_ref, v_ref, s_ref, refs = *refs[:3], refs[3:]
-    send_refs, ext_ref = refs[:sends], refs[-1]
-    q_ref, wq_ref, wk_ref, halo_ref = (None,) * 4 if others else refs[:4]
+    ext_ref = refs[-1]
+    sum_ref, q_ref, wq_ref, wk_ref, halo_ref = (refs[0],) + (None,) * 4 if others else (None, *refs[:4])
     rows = v_ref.shape[0]
     qk_width, width = k_ref.shape[1], v_ref.shape[1]
     me = j_ref[0]
@@ -158,12 +158,11 @@
             second = got[:, (2 * p + 1) * FQK : (2 * p + 2) * FQK, cols]
             state = jnp.where(low_half, first, second).reshape(FEATS, LANES)
             s_ref[g * in_group * DV // LANES + p] = state * weight_ref[...]
-    for r in range(sends):
-        pair = jnp.bitwise_xor(j_ref[1], r)
-        total = s_ref[pair]
+    for p in range(heads * DV // LANES if others else 0):
+        total = s_ref[p]
         for ref in other_refs:
-            total = total + ref[pair]
-        send_refs[r][...] = total.astype(BF16)
+            total = total + ref[p]
+        sum_ref[p] = total.astype(BF16)
 
     if not others:
         halo_ref[0:EDGE, :] = raw[raw.shape[0] - EDGE :]
@@ -227,7 +226,7 @@
     band = inside.astype(F32).astype(BF16)
     first_band = band
     if first:
-        first_band = (inside & (col >= jnp.where(a_ref[2] == 0, WIN, 0))).astype(F32).astype(BF16)
+        first_band = (inside & (col >= jnp.where(a_ref[1] == 0, WIN, 0))).astype(F32).astype(BF16)
     ones = jnp.ones((span, LANES), BF16)
     q = q * jnp.asarray(1.0 / FQK**0.5, BF16)
     for p in range(heads * DV // LANES):
@@ -253,13 +252,8 @@
             win_ref[here, cols] = got[:, :LANES] / got[:, LANES:]
 
 
-def finish_kernel(a_ref, mean_ref, gain_ref, *refs, heads, before):
-    pairs = heads * DV // LANES
-    prior_refs, refs = refs[:pairs], refs[pairs:]
-    states, (phi_ref, lin_ref, win_ref, mix_ref, held_ref) = refs[:before], refs[before:]
-    rows = phi_ref.shape[0]
-    for r in range(pairs):
-        held_ref[r] = prior_refs[r][...].astype(F32)
+def finish_kernel(_, mean_ref, gain_ref, prior_ref, *refs, heads, before):
+    states, (phi_ref, lin_ref, win_ref, mix_ref) = refs[:before], refs[before:]
     in_group, lanes, slots = feature_layout(heads)
     in_pairs = in_group * DV // LANES
     low_half = lax.broadcasted_iota(jnp.int32, (SHIFTS + 1, FQK, LANES), 2) < DV
@@ -267,7 +261,7 @@
         columns = []
         for p in range(in_pairs):
             pair = g * in_pairs + p
-            state = held_ref[jnp.bitwise_xor(a_ref[1], pair)]
+            state = prior_ref[pair].astype(F32)
             for ref in states:
                 state = state + ref[pair]
             state = state.reshape(SHIFTS + 1, FQK, LANES)
@@ -300,7 +294,7 @@
         for i in range(parts):
             ref = weights[r * parts + i]
             depth = ref.shape[0]
-            at = depth * (jnp.bitwise_xor(a_ref[2] % 2, i) if parts > 1 else 0)
+            at = depth * (jnp.bitwise_xor(a_ref[1] % 2, i) if parts > 1 else 0)
             got = jnp.dot(m_ref[:, pl.ds(pl.multiple_of(at, depth), depth)], ref[...], preferred_element_type=F32)
             part = got if part is None else part + got
         total = total + part.astype(BF16).astype(F32)
@@ -319,58 +313,57 @@
     return lax.ppermute(value, axis, [(i, i ^ flip) for i in range(count)])
 
 
-def plane_kernel(a_ref, *refs):
-    helds, plane_ref, ahead_refs = refs[:PLANE], refs[PLANE], refs[PLANE + 1 :]
-    place = a_ref[1]
-    held = [ref[...].astype(F32) for ref in helds]
-    plane_ref[...] = (held[0] + held[1] + held[2] + held[3]).astype(BF16)
-    for r in range(PLANE):
-        total = jnp.zeros_like(held[0])
-        for s in range(PLANE):
-            before = jnp.bitwise_xor(place, s) < jnp.bitwise_xor(place, r)
-            total = total + held[s] * before.astype(F32)
-        ahead_refs[r][...] = total
-
-
-def earlier_kernel(a_ref, *refs, planes):
-    ahead_refs, plane_refs, back_refs = refs[:PLANE], refs[PLANE : PLANE + planes], refs[PLANE + planes :]
-    mine = a_ref[2] // PLANE
-    earlier = jnp.zeros(ahead_refs[0].shape, F32)
-    for d, ref in enumerate(plane_refs, 1):
-        before = jnp.bitwise_xor(mine, d) < mine
-        earlier = earlier + ref[...].astype(F32) * before.astype(F32)
-    for r in range(PLANE):
-        back_refs[r][...] = (ahead_refs[r][...] + earlier).astype(BF16)
+def plane_kernel(_, held_ref, plane_ref, ahead_ref):
+    total = jnp.zeros(held_ref.shape[1:], F32)
+    for p in range(PLANE):
+        ahead_ref[p] = total
+        total = total + held_ref[p].astype(F32)
+    for z in range(plane_ref.shape[0]):
+        plane_ref[z] = total.astype(BF16)
+
+
+def earlier_kernel(a_ref, ahead_ref, plane_ref, back_ref):
+    mine = a_ref[1] // PLANE
+    earlier = jnp.zeros(ahead_ref.shape[1:], F32)
+    for z in range(plane_ref.shape[0]):
+        earlier = earlier + plane_ref[z].astype(F32) * (mine > z).astype(F32)
+    for p in range(PLANE):
+        back_ref[p] = (ahead_ref[p] + earlier).astype(BF16)
 
 
 def after(value, earlier):
     return lax.optimization_barrier((value, earlier))[0]
 
 
-def prior_in_planes(held, places, beside):
+def swap_all(value, groups):
+    return lax.all_to_all(value, "ctx", 0, 0, axis_index_groups=groups, tiled=True)
+
+
+def prior_in_planes(sums, places, beside):
     ctx = lax.axis_size("ctx")
+    planes = ctx // PLANE
     whole = pl.BlockSpec(memory_space=pltpu.VMEM)
     scalar = pl.BlockSpec(memory_space=pltpu.SMEM)
-    narrow = jax.ShapeDtypeStruct((FEATS, LANES), BF16)
-    wide = jax.ShapeDtypeStruct((FEATS, LANES), F32)
-    plane, *ahead = call(
+    in_plane = [list(range(z * PLANE, (z + 1) * PLANE)) for z in range(planes)]
+    across = [list(range(p, ctx, PLANE)) for p in range(PLANE)]
+    plane, ahead = call(
         plane_kernel,
-        [narrow] + [wide] * PLANE,
-        in_specs=[scalar] + [whole] * PLANE,
-        out_specs=[whole] * (1 + PLANE),
+        [
+            jax.ShapeDtypeStruct((planes, FEATS, LANES), BF16),
+            jax.ShapeDtypeStruct((PLANE, FEATS, LANES), F32),
+        ],
+        in_specs=[scalar, whole],
+        out_specs=[whole] * 2,
         vmem=4 << 20,
-    )(after(places, beside[0]), *held)
-    earlier = []
-    for d in range(1, ctx // PLANE):
-        earlier.append(exchange(plane, "ctx", d * PLANE))
+    )(after(places, beside[0]), swap_all(sums, in_plane))
     back = call(
-        functools.partial(earlier_kernel, planes=len(earlier)),
-        [narrow] * PLANE,
-        in_specs=[scalar] + [whole] * (PLANE + len(earlier)),
-        out_specs=[whole] * PLANE,
+        earlier_kernel,
+        jax.ShapeDtypeStruct((PLANE, FEATS, LANES), BF16),
+        in_specs=[scalar] + [whole] * 2,
+        out_specs=whole,
         vmem=4 << 20,
-    )(after(places, beside[1]), *ahead, *earlier)
-    return [back[0]] + [exchange(back[r], "ctx", r) for r in range(1, PLANE)]
+    )(after(places, beside[1]), ahead, swap_all(plane, across))
+    return swap_all(back, in_plane)
 
 
 def prior_by_doubling(total, position):
@@ -382,7 +375,7 @@
         prior = prior + jnp.where((position & bit) != 0, got, 0.0)
         total = total + got
         bit *= 2
-    return [prior[p].astype(BF16) for p in range(total.shape[0])]
+    return prior.astype(BF16)
 
 
 def per_device(hidden_in, proj_weight, conv_weight, norm_gain, out_weight):
@@ -395,8 +388,8 @@
     heads = out_weight.shape[0] // DV
     width = heads * DV
     pairs = width // LANES
-    in_planes = pairs == PLANE and ctx % PLANE == 0 and ctx & (ctx - 1) == 0
-    places = jnp.stack([me, position % PLANE if in_planes else jnp.zeros_like(position), position])
+    in_planes = pairs == PLANE and ctx % PLANE == 0
+    places = jnp.stack([me, position])
     hidden_in, places = lax.optimization_barrier((hidden_in, places))
     step = row_count // 8
     blocks = [(0, 2 * step), (2 * step, 2 * step), (4 * step, step), (5 * step, step), (6 * step, 2 * step)]
@@ -437,7 +430,7 @@
                 num_scalar_prefetch=1,
                 grid=(1,),
                 in_specs=[
-                    pl.BlockSpec((share, cols), functools.partial(lambda i, a, r: (a[2] % out_parts, (a[0] + r) % n), r=r))
+                    pl.BlockSpec((share, cols), functools.partial(lambda i, a, r: (a[1] % out_parts, (a[0] + r) % n), r=r))
                 ],
                 out_specs=pl.BlockSpec((share, cols), lambda i, a: (0, 0)),
             ),
@@ -463,11 +456,10 @@
     def do_block(b, prev, behind, others=()):
         rows = blocks[b][1]
         extra = EDGE if prev is None else 0
-        sends = PLANE if in_planes and others else 0
         tokens = places if behind is None else after(places, behind)
         shapes = bf16(rows, qk_width, width) + [jax.ShapeDtypeStruct((pairs, FEATS, LANES), F32)]
         if others:
-            shapes += bf16(FEATS, LANES) * sends
+            shapes.append(jax.ShapeDtypeStruct((pairs, FEATS, LANES), BF16))
         else:
             shapes += bf16(rows, qk_width, width, width) + bf16(HALO, width)
         operands = [tokens, means, conv_weight, turn_rows, weight, arranged, *pieces[b]]
@@ -476,7 +468,7 @@
         operands += others
         return call(
             functools.partial(
-                block_kernel, n=n, heads=heads, extra=extra, others=len(others), sends=sends
+                block_kernel, n=n, heads=heads, extra=extra, others=len(others)
             ),
             shapes,
             in_specs=[scalar] + [whole] * (len(operands) - 1),
@@ -495,7 +487,7 @@
             vmem=32 << 20,
         )(places, means, arranged, v, *pieces[b])
 
-    def attend(b, prev):
+    def attend(b, prev, places=places):
         rows = blocks[b][1]
         k, v, _, q, wq, wk, _ = done[b]
         return call(
@@ -504,7 +496,7 @@
             in_specs=[scalar] + [whole] * 7,
             out_specs=[whole] * 3,
             scratch_shapes=[pltpu.VMEM((WIN + rows, width), BF16)] * 2,
-            flops=4850 * 10**6 if b == last else 1,
+            flops=1,
             vmem=16 << 20,
         )(places, turn, prev, q, k, v, wq, wk)
 
@@ -515,20 +507,18 @@
     for b in range(last - 1):
         done[b] = do_block(b, prevs[b], attended[b - 1][1] if b else None)
         prevs[b + 1] = done[b][6]
-        attended[b] = attend(b, prevs[b])
+        attended[b] = attend(b, prevs[b], after(places, picked[0]) if b == 0 else places)
     b = last - 1
-    k, v, state, *sends = do_block(b, prevs[b], attended[b - 1][1], [done[c][2] for c in (last, *range(b))])
+    k, v, state, sums = do_block(b, prevs[b], attended[b - 1][1], [done[c][2] for c in (last, *range(b))])
     done[b] = (k, v, state, *do_queries(b, v))
     prevs[last] = done[b][6]
     for b in (last - 1, last):
         attended[b] = attend(b, prevs[b])
-    held = sends[:1] + [exchange(sends[r], "ctx", r) for r in range(1, len(sends))]
-    mark = done[last - 1][6]
-    fetched = [from_head(after(block, mark), r) for r, block in enumerate(picked, 1)]
+    fetched = [from_head(after(block, done[last - 1][6]), r) for r, block in enumerate(picked, 1)]
     if in_planes:
-        priors = prior_in_planes(held, places, [done[last - 1][6], attended[last - 1][1]])
+        prior = prior_in_planes(sums, places, [done[last - 1][6], attended[last - 1][1]])
     else:
-        priors = prior_by_doubling(sum(done[b][2] for b in range(last + 1)), position)
+        prior = prior_by_doubling(sum(done[b][2] for b in range(last + 1)), position)
 
     result = None
     out_rows = []
@@ -538,11 +528,10 @@
         mixed = call(
             functools.partial(finish_kernel, heads=heads, before=b),
             jax.ShapeDtypeStruct((rows, width), BF16),
-            in_specs=[scalar] + [whole] * (2 + pairs + b + 3),
+            in_specs=[scalar] + [whole] * (3 + b + 3),
             out_specs=whole,
-            scratch_shapes=[pltpu.VMEM((pairs, FEATS, LANES), F32)],
             vmem=16 << 20,
-        )(after(places, mixed), means, gain, *priors, *[done[c][2] for c in range(b)], *attended[b])
+        )(after(places, mixed), means, gain, prior, *[done[c][2] for c in range(b)], *attended[b])
         others = [from_head(mixed, r) for r in range(1, n)]
         if not out_rows:
             for got in fetched:

time: 103 us -> 136 us (1.32)
  local copies, waits for them, and re-layouts: 6.53 us -> 38.9 us
  waiting for transfers between devices: 20.5 us -> 15.4 us
  starting transfers between devices: 24.2 us -> 27.7 us
    unnamed x16 -> x142, local copies, waits for them, and re-layouts: 3.11 us -> 35.5 us
    all_to_all x0 -> x3, starting transfers between devices: none -> 11.6 us  [swap_all(): lax.all_to_all(value, 'ctx', 0, 0, axis_index_groups=groups, tiled=True)]
    ppermute x10 -> x1, starting transfers between devices: 8.75 us -> 0.53 us  [exchange(): return lax.ppermute(value, axis, [(i, i ^ flip) for i in range(count)])]
    ppermute x11, waiting for transfers between devices: 16.9 us -> 10.4 us  [from_head(): return lax.ppermute(value, 'head', [(i, (i + by) % n) for i in range(n)])]
    all_to_all x0 -> x3, waiting for transfers between devices: none -> 4.95 us  [swap_all(): lax.all_to_all(value, 'ctx', 0, 0, axis_index_groups=groups, tiled=True)]
    ppermute x10 -> x1, waiting for transfers between devices: 3.63 us -> 0.01 us  [exchange(): return lax.ppermute(value, axis, [(i, i ^ flip) for i in range(count)])]
  transfers between devices with their start and end apart: 22 -> 16, of which waited for: 10 -> 7; matrix products, arithmetic and copies ran while one was open for 2% -> 2% of each run, Pallas kernels for 46% -> 35%
where the time goes in v7:
time: 136 us; the launch traced here: 135 us
  Pallas kernels  52.1 us (38%)
  local copies, waits for them, and re-layouts  38.9 us (29%)
  starting transfers between devices  27.7 us (20%)
  waiting for transfers between devices  15.4 us (11%)
    unnamed x142, local copies, waits for them, and re-layouts  35.5 us
    pallas_call x5, Pallas kernels, do_block(): call(functools.partial(block_kernel, n=n, heads=heads, extra=extra, other...  16.3 us
    ppermute x11, starting transfers between devices, from_head(): return lax.ppermute(value, 'head', [(i, (i + by) % n) for i in range(n)])  14.1 us
    all_to_all x3, starting transfers between devices, swap_all(): lax.all_to_all(value, 'ctx', 0, 0, axis_index_groups=groups, tiled=True)  11.6 us
    ppermute x11, waiting for transfers between devices, from_head(): return lax.ppermute(value, 'head', [(i, (i + by) % n) for i in range(n)])  10.4 us
    pallas_call x5, Pallas kernels, attend(): call(functools.partial(attend_kernel, heads=heads, first=b == 0), [jax.Sh...  9.77 us
    pallas_call x5, Pallas kernels, per_device(): call(functools.partial(output_kernel, n=n, offset=at, parts=out_parts), j...  9.61 us
    pallas_call x5, Pallas kernels, per_device(): call(functools.partial(finish_kernel, heads=heads, before=b), jax.ShapeDt...  6.9 us
  transfers between devices with their start and end apart: 16, of which 7 were waited for; matrix products, arithmetic and copies ran while one was open for 2% of the time, Pallas kernels for 35%

profile of v7, /device:TPU:0, one launch (start us, length us, event | category | flops | bytes accessed | tf_op | source)
XLA Modules:
  0.0 134.9 jit_solution(1391303523743124508)
XLA Ops:
  1.2 3.0 %collective-permute-start = (bf16[272,1024]{1,0:T(8,128)(2,1)S(1)}, bf16[272,1024]{1,0:T(8,128)(2,1)S(1)}, u32[]{:S(2)}, u32[]{:S(2)}) collective-permute-start(bf16[272,1024]{1,0:T(8,128)(2,1)S(1)} %slice.15.refs_0_), channel_id=1, source_target_pairs={{0,1},{1,0},{2,3},{3,2},{4,5},{5,4},{6,7},{7,6},{8,9},{9,8},{10,11... | collective-permute-start | bytes 1671176 | tf_op jit(solution)/shard_map/ppermute | solution.py:404
  5.6 2.0 %collective-permute-start.3 = (bf16[256,1024]{1,0:T(8,128)(2,1)S(1)}, bf16[256,1024]{1,0:T(8,128)(2,1)S(1)}, u32[]{:S(2)}, u32[]{:S(2)}) collective-permute-start(bf16[256,1024]{1,0:T(8,128)(2,1)S(1)} %get-tuple-element.89.refs_0_), channel_id=1, source_target_pairs={{0,1},{1,0},{2,3},{3,2},{4,5},{5,4},{6,7},{7,6},{8,9},{9,8},{10,11... | collective-permute-start | bytes 1572872 | tf_op jit(solution)/shard_map/ppermute | solution.py:404
  8.8 1.9 %collective-permute-start.5 = (bf16[128,1024]{1,0:T(8,128)(2,1)S(1)}, bf16[128,1024]{1,0:T(8,128)(2,1)S(1)}, u32[]{:S(2)}, u32[]{:S(2)}) collective-permute-start(bf16[128,1024]{1,0:T(8,128)(2,1)S(1)} %get-tuple-element.107.refs_0_), channel_id=1, source_target_pairs={{0,1},{1,0},{2,3},{3,2},{4,5},{5,4},{6,7},{7,6},{8,9},{9,8},{10,11... | collective-permute-start | bytes 786440 | tf_op jit(solution)/shard_map/ppermute | solution.py:404
  10.7 3.1 %copy-done.4 = bf16[2048,1792]{1,0:T(8,128)(2,1)S(1)} copy-done((bf16[2048,1792]{1,0:T(8,128)(2,1)S(1)}, bf16[2048,1792]{1,0:T(8,128)(2,1)}, u32[]{:S(2)}) %copy-start.4) | copy-done | bytes 7340056
  13.8 5.2 %shard_map.91.w_ref = bf16[2048,1792]{1,0:T(8,128)(2,1)S(1)} custom-call(bf16[2048,1792]{1,0:T(8,128)(2,1)S(1)} %copy-done.4), custom_call_target="tpu_custom_call" | custom-call | flops 1 | bytes 1 | tf_op jit(solution)/shard_map/pallas_call | solution.py:444
  19.1 3.9 %shard_map.93 = (bf16[256,128]{1,0:T(8,128)(2,1)S(1)}, bf16[256,512]{1,0:T(8,128)(2,1)S(1)}, f32[4,160,128]{2,1,0:T(8,128)S(1)}, bf16[256,128]{1,0:T(8,128)(2,1)...) custom-call(s32[2]{0:T(128)S(1)} %pad_add_fusion.a_ref.j_ref._, ...), custom_call_target="tpu_custom_call" | custom-call | flops 1 | bytes 1 | tf_op jit(solution)/shard_map/pallas_call | solution.py:469
  25.9 3.0 %collective-permute-done.2.refs_1_ = bf16[256,1024]{1,0:T(8,128)(2,1)S(1)} collective-permute-done((bf16[256,1024]{1,0:T(8,128)(2,1)S(1)}, bf16[256,1024]{1,0:T(8,128)(2,1)S(1)}, u32[]{:S(2)}, u32[]{:S(2)}) %collective-permute-start.2) | collective-permute-done | bytes 524320 | tf_op jit(solution)/shard_map/ppermute | solution.py:404
  28.9 3.9 %shard_map.94 = (bf16[256,128]{1,0:T(8,128)(2,1)S(1)}, bf16[256,512]{1,0:T(8,128)(2,1)S(1)}, f32[4,160,128]{2,1,0:T(8,128)S(1)}, bf16[256,128]{1,0:T(8,128)(2,1)...) custom-call(s32[2]{0:T(128)S(1)} %pad_add_fusion.a_ref.j_ref._, ...), custom_call_target="tpu_custom_call" | custom-call | flops 1 | bytes 1 | tf_op jit(solution)/shard_map/pallas_call | solution.py:469
  32.8 2.1 %shard_map.95 = (bf16[256,1280]{1,0:T(8,128)(2,1)S(1)}, f32[256,512]{1,0:T(8,128)S(1)}, f32[256,512]{1,0:T(8,128)S(1)}) custom-call(s32[2]{0:T(128)S(1)} %pad_add_fusion.a_ref.j_ref._, bf16[128,1280]{1,0:T(8,128)(2,1)S(1)} %copy-done.2, bf16[144,512]{1,0:T(8,128)(2,1)S(1)} %collective-permute-done.1.refs_2_.prev_ref, ...), custom_call_target="tpu_custom_call" | custom-call | flops 1 | bytes 1 | tf_op jit(solution)/shard_map/pallas_call | solution.py:493
  37.4 2.7 %collective-permute-done.3.refs_1_ = bf16[256,1024]{1,0:T(8,128)(2,1)S(1)} collective-permute-done((bf16[256,1024]{1,0:T(8,128)(2,1)S(1)}, bf16[256,1024]{1,0:T(8,128)(2,1)S(1)}, u32[]{:S(2)}, u32[]{:S(2)}) %collective-permute-start.3) | collective-permute-done | bytes 524320 | tf_op jit(solution)/shard_map/ppermute | solution.py:404
  40.1 3.9 %shard_map.96 = (bf16[256,128]{1,0:T(8,128)(2,1)S(1)}, bf16[256,512]{1,0:T(8,128)(2,1)S(1)}, f32[4,160,128]{2,1,0:T(8,128)S(1)}, bf16[256,128]{1,0:T(8,128)(2,1)...) custom-call(s32[2]{0:T(128)S(1)} %pad_add_fusion.a_ref.j_ref._, ...), custom_call_target="tpu_custom_call" | custom-call | flops 1 | bytes 1 | tf_op jit(solution)/shard_map/pallas_call | solution.py:469
  44.0 2.1 %shard_map.97 = (bf16[256,1280]{1,0:T(8,128)(2,1)S(1)}, f32[256,512]{1,0:T(8,128)S(1)}, f32[256,512]{1,0:T(8,128)S(1)}) custom-call(s32[2]{0:T(128)S(1)} %pad_add_fusion.a_ref.j_ref._, bf16[128,1280]{1,0:T(8,128)(2,1)S(1)} %copy-done.2, bf16[144,512]{1,0:T(8,128)(2,1)S(1)} %get-tuple-element.90.refs_2_.prev_ref, ...), custom_call_target="tpu_custom_call" | custom-call | flops 1 | bytes 1 | tf_op jit(solution)/shard_map/pallas_call | solution.py:493
  48.6 2.7 %shard_map.98 = (bf16[128,128]{1,0:T(8,128)(2,1)S(1)}, bf16[128,512]{1,0:T(8,128)(2,1)S(1)}, f32[4,160,128]{2,1,0:T(8,128)S(1)}, bf16[128,128]{1,0:T(8,128)(2,1)...) custom-call(s32[2]{0:T(128)S(1)} %pad_add_fusion.a_ref.j_ref._, ...), custom_call_target="tpu_custom_call" | custom-call | flops 1 | bytes 1 | tf_op jit(solution)/shard_map/pallas_call | solution.py:469
  51.3 1.7 %shard_map.99 = (bf16[128,1280]{1,0:T(8,128)(2,1)S(1)}, f32[128,512]{1,0:T(8,128)S(1)}, f32[128,512]{1,0:T(8,128)S(1)}) custom-call(s32[2]{0:T(128)S(1)} %pad_add_fusion.a_ref.j_ref._, bf16[128,1280]{1,0:T(8,128)(2,1)S(1)} %copy-done.2, bf16[144,512]{1,0:T(8,128)(2,1)S(1)} %get-tuple-element.91.refs_2_.prev_ref, ...), custom_call_target="tpu_custom_call" | custom-call | flops 1 | bytes 1 | tf_op jit(solution)/shard_map/pallas_call | solution.py:493
  55.2 1.9 %shard_map.100 = (bf16[128,128]{1,0:T(8,128)(2,1)S(1)}, bf16[128,512]{1,0:T(8,128)(2,1)S(1)}, f32[4,160,128]{2,1,0:T(8,128)S(1)}, bf16[4,160,128]{2,1,0:T(8,128)(2,1)S(1)}) custom-call(s32[2]{0:T(128)S(1)} %pad_add_fusion.a_ref.j_ref._, bf16[256,128]{1,0:T(8,128)(2,1)S(1)} %copy-done.3, f32[3,512]{1,0:T(4,128)S(1)} %copy-done.55, ...), custom_call_target="tpu_custom_call" | custom-call | flops 1 | bytes 1 | tf_op jit(solution)/shard_map/pallas_call | solution.py:469
  57.2 1.8 %shard_map.101 = (bf16[128,128]{1,0:T(8,128)(2,1)S(1)}, bf16[128,512]{1,0:T(8,128)(2,1)S(1)}, bf16[128,512]{1,0:T(8,128)(2,1)S(1)}, bf16[144,512]{1,0:T(8,128)(2,1)S(1)}) custom-call(s32[2]{0:T(128)S(1)} %pad_add_fusion.a_ref.j_ref._, bf16[256,128]{1,0:T(8,128)(2,1)S(1)} %copy-done.3, bf16[2048,1792]{1,0:T(8,128)(2,1)S(1)} %shard_map.91.w_ref, ...), custom_call_target="tpu_custom_call" | custom-call | flops 1 | bytes 1 | tf_op jit(solution)/shard_map/pallas_call | solution.py:482
  61.5 2.1 %collective-permute-start.7 = (bf16[256,1024]{1,0:T(8,128)(2,1)}, bf16[256,1024]{1,0:T(8,128)(2,1)S(1)}, u32[]{:S(2)}, u32[]{:S(2)}) collective-permute-start(bf16[256,1024]{1,0:T(8,128)(2,1)} %shard_map.92), channel_id=1, source_target_pairs={{0,1},{1,0},{2,3},{3,2},{4,5},{5,4},{6,7},{7,6},{8,9},{9,8},{10,11... | collective-permute-start | bytes 1572872 | tf_op jit(solution)/shard_map/ppermute | solution.py:404
  63.6 3.3 %all-to-all-start = ((bf16[4,160,128]{2,1,0:T(8,128)(2,1)}), bf16[4,160,128]{2,1,0:T(8,128)(2,1)S(1)}, u32[]{:S(2)}, u32[]{:S(2)}) async-start(bf16[4,160,128]{2,1,0:T(8,128)(2,1)} %copy-done.56), calls=%async_computation | async-start | bytes 327680 | tf_op jit(solution)/shard_map/all_to_all | solution.py:339
  67.0 4.9 %all-to-all-done.held_ref = bf16[4,160,128]{2,1,0:T(8,128)(2,1)S(1)} async-done(((bf16[4,160,128]{2,1,0:T(8,128)(2,1)}), bf16[4,160,128]{2,1,0:T(8,128)(2,1)S(1)}, u32[]{:S(2)}, u32[]{:S(2)}) %all-to-all-start) | async-done | bytes 163872 | tf_op jit(solution)/shard_map/all_to_all | solution.py:339
  73.9 4.9 %all-to-all-start.1 = ((bf16[4,160,128]{2,1,0:T(8,128)(2,1)}), bf16[4,160,128]{2,1,0:T(8,128)(2,1)S(1)}, u32[]{:S(2)}, u32[]{:S(2)}) async-start(bf16[4,160,128]{2,1,0:T(8,128)(2,1)} %copy-done.57), calls=%async_computation.1 | async-start | bytes 327680 | tf_op jit(solution)/shard_map/all_to_all | solution.py:339
  83.1 1.7 %shard_map.103 = (bf16[128,1280]{1,0:T(8,128)(2,1)S(1)}, f32[128,512]{1,0:T(8,128)S(1)}, f32[128,512]{1,0:T(8,128)S(1)}) custom-call(s32[2]{0:T(128)S(1)} %pad_add_fusion.a_ref.j_ref._, bf16[128,1280]{1,0:T(8,128)(2,1)S(1)} %copy-done.2, bf16[144,512]{1,0:T(8,128)(2,1)S(1)} %copy-done.18, bf16[128,128]{1,0:T(8,128)(2,1)S(1)} %copy-done.70, ...), custom_call_target="tpu_custom_call" | custom-call | flops 1 | bytes 1 | tf_op jit(solution)/shard_map/pallas_call | solution.py:493
  89.2 3.3 %all-to-all-start.2 = ((bf16[4,160,128]{2,1,0:T(8,128)(2,1)}), bf16[4,160,128]{2,1,0:T(8,128)(2,1)S(1)}, u32[]{:S(2)}, u32[]{:S(2)}) async-start(bf16[4,160,128]{2,1,0:T(8,128)(2,1)} %copy-done.12), calls=%async_computation.2 | async-start | bytes 327680 | tf_op jit(solution)/shard_map/all_to_all | solution.py:339
  98.0 2.1 %shard_map.102 = (bf16[256,1280]{1,0:T(8,128)(2,1)S(1)}, f32[256,512]{1,0:T(8,128)S(1)}, f32[256,512]{1,0:T(8,128)S(1)}) custom-call(s32[2]{0:T(128)S(1)} %pad_add_fusion.a_ref.j_ref._, bf16[128,1280]{1,0:T(8,128)(2,1)S(1)} %copy-done.2, bf16[144,512]{1,0:T(8,128)(2,1)S(1)} %copy-done.59, bf16[256,128]{1,0:T(8,128)(2,1)S(1)} %copy-done.67, ...), custom_call_target="tpu_custom_call" | custom-call | flops 1 | bytes 1 | tf_op jit(solution)/shard_map/pallas_call | solution.py:493
  112.0 1.6 %collective-permute-start.11 = (bf16[256,512]{1,0:T(8,128)(2,1)S(1)}, bf16[256,512]{1,0:T(8,128)(2,1)S(1)}, u32[]{:S(2)}, u32[]{:S(2)}) collective-permute-start(bf16[256,512]{1,0:T(8,128)(2,1)S(1)} %shard_map.107.own_ref), channel_id=1, source_target_pairs={{0,1},{1,0},{2,3},{3,2},{4,5},{5,4},{6,7},{7,6},{8,9},{9,8},{10,11... | collective-permute-start | bytes 786440 | tf_op jit(solution)/shard_map/ppermute | solution.py:404
  113.6 1.5 %shard_map.108.own_ref = bf16[256,512]{1,0:T(8,128)(2,1)S(1)} custom-call(s32[2]{0:T(128)S(1)} %pad_add_fusion.a_ref.j_ref._, bf16[256,128]{1,0:T(8,128)(2,1)S(1)} %copy-done.3, f32[1,512]{1,0:T(1,128)S(1)} %bitcast.5, bf16[4,160,128]{2,1,0:T(8,128)(2,1)S(1)} %all-to-all-done.2.prior_ref, f32[4,160,128]{2,1,0:T(8,128)S(1)} %get-tuple-element.110.refs_4_.refs_0_, ...), custom_call_target="tpu_custom_call" | custom-call | flops 1 | bytes 1 | tf_op jit(solution)/shard_map/pallas_call | solution.py:528
  116.9 1.6 %collective-permute-start.9 = (bf16[128,512]{1,0:T(8,128)(2,1)S(1)}, bf16[128,512]{1,0:T(8,128)(2,1)S(1)}, u32[]{:S(2)}, u32[]{:S(2)}) collective-permute-start(bf16[128,512]{1,0:T(8,128)(2,1)S(1)} %shard_map.109.own_ref), channel_id=1, source_target_pairs={{0,1},{1,0},{2,3},{3,2},{4,5},{5,4},{6,7},{7,6},{8,9},{9,8},{10,11... | collective-permute-start | bytes 393224 | tf_op jit(solution)/shard_map/ppermute | solution.py:404
  120.3 2.1 %shard_map.111.refs_3_ = bf16[1024,1024]{1,0:T(8,128)(2,1)} custom-call(s32[2]{0:T(128)S(1)} %pad_add_fusion.a_ref.j_ref._, bf16[256,512]{1,0:T(8,128)(2,1)S(1)} %shard_map.106.own_ref, bf16[512,2048]{1,0:T(8,128)(2,1)S(1)} %copy-done, bf16[256,512]{1,0:T(8,128)(2,1)S(1)} %collective-permute-done.12.refs_0_, ...), custom_call_target="tpu_custom_call" | custom-call | flops 1 | bytes 1 | tf_op jit(solution)/shard_map/pallas_call | solution.py:546
  122.6 2.1 %shard_map.112.refs_3_ = bf16[1024,1024]{1,0:T(8,128)(2,1)} custom-call(s32[2]{0:T(128)S(1)} %pad_add_fusion.a_ref.j_ref._, bf16[256,512]{1,0:T(8,128)(2,1)S(1)} %shard_map.107.own_ref, bf16[512,2048]{1,0:T(8,128)(2,1)S(1)} %copy-done, bf16[256,512]{1,0:T(8,128)(2,1)S(1)} %collective-permute-done.11.refs_0_, ...), custom_call_target="tpu_custom_call", output_to_operand_aliasing={{}: (6, {})} | custom-call | flops 1 | bytes 1 | tf_op jit(solution)/shard_map/pallas_call | solution.py:546
  124.7 3.5 %collective-permute-done.10.refs_0_ = bf16[256,512]{1,0:T(8,128)(2,1)S(1)} collective-permute-done((bf16[256,512]{1,0:T(8,128)(2,1)S(1)}, bf16[256,512]{1,0:T(8,128)(2,1)S(1)}, u32[]{:S(2)}, u32[]{:S(2)}) %collective-permute-start.10) | collective-permute-done | bytes 262176 | tf_op jit(solution)/shard_map/ppermute | solution.py:404
  128.3 2.1 %shard_map.113.refs_3_ = bf16[1024,1024]{1,0:T(8,128)(2,1)} custom-call(s32[2]{0:T(128)S(1)} %pad_add_fusion.a_ref.j_ref._, bf16[256,512]{1,0:T(8,128)(2,1)S(1)} %shard_map.108.own_ref, bf16[512,2048]{1,0:T(8,128)(2,1)S(1)} %copy-done, bf16[256,512]{1,0:T(8,128)(2,1)S(1)} %collective-permute-done.10.refs_0_, ...), custom_call_target="tpu_custom_call", output_to_operand_aliasing={{}: (6, {})} | custom-call | flops 1 | bytes 1 | tf_op jit(solution)/shard_map/pallas_call | solution.py:546
  131.1 1.7 %shard_map.114.refs_3_ = bf16[1024,1024]{1,0:T(8,128)(2,1)} custom-call(s32[2]{0:T(128)S(1)} %pad_add_fusion.a_ref.j_ref._, bf16[128,512]{1,0:T(8,128)(2,1)S(1)} %shard_map.109.own_ref, bf16[512,2048]{1,0:T(8,128)(2,1)S(1)} %copy-done, bf16[128,512]{1,0:T(8,128)(2,1)S(1)} %collective-permute-done.9.refs_0_, ...), custom_call_target="tpu_custom_call", output_to_operand_aliasing={{}: (6, {})} | custom-call | flops 1 | bytes 1 | tf_op jit(solution)/shard_map/pallas_call | solution.py:546
  133.0 1.7 %shard_map.115 = bf16[1024,1024]{1,0:T(8,128)(2,1)} custom-call(s32[2]{0:T(128)S(1)} %pad_add_fusion.a_ref.j_ref._, bf16[128,512]{1,0:T(8,128)(2,1)S(1)} %shard_map.110.own_ref, bf16[512,2048]{1,0:T(8,128)(2,1)S(1)} %copy-done, bf16[128,512]{1,0:T(8,128)(2,1)S(1)} %collective-permute-done.6.refs_0_, ...), custom_call_target="tpu_custom_call", output_to_operand_aliasing={{}: (6, {})} | custom-call | flops 1 | bytes 1 | tf_op jit(solution)/shard_map/pallas_call | solution.py:546
  (171 shorter events, 48.9 us)
Async XLA Ops:
  1.2 17.9 %collective-permute-start = (bf16[272,1024]{1,0:T(8,128)(2,1)S(1)}, bf16[272,1024]{1,0:T(8,128)(2,1)S(1)}, u32[]{:S(2)}, u32[]{:S(2)}) collective-permute-start(bf16[272,1024]{1,0:T(8,128)(2,1)S(1)} %slice.15.refs_0_), channel_id=1, source_target_pairs={{0,1},{1,0},{2,3},{3,2},{4,5},{5,4},{6,7},{7,6},{8,9},{9,8},{10,11... | collective-permute-start | bytes 1671176 | tf_op jit(solution)/shard_map/ppermute | solution.py:404
  5.5 23.4 %collective-permute-start.2 = (bf16[256,1024]{1,0:T(8,128)(2,1)S(1)}, bf16[256,1024]{1,0:T(8,128)(2,1)S(1)}, u32[]{:S(2)}, u32[]{:S(2)}) collective-permute-start(bf16[256,1024]{1,0:T(8,128)(2,1)S(1)} %get-tuple-element.81.refs_0_), channel_id=1, source_target_pairs={{0,1},{1,0},{2,3},{3,2},{4,5},{5,4},{6,7},{7,6},{8,9},{9,8},{10,11... | collective-permute-start | bytes 1572872 | tf_op jit(solution)/shard_map/ppermute | solution.py:404
  5.6 34.6 %collective-permute-start.3 = (bf16[256,1024]{1,0:T(8,128)(2,1)S(1)}, bf16[256,1024]{1,0:T(8,128)(2,1)S(1)}, u32[]{:S(2)}, u32[]{:S(2)}) collective-permute-start(bf16[256,1024]{1,0:T(8,128)(2,1)S(1)} %get-tuple-element.89.refs_0_), channel_id=1, source_target_pairs={{0,1},{1,0},{2,3},{3,2},{4,5},{5,4},{6,7},{7,6},{8,9},{9,8},{10,11... | collective-permute-start | bytes 1572872 | tf_op jit(solution)/shard_map/ppermute | solution.py:404
  8.6 40.0 %collective-permute-start.4 = (bf16[128,1024]{1,0:T(8,128)(2,1)S(1)}, bf16[128,1024]{1,0:T(8,128)(2,1)S(1)}, u32[]{:S(2)}, u32[]{:S(2)}) collective-permute-start(bf16[128,1024]{1,0:T(8,128)(2,1)S(1)} %get-tuple-element.99.refs_0_), channel_id=1, source_target_pairs={{0,1},{1,0},{2,3},{3,2},{4,5},{5,4},{6,7},{7,6},{8,9},{9,8},{10,11... | collective-permute-start | bytes 786440 | tf_op jit(solution)/shard_map/ppermute | solution.py:404
  8.8 10.3 %copy-start.1 = (bf16[1408,128]{1,0:T(8,128)(2,1)S(1)}, bf16[1408,128]{1,0:T(8,128)(2,1)}, u32[]{:S(2)}) copy-start(bf16[1408,128]{1,0:T(8,128)(2,1)} %constant.17.clone.turn_ref) | copy-start | bytes 1081348
  8.8 10.3 %copy-start.3 = (bf16[256,128]{1,0:T(8,128)(2,1)S(1)}, bf16[256,128]{1,0:T(8,128)(2,1)}, u32[]{:S(2)}) copy-start(bf16[256,128]{1,0:T(8,128)(2,1)} %constant.19.clone.mean_ref) | copy-start | bytes 196612
  8.8 46.4 %collective-permute-start.5 = (bf16[128,1024]{1,0:T(8,128)(2,1)S(1)}, bf16[128,1024]{1,0:T(8,128)(2,1)S(1)}, u32[]{:S(2)}, u32[]{:S(2)}) collective-permute-start(bf16[128,1024]{1,0:T(8,128)(2,1)S(1)} %get-tuple-element.107.refs_0_), channel_id=1, source_target_pairs={{0,1},{1,0},{2,3},{3,2},{4,5},{5,4},{6,7},{7,6},{8,9},{9,8},{10,11... | collective-permute-start | bytes 786440 | tf_op jit(solution)/shard_map/ppermute | solution.py:404
  19.0 5.5 %copy-start = (bf16[512,2048]{1,0:T(8,128)(2,1)S(1)}, bf16[512,2048]{1,0:T(8,128)(2,1)}, u32[]{:S(2)}) copy-start(bf16[512,2048]{1,0:T(8,128)(2,1)} %w_ref.13) | copy-start | bytes 6291460
  23.0 5.9 %copy-start.41 = (bf16[256,512]{1,0:T(8,128)(2,1)}, bf16[256,512]{1,0:T(8,128)(2,1)S(1)}, u32[]{:S(2)}) copy-start(bf16[256,512]{1,0:T(8,128)(2,1)S(1)} %get-tuple-element.117.v_ref) | copy-start | bytes 786436
  23.0 5.9 %copy-start.43 = (bf16[256,512]{1,0:T(8,128)(2,1)}, bf16[256,512]{1,0:T(8,128)(2,1)S(1)}, u32[]{:S(2)}) copy-start(bf16[256,512]{1,0:T(8,128)(2,1)S(1)} %get-tuple-element.118.wq_ref) | copy-start | bytes 786436
  23.0 5.9 %copy-start.45 = (bf16[256,512]{1,0:T(8,128)(2,1)}, bf16[256,512]{1,0:T(8,128)(2,1)S(1)}, u32[]{:S(2)}) copy-start(bf16[256,512]{1,0:T(8,128)(2,1)S(1)} %get-tuple-element.119.wk_ref) | copy-start | bytes 786436
  23.0 9.8 %copy-start.64 = (bf16[256,128]{1,0:T(8,128)(2,1)}, bf16[256,128]{1,0:T(8,128)(2,1)S(1)}, u32[]{:S(2)}) copy-start(bf16[256,128]{1,0:T(8,128)(2,1)S(1)} %get-tuple-element.116.k_ref) | copy-start | bytes 196612
  23.0 9.8 %copy-start.66 = (bf16[256,128]{1,0:T(8,128)(2,1)}, bf16[256,128]{1,0:T(8,128)(2,1)S(1)}, u32[]{:S(2)}) copy-start(bf16[256,128]{1,0:T(8,128)(2,1)S(1)} %get-tuple-element.115.q_ref) | copy-start | bytes 196612
  23.1 5.8 %collective-permute-start.1 = (bf16[144,512]{1,0:T(8,128)(2,1)S(1)}, bf16[144,512]{1,0:T(8,128)(2,1)S(1)}, u32[]{:S(2)}, u32[]{:S(2)}) collective-permute-start(bf16[144,512]{1,0:T(8,128)(2,1)S(1)} %get-tuple-element.80), channel_id=1, source_target_pairs={{0,2},{2,4},{4,6},{6,8},{8,10},{10,12},{12,14},{14,16},{16,18},{18... | collective-permute-start | bytes 442376 | tf_op jit(solution)/shard_map/ppermute | solution.py:505
  25.9 6.9 %copy-start.2 = (bf16[128,1280]{1,0:T(8,128)(2,1)S(1)}, bf16[128,1280]{1,0:T(8,128)(2,1)}, u32[]{:S(2)}) copy-start(bf16[128,1280]{1,0:T(8,128)(2,1)} %constant.16.clone.turn_ref) | copy-start | bytes 983044
  44.0 11.2 %copy-start.5 = (f32[4,160,128]{2,1,0:T(8,128)}, f32[4,160,128]{2,1,0:T(8,128)S(1)}, u32[]{:S(2)}) copy-start(f32[4,160,128]{2,1,0:T(8,128)S(1)} %get-tuple-element.111.refs_5_.refs_1_) | copy-start | bytes 983044
  51.3 5.8 %copy-start.7 = (f32[4,160,128]{2,1,0:T(8,128)}, f32[4,160,128]{2,1,0:T(8,128)S(1)}, u32[]{:S(2)}) copy-start(f32[4,160,128]{2,1,0:T(8,128)S(1)} %get-tuple-element.112.refs_6_.refs_2_) | copy-start | bytes 983044
  51.3 5.8 %copy-start.17 = (bf16[144,512]{1,0:T(8,128)(2,1)}, bf16[144,512]{1,0:T(8,128)(2,1)S(1)}, u32[]{:S(2)}) copy-start(bf16[144,512]{1,0:T(8,128)(2,1)S(1)} %get-tuple-element.108.refs_2_.prev_ref) | copy-start | bytes 442372
  61.5 41.1 %copy-start.68 = (f32[512]{0:T(512)S(1)}, f32[512]{0:T(512)}, u32[]{:S(2)}) copy-start(f32[512]{0:T(512)} %param.12) | copy-start | bytes 6148
  61.5 45.8 %collective-permute-start.7 = (bf16[256,1024]{1,0:T(8,128)(2,1)}, bf16[256,1024]{1,0:T(8,128)(2,1)S(1)}, u32[]{:S(2)}, u32[]{:S(2)}) collective-permute-start(bf16[256,1024]{1,0:T(8,128)(2,1)} %shard_map.92), channel_id=1, source_target_pairs={{0,1},{1,0},{2,3},{3,2},{4,5},{5,4},{6,7},{7,6},{8,9},{9,8},{10,11... | collective-permute-start | bytes 1572872 | tf_op jit(solution)/shard_map/ppermute | solution.py:404
  63.6 8.3 %all-to-all-start = ((bf16[4,160,128]{2,1,0:T(8,128)(2,1)}), bf16[4,160,128]{2,1,0:T(8,128)(2,1)S(1)}, u32[]{:S(2)}, u32[]{:S(2)}) async-start(bf16[4,160,128]{2,1,0:T(8,128)(2,1)} %copy-done.56), calls=%async_computation | async-start | bytes 327680 | tf_op jit(solution)/shard_map/all_to_all | solution.py:339
  73.9 13.1 %all-to-all-start.1 = ((bf16[4,160,128]{2,1,0:T(8,128)(2,1)}), bf16[4,160,128]{2,1,0:T(8,128)(2,1)S(1)}, u32[]{:S(2)}, u32[]{:S(2)}) async-start(bf16[4,160,128]{2,1,0:T(8,128)(2,1)} %copy-done.57), calls=%async_computation.1 | async-start | bytes 327680 | tf_op jit(solution)/shard_map/all_to_all | solution.py:339
  89.2 13.4 %all-to-all-start.2 = ((bf16[4,160,128]{2,1,0:T(8,128)(2,1)}), bf16[4,160,128]{2,1,0:T(8,128)(2,1)S(1)}, u32[]{:S(2)}, u32[]{:S(2)}) async-start(bf16[4,160,128]{2,1,0:T(8,128)(2,1)} %copy-done.12), calls=%async_computation.2 | async-start | bytes 327680 | tf_op jit(solution)/shard_map/all_to_all | solution.py:339
  105.8 7.8 %copy-start.6 = (f32[4,160,128]{2,1,0:T(8,128)S(1)}, f32[4,160,128]{2,1,0:T(8,128)}, u32[]{:S(2)}) copy-start(f32[4,160,128]{2,1,0:T(8,128)} %copy-done.5) | copy-start | bytes 983044
  105.8 7.8 %copy-start.8 = (f32[4,160,128]{2,1,0:T(8,128)S(1)}, f32[4,160,128]{2,1,0:T(8,128)}, u32[]{:S(2)}) copy-start(f32[4,160,128]{2,1,0:T(8,128)} %copy-done.7) | copy-start | bytes 983044
  105.8 7.8 %copy-start.16 = (bf16[256,1280]{1,0:T(8,128)(2,1)S(1)}, bf16[256,1280]{1,0:T(8,128)(2,1)}, u32[]{:S(2)}) copy-start(bf16[256,1280]{1,0:T(8,128)(2,1)} %copy-done.15) | copy-start | bytes 1966084
  107.3 13.0 %collective-permute-start.8 = (bf16[256,1024]{1,0:T(8,128)(2,1)S(1)}, bf16[256,1024]{1,0:T(8,128)(2,1)S(1)}, u32[]{:S(2)}, u32[]{:S(2)}) collective-permute-start(bf16[256,1024]{1,0:T(8,128)(2,1)S(1)} %collective-permute-done.7.refs_1_), channel_id=1, source_target_pairs={{0,2},{2,0},{4,6},{6,4},{8,10},{10,8},{12,14},{14,12},{16,18},{18,... | collective-permute-start | bytes 1572872 | tf_op jit(solution)/shard_map/ppermute | solution.py:313
  107.9 11.9 %collective-permute-start.12 = (bf16[256,512]{1,0:T(8,128)(2,1)S(1)}, bf16[256,512]{1,0:T(8,128)(2,1)S(1)}, u32[]{:S(2)}, u32[]{:S(2)}) collective-permute-start(bf16[256,512]{1,0:T(8,128)(2,1)S(1)} %shard_map.106.own_ref), channel_id=1, source_target_pairs={{0,1},{1,0},{2,3},{3,2},{4,5},{5,4},{6,7},{7,6},{8,9},{9,8},{10,11... | collective-permute-start | bytes 786440 | tf_op jit(solution)/shard_map/ppermute | solution.py:404
  112.0 10.6 %collective-permute-start.11 = (bf16[256,512]{1,0:T(8,128)(2,1)S(1)}, bf16[256,512]{1,0:T(8,128)(2,1)S(1)}, u32[]{:S(2)}, u32[]{:S(2)}) collective-permute-start(bf16[256,512]{1,0:T(8,128)(2,1)S(1)} %shard_map.107.own_ref), channel_id=1, source_target_pairs={{0,1},{1,0},{2,3},{3,2},{4,5},{5,4},{6,7},{7,6},{8,9},{9,8},{10,11... | collective-permute-start | bytes 786440 | tf_op jit(solution)/shard_map/ppermute | solution.py:404
  115.1 13.1 %collective-permute-start.10 = (bf16[256,512]{1,0:T(8,128)(2,1)S(1)}, bf16[256,512]{1,0:T(8,128)(2,1)S(1)}, u32[]{:S(2)}, u32[]{:S(2)}) collective-permute-start(bf16[256,512]{1,0:T(8,128)(2,1)S(1)} %shard_map.108.own_ref), channel_id=1, source_target_pairs={{0,1},{1,0},{2,3},{3,2},{4,5},{5,4},{6,7},{7,6},{8,9},{9,8},{10,11... | collective-permute-start | bytes 786440 | tf_op jit(solution)/shard_map/ppermute | solution.py:404
  116.9 14.1 %collective-permute-start.9 = (bf16[128,512]{1,0:T(8,128)(2,1)S(1)}, bf16[128,512]{1,0:T(8,128)(2,1)S(1)}, u32[]{:S(2)}, u32[]{:S(2)}) collective-permute-start(bf16[128,512]{1,0:T(8,128)(2,1)S(1)} %shard_map.109.own_ref), channel_id=1, source_target_pairs={{0,1},{1,0},{2,3},{3,2},{4,5},{5,4},{6,7},{7,6},{8,9},{9,8},{10,11... | collective-permute-start | bytes 393224 | tf_op jit(solution)/shard_map/ppermute | solution.py:404
  119.7 13.3 %collective-permute-start.6 = (bf16[128,512]{1,0:T(8,128)(2,1)S(1)}, bf16[128,512]{1,0:T(8,128)(2,1)S(1)}, u32[]{:S(2)}, u32[]{:S(2)}) collective-permute-start(bf16[128,512]{1,0:T(8,128)(2,1)S(1)} %shard_map.110.own_ref), channel_id=1, source_target_pairs={{0,1},{1,0},{2,3},{3,2},{4,5},{5,4},{6,7},{7,6},{8,9},{9,8},{10,11... | collective-permute-start | bytes 393224 | tf_op jit(solution)/shard_map/ppermute | solution.py:404
  (55 other events, 89.2 us)

commit v8 on v6

--- a/solution.py
+++ b/solution.py
@@ -363,14 +363,13 @@
     earlier = []
     for d in range(1, ctx // PLANE):
         earlier.append(exchange(plane, "ctx", d * PLANE))
-    back = call(
+    return call(
         functools.partial(earlier_kernel, planes=len(earlier)),
         [narrow] * PLANE,
         in_specs=[scalar] + [whole] * (PLANE + len(earlier)),
         out_specs=[whole] * PLANE,
         vmem=4 << 20,
     )(after(places, beside[1]), *ahead, *earlier)
-    return [back[0]] + [exchange(back[r], "ctx", r) for r in range(1, PLANE)]
 
 
 def prior_by_doubling(total, position):
@@ -428,22 +427,19 @@
     cols = out_weight.shape[1] // n
     out_parts = 2 if width // 2 % LANES == 0 and ctx % 2 == 0 else 1
     share = width // out_parts
-    picked = []
-    for r in range(1, n):
-        block = call(
+    def pick(r):
+        column = functools.partial(lambda i, a, r: (a[2] % out_parts, (a[0] + r) % n), r=r)
+        return call(
             pick_kernel,
             jax.ShapeDtypeStruct((share, cols), BF16),
             grid_spec=pltpu.PrefetchScalarGridSpec(
                 num_scalar_prefetch=1,
                 grid=(1,),
-                in_specs=[
-                    pl.BlockSpec((share, cols), functools.partial(lambda i, a, r: (a[2] % out_parts, (a[0] + r) % n), r=r))
-                ],
+                in_specs=[pl.BlockSpec((share, cols), column)],
                 out_specs=pl.BlockSpec((share, cols), lambda i, a: (0, 0)),
             ),
             vmem=8 << 20,
-        )(places, out_weight)
-        picked.append(block)
+        )(after(places, done[last - 1][1]), out_weight)
 
     qk_width = -(-heads * FQK // LANES) * LANES
     arranged_width = 2 * qk_width + 3 * width
@@ -495,7 +491,7 @@
             vmem=32 << 20,
         )(places, means, arranged, v, *pieces[b])
 
-    def attend(b, prev):
+    def attend(b, prev, places=places):
         rows = blocks[b][1]
         k, v, _, q, wq, wk, _ = done[b]
         return call(
@@ -520,34 +516,43 @@
     k, v, state, *sends = do_block(b, prevs[b], attended[b - 1][1], [done[c][2] for c in (last, *range(b))])
     done[b] = (k, v, state, *do_queries(b, v))
     prevs[last] = done[b][6]
-    for b in (last - 1, last):
-        attended[b] = attend(b, prevs[b])
+    attended[last - 1] = attend(last - 1, prevs[last - 1])
     held = sends[:1] + [exchange(sends[r], "ctx", r) for r in range(1, len(sends))]
-    mark = done[last - 1][6]
-    fetched = [from_head(after(block, mark), r) for r, block in enumerate(picked, 1)]
+    fetched = [from_head(pick(r), r) for r in range(1, n)]
     if in_planes:
-        priors = prior_in_planes(held, places, [done[last - 1][6], attended[last - 1][1]])
+        back = prior_in_planes(held, places, [done[last - 1][1], attended[last - 1][1]])
+        priors = [back[0]] + [exchange(back[r], "ctx", r) for r in range(1, PLANE)]
+        attended[last] = attend(last, prevs[last], after(places, back[0]))
     else:
         priors = prior_by_doubling(sum(done[b][2] for b in range(last + 1)), position)
-
-    result = None
-    out_rows = []
+        attended[last] = attend(last, prevs[last])
+
+    order = (0, 1, 4, 2, 3)
     mixed = attended[last][1]
-    for b in (0, 1, 4, 2, 3):
-        at, rows = blocks[b]
+    mixes = {}
+    for b in order:
+        rows = blocks[b][1]
         mixed = call(
             functools.partial(finish_kernel, heads=heads, before=b),
             jax.ShapeDtypeStruct((rows, width), BF16),
             in_specs=[scalar] + [whole] * (2 + pairs + b + 3),
             out_specs=whole,
             scratch_shapes=[pltpu.VMEM((pairs, FEATS, LANES), F32)],
+            flops=20 * 10**9 if b == order[0] else 1,
             vmem=16 << 20,
         )(after(places, mixed), means, gain, *priors, *[done[c][2] for c in range(b)], *attended[b])
-        others = [from_head(mixed, r) for r in range(1, n)]
-        if not out_rows:
-            for got in fetched:
-                out_rows += [got] + ([exchange(after(got, mixed), "ctx", 1)] if out_parts > 1 else [])
-        operands = [places, mixed, out_weight] + others + out_rows
+        mixes[b] = [mixed] + [from_head(mixed, r) for r in range(1, n)]
+
+    out_rows = []
+    for got in fetched:
+        out_rows.append(got)
+        if out_parts > 1:
+            out_rows.append(exchange(after(got, attended[last][1]), "ctx", 1))
+
+    result = None
+    for b in order:
+        at, rows = blocks[b]
+        operands = [places, mixes[b][0], out_weight] + mixes[b][1:] + out_rows
         specs = [scalar] + [whole] * (len(operands) - 1)
         aliases = {}
         if result is not None:

time: 103 us -> 102 us (level)
  waiting for transfers between devices: 20.5 us -> 17.6 us
  starting transfers between devices: 24.2 us -> 25.7 us
    ppermute x10, waiting for transfers between devices: 3.63 us -> 2.01 us  [exchange(): return lax.ppermute(value, axis, [(i, i ^ flip) for i in range(count)])]
    ppermute x11, waiting for transfers between devices: 16.9 us -> 15.6 us  [from_head(): return lax.ppermute(value, 'head', [(i, (i + by) % n) for i in range(n)])]
    ppermute x11, starting transfers between devices: 13.9 us -> 14.9 us  [from_head(): return lax.ppermute(value, 'head', [(i, (i + by) % n) for i in range(n)])]
  transfers between devices with their start and end apart: 22 -> 22, of which waited for: 10 -> 10; matrix products, arithmetic and copies ran while one was open for 2% -> 2% of each run, Pallas kernels for 46% -> 47%
where the time goes in v8:
time: 102 us; the launch traced here: 101 us
  Pallas kernels  51 us (50%)
  starting transfers between devices  25.7 us (25%)
  waiting for transfers between devices  17.6 us (17%)
  local copies, waits for them, and re-layouts  6.53 us (6%)
    pallas_call x5, Pallas kernels, do_block(): call(functools.partial(block_kernel, n=n, heads=heads, extra=extra, other...  15.9 us
    ppermute x11, waiting for transfers between devices, from_head(): return lax.ppermute(value, 'head', [(i, (i + by) % n) for i in range(n)])  15.6 us
    ppermute x11, starting transfers between devices, from_head(): return lax.ppermute(value, 'head', [(i, (i + by) % n) for i in range(n)])  14.9 us
    pallas_call x5, Pallas kernels, attend(): call(functools.partial(attend_kernel, heads=heads, first=b == 0), [jax.Sh...  9.74 us
    pallas_call x5, Pallas kernels, per_device(): call(functools.partial(output_kernel, n=n, offset=at, parts=out_parts), j...  9.65 us
    ppermute x10, starting transfers between devices, exchange(): return lax.ppermute(value, axis, [(i, i ^ flip) for i in range(count)])  9.14 us
    pallas_call x5, Pallas kernels, per_device(): call(functools.partial(finish_kernel, heads=heads, before=b), jax.ShapeDt...  7.02 us
    pallas_call x1, Pallas kernels, per_device(): call(functools.partial(arrange_kernel, heads=heads), jax.ShapeDtypeStruct...  5.09 us
  transfers between devices with their start and end apart: 22, of which 10 were waited for; matrix products, arithmetic and copies ran while one was open for 2% of the time, Pallas kernels for 47%

profile of v8, /device:TPU:0, one launch (start us, length us, event | category | flops | bytes accessed | tf_op | source)
XLA Modules:
  0.0 101.4 jit_solution(7938387842628477707)
XLA Ops:
  1.2 3.0 %collective-permute-start.1 = (bf16[272,1024]{1,0:T(8,128)(2,1)S(1)}, bf16[272,1024]{1,0:T(8,128)(2,1)S(1)}, u32[]{:S(2)}, u32[]{:S(2)}) collective-permute-start(bf16[272,1024]{1,0:T(8,128)(2,1)S(1)} %slice.16.refs_0_), channel_id=1, source_target_pairs={{0,1},{1,0},{2,3},{3,2},{4,5},{5,4},{6,7},{7,6},{8,9},{9,8},{10,11... | collective-permute-start | bytes 1671176 | tf_op jit(solution)/shard_map/ppermute | solution.py:410
  5.6 2.0 %collective-permute-start.3 = (bf16[256,1024]{1,0:T(8,128)(2,1)S(1)}, bf16[256,1024]{1,0:T(8,128)(2,1)S(1)}, u32[]{:S(2)}, u32[]{:S(2)}) collective-permute-start(bf16[256,1024]{1,0:T(8,128)(2,1)S(1)} %get-tuple-element.98.refs_0_), channel_id=1, source_target_pairs={{0,1},{1,0},{2,3},{3,2},{4,5},{5,4},{6,7},{7,6},{8,9},{9,8},{10,11... | collective-permute-start | bytes 1572872 | tf_op jit(solution)/shard_map/ppermute | solution.py:410
  8.8 1.9 %collective-permute-start.5 = (bf16[128,1024]{1,0:T(8,128)(2,1)S(1)}, bf16[128,1024]{1,0:T(8,128)(2,1)S(1)}, u32[]{:S(2)}, u32[]{:S(2)}) collective-permute-start(bf16[128,1024]{1,0:T(8,128)(2,1)S(1)} %get-tuple-element.116.refs_0_), channel_id=1, source_target_pairs={{0,1},{1,0},{2,3},{3,2},{4,5},{5,4},{6,7},{7,6},{8,9},{9,8},{10,11... | collective-permute-start | bytes 786440 | tf_op jit(solution)/shard_map/ppermute | solution.py:410
  10.7 3.1 %copy-done.2 = bf16[2048,1792]{1,0:T(8,128)(2,1)S(1)} copy-done((bf16[2048,1792]{1,0:T(8,128)(2,1)S(1)}, bf16[2048,1792]{1,0:T(8,128)(2,1)}, u32[]{:S(2)}) %copy-start.2) | copy-done | bytes 7340056
  13.8 5.1 %shard_map.91.w_ref = bf16[2048,1792]{1,0:T(8,128)(2,1)S(1)} custom-call(bf16[2048,1792]{1,0:T(8,128)(2,1)S(1)} %copy-done.2), custom_call_target="tpu_custom_call" | custom-call | flops 1 | bytes 1 | tf_op jit(solution)/shard_map/pallas_call | solution.py:447
  19.0 3.8 %shard_map.92 = (bf16[256,128]{1,0:T(8,128)(2,1)S(1)}, bf16[256,512]{1,0:T(8,128)(2,1)S(1)}, f32[4,160,128]{2,1,0:T(8,128)S(1)}, bf16[256,128]{1,0:T(8,128)(2,1)...) custom-call(s32[3]{0:T(128)S(1)} %pad_add_fusion.j_ref.a_ref, ...), custom_call_target="tpu_custom_call" | custom-call | flops 1 | bytes 1 | tf_op jit(solution)/shard_map/pallas_call | solution.py:473
  22.8 1.6 %collective-permute-start.2 = (bf16[144,512]{1,0:T(8,128)(2,1)S(1)}, bf16[144,512]{1,0:T(8,128)(2,1)S(1)}, u32[]{:S(2)}, u32[]{:S(2)}) collective-permute-start(bf16[144,512]{1,0:T(8,128)(2,1)S(1)} %get-tuple-element.89), channel_id=1, source_target_pairs={{0,2},{2,4},{4,6},{6,8},{8,10},{10,12},{12,14},{14,16},{16,18},{18... | collective-permute-start | bytes 442376 | tf_op jit(solution)/shard_map/ppermute | solution.py:509
  24.4 4.5 %collective-permute-done.refs_1_ = bf16[256,1024]{1,0:T(8,128)(2,1)S(1)} collective-permute-done((bf16[256,1024]{1,0:T(8,128)(2,1)S(1)}, bf16[256,1024]{1,0:T(8,128)(2,1)S(1)}, u32[]{:S(2)}, u32[]{:S(2)}) %collective-permute-start) | collective-permute-done | bytes 524320 | tf_op jit(solution)/shard_map/ppermute | solution.py:410
  28.9 3.8 %shard_map.93 = (bf16[256,128]{1,0:T(8,128)(2,1)S(1)}, bf16[256,512]{1,0:T(8,128)(2,1)S(1)}, f32[4,160,128]{2,1,0:T(8,128)S(1)}, bf16[256,128]{1,0:T(8,128)(2,1)...) custom-call(s32[3]{0:T(128)S(1)} %pad_add_fusion.j_ref.a_ref, ...), custom_call_target="tpu_custom_call" | custom-call | flops 1 | bytes 1 | tf_op jit(solution)/shard_map/pallas_call | solution.py:473
  32.7 2.1 %shard_map.94 = (bf16[256,1280]{1,0:T(8,128)(2,1)S(1)}, f32[256,512]{1,0:T(8,128)S(1)}, f32[256,512]{1,0:T(8,128)S(1)}) custom-call(s32[3]{0:T(128)S(1)} %pad_add_fusion.j_ref.a_ref, bf16[128,1280]{1,0:T(8,128)(2,1)S(1)} %copy-done.4, bf16[144,512]{1,0:T(8,128)(2,1)S(1)} %collective-permute-done.2.refs_2_.prev_ref, ...), custom_call_target="tpu_custom_call" | custom-call | flops 1 | bytes 1 | tf_op jit(solution)/shard_map/pallas_call | solution.py:497
  34.9 5.2 %collective-permute-done.3.refs_1_ = bf16[256,1024]{1,0:T(8,128)(2,1)S(1)} collective-permute-done((bf16[256,1024]{1,0:T(8,128)(2,1)S(1)}, bf16[256,1024]{1,0:T(8,128)(2,1)S(1)}, u32[]{:S(2)}, u32[]{:S(2)}) %collective-permute-start.3) | collective-permute-done | bytes 524320 | tf_op jit(solution)/shard_map/ppermute | solution.py:410
  40.1 3.8 %shard_map.95 = (bf16[256,128]{1,0:T(8,128)(2,1)S(1)}, bf16[256,512]{1,0:T(8,128)(2,1)S(1)}, f32[4,160,128]{2,1,0:T(8,128)S(1)}, bf16[256,128]{1,0:T(8,128)(2,1)...) custom-call(s32[3]{0:T(128)S(1)} %pad_add_fusion.j_ref.a_ref, ...), custom_call_target="tpu_custom_call" | custom-call | flops 1 | bytes 1 | tf_op jit(solution)/shard_map/pallas_call | solution.py:473
  44.0 2.1 %shard_map.96 = (bf16[256,1280]{1,0:T(8,128)(2,1)S(1)}, f32[256,512]{1,0:T(8,128)S(1)}, f32[256,512]{1,0:T(8,128)S(1)}) custom-call(s32[3]{0:T(128)S(1)} %pad_add_fusion.j_ref.a_ref, bf16[128,1280]{1,0:T(8,128)(2,1)S(1)} %copy-done.4, bf16[144,512]{1,0:T(8,128)(2,1)S(1)} %get-tuple-element.90.refs_2_.prev_ref, bf16[256,128]{1,0:T(8,128)(2,1)S(1)} %get-tuple-element.99.q_ref, ...), custom_call_target="tpu_custom_call" | custom-call | flops 1 | bytes 1 | tf_op jit(solution)/shard_map/pallas_call | solution.py:497
  46.1 2.6 %shard_map.97 = (bf16[128,128]{1,0:T(8,128)(2,1)S(1)}, bf16[128,512]{1,0:T(8,128)(2,1)S(1)}, f32[4,160,128]{2,1,0:T(8,128)S(1)}, bf16[128,128]{1,0:T(8,128)(2,1)...) custom-call(s32[3]{0:T(128)S(1)} %pad_add_fusion.j_ref.a_ref, ...), custom_call_target="tpu_custom_call" | custom-call | flops 1 | bytes 1 | tf_op jit(solution)/shard_map/pallas_call | solution.py:473
  48.7 1.7 %shard_map.98 = (bf16[128,1280]{1,0:T(8,128)(2,1)S(1)}, f32[128,512]{1,0:T(8,128)S(1)}, f32[128,512]{1,0:T(8,128)S(1)}) custom-call(s32[3]{0:T(128)S(1)} %pad_add_fusion.j_ref.a_ref, bf16[128,1280]{1,0:T(8,128)(2,1)S(1)} %copy-done.4, bf16[144,512]{1,0:T(8,128)(2,1)S(1)} %get-tuple-element.107.refs_2_.prev_ref, ...), custom_call_target="tpu_custom_call" | custom-call | flops 1 | bytes 1 | tf_op jit(solution)/shard_map/pallas_call | solution.py:497
  50.5 1.8 %shard_map.99 = (bf16[128,128]{1,0:T(8,128)(2,1)S(1)}, bf16[128,512]{1,0:T(8,128)(2,1)S(1)}, f32[4,160,128]{2,1,0:T(8,128)S(1)}, bf16[160,128]{1,0:T(8,128)(2,1)...) custom-call(s32[3]{0:T(128)S(1)} %pad_add_fusion.j_ref.a_ref, ...), custom_call_target="tpu_custom_call" | custom-call | flops 1 | bytes 1 | tf_op jit(solution)/shard_map/pallas_call | solution.py:473
  52.6 2.0 %collective-permute-start.7 = (bf16[160,128]{1,0:T(8,128)(2,1)S(1)}, bf16[160,128]{1,0:T(8,128)(2,1)S(1)}, u32[]{:S(2)}, u32[]{:S(2)}) collective-permute-start(bf16[160,128]{1,0:T(8,128)(2,1)S(1)} %get-tuple-element.131), channel_id=1, source_target_pairs={{0,4},{2,6},{4,0},{6,2},{8,12},{10,14},{12,8},{14,10},{16,20},{18,... | collective-permute-start | bytes 122888 | tf_op jit(solution)/shard_map/ppermute | solution.py:319
  55.3 1.8 %collective-permute-start.16 = (bf16[256,1024]{1,0:T(8,128)(2,1)S(1)}, bf16[256,1024]{1,0:T(8,128)(2,1)S(1)}, u32[]{:S(2)}, u32[]{:S(2)}) collective-permute-start(bf16[256,1024]{1,0:T(8,128)(2,1)S(1)} %shard_map.110), channel_id=1, source_target_pairs={{0,1},{1,0},{2,3},{3,2},{4,5},{5,4},{6,7},{7,6},{8,9},{9,8},{10,11... | collective-permute-start | bytes 1572872 | tf_op jit(solution)/shard_map/ppermute | solution.py:410
  58.8 3.7 %collective-permute-start.11 = (bf16[160,128]{1,0:T(8,128)(2,1)S(1)}, bf16[160,128]{1,0:T(8,128)(2,1)S(1)}, u32[]{:S(2)}, u32[]{:S(2)}) collective-permute-start(bf16[160,128]{1,0:T(8,128)(2,1)S(1)} %get-tuple-element.137), channel_id=1, source_target_pairs={{0,24},{2,26},{4,28},{6,30},{8,16},{10,18},{12,20},{14,22},{16,8},... | collective-permute-start | bytes 122888 | tf_op jit(solution)/shard_map/ppermute | solution.py:319
  63.2 1.8 %shard_map.100 = (bf16[128,128]{1,0:T(8,128)(2,1)S(1)}, bf16[128,512]{1,0:T(8,128)(2,1)S(1)}, bf16[128,512]{1,0:T(8,128)(2,1)S(1)}, bf16[144,512]{1,0:T(8,128)(2,1)S(1)}) custom-call(s32[3]{0:T(128)S(1)} %pad_add_fusion.j_ref.a_ref, bf16[256,128]{1,0:T(8,128)(2,1)S(1)} %copy-done.3, bf16[2048,1792]{1,0:T(8,128)(2,1)S(1)} %shard_map.91.w_ref, ...), custom_call_target="tpu_custom_call" | custom-call | flops 1 | bytes 1 | tf_op jit(solution)/shard_map/pallas_call | solution.py:486
  65.0 1.7 %shard_map.101 = (bf16[128,1280]{1,0:T(8,128)(2,1)S(1)}, f32[128,512]{1,0:T(8,128)S(1)}, f32[128,512]{1,0:T(8,128)S(1)}) custom-call(s32[3]{0:T(128)S(1)} %pad_add_fusion.j_ref.a_ref, bf16[128,1280]{1,0:T(8,128)(2,1)S(1)} %copy-done.4, bf16[144,512]{1,0:T(8,128)(2,1)S(1)} %get-tuple-element.108.refs_2_.prev_ref, ...), custom_call_target="tpu_custom_call" | custom-call | flops 1 | bytes 1 | tf_op jit(solution)/shard_map/pallas_call | solution.py:497
  69.9 2.1 %shard_map.104 = (bf16[256,1280]{1,0:T(8,128)(2,1)S(1)}, f32[256,512]{1,0:T(8,128)S(1)}, f32[256,512]{1,0:T(8,128)S(1)}) custom-call(s32[3]{0:T(128)S(1)} %pad_add_fusion.j_ref.a_ref, bf16[128,1280]{1,0:T(8,128)(2,1)S(1)} %copy-done.4, bf16[144,512]{1,0:T(8,128)(2,1)S(1)} %get-tuple-element.140.prev_ref, bf16[256,128]{1,0:T(8,128)(2,1)S(1)} %get-tuple-element.141.q_ref, ...), custom_call_target="tpu_custom_call" | custom-call | flops 4849999872 | bytes 1 | tf_op jit(solution)/shard_map/pallas_call | solution.py:497
  74.3 1.6 %collective-permute-start.21 = (bf16[256,512]{1,0:T(8,128)(2,1)S(1)}, bf16[256,512]{1,0:T(8,128)(2,1)S(1)}, u32[]{:S(2)}, u32[]{:S(2)}) collective-permute-start(bf16[256,512]{1,0:T(8,128)(2,1)S(1)} %shard_map.105.own_ref), channel_id=1, source_target_pairs={{0,1},{1,0},{2,3},{3,2},{4,5},{5,4},{6,7},{7,6},{8,9},{9,8},{10,11... | collective-permute-start | bytes 786440 | tf_op jit(solution)/shard_map/ppermute | solution.py:410
  78.0 1.5 %shard_map.107.own_ref = bf16[256,512]{1,0:T(8,128)(2,1)S(1)} custom-call(s32[3]{0:T(128)S(1)} %pad_add_fusion.j_ref.a_ref, bf16[256,128]{1,0:T(8,128)(2,1)S(1)} %copy-done.3, f32[1,512]{1,0:T(1,128)S(1)} %bitcast.6, bf16[160,128]{1,0:T(8,128)(2,1)S(1)} %get-tuple-element.138.refs_0_, bf16[160,128]{1,0:T(8,128)(2,1)S(1)} %collective-permute-done.12.refs_1_, ...), custom_call_target="tpu_custom_call" | custom-call | flops 1 | bytes 1 | tf_op jit(solution)/shard_map/pallas_call | solution.py:535
  79.5 1.6 %collective-permute-start.19 = (bf16[256,512]{1,0:T(8,128)(2,1)S(1)}, bf16[256,512]{1,0:T(8,128)(2,1)S(1)}, u32[]{:S(2)}, u32[]{:S(2)}) collective-permute-start(bf16[256,512]{1,0:T(8,128)(2,1)S(1)} %shard_map.107.own_ref), channel_id=1, source_target_pairs={{0,1},{1,0},{2,3},{3,2},{4,5},{5,4},{6,7},{7,6},{8,9},{9,8},{10,11... | collective-permute-start | bytes 786440 | tf_op jit(solution)/shard_map/ppermute | solution.py:410
  84.1 1.6 %collective-permute-start.15 = (bf16[128,512]{1,0:T(8,128)(2,1)S(1)}, bf16[128,512]{1,0:T(8,128)(2,1)S(1)}, u32[]{:S(2)}, u32[]{:S(2)}) collective-permute-start(bf16[128,512]{1,0:T(8,128)(2,1)S(1)} %shard_map.109.own_ref), channel_id=1, source_target_pairs={{0,1},{1,0},{2,3},{3,2},{4,5},{5,4},{6,7},{7,6},{8,9},{9,8},{10,11... | collective-permute-start | bytes 393224 | tf_op jit(solution)/shard_map/ppermute | solution.py:410
  85.7 2.1 %shard_map.111.refs_3_ = bf16[1024,1024]{1,0:T(8,128)(2,1)} custom-call(s32[3]{0:T(128)S(1)} %pad_add_fusion.j_ref.a_ref, bf16[256,512]{1,0:T(8,128)(2,1)S(1)} %shard_map.105.own_ref, bf16[512,2048]{1,0:T(8,128)(2,1)S(1)} %copy-done, bf16[256,512]{1,0:T(8,128)(2,1)S(1)} %collective-permute-done.21.refs_0_, ...), custom_call_target="tpu_custom_call" | custom-call | flops 1 | bytes 1 | tf_op jit(solution)/shard_map/pallas_call | solution.py:562
  89.1 2.1 %shard_map.112.refs_3_ = bf16[1024,1024]{1,0:T(8,128)(2,1)} custom-call(s32[3]{0:T(128)S(1)} %pad_add_fusion.j_ref.a_ref, bf16[256,512]{1,0:T(8,128)(2,1)S(1)} %shard_map.106.own_ref, bf16[512,2048]{1,0:T(8,128)(2,1)S(1)} %copy-done, bf16[256,512]{1,0:T(8,128)(2,1)S(1)} %collective-permute-done.20.refs_0_, ...), custom_call_target="tpu_custom_call", output_to_operand_aliasing={{}: (6, {})} | custom-call | flops 1 | bytes 1 | tf_op jit(solution)/shard_map/pallas_call | solution.py:562
  91.2 3.5 %collective-permute-done.19.refs_0_ = bf16[256,512]{1,0:T(8,128)(2,1)S(1)} collective-permute-done((bf16[256,512]{1,0:T(8,128)(2,1)S(1)}, bf16[256,512]{1,0:T(8,128)(2,1)S(1)}, u32[]{:S(2)}, u32[]{:S(2)}) %collective-permute-start.19) | collective-permute-done | bytes 262176 | tf_op jit(solution)/shard_map/ppermute | solution.py:410
  94.7 2.1 %shard_map.113.refs_3_ = bf16[1024,1024]{1,0:T(8,128)(2,1)} custom-call(s32[3]{0:T(128)S(1)} %pad_add_fusion.j_ref.a_ref, bf16[256,512]{1,0:T(8,128)(2,1)S(1)} %shard_map.107.own_ref, bf16[512,2048]{1,0:T(8,128)(2,1)S(1)} %copy-done, bf16[256,512]{1,0:T(8,128)(2,1)S(1)} %collective-permute-done.19.refs_0_, ...), custom_call_target="tpu_custom_call", output_to_operand_aliasing={{}: (6, {})} | custom-call | flops 1 | bytes 1 | tf_op jit(solution)/shard_map/pallas_call | solution.py:562
  97.5 1.7 %shard_map.114.refs_3_ = bf16[1024,1024]{1,0:T(8,128)(2,1)} custom-call(s32[3]{0:T(128)S(1)} %pad_add_fusion.j_ref.a_ref, bf16[128,512]{1,0:T(8,128)(2,1)S(1)} %shard_map.108.own_ref, bf16[512,2048]{1,0:T(8,128)(2,1)S(1)} %copy-done, bf16[128,512]{1,0:T(8,128)(2,1)S(1)} %collective-permute-done.18.refs_0_, ...), custom_call_target="tpu_custom_call", output_to_operand_aliasing={{}: (6, {})} | custom-call | flops 1 | bytes 1 | tf_op jit(solution)/shard_map/pallas_call | solution.py:562
  99.5 1.7 %shard_map.115 = bf16[1024,1024]{1,0:T(8,128)(2,1)} custom-call(s32[3]{0:T(128)S(1)} %pad_add_fusion.j_ref.a_ref, bf16[128,512]{1,0:T(8,128)(2,1)S(1)} %shard_map.109.own_ref, bf16[512,2048]{1,0:T(8,128)(2,1)S(1)} %copy-done, bf16[128,512]{1,0:T(8,128)(2,1)S(1)} %collective-permute-done.15.refs_0_, ...), custom_call_target="tpu_custom_call", output_to_operand_aliasing={{}: (6, {})} | custom-call | flops 1 | bytes 1 | tf_op jit(solution)/shard_map/pallas_call | solution.py:562
  (57 shorter events, 20.1 us)
Async XLA Ops:
  1.2 17.7 %collective-permute-start.1 = (bf16[272,1024]{1,0:T(8,128)(2,1)S(1)}, bf16[272,1024]{1,0:T(8,128)(2,1)S(1)}, u32[]{:S(2)}, u32[]{:S(2)}) collective-permute-start(bf16[272,1024]{1,0:T(8,128)(2,1)S(1)} %slice.16.refs_0_), channel_id=1, source_target_pairs={{0,1},{1,0},{2,3},{3,2},{4,5},{5,4},{6,7},{7,6},{8,9},{9,8},{10,11... | collective-permute-start | bytes 1671176 | tf_op jit(solution)/shard_map/ppermute | solution.py:410
  5.5 23.4 %collective-permute-start = (bf16[256,1024]{1,0:T(8,128)(2,1)S(1)}, bf16[256,1024]{1,0:T(8,128)(2,1)S(1)}, u32[]{:S(2)}, u32[]{:S(2)}) collective-permute-start(bf16[256,1024]{1,0:T(8,128)(2,1)S(1)} %get-tuple-element.88.refs_0_), channel_id=1, source_target_pairs={{0,1},{1,0},{2,3},{3,2},{4,5},{5,4},{6,7},{7,6},{8,9},{9,8},{10,11... | collective-permute-start | bytes 1572872 | tf_op jit(solution)/shard_map/ppermute | solution.py:410
  5.6 34.6 %collective-permute-start.3 = (bf16[256,1024]{1,0:T(8,128)(2,1)S(1)}, bf16[256,1024]{1,0:T(8,128)(2,1)S(1)}, u32[]{:S(2)}, u32[]{:S(2)}) collective-permute-start(bf16[256,1024]{1,0:T(8,128)(2,1)S(1)} %get-tuple-element.98.refs_0_), channel_id=1, source_target_pairs={{0,1},{1,0},{2,3},{3,2},{4,5},{5,4},{6,7},{7,6},{8,9},{9,8},{10,11... | collective-permute-start | bytes 1572872 | tf_op jit(solution)/shard_map/ppermute | solution.py:410
  8.6 37.5 %collective-permute-start.4 = (bf16[128,1024]{1,0:T(8,128)(2,1)S(1)}, bf16[128,1024]{1,0:T(8,128)(2,1)S(1)}, u32[]{:S(2)}, u32[]{:S(2)}) collective-permute-start(bf16[128,1024]{1,0:T(8,128)(2,1)S(1)} %get-tuple-element.106.refs_0_), channel_id=1, source_target_pairs={{0,1},{1,0},{2,3},{3,2},{4,5},{5,4},{6,7},{7,6},{8,9},{9,8},{10,11... | collective-permute-start | bytes 786440 | tf_op jit(solution)/shard_map/ppermute | solution.py:410
  8.8 10.1 %copy-start.1 = (bf16[1408,128]{1,0:T(8,128)(2,1)S(1)}, bf16[1408,128]{1,0:T(8,128)(2,1)}, u32[]{:S(2)}) copy-start(bf16[1408,128]{1,0:T(8,128)(2,1)} %constant.30.clone.turn_ref) | copy-start | bytes 1081348
  8.8 41.8 %collective-permute-start.5 = (bf16[128,1024]{1,0:T(8,128)(2,1)S(1)}, bf16[128,1024]{1,0:T(8,128)(2,1)S(1)}, u32[]{:S(2)}, u32[]{:S(2)}) collective-permute-start(bf16[128,1024]{1,0:T(8,128)(2,1)S(1)} %get-tuple-element.116.refs_0_), channel_id=1, source_target_pairs={{0,1},{1,0},{2,3},{3,2},{4,5},{5,4},{6,7},{7,6},{8,9},{9,8},{10,11... | collective-permute-start | bytes 786440 | tf_op jit(solution)/shard_map/ppermute | solution.py:410
  10.7 3.1 %copy-start.2 = (bf16[2048,1792]{1,0:T(8,128)(2,1)S(1)}, bf16[2048,1792]{1,0:T(8,128)(2,1)}, u32[]{:S(2)}) copy-start(bf16[2048,1792]{1,0:T(8,128)(2,1)} %w_ref.7) | copy-start | bytes 22020100
  13.8 5.1 %copy-start.3 = (bf16[256,128]{1,0:T(8,128)(2,1)S(1)}, bf16[256,128]{1,0:T(8,128)(2,1)}, u32[]{:S(2)}) copy-start(bf16[256,128]{1,0:T(8,128)(2,1)} %constant.32.clone.mean_ref) | copy-start | bytes 196612
  13.8 5.1 %copy-start.5 = (f32[160,128]{1,0:T(8,128)S(1)}, f32[160,128]{1,0:T(8,128)}, u32[]{:S(2)}) copy-start(f32[160,128]{1,0:T(8,128)} %constant.31.clone.weight_ref) | copy-start | bytes 245764
  13.8 5.1 %copy-start.6 = (f32[3,512]{1,0:T(4,128)S(1)}, f32[3,512]{1,0:T(4,128)}, u32[]{:S(2)}) copy-start(f32[3,512]{1,0:T(4,128)} %conv_ref.9) | copy-start | bytes 18436
  22.8 9.9 %copy-start.4 = (bf16[128,1280]{1,0:T(8,128)(2,1)S(1)}, bf16[128,1280]{1,0:T(8,128)(2,1)}, u32[]{:S(2)}) copy-start(bf16[128,1280]{1,0:T(8,128)(2,1)} %constant.29.clone.turn_ref) | copy-start | bytes 983044
  22.8 6.1 %collective-permute-start.2 = (bf16[144,512]{1,0:T(8,128)(2,1)S(1)}, bf16[144,512]{1,0:T(8,128)(2,1)S(1)}, u32[]{:S(2)}, u32[]{:S(2)}) collective-permute-start(bf16[144,512]{1,0:T(8,128)(2,1)S(1)} %get-tuple-element.89), channel_id=1, source_target_pairs={{0,2},{2,4},{4,6},{6,8},{8,10},{10,12},{12,14},{14,16},{16,18},{18... | collective-permute-start | bytes 442376 | tf_op jit(solution)/shard_map/ppermute | solution.py:509
  50.5 4.2 %copy-start = (bf16[512,2048]{1,0:T(8,128)(2,1)S(1)}, bf16[512,2048]{1,0:T(8,128)(2,1)}, u32[]{:S(2)}) copy-start(bf16[512,2048]{1,0:T(8,128)(2,1)} %w_ref.13) | copy-start | bytes 6291460
  52.3 4.8 %collective-permute-start.6 = (bf16[160,128]{1,0:T(8,128)(2,1)S(1)}, bf16[160,128]{1,0:T(8,128)(2,1)S(1)}, u32[]{:S(2)}, u32[]{:S(2)}) collective-permute-start(bf16[160,128]{1,0:T(8,128)(2,1)S(1)} %get-tuple-element.130), channel_id=1, source_target_pairs={{0,2},{2,0},{4,6},{6,4},{8,10},{10,8},{12,14},{14,12},{16,18},{18,... | collective-permute-start | bytes 122888 | tf_op jit(solution)/shard_map/ppermute | solution.py:319
  52.6 4.5 %collective-permute-start.7 = (bf16[160,128]{1,0:T(8,128)(2,1)S(1)}, bf16[160,128]{1,0:T(8,128)(2,1)S(1)}, u32[]{:S(2)}, u32[]{:S(2)}) collective-permute-start(bf16[160,128]{1,0:T(8,128)(2,1)S(1)} %get-tuple-element.131), channel_id=1, source_target_pairs={{0,4},{2,6},{4,0},{6,2},{8,12},{10,14},{12,8},{14,10},{16,20},{18,... | collective-permute-start | bytes 122888 | tf_op jit(solution)/shard_map/ppermute | solution.py:319
  54.6 3.5 %collective-permute-start.8 = (bf16[160,128]{1,0:T(8,128)(2,1)S(1)}, bf16[160,128]{1,0:T(8,128)(2,1)S(1)}, u32[]{:S(2)}, u32[]{:S(2)}) collective-permute-start(bf16[160,128]{1,0:T(8,128)(2,1)S(1)} %get-tuple-element.132), channel_id=1, source_target_pairs={{0,6},{2,4},{4,2},{6,0},{8,14},{10,12},{12,10},{14,8},{16,22},{18,... | collective-permute-start | bytes 122888 | tf_op jit(solution)/shard_map/ppermute | solution.py:319
  55.3 16.8 %collective-permute-start.16 = (bf16[256,1024]{1,0:T(8,128)(2,1)S(1)}, bf16[256,1024]{1,0:T(8,128)(2,1)S(1)}, u32[]{:S(2)}, u32[]{:S(2)}) collective-permute-start(bf16[256,1024]{1,0:T(8,128)(2,1)S(1)} %shard_map.110), channel_id=1, source_target_pairs={{0,1},{1,0},{2,3},{3,2},{4,5},{5,4},{6,7},{7,6},{8,9},{9,8},{10,11... | collective-permute-start | bytes 1572872 | tf_op jit(solution)/shard_map/ppermute | solution.py:410
  58.8 7.9 %collective-permute-start.11 = (bf16[160,128]{1,0:T(8,128)(2,1)S(1)}, bf16[160,128]{1,0:T(8,128)(2,1)S(1)}, u32[]{:S(2)}, u32[]{:S(2)}) collective-permute-start(bf16[160,128]{1,0:T(8,128)(2,1)S(1)} %get-tuple-element.137), channel_id=1, source_target_pairs={{0,24},{2,26},{4,28},{6,30},{8,16},{10,18},{12,20},{14,22},{16,8},... | collective-permute-start | bytes 122888 | tf_op jit(solution)/shard_map/ppermute | solution.py:319
  62.5 4.9 %collective-permute-start.10 = (bf16[160,128]{1,0:T(8,128)(2,1)S(1)}, bf16[160,128]{1,0:T(8,128)(2,1)S(1)}, u32[]{:S(2)}, u32[]{:S(2)}) collective-permute-start(bf16[160,128]{1,0:T(8,128)(2,1)S(1)} %get-tuple-element.137), channel_id=1, source_target_pairs={{0,16},{2,18},{4,20},{6,22},{8,24},{10,26},{12,28},{14,30},{16,0},... | collective-permute-start | bytes 122888 | tf_op jit(solution)/shard_map/ppermute | solution.py:319
  62.5 4.9 %collective-permute-start.9 = (bf16[160,128]{1,0:T(8,128)(2,1)S(1)}, bf16[160,128]{1,0:T(8,128)(2,1)S(1)}, u32[]{:S(2)}, u32[]{:S(2)}) collective-permute-start(bf16[160,128]{1,0:T(8,128)(2,1)S(1)} %get-tuple-element.137), channel_id=1, source_target_pairs={{0,8},{2,10},{4,12},{6,14},{8,0},{10,2},{12,4},{14,6},{16,24},{18,... | collective-permute-start | bytes 122888 | tf_op jit(solution)/shard_map/ppermute | solution.py:319
  68.0 4.5 %collective-permute-start.12 = (bf16[160,128]{1,0:T(8,128)(2,1)S(1)}, bf16[160,128]{1,0:T(8,128)(2,1)S(1)}, u32[]{:S(2)}, u32[]{:S(2)}) collective-permute-start(bf16[160,128]{1,0:T(8,128)(2,1)S(1)} %get-tuple-element.148), channel_id=1, source_target_pairs={{0,2},{2,0},{4,6},{6,4},{8,10},{10,8},{12,14},{14,12},{16,18},{18,... | collective-permute-start | bytes 122888 | tf_op jit(solution)/shard_map/ppermute | solution.py:319
  68.0 4.4 %collective-permute-start.13 = (bf16[160,128]{1,0:T(8,128)(2,1)S(1)}, bf16[160,128]{1,0:T(8,128)(2,1)S(1)}, u32[]{:S(2)}, u32[]{:S(2)}) collective-permute-start(bf16[160,128]{1,0:T(8,128)(2,1)S(1)} %get-tuple-element.149), channel_id=1, source_target_pairs={{0,4},{2,6},{4,0},{6,2},{8,12},{10,14},{12,8},{14,10},{16,20},{18,... | collective-permute-start | bytes 122888 | tf_op jit(solution)/shard_map/ppermute | solution.py:319
  69.0 3.8 %collective-permute-start.14 = (bf16[160,128]{1,0:T(8,128)(2,1)S(1)}, bf16[160,128]{1,0:T(8,128)(2,1)S(1)}, u32[]{:S(2)}, u32[]{:S(2)}) collective-permute-start(bf16[160,128]{1,0:T(8,128)(2,1)S(1)} %get-tuple-element.150), channel_id=1, source_target_pairs={{0,6},{2,4},{4,2},{6,0},{8,14},{10,12},{12,10},{14,8},{16,22},{18,... | collective-permute-start | bytes 122888 | tf_op jit(solution)/shard_map/ppermute | solution.py:319
  69.9 2.9 %copy-start.7 = (f32[512]{0:T(512)S(1)}, f32[512]{0:T(512)}, u32[]{:S(2)}) copy-start(f32[512]{0:T(512)} %param.12) | copy-start | bytes 6148
  72.0 13.7 %collective-permute-start.17 = (bf16[256,1024]{1,0:T(8,128)(2,1)S(1)}, bf16[256,1024]{1,0:T(8,128)(2,1)S(1)}, u32[]{:S(2)}, u32[]{:S(2)}) collective-permute-start(bf16[256,1024]{1,0:T(8,128)(2,1)S(1)} %collective-permute-done.16.refs_1_), channel_id=1, source_target_pairs={{0,2},{2,0},{4,6},{6,4},{8,10},{10,8},{12,14},{14,12},{16,18},{18,... | collective-permute-start | bytes 1572872 | tf_op jit(solution)/shard_map/ppermute | solution.py:319
  74.3 9.9 %collective-permute-start.21 = (bf16[256,512]{1,0:T(8,128)(2,1)S(1)}, bf16[256,512]{1,0:T(8,128)(2,1)S(1)}, u32[]{:S(2)}, u32[]{:S(2)}) collective-permute-start(bf16[256,512]{1,0:T(8,128)(2,1)S(1)} %shard_map.105.own_ref), channel_id=1, source_target_pairs={{0,1},{1,0},{2,3},{3,2},{4,5},{5,4},{6,7},{7,6},{8,9},{9,8},{10,11... | collective-permute-start | bytes 786440 | tf_op jit(solution)/shard_map/ppermute | solution.py:410
  77.4 11.7 %collective-permute-start.20 = (bf16[256,512]{1,0:T(8,128)(2,1)S(1)}, bf16[256,512]{1,0:T(8,128)(2,1)S(1)}, u32[]{:S(2)}, u32[]{:S(2)}) collective-permute-start(bf16[256,512]{1,0:T(8,128)(2,1)S(1)} %shard_map.106.own_ref), channel_id=1, source_target_pairs={{0,1},{1,0},{2,3},{3,2},{4,5},{5,4},{6,7},{7,6},{8,9},{9,8},{10,11... | collective-permute-start | bytes 786440 | tf_op jit(solution)/shard_map/ppermute | solution.py:410
  79.5 15.3 %collective-permute-start.19 = (bf16[256,512]{1,0:T(8,128)(2,1)S(1)}, bf16[256,512]{1,0:T(8,128)(2,1)S(1)}, u32[]{:S(2)}, u32[]{:S(2)}) collective-permute-start(bf16[256,512]{1,0:T(8,128)(2,1)S(1)} %shard_map.107.own_ref), channel_id=1, source_target_pairs={{0,1},{1,0},{2,3},{3,2},{4,5},{5,4},{6,7},{7,6},{8,9},{9,8},{10,11... | collective-permute-start | bytes 786440 | tf_op jit(solution)/shard_map/ppermute | solution.py:410
  82.3 15.2 %collective-permute-start.18 = (bf16[128,512]{1,0:T(8,128)(2,1)S(1)}, bf16[128,512]{1,0:T(8,128)(2,1)S(1)}, u32[]{:S(2)}, u32[]{:S(2)}) collective-permute-start(bf16[128,512]{1,0:T(8,128)(2,1)S(1)} %shard_map.108.own_ref), channel_id=1, source_target_pairs={{0,1},{1,0},{2,3},{3,2},{4,5},{5,4},{6,7},{7,6},{8,9},{9,8},{10,11... | collective-permute-start | bytes 393224 | tf_op jit(solution)/shard_map/ppermute | solution.py:410
  84.1 15.4 %collective-permute-start.15 = (bf16[128,512]{1,0:T(8,128)(2,1)S(1)}, bf16[128,512]{1,0:T(8,128)(2,1)S(1)}, u32[]{:S(2)}, u32[]{:S(2)}) collective-permute-start(bf16[128,512]{1,0:T(8,128)(2,1)S(1)} %shard_map.109.own_ref), channel_id=1, source_target_pairs={{0,1},{1,0},{2,3},{3,2},{4,5},{5,4},{6,7},{7,6},{8,9},{9,8},{10,11... | collective-permute-start | bytes 393224 | tf_op jit(solution)/shard_map/ppermute | solution.py:410

commit v9 on v8

--- a/solution.py
+++ b/solution.py
@@ -186,6 +186,37 @@
     query_part(j_ref[0], xs, w_ref, mean_ref, v_ref, wq_ref, wk_ref, halo_ref, 2 * qk_width + width, 0)
 
 
+def band_of(tile, span, first):
+    col = lax.broadcasted_iota(jnp.int32, (2 * tile, span), 1)
+    ahead = col - lax.broadcasted_iota(jnp.int32, (2 * tile, span), 0) % tile
+    seen = (ahead >= 1) & (ahead <= WIN)
+    if first is not None:
+        seen = seen & (col >= first)
+    return seen.astype(F32).astype(BF16)
+
+
+def window_tile(wq, keys, values, band, low):
+    none = jnp.zeros_like(wq)
+    scores = nt_dot(jnp.concatenate([jnp.where(low, wq, none), jnp.where(low, none, wq)], 0), keys)
+    expo = jnp.exp(scores).astype(BF16) * band
+    ones = jnp.ones(values.shape, BF16)
+    got = jnp.dot(expo, jnp.concatenate([values, ones], 1), preferred_element_type=F32)
+    tile = wq.shape[0]
+    got = jnp.where(jnp.concatenate([low, low], 1), got[:tile], got[tile:])
+    return got[:, :LANES] / got[:, LANES:]
+
+
+def edge_kernel(_, prev_ref, v_ref, wq_ref, wk_ref, win_ref):
+    tile = win_ref.shape[0]
+    band = band_of(tile, tile + WIN, None)
+    low = lax.broadcasted_iota(jnp.int32, (tile, LANES), 1) < DV
+    for p in range(win_ref.shape[1] // LANES):
+        cols = slice(p * LANES, (p + 1) * LANES)
+        values = jnp.concatenate([prev_ref[EDGE : EDGE + WIN, cols], v_ref[:tile, cols]], 0)
+        keys = jnp.concatenate([prev_ref[EDGE + WIN : HALO, cols], wk_ref[:tile, cols]], 0)
+        win_ref[:, cols] = window_tile(wq_ref[:tile, cols], keys, values, band, low)
+
+
 def attend_kernel(
     a_ref, turn_ref, prev_ref, q_ref, k_ref, v_ref, wq_ref, wk_ref, phi_ref, lin_ref, win_ref,
     vext_ref, kext_ref, *, heads, first
@@ -221,14 +252,10 @@
 
     down = lax.broadcasted_iota(jnp.int32, (2 * rows, rows), 0) % rows
     causal = lax.broadcasted_iota(jnp.int32, (2 * rows, rows), 1) <= down
-    col = lax.broadcasted_iota(jnp.int32, (2 * tile, span), 1)
-    ahead = col - lax.broadcasted_iota(jnp.int32, (2 * tile, span), 0) % tile
-    inside = (ahead >= 1) & (ahead <= WIN)
-    band = inside.astype(F32).astype(BF16)
+    band = band_of(tile, span, None)
     first_band = band
     if first:
-        first_band = (inside & (col >= jnp.where(a_ref[2] == 0, WIN, 0))).astype(F32).astype(BF16)
-    ones = jnp.ones((span, LANES), BF16)
+        first_band = band_of(tile, span, jnp.where(a_ref[2] == 0, WIN, 0))
     q = q * jnp.asarray(1.0 / FQK**0.5, BF16)
     for p in range(heads * DV // LANES):
         cols = slice(p * LANES, (p + 1) * LANES)
@@ -241,71 +268,88 @@
         lin_ref[:, cols] = 0.5 * jnp.where(low_half, got[:rows], got[rows:])
         for i in range(rows // tile):
             here = slice(i * tile, (i + 1) * tile)
-            wq = wq_ref[here, cols]
-            none = jnp.zeros_like(wq)
-            low = low_half[:tile]
             keys = kext_ref[i * tile : i * tile + span, cols]
             values = vext_ref[i * tile : i * tile + span, cols]
-            scores = nt_dot(jnp.concatenate([jnp.where(low, wq, none), jnp.where(low, none, wq)], 0), keys)
-            expo = jnp.exp(scores).astype(BF16) * (first_band if i == 0 else band)
-            got = jnp.dot(expo, jnp.concatenate([values, ones], 1), preferred_element_type=F32)
-            got = jnp.where(jnp.concatenate([low, low], 1), got[:tile], got[tile:])
-            win_ref[here, cols] = got[:, :LANES] / got[:, LANES:]
-
-
-def finish_kernel(a_ref, mean_ref, gain_ref, *refs, heads, before):
-    pairs = heads * DV // LANES
-    prior_refs, refs = refs[:pairs], refs[pairs:]
-    states, (phi_ref, lin_ref, win_ref, mix_ref, held_ref) = refs[:before], refs[before:]
-    rows = phi_ref.shape[0]
-    for r in range(pairs):
-        held_ref[r] = prior_refs[r][...].astype(F32)
+            win_ref[here, cols] = window_tile(
+                wq_ref[here, cols], keys, values, first_band if i == 0 else band, low_half[:tile]
+            )
+
+
+def carry_table(state, p, heads):
     in_group, lanes, slots = feature_layout(heads)
     in_pairs = in_group * DV // LANES
-    low_half = lax.broadcasted_iota(jnp.int32, (SHIFTS + 1, FQK, LANES), 2) < DV
-    for g in range(heads // in_group):
-        columns = []
-        for p in range(in_pairs):
-            pair = g * in_pairs + p
-            state = held_ref[jnp.bitwise_xor(a_ref[1], pair)]
-            for ref in states:
-                state = state + ref[pair]
-            state = state.reshape(SHIFTS + 1, FQK, LANES)
-            parts = [jnp.where(low_half, state, 0.0), jnp.where(low_half, 0.0, state)]
-            none = jnp.zeros_like(state)
-            parts = [none] * (2 * p) + parts + [none] * (in_group - 2 * p - 2)
-            parts = jnp.concatenate(parts, 1).reshape((SHIFTS + 1) * lanes, LANES)
-            if slots > SHIFTS + 1:
-                parts = jnp.concatenate([parts, jnp.zeros(((slots - SHIFTS - 1) * lanes, LANES), F32)], 0)
-            columns.append(parts.astype(BF16))
-        table = jnp.concatenate(columns, 1)
-        carried = jnp.dot(
-            phi_ref[:, g * slots * lanes : (g + 1) * slots * lanes], table, preferred_element_type=F32
-        )
-        for p in range(in_pairs):
-            at = (g * in_pairs + p) * LANES
-            cols = slice(at, at + LANES)
-            lin = lin_ref[:, cols] + carried[:, p * LANES : (p + 1) * LANES]
+    state = state.reshape(SHIFTS + 1, FQK, LANES)
+    low_half = lax.broadcasted_iota(jnp.int32, state.shape, 2) < DV
+    parts = [jnp.where(low_half, state, 0.0), jnp.where(low_half, 0.0, state)] * in_pairs
+    parts = jnp.concatenate(parts, 1)
+    if in_pairs > 1:
+        here = lax.broadcasted_iota(jnp.int32, parts.shape, 1) // (2 * FQK) == p
+        parts = jnp.where(here, parts, 0.0)
+    parts = parts.reshape((SHIFTS + 1) * lanes, LANES)
+    if slots > SHIFTS + 1:
+        parts = jnp.concatenate([parts, jnp.zeros(((slots - SHIFTS - 1) * lanes, LANES), F32)], 0)
+    return parts.astype(BF16)
+
+
+def finish_kernel(a_ref, mean_ref, gain_ref, *refs, heads, turns, before, edged):
+    prior_refs, refs = refs[: len(turns)], refs[len(turns) :]
+    states, refs = refs[: max(before)], refs[max(before) :]
+    edge_ref, refs = (refs[0], refs[1:]) if edged is not None else (None, refs)
+    mix_ref = refs[-1]
+    in_group, lanes, slots = feature_layout(heads)
+    in_pairs = in_group * DV // LANES
+    for i, r in enumerate(turns):
+        pair = jnp.bitwise_xor(a_ref[1], r)
+        group = lax.div(pair, in_pairs)
+        own = pl.ds(pl.multiple_of(group * (slots * lanes), LANES), slots * lanes)
+        cols = pl.ds(pl.multiple_of(pair * LANES, LANES), LANES)
+        state = prior_refs[i][...].astype(F32)
+        added, at = 0, 0
+        for b, count in enumerate(before):
+            phi_ref, lin_ref, win_ref = refs[3 * b : 3 * b + 3]
+            for c in range(added, count):
+                state = state + states[c][pair]
+            added = count
+            table = carry_table(state, lax.rem(pair, in_pairs), heads)
+            lin = lin_ref[:, cols] + jnp.dot(phi_ref[:, own], table, preferred_element_type=F32)
             scale = lax.rsqrt(head_mean(lin * lin, mean_ref[...]) + 1e-5)
-            mix_ref[:, cols] = (lin * scale * gain_ref[:, cols] + win_ref[:, cols]).astype(BF16)
-
-
-def output_kernel(a_ref, own_ref, w_ref, *refs, n, offset, parts):
-    others, weights, (o_ref, held_ref, sem) = refs[: n - 1], refs[n - 1 : n - 1 + parts * (n - 1)], refs[-3:]
-    cols = held_ref.shape[1]
+            win = win_ref[:, cols]
+            if b == edged:
+                win = jnp.concatenate([edge_ref[:, cols], win[edge_ref.shape[0] :]], 0)
+            rows = lin.shape[0]
+            mix_ref[at : at + rows, i * LANES : (i + 1) * LANES] = (
+                lin * scale * gain_ref[:, cols] + win
+            ).astype(BF16)
+            at += rows
+
+
+def output_kernel(a_ref, w_ref, *refs, n, offset, parts, turns):
+    pieces, refs = refs[: n * len(turns)], refs[n * len(turns) :]
+    weights, (o_ref, held_ref, mixed_ref, sem) = refs[: parts * (n - 1)], refs[-4:]
+    rows, cols = held_ref.shape
     mine = pl.ds(pl.multiple_of(a_ref[0] * cols, cols), cols)
-    total = jnp.dot(own_ref[...], w_ref[:, mine], preferred_element_type=F32).astype(BF16).astype(F32)
-    for r, m_ref in enumerate(others):
-        part = None
-        for i in range(parts):
-            ref = weights[r * parts + i]
-            depth = ref.shape[0]
-            at = depth * (jnp.bitwise_xor(a_ref[2] % 2, i) if parts > 1 else 0)
-            got = jnp.dot(m_ref[:, pl.ds(pl.multiple_of(at, depth), depth)], ref[...], preferred_element_type=F32)
-            part = got if part is None else part + got
-        total = total + part.astype(BF16).astype(F32)
+    total = None
+    for r in range(n):
+        for i, (all_rows, pairs) in enumerate(turns):
+            here = slice(offset, offset + rows) if all_rows else slice(0, rows)
+            for k, turn in enumerate(pairs):
+                at = pl.multiple_of(jnp.bitwise_xor(a_ref[1], turn) * LANES, LANES)
+                mixed_ref[r, :, pl.ds(at, LANES)] = pieces[r * len(turns) + i][here, k * LANES : (k + 1) * LANES]
+        if r == 0:
+            part = jnp.dot(mixed_ref[0], w_ref[:, mine], preferred_element_type=F32)
+        else:
+            part = None
+            for i in range(parts):
+                ref = weights[(r - 1) * parts + i]
+                depth = ref.shape[0]
+                at = depth * (jnp.bitwise_xor(a_ref[2] % 2, i) if parts > 1 else 0)
+                rows_of = pl.ds(pl.multiple_of(at, depth), depth)
+                got = jnp.dot(mixed_ref[r, :, rows_of], ref[...], preferred_element_type=F32)
+                part = got if part is None else part + got
+        part = part.astype(BF16).astype(F32)
+        total = part if total is None else total + part
     held_ref[...] = total.astype(BF16)
-    copy = pltpu.make_async_copy(held_ref, o_ref.at[pl.ds(offset, held_ref.shape[0]), :], sem)
+    copy = pltpu.make_async_copy(held_ref, o_ref.at[pl.ds(offset, rows), :], sem)
     copy.start()
     copy.wait()
 
@@ -491,7 +535,7 @@
             vmem=32 << 20,
         )(places, means, arranged, v, *pieces[b])
 
-    def attend(b, prev, places=places):
+    def attend(b, prev):
         rows = blocks[b][1]
         k, v, _, q, wq, wk, _ = done[b]
         return call(
@@ -500,7 +544,6 @@
             in_specs=[scalar] + [whole] * 7,
             out_specs=[whole] * 3,
             scratch_shapes=[pltpu.VMEM((WIN + rows, width), BF16)] * 2,
-            flops=4850 * 10**6 if b == last else 1,
             vmem=16 << 20,
         )(places, turn, prev, q, k, v, wq, wk)
 
@@ -509,50 +552,75 @@
     halo = lax.ppermute(done[last][6], "ctx", [(i, i + 1) for i in range(ctx - 1)])
     prevs = {0: halo}
     for b in range(last - 1):
-        done[b] = do_block(b, prevs[b], attended[b - 1][1] if b else None)
+        done[b] = do_block(b, prevs[b], [a[1] for a in attended.values()] if b else None)
         prevs[b + 1] = done[b][6]
         attended[b] = attend(b, prevs[b])
+        if b == 0:
+            attended[last] = attend(last, halo)
     b = last - 1
     k, v, state, *sends = do_block(b, prevs[b], attended[b - 1][1], [done[c][2] for c in (last, *range(b))])
     done[b] = (k, v, state, *do_queries(b, v))
     prevs[last] = done[b][6]
     attended[last - 1] = attend(last - 1, prevs[last - 1])
-    held = sends[:1] + [exchange(sends[r], "ctx", r) for r in range(1, len(sends))]
-    fetched = [from_head(pick(r), r) for r in range(1, n)]
+    tile = 128
+    edge = call(
+        edge_kernel,
+        jax.ShapeDtypeStruct((tile, width), F32),
+        in_specs=[scalar] + [whole] * 4,
+        out_specs=whole,
+        vmem=16 << 20,
+    )(places, done[last - 1][6], done[last][1], done[last][4], done[last][5])
+
+    def finish(turns, priors, some, behind):
+        before = list(some)
+        operands = [after(places, behind), means, gain, *priors, *[done[c][2] for c in range(max(before))]]
+        edged = before.index(last) if last in before else None
+        if edged is not None:
+            operands.append(edge)
+        for b in some:
+            operands += attended[b]
+        rows = sum(blocks[b][1] for b in some)
+        return call(
+            functools.partial(finish_kernel, heads=heads, turns=turns, before=before, edged=edged),
+            jax.ShapeDtypeStruct((rows, len(turns) * LANES), BF16),
+            in_specs=[scalar] + [whole] * (len(operands) - 1),
+            out_specs=whole,
+            flops=20 * 10**9 if tuple(some) == order[:1] else 4850 * 10**6 if len(some) > 1 else 1,
+            vmem=24 << 20,
+        )(*operands)
+
+    order = (0, 1, 4, 2, 3)
+    early = []
     if in_planes:
-        back = prior_in_planes(held, places, [done[last - 1][1], attended[last - 1][1]])
-        priors = [back[0]] + [exchange(back[r], "ctx", r) for r in range(1, PLANE)]
-        attended[last] = attend(last, prevs[last], after(places, back[0]))
+        held = sends[:1] + [exchange(sends[r], "ctx", r) for r in range(1, PLANE)]
+        back = prior_in_planes(held, places, [done[last - 1][1], (attended[last - 1][1], edge)])
+        priors = [exchange(back[r], "ctx", r) for r in range(1, PLANE)]
+        turns = tuple(range(1, PLANE))
+        mixed = finish((0,), back[:1], range(last + 1), done[last][1])
+        early = [mixed] + [from_head(mixed, r) for r in range(1, n)]
     else:
         priors = prior_by_doubling(sum(done[b][2] for b in range(last + 1)), position)
-        attended[last] = attend(last, prevs[last])
-
-    order = (0, 1, 4, 2, 3)
-    mixed = attended[last][1]
-    mixes = {}
-    for b in order:
-        rows = blocks[b][1]
-        mixed = call(
-            functools.partial(finish_kernel, heads=heads, before=b),
-            jax.ShapeDtypeStruct((rows, width), BF16),
-            in_specs=[scalar] + [whole] * (2 + pairs + b + 3),
-            out_specs=whole,
-            scratch_shapes=[pltpu.VMEM((pairs, FEATS, LANES), F32)],
-            flops=20 * 10**9 if b == order[0] else 1,
-            vmem=16 << 20,
-        )(after(places, mixed), means, gain, *priors, *[done[c][2] for c in range(b)], *attended[b])
-        mixes[b] = [mixed] + [from_head(mixed, r) for r in range(1, n)]
-
+        turns = tuple(range(pairs))
+        mixed = attended[last][1]
+    fetched = [from_head(pick(r), r) for r in range(1, n)]
     out_rows = []
     for got in fetched:
         out_rows.append(got)
         if out_parts > 1:
-            out_rows.append(exchange(after(got, attended[last][1]), "ctx", 1))
+            out_rows.append(exchange(after(got, mixed), "ctx", 1))
+
+    mixes = {}
+    for b in order:
+        mixed = finish(turns, priors, (b,), mixed)
+        mixes[b] = [mixed] + [from_head(mixed, r) for r in range(1, n)]
 
     result = None
     for b in order:
         at, rows = blocks[b]
-        operands = [places, mixes[b][0], out_weight] + mixes[b][1:] + out_rows
+        operands = [places, out_weight]
+        for r in range(n):
+            operands += ([early[r]] if early else []) + [mixes[b][r]]
+        operands += out_rows
         specs = [scalar] + [whole] * (len(operands) - 1)
         aliases = {}
         if result is not None:
@@ -560,11 +628,21 @@
             operands.append(result)
             specs.append(pl.BlockSpec(memory_space=pl.ANY))
         result = call(
-            functools.partial(output_kernel, n=n, offset=at, parts=out_parts),
+            functools.partial(
+                output_kernel,
+                n=n,
+                offset=at,
+                parts=out_parts,
+                turns=([(True, (0,))] if early else []) + [(False, turns)],
+            ),
             jax.ShapeDtypeStruct((row_count, cols), BF16),
             in_specs=specs,
             out_specs=pl.BlockSpec(memory_space=pl.ANY),
-            scratch_shapes=[pltpu.VMEM((rows, cols), BF16), pltpu.SemaphoreType.DMA],
+            scratch_shapes=[
+                pltpu.VMEM((rows, cols), BF16),
+                pltpu.VMEM((n, rows, width), BF16),
+                pltpu.SemaphoreType.DMA,
+            ],
             input_output_aliases=aliases,
             vmem=16 << 20,
         )(*operands)

time: 102 us -> 100 us (0.980)
  waiting for transfers between devices: 17.6 us -> 12.6 us
  Pallas kernels: 51 us -> 53.8 us
    ppermute x11 -> x12, waiting for transfers between devices: 15.6 us -> 11.6 us  [from_head(): return lax.ppermute(value, 'head', [(i, (i + by) % n) for i in range(n)])]
    pallas_call x10 -> x12, Pallas kernels: 16.7 us -> 19.2 us  [the longest x5 9.73 us: per_device(): call(functools.partial(output_kernel, n=n, offset=at, parts=out_parts, tu...]
    ppermute x11 -> x12, starting transfers between devices: 14.9 us -> 15.9 us  [from_head(): return lax.ppermute(value, 'head', [(i, (i + by) % n) for i in range(n)])]
  transfers between devices with their start and end apart: 22 -> 23, of which waited for: 10 -> 6; matrix products, arithmetic and copies ran while one was open for 2% -> 2% of each run, Pallas kernels for 47% -> 50%
where the time goes in v9:
time: 100 us; the launch traced here: 99.7 us
  Pallas kernels  53.8 us (54%)
  starting transfers between devices  26.2 us (26%)
  waiting for transfers between devices  12.6 us (13%)
  local copies, waits for them, and re-layouts  6.54 us (7%)
    ppermute x12, starting transfers between devices, from_head(): return lax.ppermute(value, 'head', [(i, (i + by) % n) for i in range(n)])  15.9 us
    pallas_call x5, Pallas kernels, do_block(): call(functools.partial(block_kernel, n=n, heads=heads, extra=extra, other...  15.9 us
    ppermute x12, waiting for transfers between devices, from_head(): return lax.ppermute(value, 'head', [(i, (i + by) % n) for i in range(n)])  11.6 us
    pallas_call x5, Pallas kernels, attend(): call(functools.partial(attend_kernel, heads=heads, first=b == 0), [jax.Sh...  9.97 us
    pallas_call x5, Pallas kernels, per_device(): call(functools.partial(output_kernel, n=n, offset=at, parts=out_parts, tu...  9.73 us
    ppermute x10, starting transfers between devices, exchange(): return lax.ppermute(value, axis, [(i, i ^ flip) for i in range(count)])  8.69 us
    pallas_call x6, Pallas kernels, finish(): call(functools.partial(finish_kernel, heads=heads, turns=turns, before=be...  8.27 us
    pallas_call x1, Pallas kernels, per_device(): call(functools.partial(arrange_kernel, heads=heads), jax.ShapeDtypeStruct...  5.09 us
  transfers between devices with their start and end apart: 23, of which 6 were waited for; matrix products, arithmetic and copies ran while one was open for 2% of the time, Pallas kernels for 50%

profile of v9, /device:TPU:0, one launch (start us, length us, event | category | flops | bytes accessed | tf_op | source)
XLA Modules:
  0.0 99.7 jit_solution(4887397694100708284)
XLA Ops:
  1.2 3.0 %collective-permute-start = (bf16[272,1024]{1,0:T(8,128)(2,1)S(1)}, bf16[272,1024]{1,0:T(8,128)(2,1)S(1)}, u32[]{:S(2)}, u32[]{:S(2)}) collective-permute-start(bf16[272,1024]{1,0:T(8,128)(2,1)S(1)} %slice.15.refs_0_), channel_id=1, source_target_pairs={{0,1},{1,0},{2,3},{3,2},{4,5},{5,4},{6,7},{7,6},{8,9},{9,8},{10,11... | collective-permute-start | bytes 1671176 | tf_op jit(solution)/shard_map/ppermute | solution.py:454
  5.6 2.0 %collective-permute-start.3 = (bf16[256,1024]{1,0:T(8,128)(2,1)S(1)}, bf16[256,1024]{1,0:T(8,128)(2,1)S(1)}, u32[]{:S(2)}, u32[]{:S(2)}) collective-permute-start(bf16[256,1024]{1,0:T(8,128)(2,1)S(1)} %get-tuple-element.105.refs_0_), channel_id=1, source_target_pairs={{0,1},{1,0},{2,3},{3,2},{4,5},{5,4},{6,7},{7,6},{8,9},{9,8},{10,11... | collective-permute-start | bytes 1572872 | tf_op jit(solution)/shard_map/ppermute | solution.py:454
  8.8 1.9 %collective-permute-start.5 = (bf16[128,1024]{1,0:T(8,128)(2,1)S(1)}, bf16[128,1024]{1,0:T(8,128)(2,1)S(1)}, u32[]{:S(2)}, u32[]{:S(2)}) collective-permute-start(bf16[128,1024]{1,0:T(8,128)(2,1)S(1)} %get-tuple-element.123.refs_0_), channel_id=1, source_target_pairs={{0,1},{1,0},{2,3},{3,2},{4,5},{5,4},{6,7},{7,6},{8,9},{9,8},{10,11... | collective-permute-start | bytes 786440 | tf_op jit(solution)/shard_map/ppermute | solution.py:454
  10.7 3.1 %copy-done.3 = bf16[2048,1792]{1,0:T(8,128)(2,1)S(1)} copy-done((bf16[2048,1792]{1,0:T(8,128)(2,1)S(1)}, bf16[2048,1792]{1,0:T(8,128)(2,1)}, u32[]{:S(2)}) %copy-start.3) | copy-done | bytes 7340056
  13.8 5.1 %shard_map.91.w_ref = bf16[2048,1792]{1,0:T(8,128)(2,1)S(1)} custom-call(bf16[2048,1792]{1,0:T(8,128)(2,1)S(1)} %copy-done.3), custom_call_target="tpu_custom_call" | custom-call | flops 1 | bytes 1 | tf_op jit(solution)/shard_map/pallas_call | solution.py:491
  19.0 3.8 %shard_map.92 = (bf16[256,128]{1,0:T(8,128)(2,1)S(1)}, bf16[256,512]{1,0:T(8,128)(2,1)S(1)}, f32[4,160,128]{2,1,0:T(8,128)S(1)}, bf16[256,128]{1,0:T(8,128)(2,1)...) custom-call(s32[3]{0:T(128)S(1)} %pad_add_fusion.j_ref.a_ref._, ...), custom_call_target="tpu_custom_call" | custom-call | flops 1 | bytes 1 | tf_op jit(solution)/shard_map/pallas_call | solution.py:517
  22.8 1.6 %collective-permute-start.1 = (bf16[144,512]{1,0:T(8,128)(2,1)S(1)}, bf16[144,512]{1,0:T(8,128)(2,1)S(1)}, u32[]{:S(2)}, u32[]{:S(2)}) collective-permute-start(bf16[144,512]{1,0:T(8,128)(2,1)S(1)} %get-tuple-element.90), channel_id=1, source_target_pairs={{0,2},{2,4},{4,6},{6,8},{8,10},{10,12},{12,14},{14,16},{16,18},{18... | collective-permute-start | bytes 442376 | tf_op jit(solution)/shard_map/ppermute | solution.py:552
  24.4 4.5 %collective-permute-done.2.refs_1_ = bf16[256,1024]{1,0:T(8,128)(2,1)S(1)} collective-permute-done((bf16[256,1024]{1,0:T(8,128)(2,1)S(1)}, bf16[256,1024]{1,0:T(8,128)(2,1)S(1)}, u32[]{:S(2)}, u32[]{:S(2)}) %collective-permute-start.2) | collective-permute-done | bytes 524320 | tf_op jit(solution)/shard_map/ppermute | solution.py:454
  28.9 3.8 %shard_map.93 = (bf16[256,128]{1,0:T(8,128)(2,1)S(1)}, bf16[256,512]{1,0:T(8,128)(2,1)S(1)}, f32[4,160,128]{2,1,0:T(8,128)S(1)}, bf16[256,128]{1,0:T(8,128)(2,1)...) custom-call(s32[3]{0:T(128)S(1)} %pad_add_fusion.j_ref.a_ref._, ...), custom_call_target="tpu_custom_call" | custom-call | flops 1 | bytes 1 | tf_op jit(solution)/shard_map/pallas_call | solution.py:517
  32.7 2.1 %shard_map.94 = (bf16[256,1280]{1,0:T(8,128)(2,1)S(1)}, f32[256,512]{1,0:T(8,128)S(1)}, f32[256,512]{1,0:T(8,128)S(1)}) custom-call(s32[3]{0:T(128)S(1)} %pad_add_fusion.j_ref.a_ref._, bf16[128,1280]{1,0:T(8,128)(2,1)S(1)} %copy-done.2, bf16[144,512]{1,0:T(8,128)(2,1)S(1)} %collective-permute-done.1.refs_2_.prev_ref, ...), custom_call_target="tpu_custom_call" | custom-call | flops 1 | bytes 1 | tf_op jit(solution)/shard_map/pallas_call | solution.py:541
  34.9 2.1 %shard_map.95 = (bf16[256,1280]{1,0:T(8,128)(2,1)S(1)}, f32[256,512]{1,0:T(8,128)S(1)}, f32[256,512]{1,0:T(8,128)S(1)}) custom-call(s32[3]{0:T(128)S(1)} %pad_add_fusion.j_ref.a_ref._, bf16[128,1280]{1,0:T(8,128)(2,1)S(1)} %copy-done.2, bf16[144,512]{1,0:T(8,128)(2,1)S(1)} %collective-permute-done.1.refs_2_.prev_ref, ...), custom_call_target="tpu_custom_call" | custom-call | flops 1 | bytes 1 | tf_op jit(solution)/shard_map/pallas_call | solution.py:541
  37.0 3.1 %collective-permute-done.3.refs_1_ = bf16[256,1024]{1,0:T(8,128)(2,1)S(1)} collective-permute-done((bf16[256,1024]{1,0:T(8,128)(2,1)S(1)}, bf16[256,1024]{1,0:T(8,128)(2,1)S(1)}, u32[]{:S(2)}, u32[]{:S(2)}) %collective-permute-start.3) | collective-permute-done | bytes 524320 | tf_op jit(solution)/shard_map/ppermute | solution.py:454
  40.1 3.8 %shard_map.96 = (bf16[256,128]{1,0:T(8,128)(2,1)S(1)}, bf16[256,512]{1,0:T(8,128)(2,1)S(1)}, f32[4,160,128]{2,1,0:T(8,128)S(1)}, bf16[256,128]{1,0:T(8,128)(2,1)...) custom-call(s32[3]{0:T(128)S(1)} %pad_add_fusion.j_ref.a_ref._, ...), custom_call_target="tpu_custom_call" | custom-call | flops 1 | bytes 1 | tf_op jit(solution)/shard_map/pallas_call | solution.py:517
  44.0 2.1 %shard_map.97 = (bf16[256,1280]{1,0:T(8,128)(2,1)S(1)}, f32[256,512]{1,0:T(8,128)S(1)}, f32[256,512]{1,0:T(8,128)S(1)}) custom-call(s32[3]{0:T(128)S(1)} %pad_add_fusion.j_ref.a_ref._, bf16[128,1280]{1,0:T(8,128)(2,1)S(1)} %copy-done.2, bf16[144,512]{1,0:T(8,128)(2,1)S(1)} %get-tuple-element.103.refs_2_.prev_ref, ...), custom_call_target="tpu_custom_call" | custom-call | flops 1 | bytes 1 | tf_op jit(solution)/shard_map/pallas_call | solution.py:541
  46.1 2.6 %shard_map.98 = (bf16[128,128]{1,0:T(8,128)(2,1)S(1)}, bf16[128,512]{1,0:T(8,128)(2,1)S(1)}, f32[4,160,128]{2,1,0:T(8,128)S(1)}, bf16[128,128]{1,0:T(8,128)(2,1)...) custom-call(s32[3]{0:T(128)S(1)} %pad_add_fusion.j_ref.a_ref._, ...), custom_call_target="tpu_custom_call" | custom-call | flops 1 | bytes 1 | tf_op jit(solution)/shard_map/pallas_call | solution.py:517
  48.7 1.9 %shard_map.99 = (bf16[128,1280]{1,0:T(8,128)(2,1)S(1)}, f32[128,512]{1,0:T(8,128)S(1)}, f32[128,512]{1,0:T(8,128)S(1)}) custom-call(s32[3]{0:T(128)S(1)} %pad_add_fusion.j_ref.a_ref._, bf16[128,1280]{1,0:T(8,128)(2,1)S(1)} %copy-done.2, bf16[144,512]{1,0:T(8,128)(2,1)S(1)} %get-tuple-element.114.refs_2_.prev_ref, ...), custom_call_target="tpu_custom_call" | custom-call | flops 1 | bytes 1 | tf_op jit(solution)/shard_map/pallas_call | solution.py:541
  50.6 1.8 %shard_map.100 = (bf16[128,128]{1,0:T(8,128)(2,1)S(1)}, bf16[128,512]{1,0:T(8,128)(2,1)S(1)}, f32[4,160,128]{2,1,0:T(8,128)S(1)}, bf16[160,128]{1,0:T(8,128)(2,1...) custom-call(s32[3]{0:T(128)S(1)} %pad_add_fusion.j_ref.a_ref._, ...), custom_call_target="tpu_custom_call" | custom-call | flops 1 | bytes 1 | tf_op jit(solution)/shard_map/pallas_call | solution.py:517
  52.5 2.1 %collective-permute-start.7 = (bf16[160,128]{1,0:T(8,128)(2,1)S(1)}, bf16[160,128]{1,0:T(8,128)(2,1)S(1)}, u32[]{:S(2)}, u32[]{:S(2)}) collective-permute-start(bf16[160,128]{1,0:T(8,128)(2,1)S(1)} %get-tuple-element.139), channel_id=1, source_target_pairs={{0,4},{2,6},{4,0},{6,2},{8,12},{10,14},{12,8},{14,10},{16,20},{18,... | collective-permute-start | bytes 122888 | tf_op jit(solution)/shard_map/ppermute | solution.py:363
  55.3 1.8 %collective-permute-start.17 = (bf16[256,1024]{1,0:T(8,128)(2,1)S(1)}, bf16[256,1024]{1,0:T(8,128)(2,1)S(1)}, u32[]{:S(2)}, u32[]{:S(2)}) collective-permute-start(bf16[256,1024]{1,0:T(8,128)(2,1)S(1)} %shard_map.112), channel_id=1, source_target_pairs={{0,1},{1,0},{2,3},{3,2},{4,5},{5,4},{6,7},{7,6},{8,9},{9,8},{10,11... | collective-permute-start | bytes 1572872 | tf_op jit(solution)/shard_map/ppermute | solution.py:454
  58.8 3.7 %collective-permute-start.11 = (bf16[160,128]{1,0:T(8,128)(2,1)S(1)}, bf16[160,128]{1,0:T(8,128)(2,1)S(1)}, u32[]{:S(2)}, u32[]{:S(2)}) collective-permute-start(bf16[160,128]{1,0:T(8,128)(2,1)S(1)} %get-tuple-element.145), channel_id=1, source_target_pairs={{0,24},{2,26},{4,28},{6,30},{8,16},{10,18},{12,20},{14,22},{16,8},... | collective-permute-start | bytes 122888 | tf_op jit(solution)/shard_map/ppermute | solution.py:363
  63.2 1.8 %shard_map.101 = (bf16[128,128]{1,0:T(8,128)(2,1)S(1)}, bf16[128,512]{1,0:T(8,128)(2,1)S(1)}, bf16[128,512]{1,0:T(8,128)(2,1)S(1)}, bf16[144,512]{1,0:T(8,128)(2,1)S(1)}) custom-call(s32[3]{0:T(128)S(1)} %pad_add_fusion.j_ref.a_ref._, bf16[256,128]{1,0:T(8,128)(2,1)S(1)} %copy-done.4, bf16[2048,1792]{1,0:T(8,128)(2,1)S(1)} %shard_map.91.w_ref, ...), custom_call_target="tpu_custom_call" | custom-call | flops 1 | bytes 1 | tf_op jit(solution)/shard_map/pallas_call | solution.py:530
  66.2 1.7 %shard_map.102 = (bf16[128,1280]{1,0:T(8,128)(2,1)S(1)}, f32[128,512]{1,0:T(8,128)S(1)}, f32[128,512]{1,0:T(8,128)S(1)}) custom-call(s32[3]{0:T(128)S(1)} %pad_add_fusion.j_ref.a_ref._, bf16[128,1280]{1,0:T(8,128)(2,1)S(1)} %copy-done.2, bf16[144,512]{1,0:T(8,128)(2,1)S(1)} %get-tuple-element.115.refs_2_.prev_ref, ...), custom_call_target="tpu_custom_call" | custom-call | flops 1 | bytes 1 | tf_op jit(solution)/shard_map/pallas_call | solution.py:541
  70.5 1.7 %shard_map.106.refs_0_ = bf16[1024,128]{1,0:T(8,128)(2,1)S(1)} custom-call(s32[3]{0:T(128)S(1)} %pad_add_fusion.j_ref.a_ref._, bf16[256,128]{1,0:T(8,128)(2,1)S(1)} %copy-done.4, f32[1,512]{1,0:T(1,128)S(1)} %bitcast.4, bf16[160,128]{1,0:T(8,128)(2,1)S(1)} %get-tuple-element.146.refs_0_, f32[4,160,128]{2,1,0:T(8,128)S(1)} %get-tuple-element.125.refs_4_.refs_1_.refs_3_, ...), custom_call_target="tpu_custom_call" | custom-call | flops 4849999872 | bytes 1 | tf_op jit(solution)/shard_map/pallas_call | solution.py:583
  72.2 1.6 %collective-permute-start.15 = (bf16[1024,128]{1,0:T(8,128)(2,1)S(1)}, bf16[1024,128]{1,0:T(8,128)(2,1)S(1)}, u32[]{:S(2)}, u32[]{:S(2)}) collective-permute-start(bf16[1024,128]{1,0:T(8,128)(2,1)S(1)} %shard_map.106.refs_0_), channel_id=1, source_target_pairs={{0,1},{1,0},{2,3},{3,2},{4,5},{5,4},{6,7},{7,6},{8,9},{9,8},{10,11... | collective-permute-start | bytes 786440 | tf_op jit(solution)/shard_map/ppermute | solution.py:454
  83.8 1.8 %collective-permute-done.22.refs_3_ = bf16[256,384]{1,0:T(8,128)(2,1)S(1)} collective-permute-done((bf16[256,384]{1,0:T(8,128)(2,1)S(1)}, bf16[256,384]{1,0:T(8,128)(2,1)S(1)}, u32[]{:S(2)}, u32[]{:S(2)}) %collective-permute-start.22) | collective-permute-done | bytes 196640 | tf_op jit(solution)/shard_map/ppermute | solution.py:454
  85.6 1.5 %collective-permute-start.19 = (bf16[128,384]{1,0:T(8,128)(2,1)S(1)}, bf16[128,384]{1,0:T(8,128)(2,1)S(1)}, u32[]{:S(2)}, u32[]{:S(2)}) collective-permute-start(bf16[128,384]{1,0:T(8,128)(2,1)S(1)} %shard_map.110.refs_1_), channel_id=1, source_target_pairs={{0,1},{1,0},{2,3},{3,2},{4,5},{5,4},{6,7},{7,6},{8,9},{9,8},{10,11... | collective-permute-start | bytes 294920 | tf_op jit(solution)/shard_map/ppermute | solution.py:454
  87.6 2.1 %shard_map.113.refs_6_ = bf16[1024,1024]{1,0:T(8,128)(2,1)} custom-call(s32[3]{0:T(128)S(1)} %pad_add_fusion.j_ref.a_ref._, bf16[512,2048]{1,0:T(8,128)(2,1)S(1)} %copy-done, bf16[1024,128]{1,0:T(8,128)(2,1)S(1)} %shard_map.106.refs_0_, bf16[256,384]{1,0:T(8,128)(2,1)S(1)} %shard_map.107.refs_1_, bf16[1024,128]{1,0:T(8,128)(2,1)S(1)} %collective-permute-done.15.refs_2_, ...), custom_call_target="tpu_custom_call" | custom-call | flops 1 | bytes 1 | tf_op jit(solution)/shard_map/pallas_call | solution.py:630
  89.8 2.1 %shard_map.114.refs_6_ = bf16[1024,1024]{1,0:T(8,128)(2,1)} custom-call(s32[3]{0:T(128)S(1)} %pad_add_fusion.j_ref.a_ref._, bf16[512,2048]{1,0:T(8,128)(2,1)S(1)} %copy-done, bf16[1024,128]{1,0:T(8,128)(2,1)S(1)} %shard_map.106.refs_0_, bf16[256,384]{1,0:T(8,128)(2,1)S(1)} %shard_map.108.refs_1_, ...), custom_call_target="tpu_custom_call", output_to_operand_aliasing={{}: (8, {})} | custom-call | flops 1 | bytes 1 | tf_op jit(solution)/shard_map/pallas_call | solution.py:630
  91.9 2.1 %collective-permute-done.20.refs_3_ = bf16[256,384]{1,0:T(8,128)(2,1)S(1)} collective-permute-done((bf16[256,384]{1,0:T(8,128)(2,1)S(1)}, bf16[256,384]{1,0:T(8,128)(2,1)S(1)}, u32[]{:S(2)}, u32[]{:S(2)}) %collective-permute-start.20) | collective-permute-done | bytes 196640 | tf_op jit(solution)/shard_map/ppermute | solution.py:454
  94.0 2.1 %shard_map.115.refs_6_ = bf16[1024,1024]{1,0:T(8,128)(2,1)} custom-call(s32[3]{0:T(128)S(1)} %pad_add_fusion.j_ref.a_ref._, bf16[512,2048]{1,0:T(8,128)(2,1)S(1)} %copy-done, bf16[1024,128]{1,0:T(8,128)(2,1)S(1)} %shard_map.106.refs_0_, bf16[256,384]{1,0:T(8,128)(2,1)S(1)} %shard_map.109.refs_1_, ...), custom_call_target="tpu_custom_call", output_to_operand_aliasing={{}: (8, {})} | custom-call | flops 1 | bytes 1 | tf_op jit(solution)/shard_map/pallas_call | solution.py:630
  96.1 1.7 %shard_map.116.refs_6_ = bf16[1024,1024]{1,0:T(8,128)(2,1)} custom-call(s32[3]{0:T(128)S(1)} %pad_add_fusion.j_ref.a_ref._, bf16[512,2048]{1,0:T(8,128)(2,1)S(1)} %copy-done, bf16[1024,128]{1,0:T(8,128)(2,1)S(1)} %shard_map.106.refs_0_, bf16[128,384]{1,0:T(8,128)(2,1)S(1)} %shard_map.110.refs_1_, ...), custom_call_target="tpu_custom_call", output_to_operand_aliasing={{}: (8, {})} | custom-call | flops 1 | bytes 1 | tf_op jit(solution)/shard_map/pallas_call | solution.py:630
  97.8 1.7 %shard_map.117 = bf16[1024,1024]{1,0:T(8,128)(2,1)} custom-call(s32[3]{0:T(128)S(1)} %pad_add_fusion.j_ref.a_ref._, bf16[512,2048]{1,0:T(8,128)(2,1)S(1)} %copy-done, bf16[1024,128]{1,0:T(8,128)(2,1)S(1)} %shard_map.106.refs_0_, bf16[128,384]{1,0:T(8,128)(2,1)S(1)} %shard_map.111.refs_1_, ...), custom_call_target="tpu_custom_call", output_to_operand_aliasing={{}: (8, {})} | custom-call | flops 1 | bytes 1 | tf_op jit(solution)/shard_map/pallas_call | solution.py:630
  (61 shorter events, 21.3 us)
Async XLA Ops:
  1.2 17.7 %collective-permute-start = (bf16[272,1024]{1,0:T(8,128)(2,1)S(1)}, bf16[272,1024]{1,0:T(8,128)(2,1)S(1)}, u32[]{:S(2)}, u32[]{:S(2)}) collective-permute-start(bf16[272,1024]{1,0:T(8,128)(2,1)S(1)} %slice.15.refs_0_), channel_id=1, source_target_pairs={{0,1},{1,0},{2,3},{3,2},{4,5},{5,4},{6,7},{7,6},{8,9},{9,8},{10,11... | collective-permute-start | bytes 1671176 | tf_op jit(solution)/shard_map/ppermute | solution.py:454
  5.5 23.4 %collective-permute-start.2 = (bf16[256,1024]{1,0:T(8,128)(2,1)S(1)}, bf16[256,1024]{1,0:T(8,128)(2,1)S(1)}, u32[]{:S(2)}, u32[]{:S(2)}) collective-permute-start(bf16[256,1024]{1,0:T(8,128)(2,1)S(1)} %get-tuple-element.91.refs_0_), channel_id=1, source_target_pairs={{0,1},{1,0},{2,3},{3,2},{4,5},{5,4},{6,7},{7,6},{8,9},{9,8},{10,11... | collective-permute-start | bytes 1572872 | tf_op jit(solution)/shard_map/ppermute | solution.py:454
  5.6 34.6 %collective-permute-start.3 = (bf16[256,1024]{1,0:T(8,128)(2,1)S(1)}, bf16[256,1024]{1,0:T(8,128)(2,1)S(1)}, u32[]{:S(2)}, u32[]{:S(2)}) collective-permute-start(bf16[256,1024]{1,0:T(8,128)(2,1)S(1)} %get-tuple-element.105.refs_0_), channel_id=1, source_target_pairs={{0,1},{1,0},{2,3},{3,2},{4,5},{5,4},{6,7},{7,6},{8,9},{9,8},{10,11... | collective-permute-start | bytes 1572872 | tf_op jit(solution)/shard_map/ppermute | solution.py:454
  8.6 37.5 %collective-permute-start.4 = (bf16[128,1024]{1,0:T(8,128)(2,1)S(1)}, bf16[128,1024]{1,0:T(8,128)(2,1)S(1)}, u32[]{:S(2)}, u32[]{:S(2)}) collective-permute-start(bf16[128,1024]{1,0:T(8,128)(2,1)S(1)} %get-tuple-element.113.refs_0_), channel_id=1, source_target_pairs={{0,1},{1,0},{2,3},{3,2},{4,5},{5,4},{6,7},{7,6},{8,9},{9,8},{10,11... | collective-permute-start | bytes 786440 | tf_op jit(solution)/shard_map/ppermute | solution.py:454
  8.8 10.1 %copy-start.1 = (bf16[1408,128]{1,0:T(8,128)(2,1)S(1)}, bf16[1408,128]{1,0:T(8,128)(2,1)}, u32[]{:S(2)}) copy-start(bf16[1408,128]{1,0:T(8,128)(2,1)} %constant.30.clone.turn_ref) | copy-start | bytes 1081348
  8.8 41.8 %collective-permute-start.5 = (bf16[128,1024]{1,0:T(8,128)(2,1)S(1)}, bf16[128,1024]{1,0:T(8,128)(2,1)S(1)}, u32[]{:S(2)}, u32[]{:S(2)}) collective-permute-start(bf16[128,1024]{1,0:T(8,128)(2,1)S(1)} %get-tuple-element.123.refs_0_), channel_id=1, source_target_pairs={{0,1},{1,0},{2,3},{3,2},{4,5},{5,4},{6,7},{7,6},{8,9},{9,8},{10,11... | collective-permute-start | bytes 786440 | tf_op jit(solution)/shard_map/ppermute | solution.py:454
  10.7 3.1 %copy-start.3 = (bf16[2048,1792]{1,0:T(8,128)(2,1)S(1)}, bf16[2048,1792]{1,0:T(8,128)(2,1)}, u32[]{:S(2)}) copy-start(bf16[2048,1792]{1,0:T(8,128)(2,1)} %w_ref.7) | copy-start | bytes 22020100
  13.8 5.1 %copy-start.4 = (bf16[256,128]{1,0:T(8,128)(2,1)S(1)}, bf16[256,128]{1,0:T(8,128)(2,1)}, u32[]{:S(2)}) copy-start(bf16[256,128]{1,0:T(8,128)(2,1)} %constant.32.clone.mean_ref) | copy-start | bytes 196612
  13.8 5.1 %copy-start.5 = (f32[160,128]{1,0:T(8,128)S(1)}, f32[160,128]{1,0:T(8,128)}, u32[]{:S(2)}) copy-start(f32[160,128]{1,0:T(8,128)} %constant.31.clone.weight_ref) | copy-start | bytes 245764
  13.8 5.1 %copy-start.6 = (f32[3,512]{1,0:T(4,128)S(1)}, f32[3,512]{1,0:T(4,128)}, u32[]{:S(2)}) copy-start(f32[3,512]{1,0:T(4,128)} %conv_ref.9) | copy-start | bytes 18436
  22.8 9.9 %copy-start.2 = (bf16[128,1280]{1,0:T(8,128)(2,1)S(1)}, bf16[128,1280]{1,0:T(8,128)(2,1)}, u32[]{:S(2)}) copy-start(bf16[128,1280]{1,0:T(8,128)(2,1)} %constant.29.clone.turn_ref) | copy-start | bytes 983044
  22.8 6.1 %collective-permute-start.1 = (bf16[144,512]{1,0:T(8,128)(2,1)S(1)}, bf16[144,512]{1,0:T(8,128)(2,1)S(1)}, u32[]{:S(2)}, u32[]{:S(2)}) collective-permute-start(bf16[144,512]{1,0:T(8,128)(2,1)S(1)} %get-tuple-element.90), channel_id=1, source_target_pairs={{0,2},{2,4},{4,6},{6,8},{8,10},{10,12},{12,14},{14,16},{16,18},{18... | collective-permute-start | bytes 442376 | tf_op jit(solution)/shard_map/ppermute | solution.py:552
  50.6 4.1 %copy-start = (bf16[512,2048]{1,0:T(8,128)(2,1)S(1)}, bf16[512,2048]{1,0:T(8,128)(2,1)}, u32[]{:S(2)}) copy-start(bf16[512,2048]{1,0:T(8,128)(2,1)} %w_ref.13) | copy-start | bytes 6291460
  52.4 4.7 %collective-permute-start.6 = (bf16[160,128]{1,0:T(8,128)(2,1)S(1)}, bf16[160,128]{1,0:T(8,128)(2,1)S(1)}, u32[]{:S(2)}, u32[]{:S(2)}) collective-permute-start(bf16[160,128]{1,0:T(8,128)(2,1)S(1)} %get-tuple-element.138), channel_id=1, source_target_pairs={{0,2},{2,0},{4,6},{6,4},{8,10},{10,8},{12,14},{14,12},{16,18},{18,... | collective-permute-start | bytes 122888 | tf_op jit(solution)/shard_map/ppermute | solution.py:363
  52.5 4.6 %collective-permute-start.7 = (bf16[160,128]{1,0:T(8,128)(2,1)S(1)}, bf16[160,128]{1,0:T(8,128)(2,1)S(1)}, u32[]{:S(2)}, u32[]{:S(2)}) collective-permute-start(bf16[160,128]{1,0:T(8,128)(2,1)S(1)} %get-tuple-element.139), channel_id=1, source_target_pairs={{0,4},{2,6},{4,0},{6,2},{8,12},{10,14},{12,8},{14,10},{16,20},{18,... | collective-permute-start | bytes 122888 | tf_op jit(solution)/shard_map/ppermute | solution.py:363
  54.6 3.5 %collective-permute-start.8 = (bf16[160,128]{1,0:T(8,128)(2,1)S(1)}, bf16[160,128]{1,0:T(8,128)(2,1)S(1)}, u32[]{:S(2)}, u32[]{:S(2)}) collective-permute-start(bf16[160,128]{1,0:T(8,128)(2,1)S(1)} %get-tuple-element.140), channel_id=1, source_target_pairs={{0,6},{2,4},{4,2},{6,0},{8,14},{10,12},{12,10},{14,8},{16,22},{18,... | collective-permute-start | bytes 122888 | tf_op jit(solution)/shard_map/ppermute | solution.py:363
  55.3 18.5 %collective-permute-start.17 = (bf16[256,1024]{1,0:T(8,128)(2,1)S(1)}, bf16[256,1024]{1,0:T(8,128)(2,1)S(1)}, u32[]{:S(2)}, u32[]{:S(2)}) collective-permute-start(bf16[256,1024]{1,0:T(8,128)(2,1)S(1)} %shard_map.112), channel_id=1, source_target_pairs={{0,1},{1,0},{2,3},{3,2},{4,5},{5,4},{6,7},{7,6},{8,9},{9,8},{10,11... | collective-permute-start | bytes 1572872 | tf_op jit(solution)/shard_map/ppermute | solution.py:454
  58.8 9.1 %collective-permute-start.11 = (bf16[160,128]{1,0:T(8,128)(2,1)S(1)}, bf16[160,128]{1,0:T(8,128)(2,1)S(1)}, u32[]{:S(2)}, u32[]{:S(2)}) collective-permute-start(bf16[160,128]{1,0:T(8,128)(2,1)S(1)} %get-tuple-element.145), channel_id=1, source_target_pairs={{0,24},{2,26},{4,28},{6,30},{8,16},{10,18},{12,20},{14,22},{16,8},... | collective-permute-start | bytes 122888 | tf_op jit(solution)/shard_map/ppermute | solution.py:363
  62.5 5.5 %collective-permute-start.10 = (bf16[160,128]{1,0:T(8,128)(2,1)S(1)}, bf16[160,128]{1,0:T(8,128)(2,1)S(1)}, u32[]{:S(2)}, u32[]{:S(2)}) collective-permute-start(bf16[160,128]{1,0:T(8,128)(2,1)S(1)} %get-tuple-element.145), channel_id=1, source_target_pairs={{0,16},{2,18},{4,20},{6,22},{8,24},{10,26},{12,28},{14,30},{16,0},... | collective-permute-start | bytes 122888 | tf_op jit(solution)/shard_map/ppermute | solution.py:363
  62.5 5.5 %collective-permute-start.9 = (bf16[160,128]{1,0:T(8,128)(2,1)S(1)}, bf16[160,128]{1,0:T(8,128)(2,1)S(1)}, u32[]{:S(2)}, u32[]{:S(2)}) collective-permute-start(bf16[160,128]{1,0:T(8,128)(2,1)S(1)} %get-tuple-element.145), channel_id=1, source_target_pairs={{0,8},{2,10},{4,12},{6,14},{8,0},{10,2},{12,4},{14,6},{16,24},{18,... | collective-permute-start | bytes 122888 | tf_op jit(solution)/shard_map/ppermute | solution.py:363
  65.0 5.5 %copy-start.7 = (f32[512]{0:T(512)S(1)}, f32[512]{0:T(512)}, u32[]{:S(2)}) copy-start(f32[512]{0:T(512)} %param.12) | copy-start | bytes 6148
  68.6 5.3 %collective-permute-start.12 = (bf16[160,128]{1,0:T(8,128)(2,1)S(1)}, bf16[160,128]{1,0:T(8,128)(2,1)S(1)}, u32[]{:S(2)}, u32[]{:S(2)}) collective-permute-start(bf16[160,128]{1,0:T(8,128)(2,1)S(1)} %get-tuple-element.159), channel_id=1, source_target_pairs={{0,2},{2,0},{4,6},{6,4},{8,10},{10,8},{12,14},{14,12},{16,18},{18,... | collective-permute-start | bytes 122888 | tf_op jit(solution)/shard_map/ppermute | solution.py:363
  68.6 5.2 %collective-permute-start.13 = (bf16[160,128]{1,0:T(8,128)(2,1)S(1)}, bf16[160,128]{1,0:T(8,128)(2,1)S(1)}, u32[]{:S(2)}, u32[]{:S(2)}) collective-permute-start(bf16[160,128]{1,0:T(8,128)(2,1)S(1)} %get-tuple-element.160), channel_id=1, source_target_pairs={{0,4},{2,6},{4,0},{6,2},{8,12},{10,14},{12,8},{14,10},{16,20},{18,... | collective-permute-start | bytes 122888 | tf_op jit(solution)/shard_map/ppermute | solution.py:363
  69.5 4.3 %collective-permute-start.14 = (bf16[160,128]{1,0:T(8,128)(2,1)S(1)}, bf16[160,128]{1,0:T(8,128)(2,1)S(1)}, u32[]{:S(2)}, u32[]{:S(2)}) collective-permute-start(bf16[160,128]{1,0:T(8,128)(2,1)S(1)} %get-tuple-element.161), channel_id=1, source_target_pairs={{0,6},{2,4},{4,2},{6,0},{8,14},{10,12},{12,10},{14,8},{16,22},{18,... | collective-permute-start | bytes 122888 | tf_op jit(solution)/shard_map/ppermute | solution.py:363
  72.2 14.9 %collective-permute-start.15 = (bf16[1024,128]{1,0:T(8,128)(2,1)S(1)}, bf16[1024,128]{1,0:T(8,128)(2,1)S(1)}, u32[]{:S(2)}, u32[]{:S(2)}) collective-permute-start(bf16[1024,128]{1,0:T(8,128)(2,1)S(1)} %shard_map.106.refs_0_), channel_id=1, source_target_pairs={{0,1},{1,0},{2,3},{3,2},{4,5},{5,4},{6,7},{7,6},{8,9},{9,8},{10,11... | collective-permute-start | bytes 786440 | tf_op jit(solution)/shard_map/ppermute | solution.py:454
  73.8 13.8 %collective-permute-start.18 = (bf16[256,1024]{1,0:T(8,128)(2,1)S(1)}, bf16[256,1024]{1,0:T(8,128)(2,1)S(1)}, u32[]{:S(2)}, u32[]{:S(2)}) collective-permute-start(bf16[256,1024]{1,0:T(8,128)(2,1)S(1)} %collective-permute-done.17.refs_4_), channel_id=1, source_target_pairs={{0,2},{2,0},{4,6},{6,4},{8,10},{10,8},{12,14},{14,12},{16,18},{18,... | collective-permute-start | bytes 1572872 | tf_op jit(solution)/shard_map/ppermute | solution.py:363
  75.2 10.3 %collective-permute-start.22 = (bf16[256,384]{1,0:T(8,128)(2,1)S(1)}, bf16[256,384]{1,0:T(8,128)(2,1)S(1)}, u32[]{:S(2)}, u32[]{:S(2)}) collective-permute-start(bf16[256,384]{1,0:T(8,128)(2,1)S(1)} %shard_map.107.refs_1_), channel_id=1, source_target_pairs={{0,1},{1,0},{2,3},{3,2},{4,5},{5,4},{6,7},{7,6},{8,9},{9,8},{10,11... | collective-permute-start | bytes 589832 | tf_op jit(solution)/shard_map/ppermute | solution.py:454
  77.7 12.1 %collective-permute-start.21 = (bf16[256,384]{1,0:T(8,128)(2,1)S(1)}, bf16[256,384]{1,0:T(8,128)(2,1)S(1)}, u32[]{:S(2)}, u32[]{:S(2)}) collective-permute-start(bf16[256,384]{1,0:T(8,128)(2,1)S(1)} %shard_map.108.refs_1_), channel_id=1, source_target_pairs={{0,1},{1,0},{2,3},{3,2},{4,5},{5,4},{6,7},{7,6},{8,9},{9,8},{10,11... | collective-permute-start | bytes 589832 | tf_op jit(solution)/shard_map/ppermute | solution.py:454
  80.2 13.8 %collective-permute-start.20 = (bf16[256,384]{1,0:T(8,128)(2,1)S(1)}, bf16[256,384]{1,0:T(8,128)(2,1)S(1)}, u32[]{:S(2)}, u32[]{:S(2)}) collective-permute-start(bf16[256,384]{1,0:T(8,128)(2,1)S(1)} %shard_map.109.refs_1_), channel_id=1, source_target_pairs={{0,1},{1,0},{2,3},{3,2},{4,5},{5,4},{6,7},{7,6},{8,9},{9,8},{10,11... | collective-permute-start | bytes 589832 | tf_op jit(solution)/shard_map/ppermute | solution.py:454
  85.6 10.5 %collective-permute-start.19 = (bf16[128,384]{1,0:T(8,128)(2,1)S(1)}, bf16[128,384]{1,0:T(8,128)(2,1)S(1)}, u32[]{:S(2)}, u32[]{:S(2)}) collective-permute-start(bf16[128,384]{1,0:T(8,128)(2,1)S(1)} %shard_map.110.refs_1_), channel_id=1, source_target_pairs={{0,1},{1,0},{2,3},{3,2},{4,5},{5,4},{6,7},{7,6},{8,9},{9,8},{10,11... | collective-permute-start | bytes 294920 | tf_op jit(solution)/shard_map/ppermute | solution.py:454
  87.1 10.7 %collective-permute-start.16 = (bf16[128,384]{1,0:T(8,128)(2,1)S(1)}, bf16[128,384]{1,0:T(8,128)(2,1)S(1)}, u32[]{:S(2)}, u32[]{:S(2)}) collective-permute-start(bf16[128,384]{1,0:T(8,128)(2,1)S(1)} %shard_map.111.refs_1_), channel_id=1, source_target_pairs={{0,1},{1,0},{2,3},{3,2},{4,5},{5,4},{6,7},{7,6},{8,9},{9,8},{10,11... | collective-permute-start | bytes 294920 | tf_op jit(solution)/shard_map/ppermute | solution.py:454

commit v10 on v9

--- a/solution.py
+++ b/solution.py
@@ -323,35 +323,74 @@
             at += rows
 
 
-def output_kernel(a_ref, w_ref, *refs, n, offset, parts, turns):
-    pieces, refs = refs[: n * len(turns)], refs[n * len(turns) :]
-    weights, (o_ref, held_ref, mixed_ref, sem) = refs[: parts * (n - 1)], refs[-4:]
+def place_pieces(a_ref, pieces, turns, offset, mixed_ref):
+    rows = mixed_ref.shape[0]
+    for ref, (all_rows, pairs) in zip(pieces, turns):
+        here = slice(offset, offset + rows) if all_rows else slice(0, rows)
+        for k, turn in enumerate(pairs):
+            at = pl.multiple_of(jnp.bitwise_xor(a_ref[1], turn) * LANES, LANES)
+            mixed_ref[:, pl.ds(at, LANES)] = ref[here, k * LANES : (k + 1) * LANES]
+
+
+def own_columns(a_ref, cols, begin, width):
+    return pl.ds(pl.multiple_of(a_ref[0] * cols + begin, LANES), width)
+
+
+def share_kernel(a_ref, w_ref, *refs, turns, blocks):
+    share_ref, mixed_ref = refs[-2:]
+    at = 0
+    for i, (offset, rows) in enumerate(blocks):
+        pieces = refs[i * len(turns) : (i + 1) * len(turns)]
+        place_pieces(a_ref, pieces, turns, offset, mixed_ref.at[pl.ds(at, rows), :])
+        at += rows
+    cols = share_ref.shape[1]
+    mine = own_columns(a_ref, cols, 0, cols)
+    share_ref[...] = jnp.dot(mixed_ref[...], w_ref[:, mine], preferred_element_type=F32).astype(BF16)
+
+
+def output_kernel(a_ref, w_ref, *refs, n, offset, parts, turns, shared):
+    weights, refs = refs[: parts * (n - 1)], refs[parts * (n - 1) :]
+    o_ref, held_ref, mixed_ref, sems = refs[-4:]
     rows, cols = held_ref.shape
-    mine = pl.ds(pl.multiple_of(a_ref[0] * cols, cols), cols)
-    total = None
-    for r in range(n):
-        for i, (all_rows, pairs) in enumerate(turns):
-            here = slice(offset, offset + rows) if all_rows else slice(0, rows)
-            for k, turn in enumerate(pairs):
-                at = pl.multiple_of(jnp.bitwise_xor(a_ref[1], turn) * LANES, LANES)
-                mixed_ref[r, :, pl.ds(at, LANES)] = pieces[r * len(turns) + i][here, k * LANES : (k + 1) * LANES]
-        if r == 0:
-            part = jnp.dot(mixed_ref[0], w_ref[:, mine], preferred_element_type=F32)
-        else:
-            part = None
-            for i in range(parts):
-                ref = weights[(r - 1) * parts + i]
-                depth = ref.shape[0]
-                at = depth * (jnp.bitwise_xor(a_ref[2] % 2, i) if parts > 1 else 0)
-                rows_of = pl.ds(pl.multiple_of(at, depth), depth)
-                got = jnp.dot(mixed_ref[r, :, rows_of], ref[...], preferred_element_type=F32)
-                part = got if part is None else part + got
-        part = part.astype(BF16).astype(F32)
-        total = part if total is None else total + part
-    held_ref[...] = total.astype(BF16)
-    copy = pltpu.make_async_copy(held_ref, o_ref.at[pl.ds(offset, rows), :], sem)
-    copy.start()
-    copy.wait()
+    first = 0
+    if shared is not None:
+        share_ref, refs = refs[0], refs[1:]
+        first = 1
+    for r in range(first, n):
+        pieces = refs[(r - first) * len(turns) : (r - first + 1) * len(turns)]
+        place_pieces(a_ref, pieces, turns, offset, mixed_ref.at[r])
+    copies = []
+    count = 2 if cols % (2 * LANES) == 0 else 1
+    width = cols // count
+    for half in range(count):
+        here = slice(half * width, (half + 1) * width)
+        total = None
+        if shared is not None:
+            total = share_ref[shared : shared + rows, here].astype(F32)
+        for r in range(first, n):
+            if r == 0:
+                part = jnp.dot(
+                    mixed_ref[0], w_ref[:, own_columns(a_ref, cols, half * width, width)], preferred_element_type=F32
+                )
+            else:
+                part = None
+                for i in range(parts):
+                    ref = weights[(r - 1) * parts + i]
+                    depth = ref.shape[0]
+                    at = depth * (jnp.bitwise_xor(a_ref[2] % 2, i) if parts > 1 else 0)
+                    rows_of = pl.ds(pl.multiple_of(at, depth), depth)
+                    got = jnp.dot(mixed_ref[r, :, rows_of], ref[:, here], preferred_element_type=F32)
+                    part = got if part is None else part + got
+            part = part.astype(BF16).astype(F32)
+            total = part if total is None else total + part
+        held_ref[:, here] = total.astype(BF16)
+        copy = pltpu.make_async_copy(
+            held_ref.at[:, here], o_ref.at[pl.ds(offset, rows), here], sems.at[half]
+        )
+        copy.start()
+        copies.append(copy)
+    for copy in copies:
+        copy.wait()
 
 
 def pick_kernel(a_ref, w_ref, o_ref):
@@ -614,13 +653,32 @@
         mixed = finish(turns, priors, (b,), mixed)
         mixes[b] = [mixed] + [from_head(mixed, r) for r in range(1, n)]
 
+    piece_turns = ([(True, (0,))] if early else []) + [(False, turns)]
+
+    def pieces_of(b, r):
+        return early[r : r + 1] + [mixes[b][r]]
+
+    tail_blocks = order[-2:]
+    tail_rows = sum(blocks[b][1] for b in tail_blocks)
+    share = call(
+        functools.partial(share_kernel, turns=piece_turns, blocks=[blocks[b] for b in tail_blocks]),
+        jax.ShapeDtypeStruct((tail_rows, cols), BF16),
+        in_specs=[scalar] + [whole] * (1 + 2 * len(piece_turns)),
+        out_specs=whole,
+        scratch_shapes=[pltpu.VMEM((tail_rows, width), BF16)],
+        vmem=16 << 20,
+    )(places, out_weight, *[piece for b in tail_blocks for piece in pieces_of(b, 0)])
+
     result = None
     for b in order:
         at, rows = blocks[b]
-        operands = [places, out_weight]
-        for r in range(n):
-            operands += ([early[r]] if early else []) + [mixes[b][r]]
-        operands += out_rows
+        shared = None
+        operands = [after(places, share) if b == order[-3] else places, out_weight] + out_rows
+        if b in tail_blocks:
+            shared = sum(blocks[c][1] for c in tail_blocks[: tail_blocks.index(b)])
+            operands.append(share)
+        for r in range(0 if shared is None else 1, n):
+            operands += pieces_of(b, r)
         specs = [scalar] + [whole] * (len(operands) - 1)
         aliases = {}
         if result is not None:
@@ -629,11 +687,7 @@
             specs.append(pl.BlockSpec(memory_space=pl.ANY))
         result = call(
             functools.partial(
-                output_kernel,
-                n=n,
-                offset=at,
-                parts=out_parts,
-                turns=([(True, (0,))] if early else []) + [(False, turns)],
+                output_kernel, n=n, offset=at, parts=out_parts, turns=piece_turns, shared=shared
             ),
             jax.ShapeDtypeStruct((row_count, cols), BF16),
             in_specs=specs,
@@ -641,7 +695,7 @@
             scratch_shapes=[
                 pltpu.VMEM((rows, cols), BF16),
                 pltpu.VMEM((n, rows, width), BF16),
-                pltpu.SemaphoreType.DMA,
+                pltpu.SemaphoreType.DMA((2,)),
             ],
             input_output_aliases=aliases,
             vmem=16 << 20,

time: 100 us -> 99.7 us (level)
    pallas_call x0 -> x1, Pallas kernels: none -> 1 us  [per_device(): call(functools.partial(share_kernel, turns=piece_turns, blocks=[blocks[b]...]
  transfers between devices with their start and end apart: 23 -> 23, of which waited for: 6 -> 5; matrix products, arithmetic and copies ran while one was open for 2% -> 2% of each run, Pallas kernels for 50% -> 51%
where the time goes in v10:
time: 99.7 us; the launch traced here: 99.4 us
  Pallas kernels  54.3 us (54%)
  starting transfers between devices  26.2 us (26%)
  waiting for transfers between devices  11.7 us (12%)
  local copies, waits for them, and re-layouts  6.54 us (7%)
    ppermute x12, starting transfers between devices, from_head(): return lax.ppermute(value, 'head', [(i, (i + by) % n) for i in range(n)])  15.9 us
    pallas_call x5, Pallas kernels, do_block(): call(functools.partial(block_kernel, n=n, heads=heads, extra=extra, other...  15.9 us
    ppermute x12, waiting for transfers between devices, from_head(): return lax.ppermute(value, 'head', [(i, (i + by) % n) for i in range(n)])  10.7 us
    pallas_call x5, Pallas kernels, attend(): call(functools.partial(attend_kernel, heads=heads, first=b == 0), [jax.Sh...  9.97 us
    pallas_call x5, Pallas kernels, per_device(): call(functools.partial(output_kernel, n=n, offset=at, parts=out_parts, tu...  9.28 us
    ppermute x10, starting transfers between devices, exchange(): return lax.ppermute(value, axis, [(i, i ^ flip) for i in range(count)])  8.7 us
    pallas_call x6, Pallas kernels, finish(): call(functools.partial(finish_kernel, heads=heads, turns=turns, before=be...  8.27 us
    pallas_call x1, Pallas kernels, per_device(): call(functools.partial(arrange_kernel, heads=heads), jax.ShapeDtypeStruct...  5.09 us
  transfers between devices with their start and end apart: 23, of which 5 were waited for; matrix products, arithmetic and copies ran while one was open for 2% of the time, Pallas kernels for 51%

profile of v10, /device:TPU:0, one launch (start us, length us, event | category | flops | bytes accessed | tf_op | source)
XLA Modules:
  0.0 99.4 jit_solution(1105041890595021635)
XLA Ops:
  1.2 3.0 %collective-permute-start = (bf16[272,1024]{1,0:T(8,128)(2,1)S(1)}, bf16[272,1024]{1,0:T(8,128)(2,1)S(1)}, u32[]{:S(2)}, u32[]{:S(2)}) collective-permute-start(bf16[272,1024]{1,0:T(8,128)(2,1)S(1)} %slice.15.refs_0_), channel_id=1, source_target_pairs={{0,1},{1,0},{2,3},{3,2},{4,5},{5,4},{6,7},{7,6},{8,9},{9,8},{10,11... | collective-permute-start | bytes 1671176 | tf_op jit(solution)/shard_map/ppermute | solution.py:493
  5.6 2.0 %collective-permute-start.3 = (bf16[256,1024]{1,0:T(8,128)(2,1)S(1)}, bf16[256,1024]{1,0:T(8,128)(2,1)S(1)}, u32[]{:S(2)}, u32[]{:S(2)}) collective-permute-start(bf16[256,1024]{1,0:T(8,128)(2,1)S(1)} %get-tuple-element.104.refs_0_), channel_id=1, source_target_pairs={{0,1},{1,0},{2,3},{3,2},{4,5},{5,4},{6,7},{7,6},{8,9},{9,8},{10,11... | collective-permute-start | bytes 1572872 | tf_op jit(solution)/shard_map/ppermute | solution.py:493
  8.8 1.9 %collective-permute-start.5 = (bf16[128,1024]{1,0:T(8,128)(2,1)S(1)}, bf16[128,1024]{1,0:T(8,128)(2,1)S(1)}, u32[]{:S(2)}, u32[]{:S(2)}) collective-permute-start(bf16[128,1024]{1,0:T(8,128)(2,1)S(1)} %get-tuple-element.122.refs_0_), channel_id=1, source_target_pairs={{0,1},{1,0},{2,3},{3,2},{4,5},{5,4},{6,7},{7,6},{8,9},{9,8},{10,11... | collective-permute-start | bytes 786440 | tf_op jit(solution)/shard_map/ppermute | solution.py:493
  10.7 3.1 %copy-done.3 = bf16[2048,1792]{1,0:T(8,128)(2,1)S(1)} copy-done((bf16[2048,1792]{1,0:T(8,128)(2,1)S(1)}, bf16[2048,1792]{1,0:T(8,128)(2,1)}, u32[]{:S(2)}) %copy-start.3) | copy-done | bytes 7340056
  13.8 5.1 %shard_map.91.w_ref = bf16[2048,1792]{1,0:T(8,128)(2,1)S(1)} custom-call(bf16[2048,1792]{1,0:T(8,128)(2,1)S(1)} %copy-done.3), custom_call_target="tpu_custom_call" | custom-call | flops 1 | bytes 1 | tf_op jit(solution)/shard_map/pallas_call | solution.py:530
  19.0 3.8 %shard_map.92 = (bf16[256,128]{1,0:T(8,128)(2,1)S(1)}, bf16[256,512]{1,0:T(8,128)(2,1)S(1)}, f32[4,160,128]{2,1,0:T(8,128)S(1)}, bf16[256,128]{1,0:T(8,128)(2,1)...) custom-call(s32[3]{0:T(128)S(1)} %pad_add_fusion.j_ref.a_ref._, ...), custom_call_target="tpu_custom_call" | custom-call | flops 1 | bytes 1 | tf_op jit(solution)/shard_map/pallas_call | solution.py:556
  22.8 1.6 %collective-permute-start.1 = (bf16[144,512]{1,0:T(8,128)(2,1)S(1)}, bf16[144,512]{1,0:T(8,128)(2,1)S(1)}, u32[]{:S(2)}, u32[]{:S(2)}) collective-permute-start(bf16[144,512]{1,0:T(8,128)(2,1)S(1)} %get-tuple-element.89), channel_id=1, source_target_pairs={{0,2},{2,4},{4,6},{6,8},{8,10},{10,12},{12,14},{14,16},{16,18},{18... | collective-permute-start | bytes 442376 | tf_op jit(solution)/shard_map/ppermute | solution.py:591
  24.4 4.5 %collective-permute-done.2.refs_1_ = bf16[256,1024]{1,0:T(8,128)(2,1)S(1)} collective-permute-done((bf16[256,1024]{1,0:T(8,128)(2,1)S(1)}, bf16[256,1024]{1,0:T(8,128)(2,1)S(1)}, u32[]{:S(2)}, u32[]{:S(2)}) %collective-permute-start.2) | collective-permute-done | bytes 524320 | tf_op jit(solution)/shard_map/ppermute | solution.py:493
  28.9 3.8 %shard_map.93 = (bf16[256,128]{1,0:T(8,128)(2,1)S(1)}, bf16[256,512]{1,0:T(8,128)(2,1)S(1)}, f32[4,160,128]{2,1,0:T(8,128)S(1)}, bf16[256,128]{1,0:T(8,128)(2,1)...) custom-call(s32[3]{0:T(128)S(1)} %pad_add_fusion.j_ref.a_ref._, ...), custom_call_target="tpu_custom_call" | custom-call | flops 1 | bytes 1 | tf_op jit(solution)/shard_map/pallas_call | solution.py:556
  32.7 2.1 %shard_map.94 = (bf16[256,1280]{1,0:T(8,128)(2,1)S(1)}, f32[256,512]{1,0:T(8,128)S(1)}, f32[256,512]{1,0:T(8,128)S(1)}) custom-call(s32[3]{0:T(128)S(1)} %pad_add_fusion.j_ref.a_ref._, bf16[128,1280]{1,0:T(8,128)(2,1)S(1)} %copy-done.2, bf16[144,512]{1,0:T(8,128)(2,1)S(1)} %collective-permute-done.1.refs_2_.prev_ref, ...), custom_call_target="tpu_custom_call" | custom-call | flops 1 | bytes 1 | tf_op jit(solution)/shard_map/pallas_call | solution.py:580
  34.9 2.1 %shard_map.95 = (bf16[256,1280]{1,0:T(8,128)(2,1)S(1)}, f32[256,512]{1,0:T(8,128)S(1)}, f32[256,512]{1,0:T(8,128)S(1)}) custom-call(s32[3]{0:T(128)S(1)} %pad_add_fusion.j_ref.a_ref._, bf16[128,1280]{1,0:T(8,128)(2,1)S(1)} %copy-done.2, bf16[144,512]{1,0:T(8,128)(2,1)S(1)} %collective-permute-done.1.refs_2_.prev_ref, ...), custom_call_target="tpu_custom_call" | custom-call | flops 1 | bytes 1 | tf_op jit(solution)/shard_map/pallas_call | solution.py:580
  37.0 3.1 %collective-permute-done.3.refs_1_ = bf16[256,1024]{1,0:T(8,128)(2,1)S(1)} collective-permute-done((bf16[256,1024]{1,0:T(8,128)(2,1)S(1)}, bf16[256,1024]{1,0:T(8,128)(2,1)S(1)}, u32[]{:S(2)}, u32[]{:S(2)}) %collective-permute-start.3) | collective-permute-done | bytes 524320 | tf_op jit(solution)/shard_map/ppermute | solution.py:493
  40.1 3.8 %shard_map.96 = (bf16[256,128]{1,0:T(8,128)(2,1)S(1)}, bf16[256,512]{1,0:T(8,128)(2,1)S(1)}, f32[4,160,128]{2,1,0:T(8,128)S(1)}, bf16[256,128]{1,0:T(8,128)(2,1)...) custom-call(s32[3]{0:T(128)S(1)} %pad_add_fusion.j_ref.a_ref._, ...), custom_call_target="tpu_custom_call" | custom-call | flops 1 | bytes 1 | tf_op jit(solution)/shard_map/pallas_call | solution.py:556
  43.9 2.1 %shard_map.97 = (bf16[256,1280]{1,0:T(8,128)(2,1)S(1)}, f32[256,512]{1,0:T(8,128)S(1)}, f32[256,512]{1,0:T(8,128)S(1)}) custom-call(s32[3]{0:T(128)S(1)} %pad_add_fusion.j_ref.a_ref._, bf16[128,1280]{1,0:T(8,128)(2,1)S(1)} %copy-done.2, bf16[144,512]{1,0:T(8,128)(2,1)S(1)} %get-tuple-element.105.refs_2_.prev_ref, ...), custom_call_target="tpu_custom_call" | custom-call | flops 1 | bytes 1 | tf_op jit(solution)/shard_map/pallas_call | solution.py:580
  46.1 2.6 %shard_map.98 = (bf16[128,128]{1,0:T(8,128)(2,1)S(1)}, bf16[128,512]{1,0:T(8,128)(2,1)S(1)}, f32[4,160,128]{2,1,0:T(8,128)S(1)}, bf16[128,128]{1,0:T(8,128)(2,1)...) custom-call(s32[3]{0:T(128)S(1)} %pad_add_fusion.j_ref.a_ref._, ...), custom_call_target="tpu_custom_call" | custom-call | flops 1 | bytes 1 | tf_op jit(solution)/shard_map/pallas_call | solution.py:556
  48.7 1.9 %shard_map.99 = (bf16[128,1280]{1,0:T(8,128)(2,1)S(1)}, f32[128,512]{1,0:T(8,128)S(1)}, f32[128,512]{1,0:T(8,128)S(1)}) custom-call(s32[3]{0:T(128)S(1)} %pad_add_fusion.j_ref.a_ref._, bf16[128,1280]{1,0:T(8,128)(2,1)S(1)} %copy-done.2, bf16[144,512]{1,0:T(8,128)(2,1)S(1)} %get-tuple-element.106.refs_2_.prev_ref, ...), custom_call_target="tpu_custom_call" | custom-call | flops 1 | bytes 1 | tf_op jit(solution)/shard_map/pallas_call | solution.py:580
  50.6 1.8 %shard_map.100 = (bf16[128,128]{1,0:T(8,128)(2,1)S(1)}, bf16[128,512]{1,0:T(8,128)(2,1)S(1)}, f32[4,160,128]{2,1,0:T(8,128)S(1)}, bf16[160,128]{1,0:T(8,128)(2,1...) custom-call(s32[3]{0:T(128)S(1)} %pad_add_fusion.j_ref.a_ref._, ...), custom_call_target="tpu_custom_call" | custom-call | flops 1 | bytes 1 | tf_op jit(solution)/shard_map/pallas_call | solution.py:556
  52.5 2.1 %collective-permute-start.8 = (bf16[160,128]{1,0:T(8,128)(2,1)S(1)}, bf16[160,128]{1,0:T(8,128)(2,1)S(1)}, u32[]{:S(2)}, u32[]{:S(2)}) collective-permute-start(bf16[160,128]{1,0:T(8,128)(2,1)S(1)} %get-tuple-element.140), channel_id=1, source_target_pairs={{0,4},{2,6},{4,0},{6,2},{8,12},{10,14},{12,8},{14,10},{16,20},{18,... | collective-permute-start | bytes 122888 | tf_op jit(solution)/shard_map/ppermute | solution.py:402
  55.3 1.8 %collective-permute-start.6 = (bf16[256,1024]{1,0:T(8,128)(2,1)S(1)}, bf16[256,1024]{1,0:T(8,128)(2,1)S(1)}, u32[]{:S(2)}, u32[]{:S(2)}) collective-permute-start(bf16[256,1024]{1,0:T(8,128)(2,1)S(1)} %shard_map.101), channel_id=1, source_target_pairs={{0,1},{1,0},{2,3},{3,2},{4,5},{5,4},{6,7},{7,6},{8,9},{9,8},{10,11... | collective-permute-start | bytes 1572872 | tf_op jit(solution)/shard_map/ppermute | solution.py:493
  58.8 3.7 %collective-permute-start.12 = (bf16[160,128]{1,0:T(8,128)(2,1)S(1)}, bf16[160,128]{1,0:T(8,128)(2,1)S(1)}, u32[]{:S(2)}, u32[]{:S(2)}) collective-permute-start(bf16[160,128]{1,0:T(8,128)(2,1)S(1)} %get-tuple-element.146), channel_id=1, source_target_pairs={{0,24},{2,26},{4,28},{6,30},{8,16},{10,18},{12,20},{14,22},{16,8},... | collective-permute-start | bytes 122888 | tf_op jit(solution)/shard_map/ppermute | solution.py:402
  63.2 1.8 %shard_map.102 = (bf16[128,128]{1,0:T(8,128)(2,1)S(1)}, bf16[128,512]{1,0:T(8,128)(2,1)S(1)}, bf16[128,512]{1,0:T(8,128)(2,1)S(1)}, bf16[144,512]{1,0:T(8,128)(2,1)S(1)}) custom-call(s32[3]{0:T(128)S(1)} %pad_add_fusion.j_ref.a_ref._, bf16[256,128]{1,0:T(8,128)(2,1)S(1)} %copy-done.4, bf16[2048,1792]{1,0:T(8,128)(2,1)S(1)} %shard_map.91.w_ref, ...), custom_call_target="tpu_custom_call" | custom-call | flops 1 | bytes 1 | tf_op jit(solution)/shard_map/pallas_call | solution.py:569
  66.3 1.7 %shard_map.103 = (bf16[128,1280]{1,0:T(8,128)(2,1)S(1)}, f32[128,512]{1,0:T(8,128)S(1)}, f32[128,512]{1,0:T(8,128)S(1)}) custom-call(s32[3]{0:T(128)S(1)} %pad_add_fusion.j_ref.a_ref._, bf16[128,1280]{1,0:T(8,128)(2,1)S(1)} %copy-done.2, bf16[144,512]{1,0:T(8,128)(2,1)S(1)} %get-tuple-element.123.refs_2_.prev_ref, ...), custom_call_target="tpu_custom_call" | custom-call | flops 1 | bytes 1 | tf_op jit(solution)/shard_map/pallas_call | solution.py:580
  70.5 1.6 %shard_map.107.refs_0_.refs_2_ = bf16[1024,128]{1,0:T(8,128)(2,1)S(1)} custom-call(s32[3]{0:T(128)S(1)} %pad_add_fusion.j_ref.a_ref._, bf16[256,128]{1,0:T(8,128)(2,1)S(1)} %copy-done.4, f32[1,512]{1,0:T(1,128)S(1)} %bitcast.4, bf16[160,128]{1,0:T(8,128)(2,1)S(1)} %get-tuple-element.147.refs_0_, ...), custom_call_target="tpu_custom_call" | custom-call | flops 4849999872 | bytes 1 | tf_op jit(solution)/shard_map/pallas_call | solution.py:622
  72.2 1.6 %collective-permute-start.17 = (bf16[1024,128]{1,0:T(8,128)(2,1)S(1)}, bf16[1024,128]{1,0:T(8,128)(2,1)S(1)}, u32[]{:S(2)}, u32[]{:S(2)}) collective-permute-start(bf16[1024,128]{1,0:T(8,128)(2,1)S(1)} %shard_map.107.refs_0_.refs_2_), channel_id=1, source_target_pairs={{0,1},{1,0},{2,3},{3,2},{4,5},{5,4},{6,7},{7,6},{8,9},{9,8},{10,11... | collective-permute-start | bytes 786440 | tf_op jit(solution)/shard_map/ppermute | solution.py:493
  78.8 1.4 %shard_map.110.refs_3_ = bf16[256,384]{1,0:T(8,128)(2,1)S(1)} custom-call(s32[3]{0:T(128)S(1)} %pad_add_fusion.j_ref.a_ref._, bf16[256,128]{1,0:T(8,128)(2,1)S(1)} %copy-done.4, f32[1,512]{1,0:T(1,128)S(1)} %bitcast.7, bf16[160,128]{1,0:T(8,128)(2,1)S(1)} %collective-permute-done.14.refs_0_, bf16[160,128]{1,0:T(8,128)(2,1)S(1)} %collective-permute-done.15.refs_1_, ...), custom_call_target="tpu_custom_call" | custom-call | flops 1 | bytes 1 | tf_op jit(solution)/shard_map/pallas_call | solution.py:622
  83.7 1.8 %collective-permute-done.22.refs_5_ = bf16[256,384]{1,0:T(8,128)(2,1)S(1)} collective-permute-done((bf16[256,384]{1,0:T(8,128)(2,1)S(1)}, bf16[256,384]{1,0:T(8,128)(2,1)S(1)}, u32[]{:S(2)}, u32[]{:S(2)}) %collective-permute-start.22) | collective-permute-done | bytes 196640 | tf_op jit(solution)/shard_map/ppermute | solution.py:493
  85.6 1.5 %collective-permute-start.19 = (bf16[128,384]{1,0:T(8,128)(2,1)S(1)}, bf16[128,384]{1,0:T(8,128)(2,1)S(1)}, u32[]{:S(2)}, u32[]{:S(2)}) collective-permute-start(bf16[128,384]{1,0:T(8,128)(2,1)S(1)} %shard_map.111.refs_1_), channel_id=1, source_target_pairs={{0,1},{1,0},{2,3},{3,2},{4,5},{5,4},{6,7},{7,6},{8,9},{9,8},{10,11... | collective-permute-start | bytes 294920 | tf_op jit(solution)/shard_map/ppermute | solution.py:493
  88.6 2.1 %shard_map.114.refs_6_ = bf16[1024,1024]{1,0:T(8,128)(2,1)} custom-call(s32[3]{0:T(128)S(1)} %pad_add_fusion.j_ref.a_ref._, bf16[512,2048]{1,0:T(8,128)(2,1)S(1)} %copy-done, bf16[256,1024]{1,0:T(8,128)(2,1)S(1)} %collective-permute-done.6.refs_0_, bf16[256,1024]{1,0:T(8,128)(2,1)S(1)} %collective-permute-done.13.refs_1_, ...), custom_call_target="tpu_custom_call" | custom-call | flops 1 | bytes 1 | tf_op jit(solution)/shard_map/pallas_call | solution.py:688
  90.7 2.1 %shard_map.115.refs_6_ = bf16[1024,1024]{1,0:T(8,128)(2,1)} custom-call(s32[3]{0:T(128)S(1)} %pad_add_fusion.j_ref.a_ref._, bf16[512,2048]{1,0:T(8,128)(2,1)S(1)} %copy-done, bf16[256,1024]{1,0:T(8,128)(2,1)S(1)} %collective-permute-done.6.refs_0_, bf16[256,1024]{1,0:T(8,128)(2,1)S(1)} %collective-permute-done.13.refs_1_, ...), custom_call_target="tpu_custom_call", output_to_operand_aliasing={{}: (8, {})} | custom-call | flops 1 | bytes 1 | tf_op jit(solution)/shard_map/pallas_call | solution.py:688
  94.0 2.1 %shard_map.116.refs_5_ = bf16[1024,1024]{1,0:T(8,128)(2,1)} custom-call(s32[3]{0:T(128)S(1)} %pad_add_fusion.j_ref.a_ref._, bf16[512,2048]{1,0:T(8,128)(2,1)S(1)} %copy-done, bf16[256,1024]{1,0:T(8,128)(2,1)S(1)} %collective-permute-done.6.refs_0_, bf16[256,1024]{1,0:T(8,128)(2,1)S(1)} %collective-permute-done.13.refs_1_, ...), custom_call_target="tpu_custom_call", output_to_operand_aliasing={{}: (8, {})} | custom-call | flops 1 | bytes 1 | tf_op jit(solution)/shard_map/pallas_call | solution.py:688
  96.1 1.5 %shard_map.117.refs_5_ = bf16[1024,1024]{1,0:T(8,128)(2,1)} custom-call(s32[3]{0:T(128)S(1)} %pad_add_fusion.j_ref.a_ref._, bf16[512,2048]{1,0:T(8,128)(2,1)S(1)} %copy-done, bf16[256,1024]{1,0:T(8,128)(2,1)S(1)} %collective-permute-done.6.refs_0_, bf16[256,1024]{1,0:T(8,128)(2,1)S(1)} %collective-permute-done.13.refs_1_, ...), custom_call_target="tpu_custom_call", output_to_operand_aliasing={{}: (7, {})} | custom-call | flops 1 | bytes 1 | tf_op jit(solution)/shard_map/pallas_call | solution.py:688
  97.7 1.5 %shard_map.118 = bf16[1024,1024]{1,0:T(8,128)(2,1)} custom-call(s32[3]{0:T(128)S(1)} %pad_add_fusion.j_ref.a_ref._, bf16[512,2048]{1,0:T(8,128)(2,1)S(1)} %copy-done, bf16[256,1024]{1,0:T(8,128)(2,1)S(1)} %collective-permute-done.6.refs_0_, bf16[256,1024]{1,0:T(8,128)(2,1)S(1)} %collective-permute-done.13.refs_1_, ...), custom_call_target="tpu_custom_call", output_to_operand_aliasing={{}: (7, {})} | custom-call | flops 1 | bytes 1 | tf_op jit(solution)/shard_map/pallas_call | solution.py:688
  (62 shorter events, 22.1 us)
Async XLA Ops:
  1.2 17.7 %collective-permute-start = (bf16[272,1024]{1,0:T(8,128)(2,1)S(1)}, bf16[272,1024]{1,0:T(8,128)(2,1)S(1)}, u32[]{:S(2)}, u32[]{:S(2)}) collective-permute-start(bf16[272,1024]{1,0:T(8,128)(2,1)S(1)} %slice.15.refs_0_), channel_id=1, source_target_pairs={{0,1},{1,0},{2,3},{3,2},{4,5},{5,4},{6,7},{7,6},{8,9},{9,8},{10,11... | collective-permute-start | bytes 1671176 | tf_op jit(solution)/shard_map/ppermute | solution.py:493
  5.5 23.4 %collective-permute-start.2 = (bf16[256,1024]{1,0:T(8,128)(2,1)S(1)}, bf16[256,1024]{1,0:T(8,128)(2,1)S(1)}, u32[]{:S(2)}, u32[]{:S(2)}) collective-permute-start(bf16[256,1024]{1,0:T(8,128)(2,1)S(1)} %get-tuple-element.90.refs_0_), channel_id=1, source_target_pairs={{0,1},{1,0},{2,3},{3,2},{4,5},{5,4},{6,7},{7,6},{8,9},{9,8},{10,11... | collective-permute-start | bytes 1572872 | tf_op jit(solution)/shard_map/ppermute | solution.py:493
  5.6 34.6 %collective-permute-start.3 = (bf16[256,1024]{1,0:T(8,128)(2,1)S(1)}, bf16[256,1024]{1,0:T(8,128)(2,1)S(1)}, u32[]{:S(2)}, u32[]{:S(2)}) collective-permute-start(bf16[256,1024]{1,0:T(8,128)(2,1)S(1)} %get-tuple-element.104.refs_0_), channel_id=1, source_target_pairs={{0,1},{1,0},{2,3},{3,2},{4,5},{5,4},{6,7},{7,6},{8,9},{9,8},{10,11... | collective-permute-start | bytes 1572872 | tf_op jit(solution)/shard_map/ppermute | solution.py:493
  8.6 37.5 %collective-permute-start.4 = (bf16[128,1024]{1,0:T(8,128)(2,1)S(1)}, bf16[128,1024]{1,0:T(8,128)(2,1)S(1)}, u32[]{:S(2)}, u32[]{:S(2)}) collective-permute-start(bf16[128,1024]{1,0:T(8,128)(2,1)S(1)} %get-tuple-element.114.refs_0_), channel_id=1, source_target_pairs={{0,1},{1,0},{2,3},{3,2},{4,5},{5,4},{6,7},{7,6},{8,9},{9,8},{10,11... | collective-permute-start | bytes 786440 | tf_op jit(solution)/shard_map/ppermute | solution.py:493
  8.8 10.1 %copy-start.1 = (bf16[1408,128]{1,0:T(8,128)(2,1)S(1)}, bf16[1408,128]{1,0:T(8,128)(2,1)}, u32[]{:S(2)}) copy-start(bf16[1408,128]{1,0:T(8,128)(2,1)} %constant.30.clone.turn_ref) | copy-start | bytes 1081348
  8.8 41.8 %collective-permute-start.5 = (bf16[128,1024]{1,0:T(8,128)(2,1)S(1)}, bf16[128,1024]{1,0:T(8,128)(2,1)S(1)}, u32[]{:S(2)}, u32[]{:S(2)}) collective-permute-start(bf16[128,1024]{1,0:T(8,128)(2,1)S(1)} %get-tuple-element.122.refs_0_), channel_id=1, source_target_pairs={{0,1},{1,0},{2,3},{3,2},{4,5},{5,4},{6,7},{7,6},{8,9},{9,8},{10,11... | collective-permute-start | bytes 786440 | tf_op jit(solution)/shard_map/ppermute | solution.py:493
  10.7 3.1 %copy-start.3 = (bf16[2048,1792]{1,0:T(8,128)(2,1)S(1)}, bf16[2048,1792]{1,0:T(8,128)(2,1)}, u32[]{:S(2)}) copy-start(bf16[2048,1792]{1,0:T(8,128)(2,1)} %w_ref.8) | copy-start | bytes 22020100
  13.8 5.1 %copy-start.4 = (bf16[256,128]{1,0:T(8,128)(2,1)S(1)}, bf16[256,128]{1,0:T(8,128)(2,1)}, u32[]{:S(2)}) copy-start(bf16[256,128]{1,0:T(8,128)(2,1)} %constant.32.clone.mean_ref) | copy-start | bytes 196612
  13.8 5.1 %copy-start.5 = (f32[160,128]{1,0:T(8,128)S(1)}, f32[160,128]{1,0:T(8,128)}, u32[]{:S(2)}) copy-start(f32[160,128]{1,0:T(8,128)} %constant.31.clone.weight_ref) | copy-start | bytes 245764
  13.8 5.1 %copy-start.6 = (f32[3,512]{1,0:T(4,128)S(1)}, f32[3,512]{1,0:T(4,128)}, u32[]{:S(2)}) copy-start(f32[3,512]{1,0:T(4,128)} %conv_ref.9) | copy-start | bytes 18436
  22.8 9.9 %copy-start.2 = (bf16[128,1280]{1,0:T(8,128)(2,1)S(1)}, bf16[128,1280]{1,0:T(8,128)(2,1)}, u32[]{:S(2)}) copy-start(bf16[128,1280]{1,0:T(8,128)(2,1)} %constant.29.clone.turn_ref) | copy-start | bytes 983044
  22.8 6.1 %collective-permute-start.1 = (bf16[144,512]{1,0:T(8,128)(2,1)S(1)}, bf16[144,512]{1,0:T(8,128)(2,1)S(1)}, u32[]{:S(2)}, u32[]{:S(2)}) collective-permute-start(bf16[144,512]{1,0:T(8,128)(2,1)S(1)} %get-tuple-element.89), channel_id=1, source_target_pairs={{0,2},{2,4},{4,6},{6,8},{8,10},{10,12},{12,14},{14,16},{16,18},{18... | collective-permute-start | bytes 442376 | tf_op jit(solution)/shard_map/ppermute | solution.py:591
  50.6 4.1 %copy-start = (bf16[512,2048]{1,0:T(8,128)(2,1)S(1)}, bf16[512,2048]{1,0:T(8,128)(2,1)}, u32[]{:S(2)}) copy-start(bf16[512,2048]{1,0:T(8,128)(2,1)} %w_ref.15) | copy-start | bytes 6291460
  52.4 4.7 %collective-permute-start.7 = (bf16[160,128]{1,0:T(8,128)(2,1)S(1)}, bf16[160,128]{1,0:T(8,128)(2,1)S(1)}, u32[]{:S(2)}, u32[]{:S(2)}) collective-permute-start(bf16[160,128]{1,0:T(8,128)(2,1)S(1)} %get-tuple-element.139), channel_id=1, source_target_pairs={{0,2},{2,0},{4,6},{6,4},{8,10},{10,8},{12,14},{14,12},{16,18},{18,... | collective-permute-start | bytes 122888 | tf_op jit(solution)/shard_map/ppermute | solution.py:402
  52.5 4.6 %collective-permute-start.8 = (bf16[160,128]{1,0:T(8,128)(2,1)S(1)}, bf16[160,128]{1,0:T(8,128)(2,1)S(1)}, u32[]{:S(2)}, u32[]{:S(2)}) collective-permute-start(bf16[160,128]{1,0:T(8,128)(2,1)S(1)} %get-tuple-element.140), channel_id=1, source_target_pairs={{0,4},{2,6},{4,0},{6,2},{8,12},{10,14},{12,8},{14,10},{16,20},{18,... | collective-permute-start | bytes 122888 | tf_op jit(solution)/shard_map/ppermute | solution.py:402
  54.6 3.5 %collective-permute-start.9 = (bf16[160,128]{1,0:T(8,128)(2,1)S(1)}, bf16[160,128]{1,0:T(8,128)(2,1)S(1)}, u32[]{:S(2)}, u32[]{:S(2)}) collective-permute-start(bf16[160,128]{1,0:T(8,128)(2,1)S(1)} %get-tuple-element.141), channel_id=1, source_target_pairs={{0,6},{2,4},{4,2},{6,0},{8,14},{10,12},{12,10},{14,8},{16,22},{18,... | collective-permute-start | bytes 122888 | tf_op jit(solution)/shard_map/ppermute | solution.py:402
  55.3 18.5 %collective-permute-start.6 = (bf16[256,1024]{1,0:T(8,128)(2,1)S(1)}, bf16[256,1024]{1,0:T(8,128)(2,1)S(1)}, u32[]{:S(2)}, u32[]{:S(2)}) collective-permute-start(bf16[256,1024]{1,0:T(8,128)(2,1)S(1)} %shard_map.101), channel_id=1, source_target_pairs={{0,1},{1,0},{2,3},{3,2},{4,5},{5,4},{6,7},{7,6},{8,9},{9,8},{10,11... | collective-permute-start | bytes 1572872 | tf_op jit(solution)/shard_map/ppermute | solution.py:493
  58.8 9.2 %collective-permute-start.12 = (bf16[160,128]{1,0:T(8,128)(2,1)S(1)}, bf16[160,128]{1,0:T(8,128)(2,1)S(1)}, u32[]{:S(2)}, u32[]{:S(2)}) collective-permute-start(bf16[160,128]{1,0:T(8,128)(2,1)S(1)} %get-tuple-element.146), channel_id=1, source_target_pairs={{0,24},{2,26},{4,28},{6,30},{8,16},{10,18},{12,20},{14,22},{16,8},... | collective-permute-start | bytes 122888 | tf_op jit(solution)/shard_map/ppermute | solution.py:402
  62.4 5.5 %collective-permute-start.11 = (bf16[160,128]{1,0:T(8,128)(2,1)S(1)}, bf16[160,128]{1,0:T(8,128)(2,1)S(1)}, u32[]{:S(2)}, u32[]{:S(2)}) collective-permute-start(bf16[160,128]{1,0:T(8,128)(2,1)S(1)} %get-tuple-element.146), channel_id=1, source_target_pairs={{0,16},{2,18},{4,20},{6,22},{8,24},{10,26},{12,28},{14,30},{16,0},... | collective-permute-start | bytes 122888 | tf_op jit(solution)/shard_map/ppermute | solution.py:402
  62.4 5.5 %collective-permute-start.10 = (bf16[160,128]{1,0:T(8,128)(2,1)S(1)}, bf16[160,128]{1,0:T(8,128)(2,1)S(1)}, u32[]{:S(2)}, u32[]{:S(2)}) collective-permute-start(bf16[160,128]{1,0:T(8,128)(2,1)S(1)} %get-tuple-element.146), channel_id=1, source_target_pairs={{0,8},{2,10},{4,12},{6,14},{8,0},{10,2},{12,4},{14,6},{16,24},{18,... | collective-permute-start | bytes 122888 | tf_op jit(solution)/shard_map/ppermute | solution.py:402
  65.0 5.5 %copy-start.7 = (f32[512]{0:T(512)S(1)}, f32[512]{0:T(512)}, u32[]{:S(2)}) copy-start(f32[512]{0:T(512)} %param.12) | copy-start | bytes 6148
  68.6 5.2 %collective-permute-start.14 = (bf16[160,128]{1,0:T(8,128)(2,1)S(1)}, bf16[160,128]{1,0:T(8,128)(2,1)S(1)}, u32[]{:S(2)}, u32[]{:S(2)}) collective-permute-start(bf16[160,128]{1,0:T(8,128)(2,1)S(1)} %get-tuple-element.161), channel_id=1, source_target_pairs={{0,2},{2,0},{4,6},{6,4},{8,10},{10,8},{12,14},{14,12},{16,18},{18,... | collective-permute-start | bytes 122888 | tf_op jit(solution)/shard_map/ppermute | solution.py:402
  68.7 5.2 %collective-permute-start.15 = (bf16[160,128]{1,0:T(8,128)(2,1)S(1)}, bf16[160,128]{1,0:T(8,128)(2,1)S(1)}, u32[]{:S(2)}, u32[]{:S(2)}) collective-permute-start(bf16[160,128]{1,0:T(8,128)(2,1)S(1)} %get-tuple-element.162), channel_id=1, source_target_pairs={{0,4},{2,6},{4,0},{6,2},{8,12},{10,14},{12,8},{14,10},{16,20},{18,... | collective-permute-start | bytes 122888 | tf_op jit(solution)/shard_map/ppermute | solution.py:402
  69.5 4.3 %collective-permute-start.16 = (bf16[160,128]{1,0:T(8,128)(2,1)S(1)}, bf16[160,128]{1,0:T(8,128)(2,1)S(1)}, u32[]{:S(2)}, u32[]{:S(2)}) collective-permute-start(bf16[160,128]{1,0:T(8,128)(2,1)S(1)} %get-tuple-element.163), channel_id=1, source_target_pairs={{0,6},{2,4},{4,2},{6,0},{8,14},{10,12},{12,10},{14,8},{16,22},{18,... | collective-permute-start | bytes 122888 | tf_op jit(solution)/shard_map/ppermute | solution.py:402
  72.2 14.9 %collective-permute-start.17 = (bf16[1024,128]{1,0:T(8,128)(2,1)S(1)}, bf16[1024,128]{1,0:T(8,128)(2,1)S(1)}, u32[]{:S(2)}, u32[]{:S(2)}) collective-permute-start(bf16[1024,128]{1,0:T(8,128)(2,1)S(1)} %shard_map.107.refs_0_.refs_2_), channel_id=1, source_target_pairs={{0,1},{1,0},{2,3},{3,2},{4,5},{5,4},{6,7},{7,6},{8,9},{9,8},{10,11... | collective-permute-start | bytes 786440 | tf_op jit(solution)/shard_map/ppermute | solution.py:493
  73.7 14.9 %collective-permute-start.13 = (bf16[256,1024]{1,0:T(8,128)(2,1)S(1)}, bf16[256,1024]{1,0:T(8,128)(2,1)S(1)}, u32[]{:S(2)}, u32[]{:S(2)}) collective-permute-start(bf16[256,1024]{1,0:T(8,128)(2,1)S(1)} %collective-permute-done.6.refs_0_), channel_id=1, source_target_pairs={{0,2},{2,0},{4,6},{6,4},{8,10},{10,8},{12,14},{14,12},{16,18},{18,... | collective-permute-start | bytes 1572872 | tf_op jit(solution)/shard_map/ppermute | solution.py:402
  75.2 10.4 %collective-permute-start.22 = (bf16[256,384]{1,0:T(8,128)(2,1)S(1)}, bf16[256,384]{1,0:T(8,128)(2,1)S(1)}, u32[]{:S(2)}, u32[]{:S(2)}) collective-permute-start(bf16[256,384]{1,0:T(8,128)(2,1)S(1)} %shard_map.108.refs_3_), channel_id=1, source_target_pairs={{0,1},{1,0},{2,3},{3,2},{4,5},{5,4},{6,7},{7,6},{8,9},{9,8},{10,11... | collective-permute-start | bytes 589832 | tf_op jit(solution)/shard_map/ppermute | solution.py:493
  77.7 13.0 %collective-permute-start.21 = (bf16[256,384]{1,0:T(8,128)(2,1)S(1)}, bf16[256,384]{1,0:T(8,128)(2,1)S(1)}, u32[]{:S(2)}, u32[]{:S(2)}) collective-permute-start(bf16[256,384]{1,0:T(8,128)(2,1)S(1)} %shard_map.109.refs_3_), channel_id=1, source_target_pairs={{0,1},{1,0},{2,3},{3,2},{4,5},{5,4},{6,7},{7,6},{8,9},{9,8},{10,11... | collective-permute-start | bytes 589832 | tf_op jit(solution)/shard_map/ppermute | solution.py:493
  80.2 13.8 %collective-permute-start.20 = (bf16[256,384]{1,0:T(8,128)(2,1)S(1)}, bf16[256,384]{1,0:T(8,128)(2,1)S(1)}, u32[]{:S(2)}, u32[]{:S(2)}) collective-permute-start(bf16[256,384]{1,0:T(8,128)(2,1)S(1)} %shard_map.110.refs_3_), channel_id=1, source_target_pairs={{0,1},{1,0},{2,3},{3,2},{4,5},{5,4},{6,7},{7,6},{8,9},{9,8},{10,11... | collective-permute-start | bytes 589832 | tf_op jit(solution)/shard_map/ppermute | solution.py:493
  85.6 10.5 %collective-permute-start.19 = (bf16[128,384]{1,0:T(8,128)(2,1)S(1)}, bf16[128,384]{1,0:T(8,128)(2,1)S(1)}, u32[]{:S(2)}, u32[]{:S(2)}) collective-permute-start(bf16[128,384]{1,0:T(8,128)(2,1)S(1)} %shard_map.111.refs_1_), channel_id=1, source_target_pairs={{0,1},{1,0},{2,3},{3,2},{4,5},{5,4},{6,7},{7,6},{8,9},{9,8},{10,11... | collective-permute-start | bytes 294920 | tf_op jit(solution)/shard_map/ppermute | solution.py:493
  87.1 10.6 %collective-permute-start.18 = (bf16[128,384]{1,0:T(8,128)(2,1)S(1)}, bf16[128,384]{1,0:T(8,128)(2,1)S(1)}, u32[]{:S(2)}, u32[]{:S(2)}) collective-permute-start(bf16[128,384]{1,0:T(8,128)(2,1)S(1)} %shard_map.112.refs_3_), channel_id=1, source_target_pairs={{0,1},{1,0},{2,3},{3,2},{4,5},{5,4},{6,7},{7,6},{8,9},{9,8},{10,11... | collective-permute-start | bytes 294920 | tf_op jit(solution)/shard_map/ppermute | solution.py:493

commit v11 on v10

--- a/solution.py
+++ b/solution.py
@@ -325,8 +325,8 @@
 
 def place_pieces(a_ref, pieces, turns, offset, mixed_ref):
     rows = mixed_ref.shape[0]
-    for ref, (all_rows, pairs) in zip(pieces, turns):
-        here = slice(offset, offset + rows) if all_rows else slice(0, rows)
+    for ref, (begin, pairs) in zip(pieces, turns):
+        here = slice(offset - begin, offset - begin + rows)
         for k, turn in enumerate(pairs):
             at = pl.multiple_of(jnp.bitwise_xor(a_ref[1], turn) * LANES, LANES)
             mixed_ref[:, pl.ds(at, LANES)] = ref[here, k * LANES : (k + 1) * LANES]
@@ -340,8 +340,8 @@
     share_ref, mixed_ref = refs[-2:]
     at = 0
     for i, (offset, rows) in enumerate(blocks):
-        pieces = refs[i * len(turns) : (i + 1) * len(turns)]
-        place_pieces(a_ref, pieces, turns, offset, mixed_ref.at[pl.ds(at, rows), :])
+        pieces = refs[i * len(turns[i]) : (i + 1) * len(turns[i])]
+        place_pieces(a_ref, pieces, turns[i], offset, mixed_ref.at[pl.ds(at, rows), :])
         at += rows
     cols = share_ref.shape[1]
     mine = own_columns(a_ref, cols, 0, cols)
@@ -522,7 +522,7 @@
                 out_specs=pl.BlockSpec((share, cols), lambda i, a: (0, 0)),
             ),
             vmem=8 << 20,
-        )(after(places, done[last - 1][1]), out_weight)
+        )(places, out_weight)
 
     qk_width = -(-heads * FQK // LANES) * LANES
     arranged_width = 2 * qk_width + 3 * width
@@ -587,11 +587,13 @@
         )(places, turn, prev, q, k, v, wq, wk)
 
     done, attended = {}, {}
+    picked = [pick(r) for r in range(1, n)]
     done[last] = do_block(last, None, None)
     halo = lax.ppermute(done[last][6], "ctx", [(i, i + 1) for i in range(ctx - 1)])
     prevs = {0: halo}
     for b in range(last - 1):
-        done[b] = do_block(b, prevs[b], [a[1] for a in attended.values()] if b else None)
+        behind = [a[1] for a in attended.values()] + (picked if b == 1 else [])
+        done[b] = do_block(b, prevs[b], behind if b else None)
         prevs[b + 1] = done[b][6]
         attended[b] = attend(b, prevs[b])
         if b == 0:
@@ -632,7 +634,7 @@
     early = []
     if in_planes:
         held = sends[:1] + [exchange(sends[r], "ctx", r) for r in range(1, PLANE)]
-        back = prior_in_planes(held, places, [done[last - 1][1], (attended[last - 1][1], edge)])
+        back = prior_in_planes(held, places, [done[last - 1][6], (attended[last - 1][1], edge)])
         priors = [exchange(back[r], "ctx", r) for r in range(1, PLANE)]
         turns = tuple(range(1, PLANE))
         mixed = finish((0,), back[:1], range(last + 1), done[last][1])
@@ -641,7 +643,7 @@
         priors = prior_by_doubling(sum(done[b][2] for b in range(last + 1)), position)
         turns = tuple(range(pairs))
         mixed = attended[last][1]
-    fetched = [from_head(pick(r), r) for r in range(1, n)]
+    fetched = [from_head(after(block, done[last - 1][1]), r) for r, block in enumerate(picked, 1)]
     out_rows = []
     for got in fetched:
         out_rows.append(got)
@@ -653,17 +655,20 @@
         mixed = finish(turns, priors, (b,), mixed)
         mixes[b] = [mixed] + [from_head(mixed, r) for r in range(1, n)]
 
-    piece_turns = ([(True, (0,))] if early else []) + [(False, turns)]
-
     def pieces_of(b, r):
         return early[r : r + 1] + [mixes[b][r]]
+
+    def turns_of(b):
+        return ([(0, (0,))] if early else []) + [(blocks[b][0], turns)]
 
     tail_blocks = order[-2:]
     tail_rows = sum(blocks[b][1] for b in tail_blocks)
     share = call(
-        functools.partial(share_kernel, turns=piece_turns, blocks=[blocks[b] for b in tail_blocks]),
+        functools.partial(
+            share_kernel, turns=[turns_of(b) for b in tail_blocks], blocks=[blocks[b] for b in tail_blocks]
+        ),
         jax.ShapeDtypeStruct((tail_rows, cols), BF16),
-        in_specs=[scalar] + [whole] * (1 + 2 * len(piece_turns)),
+        in_specs=[scalar] + [whole] * (1 + 2 * len(turns_of(last))),
         out_specs=whole,
         scratch_shapes=[pltpu.VMEM((tail_rows, width), BF16)],
         vmem=16 << 20,
@@ -687,7 +692,7 @@
             specs.append(pl.BlockSpec(memory_space=pl.ANY))
         result = call(
             functools.partial(
-                output_kernel, n=n, offset=at, parts=out_parts, turns=piece_turns, shared=shared
+                output_kernel, n=n, offset=at, parts=out_parts, turns=turns_of(b), shared=shared
             ),
             jax.ShapeDtypeStruct((row_count, cols), BF16),
             in_specs=specs,

time: 99.7 us -> 99.1 us (level)
  transfers between devices with their start and end apart: 23 -> 23, of which waited for: 5 -> 5; matrix products, arithmetic and copies ran while one was open for 2% -> 2% of each run, Pallas kernels for 51% -> 52%
where the time goes in v11:
time: 99.1 us; the launch traced here: 98.9 us
  Pallas kernels  54.3 us (55%)
  starting transfers between devices  25.9 us (26%)
  waiting for transfers between devices  11.5 us (12%)
  local copies, waits for them, and re-layouts  6.54 us (7%)
    pallas_call x5, Pallas kernels, do_block(): call(functools.partial(block_kernel, n=n, heads=heads, extra=extra, other...  15.9 us
    ppermute x12, starting transfers between devices, from_head(): return lax.ppermute(value, 'head', [(i, (i + by) % n) for i in range(n)])  15.7 us
    ppermute x12, waiting for transfers between devices, from_head(): return lax.ppermute(value, 'head', [(i, (i + by) % n) for i in range(n)])  10.3 us
    pallas_call x5, Pallas kernels, attend(): call(functools.partial(attend_kernel, heads=heads, first=b == 0), [jax.Sh...  9.97 us
    pallas_call x5, Pallas kernels, per_device(): call(functools.partial(output_kernel, n=n, offset=at, parts=out_parts, tu...  9.28 us
    ppermute x10, starting transfers between devices, exchange(): return lax.ppermute(value, axis, [(i, i ^ flip) for i in range(count)])  8.69 us
    pallas_call x6, Pallas kernels, finish(): call(functools.partial(finish_kernel, heads=heads, turns=turns, before=be...  8.27 us
    pallas_call x1, Pallas kernels, per_device(): call(functools.partial(arrange_kernel, heads=heads), jax.ShapeDtypeStruct...  5.09 us
  transfers between devices with their start and end apart: 23, of which 5 were waited for; matrix products, arithmetic and copies ran while one was open for 2% of the time, Pallas kernels for 52%

profile of v11, /device:TPU:0, one launch (start us, length us, event | category | flops | bytes accessed | tf_op | source)
XLA Modules:
  0.0 98.9 jit_solution(177920419112482736)
XLA Ops:
  1.2 3.0 %collective-permute-start = (bf16[272,1024]{1,0:T(8,128)(2,1)S(1)}, bf16[272,1024]{1,0:T(8,128)(2,1)S(1)}, u32[]{:S(2)}, u32[]{:S(2)}) collective-permute-start(bf16[272,1024]{1,0:T(8,128)(2,1)S(1)} %slice.15.refs_0_), channel_id=1, source_target_pairs={{0,1},{1,0},{2,3},{3,2},{4,5},{5,4},{6,7},{7,6},{8,9},{9,8},{10,11... | collective-permute-start | bytes 1671176 | tf_op jit(solution)/shard_map/ppermute | solution.py:493
  5.6 2.0 %collective-permute-start.3 = (bf16[256,1024]{1,0:T(8,128)(2,1)S(1)}, bf16[256,1024]{1,0:T(8,128)(2,1)S(1)}, u32[]{:S(2)}, u32[]{:S(2)}) collective-permute-start(bf16[256,1024]{1,0:T(8,128)(2,1)S(1)} %get-tuple-element.105.refs_0_), channel_id=1, source_target_pairs={{0,1},{1,0},{2,3},{3,2},{4,5},{5,4},{6,7},{7,6},{8,9},{9,8},{10,11... | collective-permute-start | bytes 1572872 | tf_op jit(solution)/shard_map/ppermute | solution.py:493
  8.8 1.9 %collective-permute-start.5 = (bf16[128,1024]{1,0:T(8,128)(2,1)S(1)}, bf16[128,1024]{1,0:T(8,128)(2,1)S(1)}, u32[]{:S(2)}, u32[]{:S(2)}) collective-permute-start(bf16[128,1024]{1,0:T(8,128)(2,1)S(1)} %get-tuple-element.123.refs_0_), channel_id=1, source_target_pairs={{0,1},{1,0},{2,3},{3,2},{4,5},{5,4},{6,7},{7,6},{8,9},{9,8},{10,11... | collective-permute-start | bytes 786440 | tf_op jit(solution)/shard_map/ppermute | solution.py:493
  10.7 3.1 %copy-done.3 = bf16[2048,1792]{1,0:T(8,128)(2,1)S(1)} copy-done((bf16[2048,1792]{1,0:T(8,128)(2,1)S(1)}, bf16[2048,1792]{1,0:T(8,128)(2,1)}, u32[]{:S(2)}) %copy-start.3) | copy-done | bytes 7340056
  13.8 5.1 %shard_map.92.w_ref = bf16[2048,1792]{1,0:T(8,128)(2,1)S(1)} custom-call(bf16[2048,1792]{1,0:T(8,128)(2,1)S(1)} %copy-done.3), custom_call_target="tpu_custom_call" | custom-call | flops 1 | bytes 1 | tf_op jit(solution)/shard_map/pallas_call | solution.py:530
  19.0 3.8 %shard_map.93 = (bf16[256,128]{1,0:T(8,128)(2,1)S(1)}, bf16[256,512]{1,0:T(8,128)(2,1)S(1)}, f32[4,160,128]{2,1,0:T(8,128)S(1)}, bf16[256,128]{1,0:T(8,128)(2,1)...) custom-call(s32[3]{0:T(128)S(1)} %pad_add_fusion.a_ref.j_ref._, ...), custom_call_target="tpu_custom_call" | custom-call | flops 1 | bytes 1 | tf_op jit(solution)/shard_map/pallas_call | solution.py:556
  22.8 1.5 %collective-permute-start.1 = (bf16[144,512]{1,0:T(8,128)(2,1)S(1)}, bf16[144,512]{1,0:T(8,128)(2,1)S(1)}, u32[]{:S(2)}, u32[]{:S(2)}) collective-permute-start(bf16[144,512]{1,0:T(8,128)(2,1)S(1)} %get-tuple-element.90), channel_id=1, source_target_pairs={{0,2},{2,4},{4,6},{6,8},{8,10},{10,12},{12,14},{14,16},{16,18},{18... | collective-permute-start | bytes 442376 | tf_op jit(solution)/shard_map/ppermute | solution.py:592
  24.9 4.0 %collective-permute-done.2.refs_1_ = bf16[256,1024]{1,0:T(8,128)(2,1)S(1)} collective-permute-done((bf16[256,1024]{1,0:T(8,128)(2,1)S(1)}, bf16[256,1024]{1,0:T(8,128)(2,1)S(1)}, u32[]{:S(2)}, u32[]{:S(2)}) %collective-permute-start.2) | collective-permute-done | bytes 524320 | tf_op jit(solution)/shard_map/ppermute | solution.py:493
  28.9 3.8 %shard_map.94 = (bf16[256,128]{1,0:T(8,128)(2,1)S(1)}, bf16[256,512]{1,0:T(8,128)(2,1)S(1)}, f32[4,160,128]{2,1,0:T(8,128)S(1)}, bf16[256,128]{1,0:T(8,128)(2,1)...) custom-call(s32[3]{0:T(128)S(1)} %pad_add_fusion.a_ref.j_ref._, ...), custom_call_target="tpu_custom_call" | custom-call | flops 1 | bytes 1 | tf_op jit(solution)/shard_map/pallas_call | solution.py:556
  32.7 2.1 %shard_map.95 = (bf16[256,1280]{1,0:T(8,128)(2,1)S(1)}, f32[256,512]{1,0:T(8,128)S(1)}, f32[256,512]{1,0:T(8,128)S(1)}) custom-call(s32[3]{0:T(128)S(1)} %pad_add_fusion.a_ref.j_ref._, bf16[128,1280]{1,0:T(8,128)(2,1)S(1)} %copy-done.2, bf16[144,512]{1,0:T(8,128)(2,1)S(1)} %collective-permute-done.1.refs_2_.prev_ref, ...), custom_call_target="tpu_custom_call" | custom-call | flops 1 | bytes 1 | tf_op jit(solution)/shard_map/pallas_call | solution.py:580
  34.9 2.1 %shard_map.96 = (bf16[256,1280]{1,0:T(8,128)(2,1)S(1)}, f32[256,512]{1,0:T(8,128)S(1)}, f32[256,512]{1,0:T(8,128)S(1)}) custom-call(s32[3]{0:T(128)S(1)} %pad_add_fusion.a_ref.j_ref._, bf16[128,1280]{1,0:T(8,128)(2,1)S(1)} %copy-done.2, bf16[144,512]{1,0:T(8,128)(2,1)S(1)} %collective-permute-done.1.refs_2_.prev_ref, ...), custom_call_target="tpu_custom_call" | custom-call | flops 1 | bytes 1 | tf_op jit(solution)/shard_map/pallas_call | solution.py:580
  37.0 3.1 %collective-permute-done.3.refs_1_ = bf16[256,1024]{1,0:T(8,128)(2,1)S(1)} collective-permute-done((bf16[256,1024]{1,0:T(8,128)(2,1)S(1)}, bf16[256,1024]{1,0:T(8,128)(2,1)S(1)}, u32[]{:S(2)}, u32[]{:S(2)}) %collective-permute-start.3) | collective-permute-done | bytes 524320 | tf_op jit(solution)/shard_map/ppermute | solution.py:493
  40.1 3.8 %shard_map.97 = (bf16[256,128]{1,0:T(8,128)(2,1)S(1)}, bf16[256,512]{1,0:T(8,128)(2,1)S(1)}, f32[4,160,128]{2,1,0:T(8,128)S(1)}, bf16[256,128]{1,0:T(8,128)(2,1)...) custom-call(s32[3]{0:T(128)S(1)} %pad_add_fusion.a_ref.j_ref._, ...), custom_call_target="tpu_custom_call" | custom-call | flops 1 | bytes 1 | tf_op jit(solution)/shard_map/pallas_call | solution.py:556
  43.9 2.1 %shard_map.98 = (bf16[256,1280]{1,0:T(8,128)(2,1)S(1)}, f32[256,512]{1,0:T(8,128)S(1)}, f32[256,512]{1,0:T(8,128)S(1)}) custom-call(s32[3]{0:T(128)S(1)} %pad_add_fusion.a_ref.j_ref._, bf16[128,1280]{1,0:T(8,128)(2,1)S(1)} %copy-done.2, bf16[144,512]{1,0:T(8,128)(2,1)S(1)} %get-tuple-element.106.refs_2_.prev_ref, ...), custom_call_target="tpu_custom_call" | custom-call | flops 1 | bytes 1 | tf_op jit(solution)/shard_map/pallas_call | solution.py:580
  46.1 2.6 %shard_map.99 = (bf16[128,128]{1,0:T(8,128)(2,1)S(1)}, bf16[128,512]{1,0:T(8,128)(2,1)S(1)}, f32[4,160,128]{2,1,0:T(8,128)S(1)}, bf16[128,128]{1,0:T(8,128)(2,1)...) custom-call(s32[3]{0:T(128)S(1)} %pad_add_fusion.a_ref.j_ref._, ...), custom_call_target="tpu_custom_call" | custom-call | flops 1 | bytes 1 | tf_op jit(solution)/shard_map/pallas_call | solution.py:556
  48.7 1.9 %shard_map.100 = (bf16[128,1280]{1,0:T(8,128)(2,1)S(1)}, f32[128,512]{1,0:T(8,128)S(1)}, f32[128,512]{1,0:T(8,128)S(1)}) custom-call(s32[3]{0:T(128)S(1)} %pad_add_fusion.a_ref.j_ref._, bf16[128,1280]{1,0:T(8,128)(2,1)S(1)} %copy-done.2, bf16[144,512]{1,0:T(8,128)(2,1)S(1)} %get-tuple-element.107.refs_2_.prev_ref, ...), custom_call_target="tpu_custom_call" | custom-call | flops 1 | bytes 1 | tf_op jit(solution)/shard_map/pallas_call | solution.py:580
  50.6 1.8 %shard_map.101 = (bf16[128,128]{1,0:T(8,128)(2,1)S(1)}, bf16[128,512]{1,0:T(8,128)(2,1)S(1)}, f32[4,160,128]{2,1,0:T(8,128)S(1)}, bf16[160,128]{1,0:T(8,128)(2,1...) custom-call(s32[3]{0:T(128)S(1)} %pad_add_fusion.a_ref.j_ref._, ...), custom_call_target="tpu_custom_call" | custom-call | flops 1 | bytes 1 | tf_op jit(solution)/shard_map/pallas_call | solution.py:556
  52.5 2.1 %collective-permute-start.8 = (bf16[160,128]{1,0:T(8,128)(2,1)S(1)}, bf16[160,128]{1,0:T(8,128)(2,1)S(1)}, u32[]{:S(2)}, u32[]{:S(2)}) collective-permute-start(bf16[160,128]{1,0:T(8,128)(2,1)S(1)} %get-tuple-element.142), channel_id=1, source_target_pairs={{0,4},{2,6},{4,0},{6,2},{8,12},{10,14},{12,8},{14,10},{16,20},{18,... | collective-permute-start | bytes 122888 | tf_op jit(solution)/shard_map/ppermute | solution.py:402
  54.7 1.8 %collective-permute-start.6 = (bf16[256,1024]{1,0:T(8,128)(2,1)S(1)}, bf16[256,1024]{1,0:T(8,128)(2,1)S(1)}, u32[]{:S(2)}, u32[]{:S(2)}) collective-permute-start(bf16[256,1024]{1,0:T(8,128)(2,1)S(1)} %shard_map.91), channel_id=1, source_target_pairs={{0,1},{1,0},{2,3},{3,2},{4,5},{5,4},{6,7},{7,6},{8,9},{9,8},{10,11... | collective-permute-start | bytes 1572872 | tf_op jit(solution)/shard_map/ppermute | solution.py:493
  56.4 1.8 %shard_map.102 = (bf16[128,128]{1,0:T(8,128)(2,1)S(1)}, bf16[128,512]{1,0:T(8,128)(2,1)S(1)}, bf16[128,512]{1,0:T(8,128)(2,1)S(1)}, bf16[144,512]{1,0:T(8,128)(2,1)S(1)}) custom-call(s32[3]{0:T(128)S(1)} %pad_add_fusion.a_ref.j_ref._, bf16[256,128]{1,0:T(8,128)(2,1)S(1)} %copy-done.4, bf16[2048,1792]{1,0:T(8,128)(2,1)S(1)} %shard_map.92.w_ref, ...), custom_call_target="tpu_custom_call" | custom-call | flops 1 | bytes 1 | tf_op jit(solution)/shard_map/pallas_call | solution.py:569
  58.9 3.7 %collective-permute-start.12 = (bf16[160,128]{1,0:T(8,128)(2,1)S(1)}, bf16[160,128]{1,0:T(8,128)(2,1)S(1)}, u32[]{:S(2)}, u32[]{:S(2)}) collective-permute-start(bf16[160,128]{1,0:T(8,128)(2,1)S(1)} %get-tuple-element.148), channel_id=1, source_target_pairs={{0,24},{2,26},{4,28},{6,30},{8,16},{10,18},{12,20},{14,22},{16,8},... | collective-permute-start | bytes 122888 | tf_op jit(solution)/shard_map/ppermute | solution.py:402
  64.6 1.7 %shard_map.103 = (bf16[128,1280]{1,0:T(8,128)(2,1)S(1)}, f32[128,512]{1,0:T(8,128)S(1)}, f32[128,512]{1,0:T(8,128)S(1)}) custom-call(s32[3]{0:T(128)S(1)} %pad_add_fusion.a_ref.j_ref._, bf16[128,1280]{1,0:T(8,128)(2,1)S(1)} %copy-done.2, bf16[144,512]{1,0:T(8,128)(2,1)S(1)} %get-tuple-element.124.refs_2_.prev_ref, ...), custom_call_target="tpu_custom_call" | custom-call | flops 1 | bytes 1 | tf_op jit(solution)/shard_map/pallas_call | solution.py:580
  68.1 1.6 %collective-permute-start.15 = (bf16[160,128]{1,0:T(8,128)(2,1)S(1)}, bf16[160,128]{1,0:T(8,128)(2,1)S(1)}, u32[]{:S(2)}, u32[]{:S(2)}) collective-permute-start(bf16[160,128]{1,0:T(8,128)(2,1)S(1)} %get-tuple-element.164), channel_id=1, source_target_pairs={{0,4},{2,6},{4,0},{6,2},{8,12},{10,14},{12,8},{14,10},{16,20},{18,... | collective-permute-start | bytes 122888 | tf_op jit(solution)/shard_map/ppermute | solution.py:402
  70.0 1.7 %shard_map.107.refs_0_.refs_2_ = bf16[1024,128]{1,0:T(8,128)(2,1)S(1)} custom-call(s32[3]{0:T(128)S(1)} %pad_add_fusion.a_ref.j_ref._, bf16[256,128]{1,0:T(8,128)(2,1)S(1)} %copy-done.4, f32[1,512]{1,0:T(1,128)S(1)} %bitcast.4, bf16[160,128]{1,0:T(8,128)(2,1)S(1)} %get-tuple-element.149.refs_0_, ...), custom_call_target="tpu_custom_call" | custom-call | flops 4849999872 | bytes 1 | tf_op jit(solution)/shard_map/pallas_call | solution.py:624
  71.7 1.5 %collective-permute-start.17 = (bf16[1024,128]{1,0:T(8,128)(2,1)S(1)}, bf16[1024,128]{1,0:T(8,128)(2,1)S(1)}, u32[]{:S(2)}, u32[]{:S(2)}) collective-permute-start(bf16[1024,128]{1,0:T(8,128)(2,1)S(1)} %shard_map.107.refs_0_.refs_2_), channel_id=1, source_target_pairs={{0,1},{1,0},{2,3},{3,2},{4,5},{5,4},{6,7},{7,6},{8,9},{9,8},{10,11... | collective-permute-start | bytes 786440 | tf_op jit(solution)/shard_map/ppermute | solution.py:493
  78.1 1.4 %shard_map.110.refs_3_ = bf16[256,384]{1,0:T(8,128)(2,1)S(1)} custom-call(s32[3]{0:T(128)S(1)} %pad_add_fusion.a_ref.j_ref._, bf16[256,128]{1,0:T(8,128)(2,1)S(1)} %copy-done.4, f32[1,512]{1,0:T(1,128)S(1)} %bitcast.7, bf16[160,128]{1,0:T(8,128)(2,1)S(1)} %collective-permute-done.14.refs_0_, bf16[160,128]{1,0:T(8,128)(2,1)S(1)} %collective-permute-done.15.refs_1_, ...), custom_call_target="tpu_custom_call" | custom-call | flops 1 | bytes 1 | tf_op jit(solution)/shard_map/pallas_call | solution.py:624
  83.1 1.9 %collective-permute-done.22.refs_5_ = bf16[256,384]{1,0:T(8,128)(2,1)S(1)} collective-permute-done((bf16[256,384]{1,0:T(8,128)(2,1)S(1)}, bf16[256,384]{1,0:T(8,128)(2,1)S(1)}, u32[]{:S(2)}, u32[]{:S(2)}) %collective-permute-start.22) | collective-permute-done | bytes 196640 | tf_op jit(solution)/shard_map/ppermute | solution.py:493
  88.1 2.1 %shard_map.114.refs_6_ = bf16[1024,1024]{1,0:T(8,128)(2,1)} custom-call(s32[3]{0:T(128)S(1)} %pad_add_fusion.a_ref.j_ref._, bf16[512,2048]{1,0:T(8,128)(2,1)S(1)} %copy-done, bf16[256,1024]{1,0:T(8,128)(2,1)S(1)} %collective-permute-done.6.refs_0_, bf16[256,1024]{1,0:T(8,128)(2,1)S(1)} %collective-permute-done.13.refs_1_, ...), custom_call_target="tpu_custom_call" | custom-call | flops 1 | bytes 1 | tf_op jit(solution)/shard_map/pallas_call | solution.py:693
  90.2 2.1 %shard_map.115.refs_6_ = bf16[1024,1024]{1,0:T(8,128)(2,1)} custom-call(s32[3]{0:T(128)S(1)} %pad_add_fusion.a_ref.j_ref._, bf16[512,2048]{1,0:T(8,128)(2,1)S(1)} %copy-done, bf16[256,1024]{1,0:T(8,128)(2,1)S(1)} %collective-permute-done.6.refs_0_, bf16[256,1024]{1,0:T(8,128)(2,1)S(1)} %collective-permute-done.13.refs_1_, ...), custom_call_target="tpu_custom_call", output_to_operand_aliasing={{}: (8, {})} | custom-call | flops 1 | bytes 1 | tf_op jit(solution)/shard_map/pallas_call | solution.py:693
  93.5 2.1 %shard_map.116.refs_5_ = bf16[1024,1024]{1,0:T(8,128)(2,1)} custom-call(s32[3]{0:T(128)S(1)} %pad_add_fusion.a_ref.j_ref._, bf16[512,2048]{1,0:T(8,128)(2,1)S(1)} %copy-done, bf16[256,1024]{1,0:T(8,128)(2,1)S(1)} %collective-permute-done.6.refs_0_, bf16[256,1024]{1,0:T(8,128)(2,1)S(1)} %collective-permute-done.13.refs_1_, ...), custom_call_target="tpu_custom_call", output_to_operand_aliasing={{}: (8, {})} | custom-call | flops 1 | bytes 1 | tf_op jit(solution)/shard_map/pallas_call | solution.py:693
  95.6 1.5 %shard_map.117.refs_5_ = bf16[1024,1024]{1,0:T(8,128)(2,1)} custom-call(s32[3]{0:T(128)S(1)} %pad_add_fusion.a_ref.j_ref._, bf16[512,2048]{1,0:T(8,128)(2,1)S(1)} %copy-done, bf16[256,1024]{1,0:T(8,128)(2,1)S(1)} %collective-permute-done.6.refs_0_, bf16[256,1024]{1,0:T(8,128)(2,1)S(1)} %collective-permute-done.13.refs_1_, ...), custom_call_target="tpu_custom_call", output_to_operand_aliasing={{}: (7, {})} | custom-call | flops 1 | bytes 1 | tf_op jit(solution)/shard_map/pallas_call | solution.py:693
  97.2 1.5 %shard_map.118 = bf16[1024,1024]{1,0:T(8,128)(2,1)} custom-call(s32[3]{0:T(128)S(1)} %pad_add_fusion.a_ref.j_ref._, bf16[512,2048]{1,0:T(8,128)(2,1)S(1)} %copy-done, bf16[256,1024]{1,0:T(8,128)(2,1)S(1)} %collective-permute-done.6.refs_0_, bf16[256,1024]{1,0:T(8,128)(2,1)S(1)} %collective-permute-done.13.refs_1_, ...), custom_call_target="tpu_custom_call", output_to_operand_aliasing={{}: (7, {})} | custom-call | flops 1 | bytes 1 | tf_op jit(solution)/shard_map/pallas_call | solution.py:693
  (62 shorter events, 22.2 us)
Async XLA Ops:
  1.2 17.8 %collective-permute-start = (bf16[272,1024]{1,0:T(8,128)(2,1)S(1)}, bf16[272,1024]{1,0:T(8,128)(2,1)S(1)}, u32[]{:S(2)}, u32[]{:S(2)}) collective-permute-start(bf16[272,1024]{1,0:T(8,128)(2,1)S(1)} %slice.15.refs_0_), channel_id=1, source_target_pairs={{0,1},{1,0},{2,3},{3,2},{4,5},{5,4},{6,7},{7,6},{8,9},{9,8},{10,11... | collective-permute-start | bytes 1671176 | tf_op jit(solution)/shard_map/ppermute | solution.py:493
  5.5 23.4 %collective-permute-start.2 = (bf16[256,1024]{1,0:T(8,128)(2,1)S(1)}, bf16[256,1024]{1,0:T(8,128)(2,1)S(1)}, u32[]{:S(2)}, u32[]{:S(2)}) collective-permute-start(bf16[256,1024]{1,0:T(8,128)(2,1)S(1)} %get-tuple-element.91.refs_0_), channel_id=1, source_target_pairs={{0,1},{1,0},{2,3},{3,2},{4,5},{5,4},{6,7},{7,6},{8,9},{9,8},{10,11... | collective-permute-start | bytes 1572872 | tf_op jit(solution)/shard_map/ppermute | solution.py:493
  5.6 34.6 %collective-permute-start.3 = (bf16[256,1024]{1,0:T(8,128)(2,1)S(1)}, bf16[256,1024]{1,0:T(8,128)(2,1)S(1)}, u32[]{:S(2)}, u32[]{:S(2)}) collective-permute-start(bf16[256,1024]{1,0:T(8,128)(2,1)S(1)} %get-tuple-element.105.refs_0_), channel_id=1, source_target_pairs={{0,1},{1,0},{2,3},{3,2},{4,5},{5,4},{6,7},{7,6},{8,9},{9,8},{10,11... | collective-permute-start | bytes 1572872 | tf_op jit(solution)/shard_map/ppermute | solution.py:493
  8.6 37.5 %collective-permute-start.4 = (bf16[128,1024]{1,0:T(8,128)(2,1)S(1)}, bf16[128,1024]{1,0:T(8,128)(2,1)S(1)}, u32[]{:S(2)}, u32[]{:S(2)}) collective-permute-start(bf16[128,1024]{1,0:T(8,128)(2,1)S(1)} %get-tuple-element.115.refs_0_), channel_id=1, source_target_pairs={{0,1},{1,0},{2,3},{3,2},{4,5},{5,4},{6,7},{7,6},{8,9},{9,8},{10,11... | collective-permute-start | bytes 786440 | tf_op jit(solution)/shard_map/ppermute | solution.py:493
  8.8 10.2 %copy-start.1 = (bf16[1408,128]{1,0:T(8,128)(2,1)S(1)}, bf16[1408,128]{1,0:T(8,128)(2,1)}, u32[]{:S(2)}) copy-start(bf16[1408,128]{1,0:T(8,128)(2,1)} %constant.30.clone.turn_ref) | copy-start | bytes 1081348
  8.8 41.8 %collective-permute-start.5 = (bf16[128,1024]{1,0:T(8,128)(2,1)S(1)}, bf16[128,1024]{1,0:T(8,128)(2,1)S(1)}, u32[]{:S(2)}, u32[]{:S(2)}) collective-permute-start(bf16[128,1024]{1,0:T(8,128)(2,1)S(1)} %get-tuple-element.123.refs_0_), channel_id=1, source_target_pairs={{0,1},{1,0},{2,3},{3,2},{4,5},{5,4},{6,7},{7,6},{8,9},{9,8},{10,11... | collective-permute-start | bytes 786440 | tf_op jit(solution)/shard_map/ppermute | solution.py:493
  10.7 3.1 %copy-start.3 = (bf16[2048,1792]{1,0:T(8,128)(2,1)S(1)}, bf16[2048,1792]{1,0:T(8,128)(2,1)}, u32[]{:S(2)}) copy-start(bf16[2048,1792]{1,0:T(8,128)(2,1)} %w_ref.9) | copy-start | bytes 22020100
  13.8 5.1 %copy-start.4 = (bf16[256,128]{1,0:T(8,128)(2,1)S(1)}, bf16[256,128]{1,0:T(8,128)(2,1)}, u32[]{:S(2)}) copy-start(bf16[256,128]{1,0:T(8,128)(2,1)} %constant.32.clone.mean_ref) | copy-start | bytes 196612
  13.8 5.1 %copy-start.5 = (f32[160,128]{1,0:T(8,128)S(1)}, f32[160,128]{1,0:T(8,128)}, u32[]{:S(2)}) copy-start(f32[160,128]{1,0:T(8,128)} %constant.31.clone.weight_ref) | copy-start | bytes 245764
  13.8 5.2 %copy-start.6 = (f32[3,512]{1,0:T(4,128)S(1)}, f32[3,512]{1,0:T(4,128)}, u32[]{:S(2)}) copy-start(f32[3,512]{1,0:T(4,128)} %conv_ref.9) | copy-start | bytes 18436
  18.9 5.4 %copy-start = (bf16[512,2048]{1,0:T(8,128)(2,1)S(1)}, bf16[512,2048]{1,0:T(8,128)(2,1)}, u32[]{:S(2)}) copy-start(bf16[512,2048]{1,0:T(8,128)(2,1)} %w_ref.15) | copy-start | bytes 6291460
  22.8 6.1 %collective-permute-start.1 = (bf16[144,512]{1,0:T(8,128)(2,1)S(1)}, bf16[144,512]{1,0:T(8,128)(2,1)S(1)}, u32[]{:S(2)}, u32[]{:S(2)}) collective-permute-start(bf16[144,512]{1,0:T(8,128)(2,1)S(1)} %get-tuple-element.90), channel_id=1, source_target_pairs={{0,2},{2,4},{4,6},{6,8},{8,10},{10,12},{12,14},{14,16},{16,18},{18... | collective-permute-start | bytes 442376 | tf_op jit(solution)/shard_map/ppermute | solution.py:592
  24.9 7.8 %copy-start.2 = (bf16[128,1280]{1,0:T(8,128)(2,1)S(1)}, bf16[128,1280]{1,0:T(8,128)(2,1)}, u32[]{:S(2)}) copy-start(bf16[128,1280]{1,0:T(8,128)(2,1)} %constant.29.clone.turn_ref) | copy-start | bytes 983044
  52.4 5.8 %collective-permute-start.7 = (bf16[160,128]{1,0:T(8,128)(2,1)S(1)}, bf16[160,128]{1,0:T(8,128)(2,1)S(1)}, u32[]{:S(2)}, u32[]{:S(2)}) collective-permute-start(bf16[160,128]{1,0:T(8,128)(2,1)S(1)} %get-tuple-element.141), channel_id=1, source_target_pairs={{0,2},{2,0},{4,6},{6,4},{8,10},{10,8},{12,14},{14,12},{16,18},{18,... | collective-permute-start | bytes 122888 | tf_op jit(solution)/shard_map/ppermute | solution.py:402
  52.5 5.7 %collective-permute-start.8 = (bf16[160,128]{1,0:T(8,128)(2,1)S(1)}, bf16[160,128]{1,0:T(8,128)(2,1)S(1)}, u32[]{:S(2)}, u32[]{:S(2)}) collective-permute-start(bf16[160,128]{1,0:T(8,128)(2,1)S(1)} %get-tuple-element.142), channel_id=1, source_target_pairs={{0,4},{2,6},{4,0},{6,2},{8,12},{10,14},{12,8},{14,10},{16,20},{18,... | collective-permute-start | bytes 122888 | tf_op jit(solution)/shard_map/ppermute | solution.py:402
  54.6 3.6 %collective-permute-start.9 = (bf16[160,128]{1,0:T(8,128)(2,1)S(1)}, bf16[160,128]{1,0:T(8,128)(2,1)S(1)}, u32[]{:S(2)}, u32[]{:S(2)}) collective-permute-start(bf16[160,128]{1,0:T(8,128)(2,1)S(1)} %get-tuple-element.143), channel_id=1, source_target_pairs={{0,6},{2,4},{4,2},{6,0},{8,14},{10,12},{12,10},{14,8},{16,22},{18,... | collective-permute-start | bytes 122888 | tf_op jit(solution)/shard_map/ppermute | solution.py:402
  54.7 18.5 %collective-permute-start.6 = (bf16[256,1024]{1,0:T(8,128)(2,1)S(1)}, bf16[256,1024]{1,0:T(8,128)(2,1)S(1)}, u32[]{:S(2)}, u32[]{:S(2)}) collective-permute-start(bf16[256,1024]{1,0:T(8,128)(2,1)S(1)} %shard_map.91), channel_id=1, source_target_pairs={{0,1},{1,0},{2,3},{3,2},{4,5},{5,4},{6,7},{7,6},{8,9},{9,8},{10,11... | collective-permute-start | bytes 1572872 | tf_op jit(solution)/shard_map/ppermute | solution.py:493
  58.2 11.8 %copy-start.7 = (f32[512]{0:T(512)S(1)}, f32[512]{0:T(512)}, u32[]{:S(2)}) copy-start(f32[512]{0:T(512)} %param.12) | copy-start | bytes 6148
  58.9 7.4 %collective-permute-start.12 = (bf16[160,128]{1,0:T(8,128)(2,1)S(1)}, bf16[160,128]{1,0:T(8,128)(2,1)S(1)}, u32[]{:S(2)}, u32[]{:S(2)}) collective-permute-start(bf16[160,128]{1,0:T(8,128)(2,1)S(1)} %get-tuple-element.148), channel_id=1, source_target_pairs={{0,24},{2,26},{4,28},{6,30},{8,16},{10,18},{12,20},{14,22},{16,8},... | collective-permute-start | bytes 122888 | tf_op jit(solution)/shard_map/ppermute | solution.py:402
  62.6 4.9 %collective-permute-start.11 = (bf16[160,128]{1,0:T(8,128)(2,1)S(1)}, bf16[160,128]{1,0:T(8,128)(2,1)S(1)}, u32[]{:S(2)}, u32[]{:S(2)}) collective-permute-start(bf16[160,128]{1,0:T(8,128)(2,1)S(1)} %get-tuple-element.148), channel_id=1, source_target_pairs={{0,16},{2,18},{4,20},{6,22},{8,24},{10,26},{12,28},{14,30},{16,0},... | collective-permute-start | bytes 122888 | tf_op jit(solution)/shard_map/ppermute | solution.py:402
  62.6 4.9 %collective-permute-start.10 = (bf16[160,128]{1,0:T(8,128)(2,1)S(1)}, bf16[160,128]{1,0:T(8,128)(2,1)S(1)}, u32[]{:S(2)}, u32[]{:S(2)}) collective-permute-start(bf16[160,128]{1,0:T(8,128)(2,1)S(1)} %get-tuple-element.148), channel_id=1, source_target_pairs={{0,8},{2,10},{4,12},{6,14},{8,0},{10,2},{12,4},{14,6},{16,24},{18,... | collective-permute-start | bytes 122888 | tf_op jit(solution)/shard_map/ppermute | solution.py:402
  68.1 5.1 %collective-permute-start.14 = (bf16[160,128]{1,0:T(8,128)(2,1)S(1)}, bf16[160,128]{1,0:T(8,128)(2,1)S(1)}, u32[]{:S(2)}, u32[]{:S(2)}) collective-permute-start(bf16[160,128]{1,0:T(8,128)(2,1)S(1)} %get-tuple-element.163), channel_id=1, source_target_pairs={{0,2},{2,0},{4,6},{6,4},{8,10},{10,8},{12,14},{14,12},{16,18},{18,... | collective-permute-start | bytes 122888 | tf_op jit(solution)/shard_map/ppermute | solution.py:402
  68.1 5.1 %collective-permute-start.15 = (bf16[160,128]{1,0:T(8,128)(2,1)S(1)}, bf16[160,128]{1,0:T(8,128)(2,1)S(1)}, u32[]{:S(2)}, u32[]{:S(2)}) collective-permute-start(bf16[160,128]{1,0:T(8,128)(2,1)S(1)} %get-tuple-element.164), channel_id=1, source_target_pairs={{0,4},{2,6},{4,0},{6,2},{8,12},{10,14},{12,8},{14,10},{16,20},{18,... | collective-permute-start | bytes 122888 | tf_op jit(solution)/shard_map/ppermute | solution.py:402
  69.7 3.5 %collective-permute-start.16 = (bf16[160,128]{1,0:T(8,128)(2,1)S(1)}, bf16[160,128]{1,0:T(8,128)(2,1)S(1)}, u32[]{:S(2)}, u32[]{:S(2)}) collective-permute-start(bf16[160,128]{1,0:T(8,128)(2,1)S(1)} %get-tuple-element.165), channel_id=1, source_target_pairs={{0,6},{2,4},{4,2},{6,0},{8,14},{10,12},{12,10},{14,8},{16,22},{18,... | collective-permute-start | bytes 122888 | tf_op jit(solution)/shard_map/ppermute | solution.py:402
  71.7 14.8 %collective-permute-start.17 = (bf16[1024,128]{1,0:T(8,128)(2,1)S(1)}, bf16[1024,128]{1,0:T(8,128)(2,1)S(1)}, u32[]{:S(2)}, u32[]{:S(2)}) collective-permute-start(bf16[1024,128]{1,0:T(8,128)(2,1)S(1)} %shard_map.107.refs_0_.refs_2_), channel_id=1, source_target_pairs={{0,1},{1,0},{2,3},{3,2},{4,5},{5,4},{6,7},{7,6},{8,9},{9,8},{10,11... | collective-permute-start | bytes 786440 | tf_op jit(solution)/shard_map/ppermute | solution.py:493
  73.1 15.0 %collective-permute-start.13 = (bf16[256,1024]{1,0:T(8,128)(2,1)S(1)}, bf16[256,1024]{1,0:T(8,128)(2,1)S(1)}, u32[]{:S(2)}, u32[]{:S(2)}) collective-permute-start(bf16[256,1024]{1,0:T(8,128)(2,1)S(1)} %collective-permute-done.6.refs_0_), channel_id=1, source_target_pairs={{0,2},{2,0},{4,6},{6,4},{8,10},{10,8},{12,14},{14,12},{16,18},{18,... | collective-permute-start | bytes 1572872 | tf_op jit(solution)/shard_map/ppermute | solution.py:402
  74.6 10.5 %collective-permute-start.22 = (bf16[256,384]{1,0:T(8,128)(2,1)S(1)}, bf16[256,384]{1,0:T(8,128)(2,1)S(1)}, u32[]{:S(2)}, u32[]{:S(2)}) collective-permute-start(bf16[256,384]{1,0:T(8,128)(2,1)S(1)} %shard_map.108.refs_3_), channel_id=1, source_target_pairs={{0,1},{1,0},{2,3},{3,2},{4,5},{5,4},{6,7},{7,6},{8,9},{9,8},{10,11... | collective-permute-start | bytes 589832 | tf_op jit(solution)/shard_map/ppermute | solution.py:493
  77.1 13.1 %collective-permute-start.21 = (bf16[256,384]{1,0:T(8,128)(2,1)S(1)}, bf16[256,384]{1,0:T(8,128)(2,1)S(1)}, u32[]{:S(2)}, u32[]{:S(2)}) collective-permute-start(bf16[256,384]{1,0:T(8,128)(2,1)S(1)} %shard_map.109.refs_3_), channel_id=1, source_target_pairs={{0,1},{1,0},{2,3},{3,2},{4,5},{5,4},{6,7},{7,6},{8,9},{9,8},{10,11... | collective-permute-start | bytes 589832 | tf_op jit(solution)/shard_map/ppermute | solution.py:493
  79.5 13.9 %collective-permute-start.20 = (bf16[256,384]{1,0:T(8,128)(2,1)S(1)}, bf16[256,384]{1,0:T(8,128)(2,1)S(1)}, u32[]{:S(2)}, u32[]{:S(2)}) collective-permute-start(bf16[256,384]{1,0:T(8,128)(2,1)S(1)} %shard_map.110.refs_3_), channel_id=1, source_target_pairs={{0,1},{1,0},{2,3},{3,2},{4,5},{5,4},{6,7},{7,6},{8,9},{9,8},{10,11... | collective-permute-start | bytes 589832 | tf_op jit(solution)/shard_map/ppermute | solution.py:493
  85.1 10.5 %collective-permute-start.19 = (bf16[128,384]{1,0:T(8,128)(2,1)S(1)}, bf16[128,384]{1,0:T(8,128)(2,1)S(1)}, u32[]{:S(2)}, u32[]{:S(2)}) collective-permute-start(bf16[128,384]{1,0:T(8,128)(2,1)S(1)} %shard_map.111.refs_1_), channel_id=1, source_target_pairs={{0,1},{1,0},{2,3},{3,2},{4,5},{5,4},{6,7},{7,6},{8,9},{9,8},{10,11... | collective-permute-start | bytes 294920 | tf_op jit(solution)/shard_map/ppermute | solution.py:493
  86.4 10.7 %collective-permute-start.18 = (bf16[128,384]{1,0:T(8,128)(2,1)S(1)}, bf16[128,384]{1,0:T(8,128)(2,1)S(1)}, u32[]{:S(2)}, u32[]{:S(2)}) collective-permute-start(bf16[128,384]{1,0:T(8,128)(2,1)S(1)} %shard_map.112.refs_3_), channel_id=1, source_target_pairs={{0,1},{1,0},{2,3},{3,2},{4,5},{5,4},{6,7},{7,6},{8,9},{9,8},{10,11... | collective-permute-start | bytes 294920 | tf_op jit(solution)/shard_map/ppermute | solution.py:493

commit v12 on v11

--- a/solution.py
+++ b/solution.py
@@ -626,7 +626,7 @@
             jax.ShapeDtypeStruct((rows, len(turns) * LANES), BF16),
             in_specs=[scalar] + [whole] * (len(operands) - 1),
             out_specs=whole,
-            flops=20 * 10**9 if tuple(some) == order[:1] else 4850 * 10**6 if len(some) > 1 else 1,
+            flops=4850 * 10**6 if len(some) > 1 else 1,
             vmem=24 << 20,
         )(*operands)
 
@@ -635,9 +635,9 @@
     if in_planes:
         held = sends[:1] + [exchange(sends[r], "ctx", r) for r in range(1, PLANE)]
         back = prior_in_planes(held, places, [done[last - 1][6], (attended[last - 1][1], edge)])
-        priors = [exchange(back[r], "ctx", r) for r in range(1, PLANE)]
+        mixed = finish((0,), back[:1], range(last + 1), done[last][1])
+        priors = [exchange(after(back[r], mixed), "ctx", r) for r in range(1, PLANE)]
         turns = tuple(range(1, PLANE))
-        mixed = finish((0,), back[:1], range(last + 1), done[last][1])
         early = [mixed] + [from_head(mixed, r) for r in range(1, n)]
     else:
         priors = prior_by_doubling(sum(done[b][2] for b in range(last + 1)), position)

time: 99.1 us -> 99.5 us (level)
    ppermute x10, waiting for transfers between devices: 1.24 us -> 4.25 us  [exchange(): return lax.ppermute(value, axis, [(i, i ^ flip) for i in range(count)])]
    ppermute x12, waiting for transfers between devices: 10.3 us -> 7.58 us  [from_head(): return lax.ppermute(value, 'head', [(i, (i + by) % n) for i in range(n)])]
  transfers between devices with their start and end apart: 23 -> 23, of which waited for: 5 -> 6; matrix products, arithmetic and copies ran while one was open for 2% -> 2% of each run, Pallas kernels for 52% -> 51%
where the time goes in v12:
time: 99.5 us; the launch traced here: 99.2 us
  Pallas kernels  54.3 us (55%)
  starting transfers between devices  25.9 us (26%)
  waiting for transfers between devices  11.8 us (12%)
  local copies, waits for them, and re-layouts  6.54 us (7%)
    pallas_call x5, Pallas kernels, do_block(): call(functools.partial(block_kernel, n=n, heads=heads, extra=extra, other...  15.9 us
    ppermute x12, starting transfers between devices, from_head(): return lax.ppermute(value, 'head', [(i, (i + by) % n) for i in range(n)])  15.7 us
    pallas_call x5, Pallas kernels, attend(): call(functools.partial(attend_kernel, heads=heads, first=b == 0), [jax.Sh...  9.97 us
    pallas_call x5, Pallas kernels, per_device(): call(functools.partial(output_kernel, n=n, offset=at, parts=out_parts, tu...  9.29 us
    ppermute x10, starting transfers between devices, exchange(): return lax.ppermute(value, axis, [(i, i ^ flip) for i in range(count)])  8.62 us
    pallas_call x6, Pallas kernels, finish(): call(functools.partial(finish_kernel, heads=heads, turns=turns, before=be...  8.28 us
    ppermute x12, waiting for transfers between devices, from_head(): return lax.ppermute(value, 'head', [(i, (i + by) % n) for i in range(n)])  7.58 us
    pallas_call x1, Pallas kernels, per_device(): call(functools.partial(arrange_kernel, heads=heads), jax.ShapeDtypeStruct...  5.09 us
  transfers between devices with their start and end apart: 23, of which 6 were waited for; matrix products, arithmetic and copies ran while one was open for 2% of the time, Pallas kernels for 51%

profile of v12, /device:TPU:0, one launch (start us, length us, event | category | flops | bytes accessed | tf_op | source)
XLA Modules:
  0.0 99.2 jit_solution(7091834099712265660)
XLA Ops:
  1.2 3.0 %collective-permute-start = (bf16[272,1024]{1,0:T(8,128)(2,1)S(1)}, bf16[272,1024]{1,0:T(8,128)(2,1)S(1)}, u32[]{:S(2)}, u32[]{:S(2)}) collective-permute-start(bf16[272,1024]{1,0:T(8,128)(2,1)S(1)} %slice.15.refs_0_), channel_id=1, source_target_pairs={{0,1},{1,0},{2,3},{3,2},{4,5},{5,4},{6,7},{7,6},{8,9},{9,8},{10,11... | collective-permute-start | bytes 1671176 | tf_op jit(solution)/shard_map/ppermute | solution.py:493
  5.6 2.0 %collective-permute-start.3 = (bf16[256,1024]{1,0:T(8,128)(2,1)S(1)}, bf16[256,1024]{1,0:T(8,128)(2,1)S(1)}, u32[]{:S(2)}, u32[]{:S(2)}) collective-permute-start(bf16[256,1024]{1,0:T(8,128)(2,1)S(1)} %get-tuple-element.108.refs_0_), channel_id=1, source_target_pairs={{0,1},{1,0},{2,3},{3,2},{4,5},{5,4},{6,7},{7,6},{8,9},{9,8},{10,11... | collective-permute-start | bytes 1572872 | tf_op jit(solution)/shard_map/ppermute | solution.py:493
  8.8 1.9 %collective-permute-start.5 = (bf16[128,1024]{1,0:T(8,128)(2,1)S(1)}, bf16[128,1024]{1,0:T(8,128)(2,1)S(1)}, u32[]{:S(2)}, u32[]{:S(2)}) collective-permute-start(bf16[128,1024]{1,0:T(8,128)(2,1)S(1)} %get-tuple-element.126.refs_0_), channel_id=1, source_target_pairs={{0,1},{1,0},{2,3},{3,2},{4,5},{5,4},{6,7},{7,6},{8,9},{9,8},{10,11... | collective-permute-start | bytes 786440 | tf_op jit(solution)/shard_map/ppermute | solution.py:493
  10.7 3.1 %copy-done.4 = bf16[2048,1792]{1,0:T(8,128)(2,1)S(1)} copy-done((bf16[2048,1792]{1,0:T(8,128)(2,1)S(1)}, bf16[2048,1792]{1,0:T(8,128)(2,1)}, u32[]{:S(2)}) %copy-start.4) | copy-done | bytes 7340056
  13.8 5.1 %shard_map.92.w_ref = bf16[2048,1792]{1,0:T(8,128)(2,1)S(1)} custom-call(bf16[2048,1792]{1,0:T(8,128)(2,1)S(1)} %copy-done.4), custom_call_target="tpu_custom_call" | custom-call | flops 1 | bytes 1 | tf_op jit(solution)/shard_map/pallas_call | solution.py:530
  19.0 3.9 %shard_map.93 = (bf16[256,128]{1,0:T(8,128)(2,1)S(1)}, bf16[256,512]{1,0:T(8,128)(2,1)S(1)}, f32[4,160,128]{2,1,0:T(8,128)S(1)}, bf16[256,128]{1,0:T(8,128)(2,1)...) custom-call(s32[3]{0:T(128)S(1)} %pad_add_fusion.a_ref.j_ref._, ...), custom_call_target="tpu_custom_call" | custom-call | flops 1 | bytes 1 | tf_op jit(solution)/shard_map/pallas_call | solution.py:556
  22.8 1.5 %collective-permute-start.1 = (bf16[144,512]{1,0:T(8,128)(2,1)S(1)}, bf16[144,512]{1,0:T(8,128)(2,1)S(1)}, u32[]{:S(2)}, u32[]{:S(2)}) collective-permute-start(bf16[144,512]{1,0:T(8,128)(2,1)S(1)} %get-tuple-element.93), channel_id=1, source_target_pairs={{0,2},{2,4},{4,6},{6,8},{8,10},{10,12},{12,14},{14,16},{16,18},{18... | collective-permute-start | bytes 442376 | tf_op jit(solution)/shard_map/ppermute | solution.py:592
  24.9 4.0 %collective-permute-done.2.refs_1_ = bf16[256,1024]{1,0:T(8,128)(2,1)S(1)} collective-permute-done((bf16[256,1024]{1,0:T(8,128)(2,1)S(1)}, bf16[256,1024]{1,0:T(8,128)(2,1)S(1)}, u32[]{:S(2)}, u32[]{:S(2)}) %collective-permute-start.2) | collective-permute-done | bytes 524320 | tf_op jit(solution)/shard_map/ppermute | solution.py:493
  28.9 3.8 %shard_map.94 = (bf16[256,128]{1,0:T(8,128)(2,1)S(1)}, bf16[256,512]{1,0:T(8,128)(2,1)S(1)}, f32[4,160,128]{2,1,0:T(8,128)S(1)}, bf16[256,128]{1,0:T(8,128)(2,1)...) custom-call(s32[3]{0:T(128)S(1)} %pad_add_fusion.a_ref.j_ref._, ...), custom_call_target="tpu_custom_call" | custom-call | flops 1 | bytes 1 | tf_op jit(solution)/shard_map/pallas_call | solution.py:556
  32.7 2.1 %shard_map.95 = (bf16[256,1280]{1,0:T(8,128)(2,1)S(1)}, f32[256,512]{1,0:T(8,128)S(1)}, f32[256,512]{1,0:T(8,128)S(1)}) custom-call(s32[3]{0:T(128)S(1)} %pad_add_fusion.a_ref.j_ref._, bf16[128,1280]{1,0:T(8,128)(2,1)S(1)} %copy-done.2, bf16[144,512]{1,0:T(8,128)(2,1)S(1)} %collective-permute-done.1.refs_2_.prev_ref, ...), custom_call_target="tpu_custom_call" | custom-call | flops 1 | bytes 1 | tf_op jit(solution)/shard_map/pallas_call | solution.py:580
  34.9 2.1 %shard_map.96 = (bf16[256,1280]{1,0:T(8,128)(2,1)S(1)}, f32[256,512]{1,0:T(8,128)S(1)}, f32[256,512]{1,0:T(8,128)S(1)}) custom-call(s32[3]{0:T(128)S(1)} %pad_add_fusion.a_ref.j_ref._, bf16[128,1280]{1,0:T(8,128)(2,1)S(1)} %copy-done.2, bf16[144,512]{1,0:T(8,128)(2,1)S(1)} %collective-permute-done.1.refs_2_.prev_ref, ...), custom_call_target="tpu_custom_call" | custom-call | flops 1 | bytes 1 | tf_op jit(solution)/shard_map/pallas_call | solution.py:580
  37.0 3.1 %collective-permute-done.3.refs_1_ = bf16[256,1024]{1,0:T(8,128)(2,1)S(1)} collective-permute-done((bf16[256,1024]{1,0:T(8,128)(2,1)S(1)}, bf16[256,1024]{1,0:T(8,128)(2,1)S(1)}, u32[]{:S(2)}, u32[]{:S(2)}) %collective-permute-start.3) | collective-permute-done | bytes 524320 | tf_op jit(solution)/shard_map/ppermute | solution.py:493
  40.1 3.8 %shard_map.97 = (bf16[256,128]{1,0:T(8,128)(2,1)S(1)}, bf16[256,512]{1,0:T(8,128)(2,1)S(1)}, f32[4,160,128]{2,1,0:T(8,128)S(1)}, bf16[256,128]{1,0:T(8,128)(2,1)...) custom-call(s32[3]{0:T(128)S(1)} %pad_add_fusion.a_ref.j_ref._, ...), custom_call_target="tpu_custom_call" | custom-call | flops 1 | bytes 1 | tf_op jit(solution)/shard_map/pallas_call | solution.py:556
  43.9 2.1 %shard_map.98 = (bf16[256,1280]{1,0:T(8,128)(2,1)S(1)}, f32[256,512]{1,0:T(8,128)S(1)}, f32[256,512]{1,0:T(8,128)S(1)}) custom-call(s32[3]{0:T(128)S(1)} %pad_add_fusion.a_ref.j_ref._, bf16[128,1280]{1,0:T(8,128)(2,1)S(1)} %copy-done.2, bf16[144,512]{1,0:T(8,128)(2,1)S(1)} %get-tuple-element.109.refs_2_.prev_ref, ...), custom_call_target="tpu_custom_call" | custom-call | flops 1 | bytes 1 | tf_op jit(solution)/shard_map/pallas_call | solution.py:580
  46.1 2.6 %shard_map.99 = (bf16[128,128]{1,0:T(8,128)(2,1)S(1)}, bf16[128,512]{1,0:T(8,128)(2,1)S(1)}, f32[4,160,128]{2,1,0:T(8,128)S(1)}, bf16[128,128]{1,0:T(8,128)(2,1)...) custom-call(s32[3]{0:T(128)S(1)} %pad_add_fusion.a_ref.j_ref._, ...), custom_call_target="tpu_custom_call" | custom-call | flops 1 | bytes 1 | tf_op jit(solution)/shard_map/pallas_call | solution.py:556
  48.7 1.9 %shard_map.100 = (bf16[128,1280]{1,0:T(8,128)(2,1)S(1)}, f32[128,512]{1,0:T(8,128)S(1)}, f32[128,512]{1,0:T(8,128)S(1)}) custom-call(s32[3]{0:T(128)S(1)} %pad_add_fusion.a_ref.j_ref._, bf16[128,1280]{1,0:T(8,128)(2,1)S(1)} %copy-done.2, bf16[144,512]{1,0:T(8,128)(2,1)S(1)} %get-tuple-element.110.refs_2_.prev_ref, ...), custom_call_target="tpu_custom_call" | custom-call | flops 1 | bytes 1 | tf_op jit(solution)/shard_map/pallas_call | solution.py:580
  50.6 1.8 %shard_map.101 = (bf16[128,128]{1,0:T(8,128)(2,1)S(1)}, bf16[128,512]{1,0:T(8,128)(2,1)S(1)}, f32[4,160,128]{2,1,0:T(8,128)S(1)}, bf16[160,128]{1,0:T(8,128)(2,1...) custom-call(s32[3]{0:T(128)S(1)} %pad_add_fusion.a_ref.j_ref._, ...), custom_call_target="tpu_custom_call" | custom-call | flops 1 | bytes 1 | tf_op jit(solution)/shard_map/pallas_call | solution.py:556
  52.5 2.1 %collective-permute-start.8 = (bf16[160,128]{1,0:T(8,128)(2,1)S(1)}, bf16[160,128]{1,0:T(8,128)(2,1)S(1)}, u32[]{:S(2)}, u32[]{:S(2)}) collective-permute-start(bf16[160,128]{1,0:T(8,128)(2,1)S(1)} %get-tuple-element.145), channel_id=1, source_target_pairs={{0,4},{2,6},{4,0},{6,2},{8,12},{10,14},{12,8},{14,10},{16,20},{18,... | collective-permute-start | bytes 122888 | tf_op jit(solution)/shard_map/ppermute | solution.py:402
  54.7 1.8 %collective-permute-start.6 = (bf16[256,1024]{1,0:T(8,128)(2,1)S(1)}, bf16[256,1024]{1,0:T(8,128)(2,1)S(1)}, u32[]{:S(2)}, u32[]{:S(2)}) collective-permute-start(bf16[256,1024]{1,0:T(8,128)(2,1)S(1)} %shard_map.91), channel_id=1, source_target_pairs={{0,1},{1,0},{2,3},{3,2},{4,5},{5,4},{6,7},{7,6},{8,9},{9,8},{10,11... | collective-permute-start | bytes 1572872 | tf_op jit(solution)/shard_map/ppermute | solution.py:493
  56.4 1.8 %shard_map.102 = (bf16[128,128]{1,0:T(8,128)(2,1)S(1)}, bf16[128,512]{1,0:T(8,128)(2,1)S(1)}, bf16[128,512]{1,0:T(8,128)(2,1)S(1)}, bf16[144,512]{1,0:T(8,128)(2,1)S(1)}) custom-call(s32[3]{0:T(128)S(1)} %pad_add_fusion.a_ref.j_ref._, bf16[256,128]{1,0:T(8,128)(2,1)S(1)} %copy-done.3, bf16[2048,1792]{1,0:T(8,128)(2,1)S(1)} %shard_map.92.w_ref, ...), custom_call_target="tpu_custom_call" | custom-call | flops 1 | bytes 1 | tf_op jit(solution)/shard_map/pallas_call | solution.py:569
  58.9 3.7 %collective-permute-start.12 = (bf16[160,128]{1,0:T(8,128)(2,1)S(1)}, bf16[160,128]{1,0:T(8,128)(2,1)S(1)}, u32[]{:S(2)}, u32[]{:S(2)}) collective-permute-start(bf16[160,128]{1,0:T(8,128)(2,1)S(1)} %get-tuple-element.151), channel_id=1, source_target_pairs={{0,24},{2,26},{4,28},{6,30},{8,16},{10,18},{12,20},{14,22},{16,8},... | collective-permute-start | bytes 122888 | tf_op jit(solution)/shard_map/ppermute | solution.py:402
  64.6 1.7 %shard_map.103 = (bf16[128,1280]{1,0:T(8,128)(2,1)S(1)}, f32[128,512]{1,0:T(8,128)S(1)}, f32[128,512]{1,0:T(8,128)S(1)}) custom-call(s32[3]{0:T(128)S(1)} %pad_add_fusion.a_ref.j_ref._, bf16[128,1280]{1,0:T(8,128)(2,1)S(1)} %copy-done.2, bf16[144,512]{1,0:T(8,128)(2,1)S(1)} %get-tuple-element.127.refs_2_.prev_ref, ...), custom_call_target="tpu_custom_call" | custom-call | flops 1 | bytes 1 | tf_op jit(solution)/shard_map/pallas_call | solution.py:580
  68.1 1.7 %shard_map.107.refs_0_.refs_2_ = bf16[1024,128]{1,0:T(8,128)(2,1)S(1)} custom-call(s32[3]{0:T(128)S(1)} %pad_add_fusion.a_ref.j_ref._, bf16[256,128]{1,0:T(8,128)(2,1)S(1)} %copy-done.3, f32[1,512]{1,0:T(1,128)S(1)} %bitcast.4, bf16[160,128]{1,0:T(8,128)(2,1)S(1)} %get-tuple-element.152.refs_0_, ...), custom_call_target="tpu_custom_call" | custom-call | flops 4849999872 | bytes 1 | tf_op jit(solution)/shard_map/pallas_call | solution.py:624
  69.8 1.5 %collective-permute-start.17 = (bf16[1024,128]{1,0:T(8,128)(2,1)S(1)}, bf16[1024,128]{1,0:T(8,128)(2,1)S(1)}, u32[]{:S(2)}, u32[]{:S(2)}) collective-permute-start(bf16[1024,128]{1,0:T(8,128)(2,1)S(1)} %shard_map.107.refs_0_.refs_2_), channel_id=1, source_target_pairs={{0,1},{1,0},{2,3},{3,2},{4,5},{5,4},{6,7},{7,6},{8,9},{9,8},{10,11... | collective-permute-start | bytes 786440 | tf_op jit(solution)/shard_map/ppermute | solution.py:493
  73.2 2.4 %collective-permute-done.15.refs_1_ = bf16[160,128]{1,0:T(8,128)(2,1)S(1)} collective-permute-done((bf16[160,128]{1,0:T(8,128)(2,1)S(1)}, bf16[160,128]{1,0:T(8,128)(2,1)S(1)}, u32[]{:S(2)}, u32[]{:S(2)}) %collective-permute-start.15) | collective-permute-done | bytes 40992 | tf_op jit(solution)/shard_map/ppermute | solution.py:402
  78.6 1.4 %shard_map.109.refs_3_ = bf16[256,384]{1,0:T(8,128)(2,1)S(1)} custom-call(s32[3]{0:T(128)S(1)} %pad_add_fusion.a_ref.j_ref._, bf16[256,128]{1,0:T(8,128)(2,1)S(1)} %copy-done.3, f32[1,512]{1,0:T(1,128)S(1)} %bitcast.6, bf16[160,128]{1,0:T(8,128)(2,1)S(1)} %collective-permute-done.14.refs_0_, bf16[160,128]{1,0:T(8,128)(2,1)S(1)} %collective-permute-done.15.refs_1_, ...), custom_call_target="tpu_custom_call" | custom-call | flops 1 | bytes 1 | tf_op jit(solution)/shard_map/pallas_call | solution.py:624
  81.1 1.4 %shard_map.110.refs_3_ = bf16[256,384]{1,0:T(8,128)(2,1)S(1)} custom-call(s32[3]{0:T(128)S(1)} %pad_add_fusion.a_ref.j_ref._, bf16[256,128]{1,0:T(8,128)(2,1)S(1)} %copy-done.3, f32[1,512]{1,0:T(1,128)S(1)} %bitcast.7, bf16[160,128]{1,0:T(8,128)(2,1)S(1)} %collective-permute-done.14.refs_0_, bf16[160,128]{1,0:T(8,128)(2,1)S(1)} %collective-permute-done.15.refs_1_, ...), custom_call_target="tpu_custom_call" | custom-call | flops 1 | bytes 1 | tf_op jit(solution)/shard_map/pallas_call | solution.py:624
  89.2 2.1 %shard_map.114.refs_6_ = bf16[1024,1024]{1,0:T(8,128)(2,1)} custom-call(s32[3]{0:T(128)S(1)} %pad_add_fusion.a_ref.j_ref._, bf16[512,2048]{1,0:T(8,128)(2,1)S(1)} %copy-done, bf16[256,1024]{1,0:T(8,128)(2,1)S(1)} %collective-permute-done.6.refs_0_, bf16[256,1024]{1,0:T(8,128)(2,1)S(1)} %collective-permute-done.13.refs_1_, ...), custom_call_target="tpu_custom_call" | custom-call | flops 1 | bytes 1 | tf_op jit(solution)/shard_map/pallas_call | solution.py:693
  91.3 2.1 %shard_map.115.refs_6_ = bf16[1024,1024]{1,0:T(8,128)(2,1)} custom-call(s32[3]{0:T(128)S(1)} %pad_add_fusion.a_ref.j_ref._, bf16[512,2048]{1,0:T(8,128)(2,1)S(1)} %copy-done, bf16[256,1024]{1,0:T(8,128)(2,1)S(1)} %collective-permute-done.6.refs_0_, bf16[256,1024]{1,0:T(8,128)(2,1)S(1)} %collective-permute-done.13.refs_1_, ...), custom_call_target="tpu_custom_call", output_to_operand_aliasing={{}: (8, {})} | custom-call | flops 1 | bytes 1 | tf_op jit(solution)/shard_map/pallas_call | solution.py:693
  93.8 2.1 %shard_map.116.refs_5_ = bf16[1024,1024]{1,0:T(8,128)(2,1)} custom-call(s32[3]{0:T(128)S(1)} %pad_add_fusion.a_ref.j_ref._, bf16[512,2048]{1,0:T(8,128)(2,1)S(1)} %copy-done, bf16[256,1024]{1,0:T(8,128)(2,1)S(1)} %collective-permute-done.6.refs_0_, bf16[256,1024]{1,0:T(8,128)(2,1)S(1)} %collective-permute-done.13.refs_1_, ...), custom_call_target="tpu_custom_call", output_to_operand_aliasing={{}: (8, {})} | custom-call | flops 1 | bytes 1 | tf_op jit(solution)/shard_map/pallas_call | solution.py:693
  95.9 1.5 %shard_map.117.refs_5_ = bf16[1024,1024]{1,0:T(8,128)(2,1)} custom-call(s32[3]{0:T(128)S(1)} %pad_add_fusion.a_ref.j_ref._, bf16[512,2048]{1,0:T(8,128)(2,1)S(1)} %copy-done, bf16[256,1024]{1,0:T(8,128)(2,1)S(1)} %collective-permute-done.6.refs_0_, bf16[256,1024]{1,0:T(8,128)(2,1)S(1)} %collective-permute-done.13.refs_1_, ...), custom_call_target="tpu_custom_call", output_to_operand_aliasing={{}: (7, {})} | custom-call | flops 1 | bytes 1 | tf_op jit(solution)/shard_map/pallas_call | solution.py:693
  97.5 1.5 %shard_map.118 = bf16[1024,1024]{1,0:T(8,128)(2,1)} custom-call(s32[3]{0:T(128)S(1)} %pad_add_fusion.a_ref.j_ref._, bf16[512,2048]{1,0:T(8,128)(2,1)S(1)} %copy-done, bf16[256,1024]{1,0:T(8,128)(2,1)S(1)} %collective-permute-done.6.refs_0_, bf16[256,1024]{1,0:T(8,128)(2,1)S(1)} %collective-permute-done.13.refs_1_, ...), custom_call_target="tpu_custom_call", output_to_operand_aliasing={{}: (7, {})} | custom-call | flops 1 | bytes 1 | tf_op jit(solution)/shard_map/pallas_call | solution.py:693
  (62 shorter events, 22.2 us)
Async XLA Ops:
  1.2 17.8 %collective-permute-start = (bf16[272,1024]{1,0:T(8,128)(2,1)S(1)}, bf16[272,1024]{1,0:T(8,128)(2,1)S(1)}, u32[]{:S(2)}, u32[]{:S(2)}) collective-permute-start(bf16[272,1024]{1,0:T(8,128)(2,1)S(1)} %slice.15.refs_0_), channel_id=1, source_target_pairs={{0,1},{1,0},{2,3},{3,2},{4,5},{5,4},{6,7},{7,6},{8,9},{9,8},{10,11... | collective-permute-start | bytes 1671176 | tf_op jit(solution)/shard_map/ppermute | solution.py:493
  5.5 23.4 %collective-permute-start.2 = (bf16[256,1024]{1,0:T(8,128)(2,1)S(1)}, bf16[256,1024]{1,0:T(8,128)(2,1)S(1)}, u32[]{:S(2)}, u32[]{:S(2)}) collective-permute-start(bf16[256,1024]{1,0:T(8,128)(2,1)S(1)} %get-tuple-element.94.refs_0_), channel_id=1, source_target_pairs={{0,1},{1,0},{2,3},{3,2},{4,5},{5,4},{6,7},{7,6},{8,9},{9,8},{10,11... | collective-permute-start | bytes 1572872 | tf_op jit(solution)/shard_map/ppermute | solution.py:493
  5.6 34.6 %collective-permute-start.3 = (bf16[256,1024]{1,0:T(8,128)(2,1)S(1)}, bf16[256,1024]{1,0:T(8,128)(2,1)S(1)}, u32[]{:S(2)}, u32[]{:S(2)}) collective-permute-start(bf16[256,1024]{1,0:T(8,128)(2,1)S(1)} %get-tuple-element.108.refs_0_), channel_id=1, source_target_pairs={{0,1},{1,0},{2,3},{3,2},{4,5},{5,4},{6,7},{7,6},{8,9},{9,8},{10,11... | collective-permute-start | bytes 1572872 | tf_op jit(solution)/shard_map/ppermute | solution.py:493
  8.6 37.5 %collective-permute-start.4 = (bf16[128,1024]{1,0:T(8,128)(2,1)S(1)}, bf16[128,1024]{1,0:T(8,128)(2,1)S(1)}, u32[]{:S(2)}, u32[]{:S(2)}) collective-permute-start(bf16[128,1024]{1,0:T(8,128)(2,1)S(1)} %get-tuple-element.118.refs_0_), channel_id=1, source_target_pairs={{0,1},{1,0},{2,3},{3,2},{4,5},{5,4},{6,7},{7,6},{8,9},{9,8},{10,11... | collective-permute-start | bytes 786440 | tf_op jit(solution)/shard_map/ppermute | solution.py:493
  8.8 10.2 %copy-start.1 = (bf16[1408,128]{1,0:T(8,128)(2,1)S(1)}, bf16[1408,128]{1,0:T(8,128)(2,1)}, u32[]{:S(2)}) copy-start(bf16[1408,128]{1,0:T(8,128)(2,1)} %constant.30.clone.turn_ref) | copy-start | bytes 1081348
  8.8 10.2 %copy-start.3 = (bf16[256,128]{1,0:T(8,128)(2,1)S(1)}, bf16[256,128]{1,0:T(8,128)(2,1)}, u32[]{:S(2)}) copy-start(bf16[256,128]{1,0:T(8,128)(2,1)} %constant.32.clone.mean_ref) | copy-start | bytes 196612
  8.8 41.8 %collective-permute-start.5 = (bf16[128,1024]{1,0:T(8,128)(2,1)S(1)}, bf16[128,1024]{1,0:T(8,128)(2,1)S(1)}, u32[]{:S(2)}, u32[]{:S(2)}) collective-permute-start(bf16[128,1024]{1,0:T(8,128)(2,1)S(1)} %get-tuple-element.126.refs_0_), channel_id=1, source_target_pairs={{0,1},{1,0},{2,3},{3,2},{4,5},{5,4},{6,7},{7,6},{8,9},{9,8},{10,11... | collective-permute-start | bytes 786440 | tf_op jit(solution)/shard_map/ppermute | solution.py:493
  10.7 3.1 %copy-start.4 = (bf16[2048,1792]{1,0:T(8,128)(2,1)S(1)}, bf16[2048,1792]{1,0:T(8,128)(2,1)}, u32[]{:S(2)}) copy-start(bf16[2048,1792]{1,0:T(8,128)(2,1)} %w_ref.9) | copy-start | bytes 22020100
  13.8 5.1 %copy-start.5 = (f32[160,128]{1,0:T(8,128)S(1)}, f32[160,128]{1,0:T(8,128)}, u32[]{:S(2)}) copy-start(f32[160,128]{1,0:T(8,128)} %constant.31.clone.weight_ref) | copy-start | bytes 245764
  13.8 5.2 %copy-start.6 = (f32[3,512]{1,0:T(4,128)S(1)}, f32[3,512]{1,0:T(4,128)}, u32[]{:S(2)}) copy-start(f32[3,512]{1,0:T(4,128)} %conv_ref.9) | copy-start | bytes 18436
  18.9 5.4 %copy-start = (bf16[512,2048]{1,0:T(8,128)(2,1)S(1)}, bf16[512,2048]{1,0:T(8,128)(2,1)}, u32[]{:S(2)}) copy-start(bf16[512,2048]{1,0:T(8,128)(2,1)} %w_ref.15) | copy-start | bytes 6291460
  22.8 6.1 %collective-permute-start.1 = (bf16[144,512]{1,0:T(8,128)(2,1)S(1)}, bf16[144,512]{1,0:T(8,128)(2,1)S(1)}, u32[]{:S(2)}, u32[]{:S(2)}) collective-permute-start(bf16[144,512]{1,0:T(8,128)(2,1)S(1)} %get-tuple-element.93), channel_id=1, source_target_pairs={{0,2},{2,4},{4,6},{6,8},{8,10},{10,12},{12,14},{14,16},{16,18},{18... | collective-permute-start | bytes 442376 | tf_op jit(solution)/shard_map/ppermute | solution.py:592
  24.9 7.8 %copy-start.2 = (bf16[128,1280]{1,0:T(8,128)(2,1)S(1)}, bf16[128,1280]{1,0:T(8,128)(2,1)}, u32[]{:S(2)}) copy-start(bf16[128,1280]{1,0:T(8,128)(2,1)} %constant.29.clone.turn_ref) | copy-start | bytes 983044
  52.4 5.8 %collective-permute-start.7 = (bf16[160,128]{1,0:T(8,128)(2,1)S(1)}, bf16[160,128]{1,0:T(8,128)(2,1)S(1)}, u32[]{:S(2)}, u32[]{:S(2)}) collective-permute-start(bf16[160,128]{1,0:T(8,128)(2,1)S(1)} %get-tuple-element.144), channel_id=1, source_target_pairs={{0,2},{2,0},{4,6},{6,4},{8,10},{10,8},{12,14},{14,12},{16,18},{18,... | collective-permute-start | bytes 122888 | tf_op jit(solution)/shard_map/ppermute | solution.py:402
  52.5 5.7 %collective-permute-start.8 = (bf16[160,128]{1,0:T(8,128)(2,1)S(1)}, bf16[160,128]{1,0:T(8,128)(2,1)S(1)}, u32[]{:S(2)}, u32[]{:S(2)}) collective-permute-start(bf16[160,128]{1,0:T(8,128)(2,1)S(1)} %get-tuple-element.145), channel_id=1, source_target_pairs={{0,4},{2,6},{4,0},{6,2},{8,12},{10,14},{12,8},{14,10},{16,20},{18,... | collective-permute-start | bytes 122888 | tf_op jit(solution)/shard_map/ppermute | solution.py:402
  54.6 3.6 %collective-permute-start.9 = (bf16[160,128]{1,0:T(8,128)(2,1)S(1)}, bf16[160,128]{1,0:T(8,128)(2,1)S(1)}, u32[]{:S(2)}, u32[]{:S(2)}) collective-permute-start(bf16[160,128]{1,0:T(8,128)(2,1)S(1)} %get-tuple-element.146), channel_id=1, source_target_pairs={{0,6},{2,4},{4,2},{6,0},{8,14},{10,12},{12,10},{14,8},{16,22},{18,... | collective-permute-start | bytes 122888 | tf_op jit(solution)/shard_map/ppermute | solution.py:402
  54.7 15.1 %collective-permute-start.6 = (bf16[256,1024]{1,0:T(8,128)(2,1)S(1)}, bf16[256,1024]{1,0:T(8,128)(2,1)S(1)}, u32[]{:S(2)}, u32[]{:S(2)}) collective-permute-start(bf16[256,1024]{1,0:T(8,128)(2,1)S(1)} %shard_map.91), channel_id=1, source_target_pairs={{0,1},{1,0},{2,3},{3,2},{4,5},{5,4},{6,7},{7,6},{8,9},{9,8},{10,11... | collective-permute-start | bytes 1572872 | tf_op jit(solution)/shard_map/ppermute | solution.py:493
  58.2 9.9 %copy-start.7 = (f32[512]{0:T(512)S(1)}, f32[512]{0:T(512)}, u32[]{:S(2)}) copy-start(f32[512]{0:T(512)} %param.12) | copy-start | bytes 6148
  58.9 7.4 %collective-permute-start.12 = (bf16[160,128]{1,0:T(8,128)(2,1)S(1)}, bf16[160,128]{1,0:T(8,128)(2,1)S(1)}, u32[]{:S(2)}, u32[]{:S(2)}) collective-permute-start(bf16[160,128]{1,0:T(8,128)(2,1)S(1)} %get-tuple-element.151), channel_id=1, source_target_pairs={{0,24},{2,26},{4,28},{6,30},{8,16},{10,18},{12,20},{14,22},{16,8},... | collective-permute-start | bytes 122888 | tf_op jit(solution)/shard_map/ppermute | solution.py:402
  62.5 4.9 %collective-permute-start.11 = (bf16[160,128]{1,0:T(8,128)(2,1)S(1)}, bf16[160,128]{1,0:T(8,128)(2,1)S(1)}, u32[]{:S(2)}, u32[]{:S(2)}) collective-permute-start(bf16[160,128]{1,0:T(8,128)(2,1)S(1)} %get-tuple-element.151), channel_id=1, source_target_pairs={{0,16},{2,18},{4,20},{6,22},{8,24},{10,26},{12,28},{14,30},{16,0},... | collective-permute-start | bytes 122888 | tf_op jit(solution)/shard_map/ppermute | solution.py:402
  62.5 4.9 %collective-permute-start.10 = (bf16[160,128]{1,0:T(8,128)(2,1)S(1)}, bf16[160,128]{1,0:T(8,128)(2,1)S(1)}, u32[]{:S(2)}, u32[]{:S(2)}) collective-permute-start(bf16[160,128]{1,0:T(8,128)(2,1)S(1)} %get-tuple-element.151), channel_id=1, source_target_pairs={{0,8},{2,10},{4,12},{6,14},{8,0},{10,2},{12,4},{14,6},{16,24},{18,... | collective-permute-start | bytes 122888 | tf_op jit(solution)/shard_map/ppermute | solution.py:402
  69.7 19.4 %collective-permute-start.13 = (bf16[256,1024]{1,0:T(8,128)(2,1)S(1)}, bf16[256,1024]{1,0:T(8,128)(2,1)S(1)}, u32[]{:S(2)}, u32[]{:S(2)}) collective-permute-start(bf16[256,1024]{1,0:T(8,128)(2,1)S(1)} %collective-permute-done.6.refs_0_), channel_id=1, source_target_pairs={{0,2},{2,0},{4,6},{6,4},{8,10},{10,8},{12,14},{14,12},{16,18},{18,... | collective-permute-start | bytes 1572872 | tf_op jit(solution)/shard_map/ppermute | solution.py:402
  69.8 17.4 %collective-permute-start.17 = (bf16[1024,128]{1,0:T(8,128)(2,1)S(1)}, bf16[1024,128]{1,0:T(8,128)(2,1)S(1)}, u32[]{:S(2)}, u32[]{:S(2)}) collective-permute-start(bf16[1024,128]{1,0:T(8,128)(2,1)S(1)} %shard_map.107.refs_0_.refs_2_), channel_id=1, source_target_pairs={{0,1},{1,0},{2,3},{3,2},{4,5},{5,4},{6,7},{7,6},{8,9},{9,8},{10,11... | collective-permute-start | bytes 786440 | tf_op jit(solution)/shard_map/ppermute | solution.py:493
  71.3 1.9 %collective-permute-start.14 = (bf16[160,128]{1,0:T(8,128)(2,1)S(1)}, bf16[160,128]{1,0:T(8,128)(2,1)S(1)}, u32[]{:S(2)}, u32[]{:S(2)}) collective-permute-start(bf16[160,128]{1,0:T(8,128)(2,1)S(1)} %get-tuple-element.167), channel_id=1, source_target_pairs={{0,2},{2,0},{4,6},{6,4},{8,10},{10,8},{12,14},{14,12},{16,18},{18,... | collective-permute-start | bytes 122888 | tf_op jit(solution)/shard_map/ppermute | solution.py:402
  71.5 4.1 %collective-permute-start.15 = (bf16[160,128]{1,0:T(8,128)(2,1)S(1)}, bf16[160,128]{1,0:T(8,128)(2,1)S(1)}, u32[]{:S(2)}, u32[]{:S(2)}) collective-permute-start(bf16[160,128]{1,0:T(8,128)(2,1)S(1)} %get-tuple-element.169), channel_id=1, source_target_pairs={{0,4},{2,6},{4,0},{6,2},{8,12},{10,14},{12,8},{14,10},{16,20},{18,... | collective-permute-start | bytes 122888 | tf_op jit(solution)/shard_map/ppermute | solution.py:402
  72.3 3.9 %collective-permute-start.16 = (bf16[160,128]{1,0:T(8,128)(2,1)S(1)}, bf16[160,128]{1,0:T(8,128)(2,1)S(1)}, u32[]{:S(2)}, u32[]{:S(2)}) collective-permute-start(bf16[160,128]{1,0:T(8,128)(2,1)S(1)} %get-tuple-element.171), channel_id=1, source_target_pairs={{0,6},{2,4},{4,2},{6,0},{8,14},{10,12},{12,10},{14,8},{16,22},{18,... | collective-permute-start | bytes 122888 | tf_op jit(solution)/shard_map/ppermute | solution.py:402
  77.6 8.5 %collective-permute-start.22 = (bf16[256,384]{1,0:T(8,128)(2,1)S(1)}, bf16[256,384]{1,0:T(8,128)(2,1)S(1)}, u32[]{:S(2)}, u32[]{:S(2)}) collective-permute-start(bf16[256,384]{1,0:T(8,128)(2,1)S(1)} %shard_map.108.refs_3_), channel_id=1, source_target_pairs={{0,1},{1,0},{2,3},{3,2},{4,5},{5,4},{6,7},{7,6},{8,9},{9,8},{10,11... | collective-permute-start | bytes 589832 | tf_op jit(solution)/shard_map/ppermute | solution.py:493
  80.0 11.2 %collective-permute-start.21 = (bf16[256,384]{1,0:T(8,128)(2,1)S(1)}, bf16[256,384]{1,0:T(8,128)(2,1)S(1)}, u32[]{:S(2)}, u32[]{:S(2)}) collective-permute-start(bf16[256,384]{1,0:T(8,128)(2,1)S(1)} %shard_map.109.refs_3_), channel_id=1, source_target_pairs={{0,1},{1,0},{2,3},{3,2},{4,5},{5,4},{6,7},{7,6},{8,9},{9,8},{10,11... | collective-permute-start | bytes 589832 | tf_op jit(solution)/shard_map/ppermute | solution.py:493
  82.5 11.3 %collective-permute-start.20 = (bf16[256,384]{1,0:T(8,128)(2,1)S(1)}, bf16[256,384]{1,0:T(8,128)(2,1)S(1)}, u32[]{:S(2)}, u32[]{:S(2)}) collective-permute-start(bf16[256,384]{1,0:T(8,128)(2,1)S(1)} %shard_map.110.refs_3_), channel_id=1, source_target_pairs={{0,1},{1,0},{2,3},{3,2},{4,5},{5,4},{6,7},{7,6},{8,9},{9,8},{10,11... | collective-permute-start | bytes 589832 | tf_op jit(solution)/shard_map/ppermute | solution.py:493
  86.1 9.8 %collective-permute-start.19 = (bf16[128,384]{1,0:T(8,128)(2,1)S(1)}, bf16[128,384]{1,0:T(8,128)(2,1)S(1)}, u32[]{:S(2)}, u32[]{:S(2)}) collective-permute-start(bf16[128,384]{1,0:T(8,128)(2,1)S(1)} %shard_map.111.refs_1_), channel_id=1, source_target_pairs={{0,1},{1,0},{2,3},{3,2},{4,5},{5,4},{6,7},{7,6},{8,9},{9,8},{10,11... | collective-permute-start | bytes 294920 | tf_op jit(solution)/shard_map/ppermute | solution.py:493
  87.2 10.3 %collective-permute-start.18 = (bf16[128,384]{1,0:T(8,128)(2,1)S(1)}, bf16[128,384]{1,0:T(8,128)(2,1)S(1)}, u32[]{:S(2)}, u32[]{:S(2)}) collective-permute-start(bf16[128,384]{1,0:T(8,128)(2,1)S(1)} %shard_map.112.refs_3_), channel_id=1, source_target_pairs={{0,1},{1,0},{2,3},{3,2},{4,5},{5,4},{6,7},{7,6},{8,9},{9,8},{10,11... | collective-permute-start | bytes 294920 | tf_op jit(solution)/shard_map/ppermute | solution.py:493

commit v13 on v11

--- a/solution.py
+++ b/solution.py
@@ -87,10 +87,12 @@
         at += padded
 
 
-def project(me, xs, w_ref, begin, width, skip):
+def project(me, xs, w_ref, begin, width, skip, own=None):
     depth = xs[0].shape[1]
-    total = None
+    total = own
     for r, x_ref in enumerate(xs):
+        if r == 0 and own is not None:
+            continue
         src = lax.rem(me - r + len(xs), len(xs))
         from_rows = pl.ds(pl.multiple_of(src * depth, depth), depth)
         part = jnp.dot(x_ref[skip:, :], w_ref[from_rows, begin : begin + width], preferred_element_type=F32)
@@ -111,6 +113,7 @@
     prev_ref = None
     if not extra:
         prev_ref, refs = refs[0], refs[1:]
+    own_ref, refs = (refs[0], refs[1:]) if others else (None, refs)
     other_refs, refs = refs[:others], refs[others:]
     k_ref, v_ref, s_ref, refs = *refs[:3], refs[3:]
     send_refs, ext_ref = refs[:sends], refs[-1]
@@ -120,12 +123,12 @@
     me = j_ref[0]
 
     if others:
-        k_ref[...] = project(me, xs, w_ref, qk_width, qk_width, extra)
+        k_ref[...] = project(me, xs, w_ref, qk_width, qk_width, 0, own_ref[:, :qk_width])
     else:
         qk = project(me, xs, w_ref, 0, 2 * qk_width, extra)
         q_ref[...] = qk[:, :qk_width]
         k_ref[...] = qk[:, qk_width:]
-    raw = project(me, xs, w_ref, 2 * qk_width, width, 0)
+    raw = project(me, xs, w_ref, 2 * qk_width, width, 0, own_ref[:, qk_width:] if others else None)
     if extra:
         ext_ref[...] = raw.astype(F32)
     else:
@@ -168,6 +171,11 @@
     if not others:
         halo_ref[0:EDGE, :] = raw[raw.shape[0] - EDGE :]
         query_part(me, xs, w_ref, mean_ref, v_ref, wq_ref, wk_ref, halo_ref, 2 * qk_width + width, extra)
+
+
+def own_share_kernel(j_ref, x_ref, w_ref, o_ref, *, begin):
+    rows_of = pl.ds(pl.multiple_of(j_ref[0] * x_ref.shape[1], x_ref.shape[1]), x_ref.shape[1])
+    o_ref[...] = jnp.dot(x_ref[...], w_ref[rows_of, begin : begin + o_ref.shape[1]], preferred_element_type=F32)
 
 
 def query_part(me, xs, w_ref, mean_ref, v_ref, wq_ref, wk_ref, halo_ref, begin, skip):
@@ -552,6 +560,8 @@
         operands = [tokens, means, conv_weight, turn_rows, weight, arranged, *pieces[b]]
         if prev is not None:
             operands.append(prev)
+        if others:
+            operands.append(own_share)
         operands += others
         return call(
             functools.partial(
@@ -586,13 +596,20 @@
             vmem=16 << 20,
         )(places, turn, prev, q, k, v, wq, wk)
 
+    own_share = call(
+        functools.partial(own_share_kernel, begin=qk_width),
+        jax.ShapeDtypeStruct((blocks[last - 1][1], qk_width + width), F32),
+        in_specs=[scalar] + [whole] * 2,
+        out_specs=whole,
+        vmem=32 << 20,
+    )(places, pieces[last - 1][0], arranged)
     done, attended = {}, {}
     picked = [pick(r) for r in range(1, n)]
     done[last] = do_block(last, None, None)
     halo = lax.ppermute(done[last][6], "ctx", [(i, i + 1) for i in range(ctx - 1)])
     prevs = {0: halo}
     for b in range(last - 1):
-        behind = [a[1] for a in attended.values()] + (picked if b == 1 else [])
+        behind = [a[1] for a in attended.values()] + (picked + [own_share] if b == 1 else [])
         done[b] = do_block(b, prevs[b], behind if b else None)
         prevs[b + 1] = done[b][6]
         attended[b] = attend(b, prevs[b])
@@ -631,17 +648,15 @@
         )(*operands)
 
     order = (0, 1, 4, 2, 3)
-    early = []
+    early, early_blocks = [], (0, 1, last)
     if in_planes:
         held = sends[:1] + [exchange(sends[r], "ctx", r) for r in range(1, PLANE)]
         back = prior_in_planes(held, places, [done[last - 1][6], (attended[last - 1][1], edge)])
         priors = [exchange(back[r], "ctx", r) for r in range(1, PLANE)]
-        turns = tuple(range(1, PLANE))
-        mixed = finish((0,), back[:1], range(last + 1), done[last][1])
+        mixed = finish((0,), back[:1], early_blocks, done[last][1])
         early = [mixed] + [from_head(mixed, r) for r in range(1, n)]
     else:
         priors = prior_by_doubling(sum(done[b][2] for b in range(last + 1)), position)
-        turns = tuple(range(pairs))
         mixed = attended[last][1]
     fetched = [from_head(after(block, done[last - 1][1]), r) for r, block in enumerate(picked, 1)]
     out_rows = []
@@ -652,14 +667,21 @@
 
     mixes = {}
     for b in order:
-        mixed = finish(turns, priors, (b,), mixed)
+        if early and b in early_blocks:
+            mixed = finish(tuple(range(1, pairs)), priors, (b,), mixed)
+        else:
+            mixed = finish(tuple(range(pairs)), [back[0], *priors] if early else priors, (b,), mixed)
         mixes[b] = [mixed] + [from_head(mixed, r) for r in range(1, n)]
 
     def pieces_of(b, r):
-        return early[r : r + 1] + [mixes[b][r]]
+        return early[r : r + 1] * (b in early_blocks) + [mixes[b][r]]
 
     def turns_of(b):
-        return ([(0, (0,))] if early else []) + [(blocks[b][0], turns)]
+        at = blocks[b][0]
+        if early and b in early_blocks:
+            ahead = sum(blocks[c][1] for c in early_blocks[: early_blocks.index(b)])
+            return [(at - ahead, (0,)), (at, tuple(range(1, pairs)))]
+        return [(at, tuple(range(pairs)))]
 
     tail_blocks = order[-2:]
     tail_rows = sum(blocks[b][1] for b in tail_blocks)
@@ -668,7 +690,7 @@
             share_kernel, turns=[turns_of(b) for b in tail_blocks], blocks=[blocks[b] for b in tail_blocks]
         ),
         jax.ShapeDtypeStruct((tail_rows, cols), BF16),
-        in_specs=[scalar] + [whole] * (1 + 2 * len(turns_of(last))),
+        in_specs=[scalar] + [whole] * (1 + 2 * len(turns_of(tail_blocks[0]))),
         out_specs=whole,
         scratch_shapes=[pltpu.VMEM((tail_rows, width), BF16)],
         vmem=16 << 20,

time: 99.1 us -> 98.7 us (level)
  waiting for transfers between devices: 11.5 us -> 10 us
    ppermute x12, waiting for transfers between devices: 10.3 us -> 8.51 us  [from_head(): return lax.ppermute(value, 'head', [(i, (i + by) % n) for i in range(n)])]
  transfers between devices with their start and end apart: 23 -> 23, of which waited for: 5 -> 7; matrix products, arithmetic and copies ran while one was open for 2% -> 2% of each run, Pallas kernels for 52% -> 53%
where the time goes in v13:
time: 98.7 us; the launch traced here: 98.4 us
  Pallas kernels  55.1 us (56%)
  starting transfers between devices  26.1 us (26%)
  waiting for transfers between devices  10 us (10%)
  local copies, waits for them, and re-layouts  6.54 us (7%)
    ppermute x12, starting transfers between devices, from_head(): return lax.ppermute(value, 'head', [(i, (i + by) % n) for i in range(n)])  15.8 us
    pallas_call x5, Pallas kernels, do_block(): call(functools.partial(block_kernel, n=n, heads=heads, extra=extra, other...  15.7 us
    pallas_call x5, Pallas kernels, attend(): call(functools.partial(attend_kernel, heads=heads, first=b == 0), [jax.Sh...  10 us
    pallas_call x5, Pallas kernels, per_device(): call(functools.partial(output_kernel, n=n, offset=at, parts=out_parts, tu...  9.33 us
    ppermute x10, starting transfers between devices, exchange(): return lax.ppermute(value, axis, [(i, i ^ flip) for i in range(count)])  8.69 us
    ppermute x12, waiting for transfers between devices, from_head(): return lax.ppermute(value, 'head', [(i, (i + by) % n) for i in range(n)])  8.51 us
    pallas_call x6, Pallas kernels, finish(): call(functools.partial(finish_kernel, heads=heads, turns=turns, before=be...  8.27 us
    pallas_call x1, Pallas kernels, per_device(): call(functools.partial(arrange_kernel, heads=heads), jax.ShapeDtypeStruct...  5.09 us
  transfers between devices with their start and end apart: 23, of which 7 were waited for; matrix products, arithmetic and copies ran while one was open for 2% of the time, Pallas kernels for 53%

profile of v13, /device:TPU:0, one launch (start us, length us, event | category | flops | bytes accessed | tf_op | source)
XLA Modules:
  0.0 98.4 jit_solution(10598940149807017266)
XLA Ops:
  1.2 3.0 %collective-permute-start = (bf16[272,1024]{1,0:T(8,128)(2,1)S(1)}, bf16[272,1024]{1,0:T(8,128)(2,1)S(1)}, u32[]{:S(2)}, u32[]{:S(2)}) collective-permute-start(bf16[272,1024]{1,0:T(8,128)(2,1)S(1)} %slice.15.refs_0_), channel_id=1, source_target_pairs={{0,1},{1,0},{2,3},{3,2},{4,5},{5,4},{6,7},{7,6},{8,9},{9,8},{10,11... | collective-permute-start | bytes 1671176 | tf_op jit(solution)/shard_map/ppermute | solution.py:501
  5.6 2.0 %collective-permute-start.3 = (bf16[256,1024]{1,0:T(8,128)(2,1)S(1)}, bf16[256,1024]{1,0:T(8,128)(2,1)S(1)}, u32[]{:S(2)}, u32[]{:S(2)}) collective-permute-start(bf16[256,1024]{1,0:T(8,128)(2,1)S(1)} %get-tuple-element.106.refs_0_), channel_id=1, source_target_pairs={{0,1},{1,0},{2,3},{3,2},{4,5},{5,4},{6,7},{7,6},{8,9},{9,8},{10,11... | collective-permute-start | bytes 1572872 | tf_op jit(solution)/shard_map/ppermute | solution.py:501
  8.8 1.9 %collective-permute-start.5 = (bf16[128,1024]{1,0:T(8,128)(2,1)S(1)}, bf16[128,1024]{1,0:T(8,128)(2,1)S(1)}, u32[]{:S(2)}, u32[]{:S(2)}) collective-permute-start(bf16[128,1024]{1,0:T(8,128)(2,1)S(1)} %get-tuple-element.104.x_ref.refs_0_), channel_id=1, source_target_pairs={{0,1},{1,0},{2,3},{3,2},{4,5},{5,4},{6,7},{7,6},{8,9},{9,8},{10,11... | collective-permute-start | bytes 786440 | tf_op jit(solution)/shard_map/ppermute | solution.py:501
  10.7 3.1 %copy-done.3 = bf16[2048,1792]{1,0:T(8,128)(2,1)S(1)} copy-done((bf16[2048,1792]{1,0:T(8,128)(2,1)S(1)}, bf16[2048,1792]{1,0:T(8,128)(2,1)}, u32[]{:S(2)}) %copy-start.3) | copy-done | bytes 7340056
  13.8 5.1 %shard_map.92.w_ref = bf16[2048,1792]{1,0:T(8,128)(2,1)S(1)} custom-call(bf16[2048,1792]{1,0:T(8,128)(2,1)S(1)} %copy-done.3), custom_call_target="tpu_custom_call" | custom-call | flops 1 | bytes 1 | tf_op jit(solution)/shard_map/pallas_call | solution.py:538
  19.0 3.8 %shard_map.93 = (bf16[256,128]{1,0:T(8,128)(2,1)S(1)}, bf16[256,512]{1,0:T(8,128)(2,1)S(1)}, f32[4,160,128]{2,1,0:T(8,128)S(1)}, bf16[256,128]{1,0:T(8,128)(2,1)...) custom-call(s32[3]{0:T(128)S(1)} %pad_add_fusion.a_ref.j_ref._, ...), custom_call_target="tpu_custom_call" | custom-call | flops 1 | bytes 1 | tf_op jit(solution)/shard_map/pallas_call | solution.py:566
  22.8 1.6 %collective-permute-start.1 = (bf16[144,512]{1,0:T(8,128)(2,1)S(1)}, bf16[144,512]{1,0:T(8,128)(2,1)S(1)}, u32[]{:S(2)}, u32[]{:S(2)}) collective-permute-start(bf16[144,512]{1,0:T(8,128)(2,1)S(1)} %get-tuple-element.90), channel_id=1, source_target_pairs={{0,2},{2,4},{4,6},{6,8},{8,10},{10,12},{12,14},{14,16},{16,18},{18... | collective-permute-start | bytes 442376 | tf_op jit(solution)/shard_map/ppermute | solution.py:609
  26.0 2.9 %collective-permute-done.2.refs_1_ = bf16[256,1024]{1,0:T(8,128)(2,1)S(1)} collective-permute-done((bf16[256,1024]{1,0:T(8,128)(2,1)S(1)}, bf16[256,1024]{1,0:T(8,128)(2,1)S(1)}, u32[]{:S(2)}, u32[]{:S(2)}) %collective-permute-start.2) | collective-permute-done | bytes 524320 | tf_op jit(solution)/shard_map/ppermute | solution.py:501
  28.9 3.8 %shard_map.94 = (bf16[256,128]{1,0:T(8,128)(2,1)S(1)}, bf16[256,512]{1,0:T(8,128)(2,1)S(1)}, f32[4,160,128]{2,1,0:T(8,128)S(1)}, bf16[256,128]{1,0:T(8,128)(2,1)...) custom-call(s32[3]{0:T(128)S(1)} %pad_add_fusion.a_ref.j_ref._, ...), custom_call_target="tpu_custom_call" | custom-call | flops 1 | bytes 1 | tf_op jit(solution)/shard_map/pallas_call | solution.py:566
  32.7 2.1 %shard_map.95 = (bf16[256,1280]{1,0:T(8,128)(2,1)S(1)}, f32[256,512]{1,0:T(8,128)S(1)}, f32[256,512]{1,0:T(8,128)S(1)}) custom-call(s32[3]{0:T(128)S(1)} %pad_add_fusion.a_ref.j_ref._, bf16[128,1280]{1,0:T(8,128)(2,1)S(1)} %copy-done.2, bf16[144,512]{1,0:T(8,128)(2,1)S(1)} %collective-permute-done.1.refs_2_.prev_ref, ...), custom_call_target="tpu_custom_call" | custom-call | flops 1 | bytes 1 | tf_op jit(solution)/shard_map/pallas_call | solution.py:590
  34.9 2.1 %shard_map.96 = (bf16[256,1280]{1,0:T(8,128)(2,1)S(1)}, f32[256,512]{1,0:T(8,128)S(1)}, f32[256,512]{1,0:T(8,128)S(1)}) custom-call(s32[3]{0:T(128)S(1)} %pad_add_fusion.a_ref.j_ref._, bf16[128,1280]{1,0:T(8,128)(2,1)S(1)} %copy-done.2, bf16[144,512]{1,0:T(8,128)(2,1)S(1)} %collective-permute-done.1.refs_2_.prev_ref, ...), custom_call_target="tpu_custom_call" | custom-call | flops 1 | bytes 1 | tf_op jit(solution)/shard_map/pallas_call | solution.py:590
  37.0 3.1 %collective-permute-done.3.refs_1_ = bf16[256,1024]{1,0:T(8,128)(2,1)S(1)} collective-permute-done((bf16[256,1024]{1,0:T(8,128)(2,1)S(1)}, bf16[256,1024]{1,0:T(8,128)(2,1)S(1)}, u32[]{:S(2)}, u32[]{:S(2)}) %collective-permute-start.3) | collective-permute-done | bytes 524320 | tf_op jit(solution)/shard_map/ppermute | solution.py:501
  40.1 3.8 %shard_map.98 = (bf16[256,128]{1,0:T(8,128)(2,1)S(1)}, bf16[256,512]{1,0:T(8,128)(2,1)S(1)}, f32[4,160,128]{2,1,0:T(8,128)S(1)}, bf16[256,128]{1,0:T(8,128)(2,1)...) custom-call(s32[3]{0:T(128)S(1)} %pad_add_fusion.a_ref.j_ref._, ...), custom_call_target="tpu_custom_call" | custom-call | flops 1 | bytes 1 | tf_op jit(solution)/shard_map/pallas_call | solution.py:566
  43.9 2.1 %shard_map.99 = (bf16[256,1280]{1,0:T(8,128)(2,1)S(1)}, f32[256,512]{1,0:T(8,128)S(1)}, f32[256,512]{1,0:T(8,128)S(1)}) custom-call(s32[3]{0:T(128)S(1)} %pad_add_fusion.a_ref.j_ref._, bf16[128,1280]{1,0:T(8,128)(2,1)S(1)} %copy-done.2, bf16[144,512]{1,0:T(8,128)(2,1)S(1)} %get-tuple-element.107.refs_2_.prev_ref, ...), custom_call_target="tpu_custom_call" | custom-call | flops 1 | bytes 1 | tf_op jit(solution)/shard_map/pallas_call | solution.py:590
  46.1 2.6 %shard_map.100 = (bf16[128,128]{1,0:T(8,128)(2,1)S(1)}, bf16[128,512]{1,0:T(8,128)(2,1)S(1)}, f32[4,160,128]{2,1,0:T(8,128)S(1)}, bf16[128,128]{1,0:T(8,128)(2,1...) custom-call(s32[3]{0:T(128)S(1)} %pad_add_fusion.a_ref.j_ref._, ...), custom_call_target="tpu_custom_call" | custom-call | flops 1 | bytes 1 | tf_op jit(solution)/shard_map/pallas_call | solution.py:566
  48.7 1.9 %shard_map.101 = (bf16[128,1280]{1,0:T(8,128)(2,1)S(1)}, f32[128,512]{1,0:T(8,128)S(1)}, f32[128,512]{1,0:T(8,128)S(1)}) custom-call(s32[3]{0:T(128)S(1)} %pad_add_fusion.a_ref.j_ref._, bf16[128,1280]{1,0:T(8,128)(2,1)S(1)} %copy-done.2, bf16[144,512]{1,0:T(8,128)(2,1)S(1)} %get-tuple-element.108.refs_2_.prev_ref, ...), custom_call_target="tpu_custom_call" | custom-call | flops 1 | bytes 1 | tf_op jit(solution)/shard_map/pallas_call | solution.py:590
  50.6 1.6 %shard_map.102 = (bf16[128,128]{1,0:T(8,128)(2,1)S(1)}, bf16[128,512]{1,0:T(8,128)(2,1)S(1)}, f32[4,160,128]{2,1,0:T(8,128)S(1)}, bf16[160,128]{1,0:T(8,128)(2,1...) custom-call(s32[3]{0:T(128)S(1)} %pad_add_fusion.a_ref.j_ref._, ...), custom_call_target="tpu_custom_call" | custom-call | flops 1 | bytes 1 | tf_op jit(solution)/shard_map/pallas_call | solution.py:566
  52.3 2.1 %collective-permute-start.8 = (bf16[160,128]{1,0:T(8,128)(2,1)S(1)}, bf16[160,128]{1,0:T(8,128)(2,1)S(1)}, u32[]{:S(2)}, u32[]{:S(2)}) collective-permute-start(bf16[160,128]{1,0:T(8,128)(2,1)S(1)} %get-tuple-element.142), channel_id=1, source_target_pairs={{0,4},{2,6},{4,0},{6,2},{8,12},{10,14},{12,8},{14,10},{16,20},{18,... | collective-permute-start | bytes 122888 | tf_op jit(solution)/shard_map/ppermute | solution.py:410
  54.5 1.8 %collective-permute-start.6 = (bf16[256,1024]{1,0:T(8,128)(2,1)S(1)}, bf16[256,1024]{1,0:T(8,128)(2,1)S(1)}, u32[]{:S(2)}, u32[]{:S(2)}) collective-permute-start(bf16[256,1024]{1,0:T(8,128)(2,1)S(1)} %shard_map.91), channel_id=1, source_target_pairs={{0,1},{1,0},{2,3},{3,2},{4,5},{5,4},{6,7},{7,6},{8,9},{9,8},{10,11... | collective-permute-start | bytes 1572872 | tf_op jit(solution)/shard_map/ppermute | solution.py:501
  56.2 1.8 %shard_map.103 = (bf16[128,128]{1,0:T(8,128)(2,1)S(1)}, bf16[128,512]{1,0:T(8,128)(2,1)S(1)}, bf16[128,512]{1,0:T(8,128)(2,1)S(1)}, bf16[144,512]{1,0:T(8,128)(2,1)S(1)}) custom-call(s32[3]{0:T(128)S(1)} %pad_add_fusion.a_ref.j_ref._, bf16[256,128]{1,0:T(8,128)(2,1)S(1)} %copy-done.4, bf16[2048,1792]{1,0:T(8,128)(2,1)S(1)} %shard_map.92.w_ref, ...), custom_call_target="tpu_custom_call" | custom-call | flops 1 | bytes 1 | tf_op jit(solution)/shard_map/pallas_call | solution.py:579
  58.7 3.7 %collective-permute-start.12 = (bf16[160,128]{1,0:T(8,128)(2,1)S(1)}, bf16[160,128]{1,0:T(8,128)(2,1)S(1)}, u32[]{:S(2)}, u32[]{:S(2)}) collective-permute-start(bf16[160,128]{1,0:T(8,128)(2,1)S(1)} %get-tuple-element.148), channel_id=1, source_target_pairs={{0,24},{2,26},{4,28},{6,30},{8,16},{10,18},{12,20},{14,22},{16,8},... | collective-permute-start | bytes 122888 | tf_op jit(solution)/shard_map/ppermute | solution.py:410
  64.4 1.7 %shard_map.104 = (bf16[128,1280]{1,0:T(8,128)(2,1)S(1)}, f32[128,512]{1,0:T(8,128)S(1)}, f32[128,512]{1,0:T(8,128)S(1)}) custom-call(s32[3]{0:T(128)S(1)} %pad_add_fusion.a_ref.j_ref._, bf16[128,1280]{1,0:T(8,128)(2,1)S(1)} %copy-done.2, bf16[144,512]{1,0:T(8,128)(2,1)S(1)} %get-tuple-element.124.refs_2_.prev_ref, ...), custom_call_target="tpu_custom_call" | custom-call | flops 1 | bytes 1 | tf_op jit(solution)/shard_map/pallas_call | solution.py:590
  68.0 1.6 %collective-permute-start.15 = (bf16[160,128]{1,0:T(8,128)(2,1)S(1)}, bf16[160,128]{1,0:T(8,128)(2,1)S(1)}, u32[]{:S(2)}, u32[]{:S(2)}) collective-permute-start(bf16[160,128]{1,0:T(8,128)(2,1)S(1)} %get-tuple-element.160), channel_id=1, source_target_pairs={{0,4},{2,6},{4,0},{6,2},{8,12},{10,14},{12,8},{14,10},{16,20},{18,... | collective-permute-start | bytes 122888 | tf_op jit(solution)/shard_map/ppermute | solution.py:410
  69.8 1.4 %shard_map.108.refs_2_ = bf16[768,128]{1,0:T(8,128)(2,1)S(1)} custom-call(s32[3]{0:T(128)S(1)} %pad_add_fusion.a_ref.j_ref._, bf16[256,128]{1,0:T(8,128)(2,1)S(1)} %copy-done.4, f32[1,512]{1,0:T(1,128)S(1)} %bitcast.4, bf16[160,128]{1,0:T(8,128)(2,1)S(1)} %get-tuple-element.149.refs_0_, ...), custom_call_target="tpu_custom_call" | custom-call | flops 4849999872 | bytes 1 | tf_op jit(solution)/shard_map/pallas_call | solution.py:641
  71.2 1.5 %collective-permute-start.19 = (bf16[768,128]{1,0:T(8,128)(2,1)S(1)}, bf16[768,128]{1,0:T(8,128)(2,1)S(1)}, u32[]{:S(2)}, u32[]{:S(2)}) collective-permute-start(bf16[768,128]{1,0:T(8,128)(2,1)S(1)} %shard_map.108.refs_2_), channel_id=1, source_target_pairs={{0,1},{1,0},{2,3},{3,2},{4,5},{5,4},{6,7},{7,6},{8,9},{9,8},{10,11... | collective-permute-start | bytes 589832 | tf_op jit(solution)/shard_map/ppermute | solution.py:501
  75.5 1.4 %shard_map.110.refs_3_ = bf16[256,384]{1,0:T(8,128)(2,1)S(1)} custom-call(s32[3]{0:T(128)S(1)} %pad_add_fusion.a_ref.j_ref._, bf16[256,128]{1,0:T(8,128)(2,1)S(1)} %copy-done.4, f32[1,512]{1,0:T(1,128)S(1)} %bitcast.6, bf16[160,128]{1,0:T(8,128)(2,1)S(1)} %collective-permute-done.14.refs_0_.refs_1_, ...), custom_call_target="tpu_custom_call" | custom-call | flops 1 | bytes 1 | tf_op jit(solution)/shard_map/pallas_call | solution.py:641
  78.0 1.4 %shard_map.111.refs_3_ = bf16[256,384]{1,0:T(8,128)(2,1)S(1)} custom-call(s32[3]{0:T(128)S(1)} %pad_add_fusion.a_ref.j_ref._, bf16[256,128]{1,0:T(8,128)(2,1)S(1)} %copy-done.4, f32[1,512]{1,0:T(1,128)S(1)} %bitcast.7, bf16[160,128]{1,0:T(8,128)(2,1)S(1)} %collective-permute-done.14.refs_0_.refs_1_, ...), custom_call_target="tpu_custom_call" | custom-call | flops 1 | bytes 1 | tf_op jit(solution)/shard_map/pallas_call | solution.py:641
  86.3 2.1 %shard_map.115.refs_6_ = bf16[1024,1024]{1,0:T(8,128)(2,1)} custom-call(s32[3]{0:T(128)S(1)} %pad_add_fusion.a_ref.j_ref._, bf16[512,2048]{1,0:T(8,128)(2,1)S(1)} %copy-done, bf16[256,1024]{1,0:T(8,128)(2,1)S(1)} %collective-permute-done.6.refs_0_, bf16[256,1024]{1,0:T(8,128)(2,1)S(1)} %collective-permute-done.13.refs_1_, ...), custom_call_target="tpu_custom_call" | custom-call | flops 1 | bytes 1 | tf_op jit(solution)/shard_map/pallas_call | solution.py:715
  88.5 2.1 %shard_map.116.refs_6_ = bf16[1024,1024]{1,0:T(8,128)(2,1)} custom-call(s32[3]{0:T(128)S(1)} %pad_add_fusion.a_ref.j_ref._, bf16[512,2048]{1,0:T(8,128)(2,1)S(1)} %copy-done, bf16[256,1024]{1,0:T(8,128)(2,1)S(1)} %collective-permute-done.6.refs_0_, bf16[256,1024]{1,0:T(8,128)(2,1)S(1)} %collective-permute-done.13.refs_1_, ...), custom_call_target="tpu_custom_call", output_to_operand_aliasing={{}: (8, {})} | custom-call | flops 1 | bytes 1 | tf_op jit(solution)/shard_map/pallas_call | solution.py:715
  91.6 2.1 %shard_map.117.refs_4_ = bf16[1024,1024]{1,0:T(8,128)(2,1)} custom-call(s32[3]{0:T(128)S(1)} %pad_add_fusion.a_ref.j_ref._, bf16[512,2048]{1,0:T(8,128)(2,1)S(1)} %copy-done, bf16[256,1024]{1,0:T(8,128)(2,1)S(1)} %collective-permute-done.6.refs_0_, bf16[256,1024]{1,0:T(8,128)(2,1)S(1)} %collective-permute-done.13.refs_1_, ...), custom_call_target="tpu_custom_call", output_to_operand_aliasing={{}: (8, {})} | custom-call | flops 1 | bytes 1 | tf_op jit(solution)/shard_map/pallas_call | solution.py:715
  94.4 1.5 %shard_map.118.refs_4_ = bf16[1024,1024]{1,0:T(8,128)(2,1)} custom-call(s32[3]{0:T(128)S(1)} %pad_add_fusion.a_ref.j_ref._, bf16[512,2048]{1,0:T(8,128)(2,1)S(1)} %copy-done, bf16[256,1024]{1,0:T(8,128)(2,1)S(1)} %collective-permute-done.6.refs_0_, bf16[256,1024]{1,0:T(8,128)(2,1)S(1)} %collective-permute-done.13.refs_1_, ...), custom_call_target="tpu_custom_call", output_to_operand_aliasing={{}: (6, {})} | custom-call | flops 1 | bytes 1 | tf_op jit(solution)/shard_map/pallas_call | solution.py:715
  96.7 1.5 %shard_map.119 = bf16[1024,1024]{1,0:T(8,128)(2,1)} custom-call(s32[3]{0:T(128)S(1)} %pad_add_fusion.a_ref.j_ref._, bf16[512,2048]{1,0:T(8,128)(2,1)S(1)} %copy-done, bf16[256,1024]{1,0:T(8,128)(2,1)S(1)} %collective-permute-done.6.refs_0_, bf16[256,1024]{1,0:T(8,128)(2,1)S(1)} %collective-permute-done.13.refs_1_, ...), custom_call_target="tpu_custom_call", output_to_operand_aliasing={{}: (6, {})} | custom-call | flops 1 | bytes 1 | tf_op jit(solution)/shard_map/pallas_call | solution.py:715
  (63 shorter events, 23.6 us)
Async XLA Ops:
  1.2 17.7 %collective-permute-start = (bf16[272,1024]{1,0:T(8,128)(2,1)S(1)}, bf16[272,1024]{1,0:T(8,128)(2,1)S(1)}, u32[]{:S(2)}, u32[]{:S(2)}) collective-permute-start(bf16[272,1024]{1,0:T(8,128)(2,1)S(1)} %slice.15.refs_0_), channel_id=1, source_target_pairs={{0,1},{1,0},{2,3},{3,2},{4,5},{5,4},{6,7},{7,6},{8,9},{9,8},{10,11... | collective-permute-start | bytes 1671176 | tf_op jit(solution)/shard_map/ppermute | solution.py:501
  5.5 23.4 %collective-permute-start.2 = (bf16[256,1024]{1,0:T(8,128)(2,1)S(1)}, bf16[256,1024]{1,0:T(8,128)(2,1)S(1)}, u32[]{:S(2)}, u32[]{:S(2)}) collective-permute-start(bf16[256,1024]{1,0:T(8,128)(2,1)S(1)} %get-tuple-element.91.refs_0_), channel_id=1, source_target_pairs={{0,1},{1,0},{2,3},{3,2},{4,5},{5,4},{6,7},{7,6},{8,9},{9,8},{10,11... | collective-permute-start | bytes 1572872 | tf_op jit(solution)/shard_map/ppermute | solution.py:501
  5.6 34.6 %collective-permute-start.3 = (bf16[256,1024]{1,0:T(8,128)(2,1)S(1)}, bf16[256,1024]{1,0:T(8,128)(2,1)S(1)}, u32[]{:S(2)}, u32[]{:S(2)}) collective-permute-start(bf16[256,1024]{1,0:T(8,128)(2,1)S(1)} %get-tuple-element.106.refs_0_), channel_id=1, source_target_pairs={{0,1},{1,0},{2,3},{3,2},{4,5},{5,4},{6,7},{7,6},{8,9},{9,8},{10,11... | collective-permute-start | bytes 1572872 | tf_op jit(solution)/shard_map/ppermute | solution.py:501
  8.6 37.5 %collective-permute-start.4 = (bf16[128,1024]{1,0:T(8,128)(2,1)S(1)}, bf16[128,1024]{1,0:T(8,128)(2,1)S(1)}, u32[]{:S(2)}, u32[]{:S(2)}) collective-permute-start(bf16[128,1024]{1,0:T(8,128)(2,1)S(1)} %get-tuple-element.116.refs_0_), channel_id=1, source_target_pairs={{0,1},{1,0},{2,3},{3,2},{4,5},{5,4},{6,7},{7,6},{8,9},{9,8},{10,11... | collective-permute-start | bytes 786440 | tf_op jit(solution)/shard_map/ppermute | solution.py:501
  8.8 10.1 %copy-start.1 = (bf16[1408,128]{1,0:T(8,128)(2,1)S(1)}, bf16[1408,128]{1,0:T(8,128)(2,1)}, u32[]{:S(2)}) copy-start(bf16[1408,128]{1,0:T(8,128)(2,1)} %constant.30.clone.turn_ref) | copy-start | bytes 1081348
  8.8 41.8 %collective-permute-start.5 = (bf16[128,1024]{1,0:T(8,128)(2,1)S(1)}, bf16[128,1024]{1,0:T(8,128)(2,1)S(1)}, u32[]{:S(2)}, u32[]{:S(2)}) collective-permute-start(bf16[128,1024]{1,0:T(8,128)(2,1)S(1)} %get-tuple-element.104.x_ref.refs_0_), channel_id=1, source_target_pairs={{0,1},{1,0},{2,3},{3,2},{4,5},{5,4},{6,7},{7,6},{8,9},{9,8},{10,11... | collective-permute-start | bytes 786440 | tf_op jit(solution)/shard_map/ppermute | solution.py:501
  10.7 3.1 %copy-start.3 = (bf16[2048,1792]{1,0:T(8,128)(2,1)S(1)}, bf16[2048,1792]{1,0:T(8,128)(2,1)}, u32[]{:S(2)}) copy-start(bf16[2048,1792]{1,0:T(8,128)(2,1)} %w_ref.9) | copy-start | bytes 22020100
  13.8 5.1 %copy-start.4 = (bf16[256,128]{1,0:T(8,128)(2,1)S(1)}, bf16[256,128]{1,0:T(8,128)(2,1)}, u32[]{:S(2)}) copy-start(bf16[256,128]{1,0:T(8,128)(2,1)} %constant.32.clone.mean_ref) | copy-start | bytes 196612
  13.8 5.1 %copy-start.5 = (f32[160,128]{1,0:T(8,128)S(1)}, f32[160,128]{1,0:T(8,128)}, u32[]{:S(2)}) copy-start(f32[160,128]{1,0:T(8,128)} %constant.31.clone.weight_ref) | copy-start | bytes 245764
  13.8 5.1 %copy-start.6 = (f32[3,512]{1,0:T(4,128)S(1)}, f32[3,512]{1,0:T(4,128)}, u32[]{:S(2)}) copy-start(f32[3,512]{1,0:T(4,128)} %conv_ref.9) | copy-start | bytes 18436
  22.8 2.6 %copy-start = (bf16[512,2048]{1,0:T(8,128)(2,1)S(1)}, bf16[512,2048]{1,0:T(8,128)(2,1)}, u32[]{:S(2)}) copy-start(bf16[512,2048]{1,0:T(8,128)(2,1)} %w_ref.15) | copy-start | bytes 6291460
  22.8 6.1 %collective-permute-start.1 = (bf16[144,512]{1,0:T(8,128)(2,1)S(1)}, bf16[144,512]{1,0:T(8,128)(2,1)S(1)}, u32[]{:S(2)}, u32[]{:S(2)}) collective-permute-start(bf16[144,512]{1,0:T(8,128)(2,1)S(1)} %get-tuple-element.90), channel_id=1, source_target_pairs={{0,2},{2,4},{4,6},{6,8},{8,10},{10,12},{12,14},{14,16},{16,18},{18... | collective-permute-start | bytes 442376 | tf_op jit(solution)/shard_map/ppermute | solution.py:609
  26.0 6.7 %copy-start.2 = (bf16[128,1280]{1,0:T(8,128)(2,1)S(1)}, bf16[128,1280]{1,0:T(8,128)(2,1)}, u32[]{:S(2)}) copy-start(bf16[128,1280]{1,0:T(8,128)(2,1)} %constant.29.clone.turn_ref) | copy-start | bytes 983044
  52.2 5.8 %collective-permute-start.7 = (bf16[160,128]{1,0:T(8,128)(2,1)S(1)}, bf16[160,128]{1,0:T(8,128)(2,1)S(1)}, u32[]{:S(2)}, u32[]{:S(2)}) collective-permute-start(bf16[160,128]{1,0:T(8,128)(2,1)S(1)} %get-tuple-element.141), channel_id=1, source_target_pairs={{0,2},{2,0},{4,6},{6,4},{8,10},{10,8},{12,14},{14,12},{16,18},{18,... | collective-permute-start | bytes 122888 | tf_op jit(solution)/shard_map/ppermute | solution.py:410
  52.3 5.7 %collective-permute-start.8 = (bf16[160,128]{1,0:T(8,128)(2,1)S(1)}, bf16[160,128]{1,0:T(8,128)(2,1)S(1)}, u32[]{:S(2)}, u32[]{:S(2)}) collective-permute-start(bf16[160,128]{1,0:T(8,128)(2,1)S(1)} %get-tuple-element.142), channel_id=1, source_target_pairs={{0,4},{2,6},{4,0},{6,2},{8,12},{10,14},{12,8},{14,10},{16,20},{18,... | collective-permute-start | bytes 122888 | tf_op jit(solution)/shard_map/ppermute | solution.py:410
  54.4 3.6 %collective-permute-start.9 = (bf16[160,128]{1,0:T(8,128)(2,1)S(1)}, bf16[160,128]{1,0:T(8,128)(2,1)S(1)}, u32[]{:S(2)}, u32[]{:S(2)}) collective-permute-start(bf16[160,128]{1,0:T(8,128)(2,1)S(1)} %get-tuple-element.143), channel_id=1, source_target_pairs={{0,6},{2,4},{4,2},{6,0},{8,14},{10,12},{12,10},{14,8},{16,22},{18,... | collective-permute-start | bytes 122888 | tf_op jit(solution)/shard_map/ppermute | solution.py:410
  54.5 18.2 %collective-permute-start.6 = (bf16[256,1024]{1,0:T(8,128)(2,1)S(1)}, bf16[256,1024]{1,0:T(8,128)(2,1)S(1)}, u32[]{:S(2)}, u32[]{:S(2)}) collective-permute-start(bf16[256,1024]{1,0:T(8,128)(2,1)S(1)} %shard_map.91), channel_id=1, source_target_pairs={{0,1},{1,0},{2,3},{3,2},{4,5},{5,4},{6,7},{7,6},{8,9},{9,8},{10,11... | collective-permute-start | bytes 1572872 | tf_op jit(solution)/shard_map/ppermute | solution.py:501
  58.0 11.8 %copy-start.7 = (f32[512]{0:T(512)S(1)}, f32[512]{0:T(512)}, u32[]{:S(2)}) copy-start(f32[512]{0:T(512)} %param.12) | copy-start | bytes 6148
  58.7 7.4 %collective-permute-start.12 = (bf16[160,128]{1,0:T(8,128)(2,1)S(1)}, bf16[160,128]{1,0:T(8,128)(2,1)S(1)}, u32[]{:S(2)}, u32[]{:S(2)}) collective-permute-start(bf16[160,128]{1,0:T(8,128)(2,1)S(1)} %get-tuple-element.148), channel_id=1, source_target_pairs={{0,24},{2,26},{4,28},{6,30},{8,16},{10,18},{12,20},{14,22},{16,8},... | collective-permute-start | bytes 122888 | tf_op jit(solution)/shard_map/ppermute | solution.py:410
  62.4 4.9 %collective-permute-start.11 = (bf16[160,128]{1,0:T(8,128)(2,1)S(1)}, bf16[160,128]{1,0:T(8,128)(2,1)S(1)}, u32[]{:S(2)}, u32[]{:S(2)}) collective-permute-start(bf16[160,128]{1,0:T(8,128)(2,1)S(1)} %get-tuple-element.148), channel_id=1, source_target_pairs={{0,16},{2,18},{4,20},{6,22},{8,24},{10,26},{12,28},{14,30},{16,0},... | collective-permute-start | bytes 122888 | tf_op jit(solution)/shard_map/ppermute | solution.py:410
  62.4 4.9 %collective-permute-start.10 = (bf16[160,128]{1,0:T(8,128)(2,1)S(1)}, bf16[160,128]{1,0:T(8,128)(2,1)S(1)}, u32[]{:S(2)}, u32[]{:S(2)}) collective-permute-start(bf16[160,128]{1,0:T(8,128)(2,1)S(1)} %get-tuple-element.148), channel_id=1, source_target_pairs={{0,8},{2,10},{4,12},{6,14},{8,0},{10,2},{12,4},{14,6},{16,24},{18,... | collective-permute-start | bytes 122888 | tf_op jit(solution)/shard_map/ppermute | solution.py:410
  67.9 4.9 %collective-permute-start.14 = (bf16[160,128]{1,0:T(8,128)(2,1)S(1)}, bf16[160,128]{1,0:T(8,128)(2,1)S(1)}, u32[]{:S(2)}, u32[]{:S(2)}) collective-permute-start(bf16[160,128]{1,0:T(8,128)(2,1)S(1)} %get-tuple-element.159), channel_id=1, source_target_pairs={{0,2},{2,0},{4,6},{6,4},{8,10},{10,8},{12,14},{14,12},{16,18},{18,... | collective-permute-start | bytes 122888 | tf_op jit(solution)/shard_map/ppermute | solution.py:410
  68.0 4.8 %collective-permute-start.15 = (bf16[160,128]{1,0:T(8,128)(2,1)S(1)}, bf16[160,128]{1,0:T(8,128)(2,1)S(1)}, u32[]{:S(2)}, u32[]{:S(2)}) collective-permute-start(bf16[160,128]{1,0:T(8,128)(2,1)S(1)} %get-tuple-element.160), channel_id=1, source_target_pairs={{0,4},{2,6},{4,0},{6,2},{8,12},{10,14},{12,8},{14,10},{16,20},{18,... | collective-permute-start | bytes 122888 | tf_op jit(solution)/shard_map/ppermute | solution.py:410
  69.5 3.5 %collective-permute-start.16 = (bf16[160,128]{1,0:T(8,128)(2,1)S(1)}, bf16[160,128]{1,0:T(8,128)(2,1)S(1)}, u32[]{:S(2)}, u32[]{:S(2)}) collective-permute-start(bf16[160,128]{1,0:T(8,128)(2,1)S(1)} %get-tuple-element.161), channel_id=1, source_target_pairs={{0,6},{2,4},{4,2},{6,0},{8,14},{10,12},{12,10},{14,8},{16,22},{18,... | collective-permute-start | bytes 122888 | tf_op jit(solution)/shard_map/ppermute | solution.py:410
  71.2 12.0 %collective-permute-start.19 = (bf16[768,128]{1,0:T(8,128)(2,1)S(1)}, bf16[768,128]{1,0:T(8,128)(2,1)S(1)}, u32[]{:S(2)}, u32[]{:S(2)}) collective-permute-start(bf16[768,128]{1,0:T(8,128)(2,1)S(1)} %shard_map.108.refs_2_), channel_id=1, source_target_pairs={{0,1},{1,0},{2,3},{3,2},{4,5},{5,4},{6,7},{7,6},{8,9},{9,8},{10,11... | collective-permute-start | bytes 589832 | tf_op jit(solution)/shard_map/ppermute | solution.py:501
  72.7 13.7 %collective-permute-start.13 = (bf16[256,1024]{1,0:T(8,128)(2,1)S(1)}, bf16[256,1024]{1,0:T(8,128)(2,1)S(1)}, u32[]{:S(2)}, u32[]{:S(2)}) collective-permute-start(bf16[256,1024]{1,0:T(8,128)(2,1)S(1)} %collective-permute-done.6.refs_0_), channel_id=1, source_target_pairs={{0,2},{2,0},{4,6},{6,4},{8,10},{10,8},{12,14},{14,12},{16,18},{18,... | collective-permute-start | bytes 1572872 | tf_op jit(solution)/shard_map/ppermute | solution.py:410
  74.4 9.9 %collective-permute-start.22 = (bf16[256,384]{1,0:T(8,128)(2,1)S(1)}, bf16[256,384]{1,0:T(8,128)(2,1)S(1)}, u32[]{:S(2)}, u32[]{:S(2)}) collective-permute-start(bf16[256,384]{1,0:T(8,128)(2,1)S(1)} %shard_map.109.refs_3_), channel_id=1, source_target_pairs={{0,1},{1,0},{2,3},{3,2},{4,5},{5,4},{6,7},{7,6},{8,9},{9,8},{10,11... | collective-permute-start | bytes 589832 | tf_op jit(solution)/shard_map/ppermute | solution.py:501
  76.9 11.5 %collective-permute-start.21 = (bf16[256,384]{1,0:T(8,128)(2,1)S(1)}, bf16[256,384]{1,0:T(8,128)(2,1)S(1)}, u32[]{:S(2)}, u32[]{:S(2)}) collective-permute-start(bf16[256,384]{1,0:T(8,128)(2,1)S(1)} %shard_map.110.refs_3_), channel_id=1, source_target_pairs={{0,1},{1,0},{2,3},{3,2},{4,5},{5,4},{6,7},{7,6},{8,9},{9,8},{10,11... | collective-permute-start | bytes 589832 | tf_op jit(solution)/shard_map/ppermute | solution.py:501
  79.4 12.3 %collective-permute-start.20 = (bf16[256,384]{1,0:T(8,128)(2,1)S(1)}, bf16[256,384]{1,0:T(8,128)(2,1)S(1)}, u32[]{:S(2)}, u32[]{:S(2)}) collective-permute-start(bf16[256,384]{1,0:T(8,128)(2,1)S(1)} %shard_map.111.refs_3_), channel_id=1, source_target_pairs={{0,1},{1,0},{2,3},{3,2},{4,5},{5,4},{6,7},{7,6},{8,9},{9,8},{10,11... | collective-permute-start | bytes 589832 | tf_op jit(solution)/shard_map/ppermute | solution.py:501
  83.2 11.2 %collective-permute-start.18 = (bf16[128,512]{1,0:T(8,128)(2,1)S(1)}, bf16[128,512]{1,0:T(8,128)(2,1)S(1)}, u32[]{:S(2)}, u32[]{:S(2)}) collective-permute-start(bf16[128,512]{1,0:T(8,128)(2,1)S(1)} %shard_map.112.refs_0_), channel_id=1, source_target_pairs={{0,1},{1,0},{2,3},{3,2},{4,5},{5,4},{6,7},{7,6},{8,9},{9,8},{10,11... | collective-permute-start | bytes 393224 | tf_op jit(solution)/shard_map/ppermute | solution.py:501
  84.3 12.4 %collective-permute-start.17 = (bf16[128,512]{1,0:T(8,128)(2,1)S(1)}, bf16[128,512]{1,0:T(8,128)(2,1)S(1)}, u32[]{:S(2)}, u32[]{:S(2)}) collective-permute-start(bf16[128,512]{1,0:T(8,128)(2,1)S(1)} %shard_map.113.refs_1_), channel_id=1, source_target_pairs={{0,1},{1,0},{2,3},{3,2},{4,5},{5,4},{6,7},{7,6},{8,9},{9,8},{10,11... | collective-permute-start | bytes 393224 | tf_op jit(solution)/shard_map/ppermute | solution.py:501
